TPU v7x, 32 devices: a whole 2x2x4 slice. The times are simulated.
32 devices in a mesh: groups: 2 (over y), blk: 4 (over z), col: 2 (over x), rep: 2 (over core).
Axes of the slice: x: 2, y: 2, z: 4, core: 2. Of those that a mesh axis runs over, the one named last changes fastest.
Arguments:
- blocks: bfloat16 [4, 2, 6, 128, 128], P('blk', 'col'), may hold values from -0.21875 to 0.21875
- block_index: int32 [4, 2, 6], P('blk', 'col'), may hold values from 0 to 7, as said below
- live: int32 [4, 2], P('blk', 'col'), may hold values from 3 to 6, as said below
- cost: float32 [1024, 512], P(('blk', 'col'), ('groups', 'rep')), parts along dimension 1
- rhs: float32 [1024, 512], P(('blk', 'col'), ('groups', 'rep')), parts along dimension 1
- upper: float32 [1024, 512], P(('blk', 'col'), ('groups', 'rep')), parts along dimension 1, may hold values from 0.5 to 1.5
- x_init: float32 [1024, 512], P(('blk', 'col'), ('groups', 'rep')), parts along dimension 1, may hold values from 0 to 1
- y_init: float32 [1024, 512], P(('blk', 'col'), ('groups', 'rep')), parts along dimension 1, may hold values from 0 to 1
- bounded: int32 [512], P(('groups', 'rep')), parts along dimension 0, may hold values from 0 to 1
Outputs:
- x_final: float32 [1024, 512], P(('blk', 'col'), ('groups', 'rep')), parts along dimension 1
- y_final: float32 [1024, 512], P(('blk', 'col'), ('groups', 'rep')), parts along dimension 1
There are 2 independent parts, one for each index of `groups`. A program takes and returns all parts, laid end to end along the dimension named above; an argument that names none is the same for every part. Nothing has to cross between parts.
Inputs may be any that keep to these rules, and one draw needn't show every extreme that they name: `block_index`: within one device the positions are distinct; a position p stands for block row p // 4 and block column p % 4 of the device's tile. `live`: some device uses all its slots.
All inputs are finite; a program needn't handle non-finite values.
Results may differ from a plain program's by a relative error of at most 0.0025.
Values may be sent and summed in bfloat16 or wider, within the bound.
No kernel may reach another device: no remote copies, remote signals or barrier semaphores. Data moves between devices by JAX's collectives and lax.ppermute only.
A program may use at most 64 MiB of HBM per device.

v0:
```python
import jax
import jax.numpy as jnp
from jax import lax
from jax.sharding import PartitionSpec as P

ITERS = 2


ETA = 0.4
EPS = 1e-06


def project_box(value, upper, bounded):
    capped = jnp.where(bounded[None, :] > 0, jnp.minimum(value, upper), value)
    return jnp.maximum(capped, 0.0)


def shards(blocks, block_index, live, cost, rhs, upper, x_init, y_init, bounded):
    block_mats = blocks[0, 0]
    slots = block_index[0, 0]
    n_blk = lax.axis_size("blk")
    n_col = lax.axis_size("col")
    tile_size = block_mats.shape[1]
    scn_count = cost.shape[1]
    row_block = slots // n_blk
    col_block = slots % n_blk
    keep_mask = (jnp.arange(slots.shape[0]) < live[0, 0]).astype(jnp.float32)[:, None, None]
    totals = lax.psum((jnp.sum(cost * cost, axis=0), jnp.sum(rhs * rhs, axis=0)), ("blk", "col"))
    weight = jnp.sqrt(totals[0] + EPS) / jnp.sqrt(totals[1] + EPS)
    tau = (ETA / weight)[None, :]
    sigma = (ETA * weight)[None, :]
    primal = x_init
    dual = y_init
    for step in range(ITERS):
        gathered = lax.all_gather(dual.astype(jnp.bfloat16), "col", axis=0, tiled=True)
        pieces = gathered.reshape(n_col, tile_size, scn_count)[row_block]
        products = (
            jnp.einsum("bkt,bks->bts", block_mats, pieces, preferred_element_type=jnp.float32)
            * keep_mask
        )
        cols = jnp.zeros((n_blk, tile_size, scn_count), jnp.float32).at[col_block].add(products)
        kty = lax.psum_scatter(
            cols.reshape(n_blk * tile_size, scn_count).astype(jnp.bfloat16),
            "blk",
            scatter_dimension=0,
            tiled=True,
        ).astype(jnp.float32)
        x_new = project_box(primal - tau * (cost - kty), upper, bounded)
        xbar = (2.0 * x_new - primal).astype(jnp.bfloat16)
        whole = lax.all_gather(xbar, "blk", axis=0, tiled=True)
        primal = x_new
        row_pieces = whole.reshape(n_blk, tile_size, scn_count)[col_block]
        row_products = (
            jnp.einsum("bkt,bts->bks", block_mats, row_pieces, preferred_element_type=jnp.float32)
            * keep_mask
        )
        rows = jnp.zeros((n_col, tile_size, scn_count), jnp.float32).at[row_block].add(row_products)
        terms = rows.reshape(n_col * tile_size, scn_count)
        kx = lax.psum_scatter(
            terms.astype(jnp.bfloat16), "col", scatter_dimension=0, tiled=True
        ).astype(jnp.float32)
        dual = jnp.maximum(dual + sigma * (rhs - kx), 0.0)
    return (primal, dual)


def solution(mesh):
    in_specs = (
        P("blk", "col", None, None, None),
        P("blk", "col", None),
        P("blk", "col"),
        P(("blk", "col"), ("groups", "rep")),
        P(("blk", "col"), ("groups", "rep")),
        P(("blk", "col"), ("groups", "rep")),
        P(("blk", "col"), ("groups", "rep")),
        P(("blk", "col"), ("groups", "rep")),
        P(("groups", "rep")),
    )
    out_specs = (P(("blk", "col"), ("groups", "rep")), P(("blk", "col"), ("groups", "rep")))
    return jax.shard_map(shards, mesh=mesh, in_specs=in_specs, out_specs=out_specs, check_vma=False)
```

profile of v0, /device:TPU:0, one launch (start us, length us, event | category | flops | bytes accessed | tf_op | source)
XLA Modules:
  0.0 127.2 jit_solution(12173755223038484867)
XLA Ops:
  7.2 0.0 copy-start
  7.2 0.0 reduce-scatter.5.cloned.1.call-start
  7.2 0.7 fusion.12
  7.9 0.8 convert_element_type.55
  8.8 5.5 %all_gather.12 = bf16[256,128]{1,0:T(8,128)(2,1)S(1)} all-gather(bf16[128,128]{1,0:T(8,128)(2,1)S(1)} %convert_element_type.55), channel_id=1, replica_groups=mesh['groups'=2,'blk'=4,'col'=2,'rep'=2] {'col'}, dimensions={0}, use_global_device_ids=true | all-gather | bytes 98304 | tf_op jit(solution)/shard_map/all_gather | solution.py:35
  14.9 0.6 gather_fusion
  15.5 0.0 copy-done
  15.5 0.3 fusion.3
  15.8 0.2 copy.16
  16.0 1.1 scatter_fusion
  17.1 0.7 convert_element_type.57
  17.7 0.0 copy-start.1
  17.7 0.0 copy-start.3
  17.7 0.0 reduce-scatter.5.cloned.1.call-update
  17.7 0.0 copy-start.4
  17.8 0.0 copy-start.6
  17.8 0.0 reduce-scatter.7.cloned.1.call-start
  17.8 0.7 copy-done.1
  18.6 0.0 copy-done.3
  18.6 22.2 %all-reduce = (f32[128]{0:T(128)S(1)}, f32[128]{0:T(128)S(1)}) all-reduce(f32[128]{0:T(128)S(1)} %get-tuple-element.12, f32[128]{0:T(128)S(1)} %get-tuple-element.13), channel_id=1, replica_groups=mesh['groups'=2,'blk'=4,'col'=2,'rep'=2] {'blk','col'}, use_global_device_ids=true, to_apply=%region_3.4 | all-reduce | flops 256 | bytes 2048 | tf_op jit(solution)/shard_map/psum | solution.py:28
  40.9 0.0 copy-start.7
  40.9 0.6 copy-done.7
  41.5 0.0 reduce-scatter.5.cloned.1.call-done
  41.5 0.0 copy-done.4
  41.5 0.0 copy-done.6
  41.5 0.8 subtract_convert_fusion.1
  42.3 13.4 %all_gather.13 = bf16[512,128]{1,0:T(8,128)(2,1)S(1)} all-gather(bf16[128,128]{1,0:T(8,128)(2,1)S(1)} %get-tuple-element.8), channel_id=1, replica_groups=mesh['groups'=2,'blk'=4,'col'=2,'rep'=2] {'blk'}, dimensions={0}, use_global_device_ids=true | all-gather | bytes 163840 | tf_op jit(solution)/shard_map/all_gather | solution.py:50
  55.7 0.6 gather_fusion.1
  56.3 0.3 fusion.2
  56.6 0.2 copy.18
  56.8 1.1 scatter_fusion.1
  57.9 0.6 convert_element_type.61
  58.5 0.0 copy-start.2
  58.5 0.0 reduce-scatter.7.cloned.1.call-update
  58.5 0.0 reduce-scatter.9.cloned.1.call-start
  58.6 7.3 %reduce-scatter.7.cloned.1.call-done = bf16[128,128]{1,0:T(8,128)(2,1)} async-done(((bf16[256,128]{1,0:T(8,128)(2,1)}), bf16[128,128]{1,0:T(8,128)(2,1)}) %reduce-scatter.7.cloned.1.call-update) | async-done | bytes 32784 | tf_op jit(solution)/shard_map/reduce_scatter | solution.py:59
  65.9 0.0 copy-done.2
  65.9 0.8 fusion.10
  66.7 4.6 %all_gather.14 = bf16[256,128]{1,0:T(8,128)(2,1)S(1)} all-gather(bf16[128,128]{1,0:T(8,128)(2,1)S(1)} %fusion.10), channel_id=1, replica_groups=mesh['groups'=2,'blk'=4,'col'=2,'rep'=2] {'col'}, dimensions={0}, use_global_device_ids=true | all-gather | bytes 98304 | tf_op jit(solution)/shard_map/all_gather | solution.py:35
  71.3 0.6 gather_fusion.2
  71.9 0.3 fusion.1
  72.1 0.2 copy.20
  72.3 1.1 scatter_fusion.2
  73.4 0.7 convert_element_type.65
  74.1 0.0 reduce-scatter.9.cloned.1.call-update
  74.1 0.0 reduce-scatter.11.cloned.1.call-start
  74.1 19.2 %reduce-scatter.9.cloned.1.call-done = bf16[128,128]{1,0:T(8,128)(2,1)} async-done(((bf16[512,128]{1,0:T(8,128)(2,1)}), bf16[128,128]{1,0:T(8,128)(2,1)}) %reduce-scatter.9.cloned.1.call-update) | async-done | bytes 32784 | tf_op jit(solution)/shard_map/reduce_scatter | solution.py:42
  93.4 1.4 %subtract_convert_fusion = (bf16[128,128]{1,0:T(8,128)(2,1)S(1)}, f32[128,128]{1,0:T(8,128)}) fusion(f32[128,128]{1,0:T(8,128)S(1)} %get-tuple-element.9, f32[128,128]{1,0:T(8,128)S(1)} %copy-done.4, f32[128,128]{1,0:T(8,128)S(1)} %copy-done.1, bf16[128,128]{1,0:T(8,128)(2,1)} %reduce-scatter.9.cloned.1.call-done, f32[128]{0:T(128)S(1)} %broadcast_divide_fusion, ...), kind=kLoop, calls=%fused_computation.25 | loop fusion | flops 163840 | bytes 328320 | tf_op jit(solution)/shard_map/convert_element_type | solution.py:49
  94.8 13.3 %all_gather.15 = bf16[512,128]{1,0:T(8,128)(2,1)S(1)} all-gather(bf16[128,128]{1,0:T(8,128)(2,1)S(1)} %get-tuple-element.4), channel_id=1, replica_groups=mesh['groups'=2,'blk'=4,'col'=2,'rep'=2] {'blk'}, dimensions={0}, use_global_device_ids=true | all-gather | bytes 163840 | tf_op jit(solution)/shard_map/all_gather | solution.py:50
  108.1 0.6 gather_fusion.3
  108.7 0.3 fusion
  109.0 0.2 copy.22
  109.2 1.1 scatter_fusion.3
  110.3 0.6 convert_element_type.69
  110.9 0.0 copy-start.5
  110.9 0.0 reduce-scatter.11.cloned.1.call-update
  110.9 8.3 %reduce-scatter.11.cloned.1.call-done = bf16[128,128]{1,0:T(8,128)(2,1)} async-done(((bf16[256,128]{1,0:T(8,128)(2,1)}), bf16[128,128]{1,0:T(8,128)(2,1)}) %reduce-scatter.11.cloned.1.call-update) | async-done | bytes 32784 | tf_op jit(solution)/shard_map/reduce_scatter | solution.py:59
  119.2 0.0 copy-done.5
  119.2 1.4 %add_maximum_fusion = f32[128,128]{1,0:T(8,128)} fusion(f32[128,128]{1,0:T(8,128)S(1)} %copy-done.3, bf16[128,128]{1,0:T(8,128)(2,1)} %reduce-scatter.11.cloned.1.call-done, f32[128,128]{1,0:T(8,128)S(1)} %copy-done.2, bf16[128,128]{1,0:T(8,128)(2,1)S(1)} %copy-done.5, f32[128]{0:T(128)S(1)} %get-tuple-element.6), kind=kLoop, calls=%fused_computation.24 | loop fusion | flops 163840 | bytes 262656 | tf_op jit(solution)/shard_map/max | solution.py:62
  (11 shorter events, 0.1 us)
Async XLA Ops:
  7.2 8.3 %copy-start = (bf16[1,1,6,128,128]{4,3,2,1,0:T(8,128)(2,1)S(1)}, bf16[1,1,6,128,128]{4,3,2,1,0:T(8,128)(2,1)}, u32[]{:S(2)}) copy-start(bf16[1,1,6,128,128]{4,3,2,1,0:T(8,128)(2,1)} %param.9) | copy-start | bytes 589828
  7.2 34.4 %reduce-scatter.5.cloned.1.call-start = ((), (), s32[]{:S(2)}) async-start(), calls=%async_computation.4 | async-start | bytes 163840 | tf_op jit(solution)/shard_map/reduce_scatter | solution.py:42
  17.7 0.8 copy-start.1
  17.7 0.9 copy-start.3
  17.7 23.8 %copy-start.4 = (f32[128,128]{1,0:T(8,128)S(1)}, f32[128,128]{1,0:T(8,128)}, u32[]{:S(2)}) copy-start(f32[128,128]{1,0:T(8,128)} %param.14) | copy-start | bytes 196612
  17.8 23.8 %copy-start.6 = (f32[128,128]{1,0:T(8,128)S(1)}, f32[128,128]{1,0:T(8,128)}, u32[]{:S(2)}) copy-start(f32[128,128]{1,0:T(8,128)} %param.15) | copy-start | bytes 196612
  17.8 48.1 %reduce-scatter.7.cloned.1.call-start = ((), (), s32[]{:S(2)}) async-start(), calls=%async_computation.5 | async-start | bytes 98304 | tf_op jit(solution)/shard_map/reduce_scatter | solution.py:59
  40.9 0.7 copy-start.7
  58.5 7.4 %copy-start.2 = (f32[128,128]{1,0:T(8,128)S(1)}, f32[128,128]{1,0:T(8,128)}, u32[]{:S(2)}) copy-start(f32[128,128]{1,0:T(8,128)} %param.16) | copy-start | bytes 196612
  58.5 34.8 %reduce-scatter.9.cloned.1.call-start = ((), (), s32[]{:S(2)}) async-start(), calls=%async_computation.6 | async-start | bytes 163840 | tf_op jit(solution)/shard_map/reduce_scatter | solution.py:42
  74.1 45.2 %reduce-scatter.11.cloned.1.call-start = ((), (), s32[]{:S(2)}) async-start(), calls=%async_computation.7 | async-start | bytes 98304 | tf_op jit(solution)/shard_map/reduce_scatter | solution.py:59
  110.9 8.3 %copy-start.5 = (bf16[128,128]{1,0:T(8,128)(2,1)S(1)}, bf16[128,128]{1,0:T(8,128)(2,1)}, u32[]{:S(2)}) copy-start(bf16[128,128]{1,0:T(8,128)(2,1)} %reduce-scatter.7.cloned.1.call-done) | copy-start | bytes 98308
Sparse Core Ops, SparseCore 0:
  17.9 20.9 reduce-scatter.4
  58.7 7.1 reduce-scatter.6
  74.2 19.1 reduce-scatter.8
  111.1 8.1 reduce-scatter.10
where the time goes:
time: 128 us; the launch traced here: 127 us
  blocking collectives  59 us (46%)
  waiting for transfers between devices  34.9 us (27%)
  between operations  14.7 us (11%)
  other arithmetic  12.9 us (10%)
  local copies, waits for them, and re-layouts  4.49 us (4%)
    all_gather x2, blocking collectives, shards(): whole = lax.all_gather(xbar, 'blk', axis=0, tiled=True)  26.7 us
    psum x1, blocking collectives, shards(): lax.psum((jnp.sum(cost * cost, axis=0), jnp.sum(rhs * rhs, axis=0)), ('bl...  22.2 us
    reduce_scatter x2, waiting for transfers between devices, shards(): lax.psum_scatter(cols.reshape(n_blk * tile_size, scn_count).astype(jnp.bf...  19.2 us
    reduce_scatter x2, waiting for transfers between devices, shards(): lax.psum_scatter(terms.astype(jnp.bfloat16), 'col', scatter_dimension=0,...  15.6 us
    all_gather x2, blocking collectives, shards(): lax.all_gather(dual.astype(jnp.bfloat16), 'col', axis=0, tiled=True)  10.1 us
  transfers between devices with their start and end apart: 4, of which 3 were waited for; matrix products, arithmetic and copies ran while one was open for 0% of the time, Pallas kernels for 0%

commit v1 on v0

--- a/solution.py
+++ b/solution.py
@@ -1,6 +1,10 @@
+import functools
+
 import jax
 import jax.numpy as jnp
 from jax import lax
+from jax.experimental import pallas as pl
+from jax.experimental.pallas import tpu as pltpu
 from jax.sharding import PartitionSpec as P
 
 ITERS = 2
@@ -8,6 +12,240 @@
 
 ETA = 0.4
 EPS = 1e-06
+MAX_PEERS = 16
+SPLIT_ROWS = 16
+
+VMEM = pl.BlockSpec(memory_space=pltpu.VMEM)
+SMEM = pl.BlockSpec(memory_space=pltpu.SMEM)
+F32 = jnp.float32
+BF16 = jnp.bfloat16
+
+
+def call(body, outs, ins_specs, args, scratch=(), flops=0):
+    nbytes = sum(a.size * a.dtype.itemsize for a in list(args) + list(outs))
+    return pl.pallas_call(
+        body,
+        out_shape=list(outs),
+        in_specs=ins_specs,
+        out_specs=[VMEM] * len(outs),
+        scratch_shapes=list(scratch),
+        compiler_params=pltpu.CompilerParams(vmem_limit_bytes=32 * 1024 * 1024),
+        cost_estimate=pl.CostEstimate(flops=flops, bytes_accessed=nbytes, transcendentals=0),
+    )(*args)
+
+
+def split_sums(values):
+    high = values.astype(BF16)
+    rest = values - high.astype(F32)
+    middle = rest.astype(BF16)
+    low = (rest - middle.astype(F32)).astype(BF16)
+    return [high, middle, low]
+
+
+def pack_sums(cost_sum, rhs_sum):
+    rows = [r.astype(F32) for r in split_sums(cost_sum) + split_sums(rhs_sum)]
+    rows.append(jnp.zeros((SPLIT_ROWS - len(rows), cost_sum.shape[1]), F32))
+    return jnp.concatenate(rows, axis=0).astype(BF16)
+
+
+def unpack_sums(packed):
+    rows = packed.astype(F32)
+    return rows[0:1] + rows[1:2] + rows[2:3], rows[3:4] + rows[4:5] + rows[5:6]
+
+
+def prep_body(cost, rhs, y, out):
+    tile = y.shape[0]
+    out[0:tile, :] = y[...].astype(BF16)
+    c, r = cost[...], rhs[...]
+    out[tile:, :] = pack_sums(jnp.sum(c * c, axis=0, keepdims=True), jnp.sum(r * r, axis=0, keepdims=True))
+
+
+def dense_body(n_blk, n_col, index, live, blocks, *outs):
+    tile = blocks.shape[-1]
+    me_c = lax.axis_index("col")
+    for out in outs:
+        out[...] = jnp.zeros(out.shape, BF16)
+
+    def one(k, carry):
+        position = index[0, 0, k]
+        rel = (position // n_blk) ^ me_c
+        col = position % n_blk
+        for s, out in enumerate(outs):
+
+            @pl.when(rel == s)
+            def _():
+                out[:, pl.ds(pl.multiple_of(col * tile, tile), tile)] = blocks[0, 0, k]
+
+        return carry
+
+    lax.fori_loop(0, live[0, 0], one, 0)
+
+
+def transposed_dot(mat, vec):
+    return lax.dot_general(mat, vec, (((0,), (0,)), ((), ())), preferred_element_type=F32)
+
+
+def first_terms_body(n_blk, n_col, *refs):
+    payloads, mats = refs[:n_col], refs[n_col : 2 * n_col]
+    outs, scratch = refs[2 * n_col : 2 * n_col + n_blk], refs[-1]
+    tile = mats[0].shape[0]
+    me_b = lax.axis_index("blk")
+    total = transposed_dot(mats[0][...], payloads[0][0:tile, :])
+    cost_sum, rhs_sum = unpack_sums(payloads[0][tile:, :])
+    for s in range(1, n_col):
+        total += transposed_dot(mats[s][...], payloads[s][0:tile, :])
+        c, r = unpack_sums(payloads[s][tile:, :])
+        cost_sum += c
+        rhs_sum += r
+    scratch[...] = total
+    packed = pack_sums(cost_sum, rhs_sum)
+    for t, out in enumerate(outs):
+        rows = pl.ds(pl.multiple_of((me_b ^ t) * tile, tile), tile)
+        out[0:tile, :] = scratch[rows, :].astype(BF16)
+        out[tile:, :] = packed
+
+
+def project(primal, grad, tau, upper, bounded):
+    value = primal - tau * grad
+    capped = jnp.where(bounded > 0, jnp.minimum(value, upper), value)
+    return jnp.maximum(capped, 0.0)
+
+
+def first_primal_body(n_blk, *refs):
+    terms = refs[:n_blk]
+    cost, primal, upper, bounded = refs[n_blk : n_blk + 4]
+    x_out, xbar_out, scales_out = refs[n_blk + 4 :]
+    tile = cost.shape[0]
+    kty = terms[0][0:tile, :].astype(F32)
+    cost_sum, rhs_sum = unpack_sums(terms[0][tile:, :])
+    for term in terms[1:]:
+        kty += term[0:tile, :].astype(F32)
+        c, r = unpack_sums(term[tile:, :])
+        cost_sum += c
+        rhs_sum += r
+    weight = jnp.sqrt(cost_sum + EPS) / jnp.sqrt(rhs_sum + EPS)
+    tau = ETA / weight
+    sigma = ETA * weight
+    scales_out[...] = jnp.concatenate([tau, sigma, jnp.zeros((6, tau.shape[1]), F32)], axis=0)
+    x = primal[...]
+    x_new = project(x, cost[...] - kty, tau, upper[...], bounded[...])
+    x_out[...] = x_new
+    xbar_out[...] = (2.0 * x_new - x).astype(BF16)
+
+
+def primal_body(n, last, *refs):
+    terms = refs[:n]
+    cost, primal, upper, bounded, scales = refs[n : n + 5]
+    x_out, xbar_out = refs[n + 5 :]
+    kty = terms[0][...].astype(F32)
+    for term in terms[1:]:
+        kty += term[...].astype(F32)
+    x = primal[...]
+    x_new = project(x, cost[...] - kty, scales[0:1, :], upper[...], bounded[...])
+    x_out[...] = x_new
+    xbar_out[...] = (2.0 * x_new - x).astype(BF16)
+
+
+def dual_body(n_blk, n_col, last, *refs):
+    n = n_blk * n_col
+    bars, slabs = refs[:n], refs[n : n + n_col]
+    dual, rhs, scales = refs[n + n_col : n + n_col + 3]
+    y_out = refs[n + n_col + 3]
+    tile = dual.shape[0]
+    me_b = lax.axis_index("blk")
+    field = refs[-2]
+    scratch = refs[-1]
+    kx = jnp.zeros(dual.shape, F32)
+    for s in range(n_col):
+        for t in range(n_blk):
+            rows = pl.ds(pl.multiple_of((me_b ^ t) * tile, tile), tile)
+            field[s, rows, :] = bars[t * n_col + s][...]
+        kx += jnp.dot(slabs[s][...], field[s], preferred_element_type=F32)
+    y_new = jnp.maximum(dual[...] + scales[1:2, :] * (rhs[...] - kx), 0.0)
+    y_out[...] = y_new
+    if not last:
+        outs = refs[n + n_col + 4 : n + n_col + 4 + n]
+        y_half = y_new.astype(BF16)
+        for s in range(n_col):
+            scratch[...] = transposed_dot(slabs[s][...], y_half)
+            for t in range(n_blk):
+                rows = pl.ds(pl.multiple_of((me_b ^ t) * tile, tile), tile)
+                outs[t * n_col + s][...] = scratch[rows, :].astype(BF16)
+
+
+def direct_plan(blocks, block_index, live, cost, rhs, upper, x_init, y_init, bounded):
+    n_blk = lax.axis_size("blk")
+    n_col = lax.axis_size("col")
+    n = n_blk * n_col
+    tile = blocks.shape[-1]
+    scn = cost.shape[1]
+    like = jax.ShapeDtypeStruct
+    field_f32 = like((tile, scn), F32)
+    field_half = like((tile, scn), BF16)
+    payload = like((tile + SPLIT_ROWS, scn), BF16)
+    limits = bounded[None, :]
+
+    def over_col(value, s):
+        return lax.ppermute(value, "col", [(c, c ^ s) for c in range(n_col)])
+
+    def over_blk(value, t):
+        return lax.ppermute(value, "blk", [(b, b ^ t) for b in range(n_blk)])
+
+    def over_both(value, t, s):
+        pairs = [(b * n_col + c, (b ^ t) * n_col + (c ^ s)) for b in range(n_blk) for c in range(n_col)]
+        return lax.ppermute(value, ("blk", "col"), pairs)
+
+    shifts = [(t, s) for t in range(n_blk) for s in range(n_col)]
+
+    def spread(values):
+        return [v if (t, s) == (0, 0) else over_both(v, t, s) for v, (t, s) in zip(values, shifts)]
+
+    (own,) = call(prep_body, [payload], [VMEM] * 3, [cost, rhs, y_init])
+    payloads = [own] + [over_col(own, s) for s in range(1, n_col)]
+    mats = call(
+        functools.partial(dense_body, n_blk, n_col),
+        [like((tile, n_blk * tile), BF16)] * n_col,
+        [SMEM, SMEM, VMEM],
+        [block_index, live, blocks],
+    )
+    slabs = [mats[0]] + [over_col(mats[s], s) for s in range(1, n_col)]
+    terms = call(
+        functools.partial(first_terms_body, n_blk, n_col),
+        [payload] * n_blk,
+        [VMEM] * (2 * n_col),
+        payloads + list(mats),
+        scratch=[pltpu.VMEM((n_blk * tile, scn), F32)],
+        flops=2 * n * tile * tile * scn,
+    )
+    terms = [terms[0]] + [over_blk(terms[t], t) for t in range(1, n_blk)]
+    primal, xbar, scales = call(
+        functools.partial(first_primal_body, n_blk),
+        [field_f32, field_half, like((8, scn), F32)],
+        [VMEM] * (n_blk + 4),
+        terms + [cost, x_init, upper, limits],
+    )
+    dual = y_init
+    for step in range(ITERS):
+        last = step == ITERS - 1
+        bars = spread([xbar] * n)
+        outs = call(
+            functools.partial(dual_body, n_blk, n_col, last),
+            [field_f32] + ([] if last else [field_half] * n),
+            [VMEM] * (n + n_col + 3),
+            bars + slabs + [dual, rhs, scales],
+            scratch=[pltpu.VMEM((n_col, n_blk * tile, scn), BF16), pltpu.VMEM((n_blk * tile, scn), F32)],
+            flops=4 * n * tile * tile * scn,
+        )
+        dual = outs[0]
+        if not last:
+            terms = spread(outs[1:])
+            primal, xbar = call(
+                functools.partial(primal_body, n, last),
+                [field_f32, field_half],
+                [VMEM] * (n + 5),
+                terms + [cost, primal, upper, limits, scales],
+            )
+    return (primal, dual)
 
 
 def project_box(value, upper, bounded):
@@ -15,7 +253,7 @@
     return jnp.maximum(capped, 0.0)
 
 
-def shards(blocks, block_index, live, cost, rhs, upper, x_init, y_init, bounded):
+def collectives_plan(blocks, block_index, live, cost, rhs, upper, x_init, y_init, bounded):
     block_mats = blocks[0, 0]
     slots = block_index[0, 0]
     n_blk = lax.axis_size("blk")
@@ -63,6 +301,13 @@
     return (primal, dual)
 
 
+def shards(*args):
+    n_blk, n_col = lax.axis_size("blk"), lax.axis_size("col")
+    powers = n_blk & (n_blk - 1) == 0 and n_col & (n_col - 1) == 0
+    plan = direct_plan if powers and n_blk * n_col <= MAX_PEERS else collectives_plan
+    return plan(*args)
+
+
 def solution(mesh):
     in_specs = (
         P("blk", "col", None, None, None),

time: 128 us -> 64.8 us (0.51)
  blocking collectives: 59 us -> 0 us
  starting transfers between devices: 0.16 us -> 41.5 us
  waiting for transfers between devices: 34.9 us -> 15.3 us
  between operations: 14.7 us -> 1.39 us
  other arithmetic: 12.9 us -> 0 us
  Pallas kernels: 0 us -> 3.15 us
  local copies, waits for them, and re-layouts: 4.49 us -> 3.18 us
    ppermute x0 -> x26, starting transfers between devices: none -> 41.5 us  [the longest x21 33.5 us: over_both(): return lax.ppermute(value, ('blk', 'col'), pairs)]
    all_gather x4 -> x0, blocking collectives: 36.8 us -> none  [the longest x2 26.7 us: shards(): whole = lax.all_gather(xbar, 'blk', axis=0, tiled=True)]
    reduce_scatter x4 -> x0, waiting for transfers between devices: 34.9 us -> none  [the longest x2 19.2 us: shards(): lax.psum_scatter(cols.reshape(n_blk * tile_size, scn_count).astype(jnp.bf...]
    psum x1 -> x0, blocking collectives: 22.2 us -> none  [shards(): lax.psum((jnp.sum(cost * cost, axis=0), jnp.sum(rhs * rhs, axis=0)), ('bl...]
    ppermute x0 -> x26, waiting for transfers between devices: none -> 15.3 us  [the longest x21 9.17 us: over_both(): return lax.ppermute(value, ('blk', 'col'), pairs)]
    convert_element_type x9 -> x0, other arithmetic: 6.41 us -> none  [the longest x2 2.2 us: shards(): xbar = (2.0 * x_new - primal).astype(jnp.bfloat16)]
    scatter-add x4 -> x0, other arithmetic: 4.27 us -> none  [the longest x2 2.13 us: shards(): jnp.zeros((n_blk, tile_size, scn_count), jnp.float32).at[col_block]]
    pallas_call x0 -> x7, Pallas kernels: none -> 3.15 us  [call(): pl.pallas_call(body, out_shape=list(outs), in_specs=ins_specs, out_specs=...]
  transfers between devices with their start and end apart: 4 -> 26, of which waited for: 3 -> 11; matrix products, arithmetic and copies ran while one was open for 0% -> 0% of each run, Pallas kernels for 0% -> 2%
where the time goes in v1:
time: 64.8 us; the launch traced here: 64.5 us
  starting transfers between devices  41.5 us (64%)
  waiting for transfers between devices  15.3 us (24%)
  local copies, waits for them, and re-layouts  3.18 us (5%)
  Pallas kernels  3.15 us (5%)
  between operations  1.39 us (2%)
    ppermute x21, starting transfers between devices, over_both(): return lax.ppermute(value, ('blk', 'col'), pairs)  33.5 us
    ppermute x21, waiting for transfers between devices, over_both(): return lax.ppermute(value, ('blk', 'col'), pairs)  9.17 us
    ppermute x3, waiting for transfers between devices, over_blk(): return lax.ppermute(value, 'blk', [(b, b ^ t) for b in range(n_blk)])  5.78 us
    ppermute x3, starting transfers between devices, over_blk(): return lax.ppermute(value, 'blk', [(b, b ^ t) for b in range(n_blk)])  4.77 us
    ppermute x2, starting transfers between devices, over_col(): return lax.ppermute(value, 'col', [(c, c ^ s) for c in range(n_col)])  3.24 us
    unnamed x22, local copies, waits for them, and re-layouts  3.18 us
    pallas_call x7, Pallas kernels, call(): pl.pallas_call(body, out_shape=list(outs), in_specs=ins_specs, out_specs=...  3.15 us
  transfers between devices with their start and end apart: 26, of which 11 were waited for; matrix products, arithmetic and copies ran while one was open for 0% of the time, Pallas kernels for 2%

profile of v1, /device:TPU:0, one launch (start us, length us, event | category | flops | bytes accessed | tf_op | source)
XLA Modules:
  0.0 64.5 jit_solution(7282864949184732540)
XLA Ops:
  0.6 0.0 copy-start
  0.6 0.8 %copy-done = f32[128,128]{1,0:T(8,128)S(1)} copy-done((f32[128,128]{1,0:T(8,128)S(1)}, f32[128,128]{1,0:T(8,128)}, u32[]{:S(2)}) %copy-start) | copy-done | bytes 65560
  1.5 0.8 %copy-done.2 = f32[128,128]{1,0:T(8,128)S(1)} copy-done((f32[128,128]{1,0:T(8,128)S(1)}, f32[128,128]{1,0:T(8,128)}, u32[]{:S(2)}) %copy-start.2) | copy-done | bytes 65560
  2.3 0.8 %copy-done.4 = f32[128,128]{1,0:T(8,128)S(1)} copy-done((f32[128,128]{1,0:T(8,128)S(1)}, f32[128,128]{1,0:T(8,128)}, u32[]{:S(2)}) %copy-start.4) | copy-done | bytes 65560
  3.2 3.0 %collective-permute-start = (bf16[144,128]{1,0:T(8,128)(2,1)S(1)}, bf16[144,128]{1,0:T(8,128)(2,1)S(1)}, u32[]{:S(2)}, u32[]{:S(2)}) collective-permute-start(bf16[144,128]{1,0:T(8,128)(2,1)S(1)} %shard_map.104.refs_0_), channel_id=1, source_target_pairs={{0,2},{2,0},{1,3},{3,1},{4,6},{6,4},{5,7},{7,5},{8,10},{10,8},{9,1... | collective-permute-start | bytes 110600 | tf_op jit(solution)/shard_map/ppermute | solution.py:189
  6.9 0.0 copy-done.7
  6.9 0.7 %shard_map.105 = (bf16[128,512]{1,0:T(8,128)(2,1)S(1)}, bf16[128,512]{1,0:T(8,128)(2,1)S(1)}) custom-call(s32[1,1,6]{2,1,0:T(1,128)S(1)} %copy-done.10, s32[1,1]{1,0:T(1,128)S(6)} %copy.11.live, bf16[1,1,6,128,128]{4,3,2,1,0:T(8,128)(2,1)S(1)} %copy-done.7), custom_call_target="tpu_custom_call" | custom-call | bytes 458780 | tf_op jit(solution)/shard_map/pallas_call | solution.py:26
  7.6 0.2 collective-permute-start.11
  7.8 0.3 collective-permute-done.refs_1_
  8.2 0.3 shard_map.106
  8.4 2.2 %collective-permute-start.1 = (bf16[144,128]{1,0:T(8,128)(2,1)S(1)}, bf16[144,128]{1,0:T(8,128)(2,1)S(1)}, u32[]{:S(2)}, u32[]{:S(2)}) collective-permute-start(bf16[144,128]{1,0:T(8,128)(2,1)S(1)} %get-tuple-element.25), channel_id=1, source_target_pairs={{0,4},{4,0},{8,12},{12,8},{1,5},{5,1},{9,13},{13,9},{2,6},{6,2},{1... | collective-permute-start | bytes 110600 | tf_op jit(solution)/shard_map/ppermute | solution.py:192
  10.6 2.6 %collective-permute-start.2 = (bf16[144,128]{1,0:T(8,128)(2,1)S(1)}, bf16[144,128]{1,0:T(8,128)(2,1)S(1)}, u32[]{:S(2)}, u32[]{:S(2)}) collective-permute-start(bf16[144,128]{1,0:T(8,128)(2,1)S(1)} %get-tuple-element.26), channel_id=1, source_target_pairs={{0,8},{4,12},{8,0},{12,4},{1,9},{5,13},{9,1},{13,5},{2,10},{6,14},... | collective-permute-start | bytes 110600 | tf_op jit(solution)/shard_map/ppermute | solution.py:192
  13.2 0.0 collective-permute-start.3
  13.2 0.0 collective-permute-done.1.refs_1_
  13.2 2.6 %collective-permute-done.2.refs_2_ = bf16[144,128]{1,0:T(8,128)(2,1)S(1)} collective-permute-done((bf16[144,128]{1,0:T(8,128)(2,1)S(1)}, bf16[144,128]{1,0:T(8,128)(2,1)S(1)}, u32[]{:S(2)}, u32[]{:S(2)}) %collective-permute-start.2) | collective-permute-done | bytes 36896 | tf_op jit(solution)/shard_map/ppermute | solution.py:192
  15.8 3.2 %collective-permute-done.3.refs_3_ = bf16[144,128]{1,0:T(8,128)(2,1)S(1)} collective-permute-done((bf16[144,128]{1,0:T(8,128)(2,1)S(1)}, bf16[144,128]{1,0:T(8,128)(2,1)S(1)}, u32[]{:S(2)}, u32[]{:S(2)}) %collective-permute-start.3) | collective-permute-done | bytes 36896 | tf_op jit(solution)/shard_map/ppermute | solution.py:192
  19.0 0.0 copy-done.6
  19.0 0.6 copy-done.9
  19.7 1.4 %collective-permute-start.10 = (bf16[128,128]{1,0:T(8,128)(2,1)S(1)}, bf16[128,128]{1,0:T(8,128)(2,1)S(1)}, u32[]{:S(2)}, u32[]{:S(2)}) collective-permute-start(bf16[128,128]{1,0:T(8,128)(2,1)S(1)} %get-tuple-element.28.refs_0_), channel_id=1, source_target_pairs={{0,14},{2,12},{4,10},{6,8},{8,6},{10,4},{12,2},{14,0},{1,15},{3,13... | collective-permute-start | bytes 98312 | tf_op jit(solution)/shard_map/ppermute | solution.py:196
  21.1 3.5 %collective-permute-start.9 = (bf16[128,128]{1,0:T(8,128)(2,1)S(1)}, bf16[128,128]{1,0:T(8,128)(2,1)S(1)}, u32[]{:S(2)}, u32[]{:S(2)}) collective-permute-start(bf16[128,128]{1,0:T(8,128)(2,1)S(1)} %get-tuple-element.28.refs_0_), channel_id=1, source_target_pairs={{0,12},{2,14},{4,8},{6,10},{8,4},{10,6},{12,0},{14,2},{1,13},{3,15... | collective-permute-start | bytes 98312 | tf_op jit(solution)/shard_map/ppermute | solution.py:196
  24.5 0.0 collective-permute-start.8
  24.5 2.9 %collective-permute-start.7 = (bf16[128,128]{1,0:T(8,128)(2,1)S(1)}, bf16[128,128]{1,0:T(8,128)(2,1)S(1)}, u32[]{:S(2)}, u32[]{:S(2)}) collective-permute-start(bf16[128,128]{1,0:T(8,128)(2,1)S(1)} %get-tuple-element.28.refs_0_), channel_id=1, source_target_pairs={{0,8},{2,10},{4,12},{6,14},{8,0},{10,2},{12,4},{14,6},{1,9},{3,11}... | collective-permute-start | bytes 98312 | tf_op jit(solution)/shard_map/ppermute | solution.py:196
  27.4 0.0 collective-permute-done.10.refs_7_
  27.4 0.0 collective-permute-start.6
  27.4 0.0 collective-permute-done.9.refs_6_
  27.4 2.9 %collective-permute-start.5 = (bf16[128,128]{1,0:T(8,128)(2,1)S(1)}, bf16[128,128]{1,0:T(8,128)(2,1)S(1)}, u32[]{:S(2)}, u32[]{:S(2)}) collective-permute-start(bf16[128,128]{1,0:T(8,128)(2,1)S(1)} %get-tuple-element.28.refs_0_), channel_id=1, source_target_pairs={{0,4},{2,6},{4,0},{6,2},{8,12},{10,14},{12,8},{14,10},{1,5},{3,7},... | collective-permute-start | bytes 98312 | tf_op jit(solution)/shard_map/ppermute | solution.py:196
  30.4 0.0 collective-permute-done.8.refs_5_
  30.4 0.5 collective-permute-start.4
  30.9 0.0 collective-permute-done.7.refs_4_
  30.9 1.4 %collective-permute-done.6.refs_3_ = bf16[128,128]{1,0:T(8,128)(2,1)S(1)} collective-permute-done((bf16[128,128]{1,0:T(8,128)(2,1)S(1)}, bf16[128,128]{1,0:T(8,128)(2,1)S(1)}, u32[]{:S(2)}, u32[]{:S(2)}) %collective-permute-start.6) | collective-permute-done | bytes 32800 | tf_op jit(solution)/shard_map/ppermute | solution.py:196
  32.4 0.6 collective-permute-done.5.refs_2_
  33.0 1.3 %collective-permute-done.4.refs_1_ = bf16[128,128]{1,0:T(8,128)(2,1)S(1)} collective-permute-done((bf16[128,128]{1,0:T(8,128)(2,1)S(1)}, bf16[128,128]{1,0:T(8,128)(2,1)S(1)}, u32[]{:S(2)}, u32[]{:S(2)}) %collective-permute-start.4) | collective-permute-done | bytes 32800 | tf_op jit(solution)/shard_map/ppermute | solution.py:196
  34.3 0.0 collective-permute-done.11.refs_9_
  34.3 0.5 shard_map.108
  34.8 1.0 %collective-permute-start.12 = (bf16[128,128]{1,0:T(8,128)(2,1)S(1)}, bf16[128,128]{1,0:T(8,128)(2,1)S(1)}, u32[]{:S(2)}, u32[]{:S(2)}) collective-permute-start(bf16[128,128]{1,0:T(8,128)(2,1)S(1)} %get-tuple-element.31), channel_id=1, source_target_pairs={{0,2},{2,0},{4,6},{6,4},{8,10},{10,8},{12,14},{14,12},{1,3},{3,1},... | collective-permute-start | bytes 98312 | tf_op jit(solution)/shard_map/ppermute | solution.py:196
  35.8 0.0 collective-permute-start.13
  35.8 2.6 %collective-permute-start.14 = (bf16[128,128]{1,0:T(8,128)(2,1)S(1)}, bf16[128,128]{1,0:T(8,128)(2,1)S(1)}, u32[]{:S(2)}, u32[]{:S(2)}) collective-permute-start(bf16[128,128]{1,0:T(8,128)(2,1)S(1)} %get-tuple-element.33), channel_id=1, source_target_pairs={{0,6},{2,4},{4,2},{6,0},{8,14},{10,12},{12,10},{14,8},{1,7},{3,5},... | collective-permute-start | bytes 98312 | tf_op jit(solution)/shard_map/ppermute | solution.py:196
  38.4 0.5 collective-permute-start.15
  38.9 2.7 %collective-permute-start.16 = (bf16[128,128]{1,0:T(8,128)(2,1)S(1)}, bf16[128,128]{1,0:T(8,128)(2,1)S(1)}, u32[]{:S(2)}, u32[]{:S(2)}) collective-permute-start(bf16[128,128]{1,0:T(8,128)(2,1)S(1)} %get-tuple-element.35), channel_id=1, source_target_pairs={{0,10},{2,8},{4,14},{6,12},{8,2},{10,0},{12,6},{14,4},{1,11},{3,9}... | collective-permute-start | bytes 98312 | tf_op jit(solution)/shard_map/ppermute | solution.py:196
  41.6 0.0 collective-permute-done.12.refs_1_
  41.6 0.3 collective-permute-start.17
  42.0 0.0 collective-permute-done.13.refs_2_
  42.0 4.1 %collective-permute-start.18 = (bf16[128,128]{1,0:T(8,128)(2,1)S(1)}, bf16[128,128]{1,0:T(8,128)(2,1)S(1)}, u32[]{:S(2)}, u32[]{:S(2)}) collective-permute-start(bf16[128,128]{1,0:T(8,128)(2,1)S(1)} %get-tuple-element.37), channel_id=1, source_target_pairs={{0,14},{2,12},{4,10},{6,8},{8,6},{10,4},{12,2},{14,0},{1,15},{3,13... | collective-permute-start | bytes 98312 | tf_op jit(solution)/shard_map/ppermute | solution.py:196
  46.0 0.0 collective-permute-done.14.refs_3_
  46.0 0.0 collective-permute-done.15.refs_4_
  46.0 0.0 collective-permute-done.16.refs_5_
  46.1 1.6 %collective-permute-done.17.refs_6_ = bf16[128,128]{1,0:T(8,128)(2,1)S(1)} collective-permute-done((bf16[128,128]{1,0:T(8,128)(2,1)S(1)}, bf16[128,128]{1,0:T(8,128)(2,1)S(1)}, u32[]{:S(2)}, u32[]{:S(2)}) %collective-permute-start.17) | collective-permute-done | bytes 32800 | tf_op jit(solution)/shard_map/ppermute | solution.py:196
  47.7 1.0 %collective-permute-done.18.refs_7_ = bf16[128,128]{1,0:T(8,128)(2,1)S(1)} collective-permute-done((bf16[128,128]{1,0:T(8,128)(2,1)S(1)}, bf16[128,128]{1,0:T(8,128)(2,1)S(1)}, u32[]{:S(2)}, u32[]{:S(2)}) %collective-permute-start.18) | collective-permute-done | bytes 32800 | tf_op jit(solution)/shard_map/ppermute | solution.py:196
  48.6 0.7 %shard_map.109 = (f32[128,128]{1,0:T(8,128)}, bf16[128,128]{1,0:T(8,128)(2,1)S(1)}) custom-call(bf16[128,128]{1,0:T(8,128)(2,1)S(1)} %get-tuple-element.30.refs_0_, bf16[128,128]{1,0:T(8,128)(2,1)S(1)} %collective-permute-done.12.refs_1_, bf16[128,128]{1,0:T(8,128)(2,1)S(1)} %collective-permute-done.13.refs_2_, ...), custom_call_target="tpu_custom_call" | custom-call | bytes 561664 | tf_op jit(solution)/shard_map/pallas_call | solution.py:26
  49.3 4.1 %collective-permute-start.25 = (bf16[128,128]{1,0:T(8,128)(2,1)S(1)}, bf16[128,128]{1,0:T(8,128)(2,1)S(1)}, u32[]{:S(2)}, u32[]{:S(2)}) collective-permute-start(bf16[128,128]{1,0:T(8,128)(2,1)S(1)} %get-tuple-element.40.refs_0_), channel_id=1, source_target_pairs={{0,14},{2,12},{4,10},{6,8},{8,6},{10,4},{12,2},{14,0},{1,15},{3,13... | collective-permute-start | bytes 98312 | tf_op jit(solution)/shard_map/ppermute | solution.py:196
  53.4 0.5 collective-permute-start.24
  53.9 0.0 collective-permute-start.23
  53.9 3.1 %collective-permute-start.22 = (bf16[128,128]{1,0:T(8,128)(2,1)S(1)}, bf16[128,128]{1,0:T(8,128)(2,1)S(1)}, u32[]{:S(2)}, u32[]{:S(2)}) collective-permute-start(bf16[128,128]{1,0:T(8,128)(2,1)S(1)} %get-tuple-element.40.refs_0_), channel_id=1, source_target_pairs={{0,8},{2,10},{4,12},{6,14},{8,0},{10,2},{12,4},{14,6},{1,9},{3,11}... | collective-permute-start | bytes 98312 | tf_op jit(solution)/shard_map/ppermute | solution.py:196
  57.0 1.7 %collective-permute-start.21 = (bf16[128,128]{1,0:T(8,128)(2,1)S(1)}, bf16[128,128]{1,0:T(8,128)(2,1)S(1)}, u32[]{:S(2)}, u32[]{:S(2)}) collective-permute-start(bf16[128,128]{1,0:T(8,128)(2,1)S(1)} %get-tuple-element.40.refs_0_), channel_id=1, source_target_pairs={{0,6},{2,4},{4,2},{6,0},{8,14},{10,12},{12,10},{14,8},{1,7},{3,5},... | collective-permute-start | bytes 98312 | tf_op jit(solution)/shard_map/ppermute | solution.py:196
  58.7 0.0 collective-permute-done.25.refs_7_
  58.7 1.1 %collective-permute-start.20 = (bf16[128,128]{1,0:T(8,128)(2,1)S(1)}, bf16[128,128]{1,0:T(8,128)(2,1)S(1)}, u32[]{:S(2)}, u32[]{:S(2)}) collective-permute-start(bf16[128,128]{1,0:T(8,128)(2,1)S(1)} %get-tuple-element.40.refs_0_), channel_id=1, source_target_pairs={{0,4},{2,6},{4,0},{6,2},{8,12},{10,14},{12,8},{14,10},{1,5},{3,7},... | collective-permute-start | bytes 98312 | tf_op jit(solution)/shard_map/ppermute | solution.py:196
  59.7 0.0 collective-permute-done.24.refs_6_
  59.7 0.7 %collective-permute-start.19 = (bf16[128,128]{1,0:T(8,128)(2,1)S(1)}, bf16[128,128]{1,0:T(8,128)(2,1)S(1)}, u32[]{:S(2)}, u32[]{:S(2)}) collective-permute-start(bf16[128,128]{1,0:T(8,128)(2,1)S(1)} %get-tuple-element.40.refs_0_), channel_id=1, source_target_pairs={{0,2},{2,0},{4,6},{6,4},{8,10},{10,8},{12,14},{14,12},{1,3},{3,1},... | collective-permute-start | bytes 98312 | tf_op jit(solution)/shard_map/ppermute | solution.py:196
  60.5 0.0 collective-permute-done.23.refs_5_
  60.5 0.0 collective-permute-done.22.refs_4_
  60.5 1.3 %collective-permute-done.21.refs_3_ = bf16[128,128]{1,0:T(8,128)(2,1)S(1)} collective-permute-done((bf16[128,128]{1,0:T(8,128)(2,1)S(1)}, bf16[128,128]{1,0:T(8,128)(2,1)S(1)}, u32[]{:S(2)}, u32[]{:S(2)}) %collective-permute-start.21) | collective-permute-done | bytes 32800 | tf_op jit(solution)/shard_map/ppermute | solution.py:196
  61.8 0.8 %collective-permute-done.20.refs_2_ = bf16[128,128]{1,0:T(8,128)(2,1)S(1)} collective-permute-done((bf16[128,128]{1,0:T(8,128)(2,1)S(1)}, bf16[128,128]{1,0:T(8,128)(2,1)S(1)}, u32[]{:S(2)}, u32[]{:S(2)}) %collective-permute-start.20) | collective-permute-done | bytes 32800 | tf_op jit(solution)/shard_map/ppermute | solution.py:196
  62.6 1.1 %collective-permute-done.19.refs_1_ = bf16[128,128]{1,0:T(8,128)(2,1)S(1)} collective-permute-done((bf16[128,128]{1,0:T(8,128)(2,1)S(1)}, bf16[128,128]{1,0:T(8,128)(2,1)S(1)}, u32[]{:S(2)}, u32[]{:S(2)}) %collective-permute-start.19) | collective-permute-done | bytes 32800 | tf_op jit(solution)/shard_map/ppermute | solution.py:196
  63.7 0.9 %shard_map.110 = f32[128,128]{1,0:T(8,128)} custom-call(bf16[128,128]{1,0:T(8,128)(2,1)S(1)} %get-tuple-element.40.refs_0_, bf16[128,128]{1,0:T(8,128)(2,1)S(1)} %collective-permute-done.19.refs_1_, bf16[128,128]{1,0:T(8,128)(2,1)S(1)} %collective-permute-done.20.refs_2_, bf16[128,128]{1,0:T(8,128)(2,1)S(1)} %collective-permute-done.21.refs_3_, ...), custom_call_target="tpu_custom_call" | custom-call | flops 67108864 | bytes 724992 | tf_op jit(solution)/shard_map/pallas_call | solution.py:26
  (17 shorter events, 0.1 us)
Async XLA Ops:
  0.6 0.8 %copy-start = (f32[128,128]{1,0:T(8,128)S(1)}, f32[128,128]{1,0:T(8,128)}, u32[]{:S(2)}) copy-start(f32[128,128]{1,0:T(8,128)} %refs_8_.1) | copy-start | bytes 196612
  1.5 0.8 %copy-start.2 = (f32[128,128]{1,0:T(8,128)S(1)}, f32[128,128]{1,0:T(8,128)}, u32[]{:S(2)}) copy-start(f32[128,128]{1,0:T(8,128)} %refs_11_.3) | copy-start | bytes 196612
  2.3 0.8 %copy-start.4 = (f32[128,128]{1,0:T(8,128)S(1)}, f32[128,128]{1,0:T(8,128)}, u32[]{:S(2)}) copy-start(f32[128,128]{1,0:T(8,128)} %refs_10_.2) | copy-start | bytes 196612
  3.2 3.7 %copy-start.7 = (bf16[1,1,6,128,128]{4,3,2,1,0:T(8,128)(2,1)S(1)}, bf16[1,1,6,128,128]{4,3,2,1,0:T(8,128)(2,1)}, u32[]{:S(2)}) copy-start(bf16[1,1,6,128,128]{4,3,2,1,0:T(8,128)(2,1)} %blocks.1) | copy-start | bytes 589828
  3.2 3.7 %copy-start.10 = (s32[1,1,6]{2,1,0:T(1,128)S(1)}, s32[1,1,6]{2,1,0:T(1,128)}, u32[]{:S(2)}) copy-start(s32[1,1,6]{2,1,0:T(1,128)} %index.1) | copy-start | bytes 76
  3.2 4.9 %collective-permute-start = (bf16[144,128]{1,0:T(8,128)(2,1)S(1)}, bf16[144,128]{1,0:T(8,128)(2,1)S(1)}, u32[]{:S(2)}, u32[]{:S(2)}) collective-permute-start(bf16[144,128]{1,0:T(8,128)(2,1)S(1)} %shard_map.104.refs_0_), channel_id=1, source_target_pairs={{0,2},{2,0},{1,3},{3,1},{4,6},{6,4},{5,7},{7,5},{8,10},{10,8},{9,1... | collective-permute-start | bytes 110600 | tf_op jit(solution)/shard_map/ppermute | solution.py:189
  7.6 26.7 %collective-permute-start.11 = (bf16[128,512]{1,0:T(8,128)(2,1)S(1)}, bf16[128,512]{1,0:T(8,128)(2,1)S(1)}, u32[]{:S(2)}, u32[]{:S(2)}) collective-permute-start(bf16[128,512]{1,0:T(8,128)(2,1)S(1)} %get-tuple-element.23.refs_3_), channel_id=1, source_target_pairs={{0,2},{2,0},{1,3},{3,1},{4,6},{6,4},{5,7},{7,5},{8,10},{10,8},{9,1... | collective-permute-start | bytes 393224 | tf_op jit(solution)/shard_map/ppermute | solution.py:189
  8.1 10.9 %copy-start.1 = (f32[128,128]{1,0:T(8,128)S(1)}, f32[128,128]{1,0:T(8,128)}, u32[]{:S(2)}) copy-start(f32[128,128]{1,0:T(8,128)} %refs_8_.1) | copy-start | bytes 196612
  8.1 10.9 %copy-start.6 = (f32[128,128]{1,0:T(8,128)S(1)}, f32[128,128]{1,0:T(8,128)}, u32[]{:S(2)}) copy-start(f32[128,128]{1,0:T(8,128)} %refs_10_.3) | copy-start | bytes 196612
  8.1 10.9 %copy-start.8 = (f32[128,128]{1,0:T(8,128)S(1)}, f32[128,128]{1,0:T(8,128)}, u32[]{:S(2)}) copy-start(f32[128,128]{1,0:T(8,128)} %refs_5_.1) | copy-start | bytes 196612
  8.4 4.8 %collective-permute-start.1 = (bf16[144,128]{1,0:T(8,128)(2,1)S(1)}, bf16[144,128]{1,0:T(8,128)(2,1)S(1)}, u32[]{:S(2)}, u32[]{:S(2)}) collective-permute-start(bf16[144,128]{1,0:T(8,128)(2,1)S(1)} %get-tuple-element.25), channel_id=1, source_target_pairs={{0,4},{4,0},{8,12},{12,8},{1,5},{5,1},{9,13},{13,9},{2,6},{6,2},{1... | collective-permute-start | bytes 110600 | tf_op jit(solution)/shard_map/ppermute | solution.py:192
  10.6 5.2 %collective-permute-start.2 = (bf16[144,128]{1,0:T(8,128)(2,1)S(1)}, bf16[144,128]{1,0:T(8,128)(2,1)S(1)}, u32[]{:S(2)}, u32[]{:S(2)}) collective-permute-start(bf16[144,128]{1,0:T(8,128)(2,1)S(1)} %get-tuple-element.26), channel_id=1, source_target_pairs={{0,8},{4,12},{8,0},{12,4},{1,9},{5,13},{9,1},{13,5},{2,10},{6,14},... | collective-permute-start | bytes 110600 | tf_op jit(solution)/shard_map/ppermute | solution.py:192
  13.2 5.8 %collective-permute-start.3 = (bf16[144,128]{1,0:T(8,128)(2,1)S(1)}, bf16[144,128]{1,0:T(8,128)(2,1)S(1)}, u32[]{:S(2)}, u32[]{:S(2)}) collective-permute-start(bf16[144,128]{1,0:T(8,128)(2,1)S(1)} %get-tuple-element.27), channel_id=1, source_target_pairs={{0,12},{4,8},{8,4},{12,0},{1,13},{5,9},{9,5},{13,1},{2,14},{6,10},... | collective-permute-start | bytes 110600 | tf_op jit(solution)/shard_map/ppermute | solution.py:192
  19.0 0.7 %copy-start.9 = (s32[128]{0:T(128)S(1)}, s32[128]{0:T(128)}, u32[]{:S(2)}) copy-start(s32[128]{0:T(128)} %param.17) | copy-start | bytes 1540
  19.7 14.7 %copy-start.3 = (f32[128,128]{1,0:T(8,128)S(1)}, f32[128,128]{1,0:T(8,128)}, u32[]{:S(2)}) copy-start(f32[128,128]{1,0:T(8,128)} %refs_11_.3) | copy-start | bytes 196612
  19.7 14.7 %copy-start.5 = (f32[128,128]{1,0:T(8,128)S(1)}, f32[128,128]{1,0:T(8,128)}, u32[]{:S(2)}) copy-start(f32[128,128]{1,0:T(8,128)} %refs_10_.2) | copy-start | bytes 196612
  19.7 7.7 %collective-permute-start.10 = (bf16[128,128]{1,0:T(8,128)(2,1)S(1)}, bf16[128,128]{1,0:T(8,128)(2,1)S(1)}, u32[]{:S(2)}, u32[]{:S(2)}) collective-permute-start(bf16[128,128]{1,0:T(8,128)(2,1)S(1)} %get-tuple-element.28.refs_0_), channel_id=1, source_target_pairs={{0,14},{2,12},{4,10},{6,8},{8,6},{10,4},{12,2},{14,0},{1,15},{3,13... | collective-permute-start | bytes 98312 | tf_op jit(solution)/shard_map/ppermute | solution.py:196
  21.1 6.4 %collective-permute-start.9 = (bf16[128,128]{1,0:T(8,128)(2,1)S(1)}, bf16[128,128]{1,0:T(8,128)(2,1)S(1)}, u32[]{:S(2)}, u32[]{:S(2)}) collective-permute-start(bf16[128,128]{1,0:T(8,128)(2,1)S(1)} %get-tuple-element.28.refs_0_), channel_id=1, source_target_pairs={{0,12},{2,14},{4,8},{6,10},{8,4},{10,6},{12,0},{14,2},{1,13},{3,15... | collective-permute-start | bytes 98312 | tf_op jit(solution)/shard_map/ppermute | solution.py:196
  24.5 5.9 %collective-permute-start.8 = (bf16[128,128]{1,0:T(8,128)(2,1)S(1)}, bf16[128,128]{1,0:T(8,128)(2,1)S(1)}, u32[]{:S(2)}, u32[]{:S(2)}) collective-permute-start(bf16[128,128]{1,0:T(8,128)(2,1)S(1)} %get-tuple-element.28.refs_0_), channel_id=1, source_target_pairs={{0,10},{2,8},{4,14},{6,12},{8,2},{10,0},{12,6},{14,4},{1,11},{3,9}... | collective-permute-start | bytes 98312 | tf_op jit(solution)/shard_map/ppermute | solution.py:196
  24.5 6.4 %collective-permute-start.7 = (bf16[128,128]{1,0:T(8,128)(2,1)S(1)}, bf16[128,128]{1,0:T(8,128)(2,1)S(1)}, u32[]{:S(2)}, u32[]{:S(2)}) collective-permute-start(bf16[128,128]{1,0:T(8,128)(2,1)S(1)} %get-tuple-element.28.refs_0_), channel_id=1, source_target_pairs={{0,8},{2,10},{4,12},{6,14},{8,0},{10,2},{12,4},{14,6},{1,9},{3,11}... | collective-permute-start | bytes 98312 | tf_op jit(solution)/shard_map/ppermute | solution.py:196
  27.4 4.9 %collective-permute-start.6 = (bf16[128,128]{1,0:T(8,128)(2,1)S(1)}, bf16[128,128]{1,0:T(8,128)(2,1)S(1)}, u32[]{:S(2)}, u32[]{:S(2)}) collective-permute-start(bf16[128,128]{1,0:T(8,128)(2,1)S(1)} %get-tuple-element.28.refs_0_), channel_id=1, source_target_pairs={{0,6},{2,4},{4,2},{6,0},{8,14},{10,12},{12,10},{14,8},{1,7},{3,5},... | collective-permute-start | bytes 98312 | tf_op jit(solution)/shard_map/ppermute | solution.py:196
  27.4 5.5 %collective-permute-start.5 = (bf16[128,128]{1,0:T(8,128)(2,1)S(1)}, bf16[128,128]{1,0:T(8,128)(2,1)S(1)}, u32[]{:S(2)}, u32[]{:S(2)}) collective-permute-start(bf16[128,128]{1,0:T(8,128)(2,1)S(1)} %get-tuple-element.28.refs_0_), channel_id=1, source_target_pairs={{0,4},{2,6},{4,0},{6,2},{8,12},{10,14},{12,8},{14,10},{1,5},{3,7},... | collective-permute-start | bytes 98312 | tf_op jit(solution)/shard_map/ppermute | solution.py:196
  30.4 3.9 %collective-permute-start.4 = (bf16[128,128]{1,0:T(8,128)(2,1)S(1)}, bf16[128,128]{1,0:T(8,128)(2,1)S(1)}, u32[]{:S(2)}, u32[]{:S(2)}) collective-permute-start(bf16[128,128]{1,0:T(8,128)(2,1)S(1)} %get-tuple-element.28.refs_0_), channel_id=1, source_target_pairs={{0,2},{2,0},{4,6},{6,4},{8,10},{10,8},{12,14},{14,12},{1,3},{3,1},... | collective-permute-start | bytes 98312 | tf_op jit(solution)/shard_map/ppermute | solution.py:196
  34.8 6.8 %collective-permute-start.12 = (bf16[128,128]{1,0:T(8,128)(2,1)S(1)}, bf16[128,128]{1,0:T(8,128)(2,1)S(1)}, u32[]{:S(2)}, u32[]{:S(2)}) collective-permute-start(bf16[128,128]{1,0:T(8,128)(2,1)S(1)} %get-tuple-element.31), channel_id=1, source_target_pairs={{0,2},{2,0},{4,6},{6,4},{8,10},{10,8},{12,14},{14,12},{1,3},{3,1},... | collective-permute-start | bytes 98312 | tf_op jit(solution)/shard_map/ppermute | solution.py:196
  35.8 6.2 %collective-permute-start.13 = (bf16[128,128]{1,0:T(8,128)(2,1)S(1)}, bf16[128,128]{1,0:T(8,128)(2,1)S(1)}, u32[]{:S(2)}, u32[]{:S(2)}) collective-permute-start(bf16[128,128]{1,0:T(8,128)(2,1)S(1)} %get-tuple-element.32), channel_id=1, source_target_pairs={{0,4},{2,6},{4,0},{6,2},{8,12},{10,14},{12,8},{14,10},{1,5},{3,7},... | collective-permute-start | bytes 98312 | tf_op jit(solution)/shard_map/ppermute | solution.py:196
  35.8 10.3 %collective-permute-start.14 = (bf16[128,128]{1,0:T(8,128)(2,1)S(1)}, bf16[128,128]{1,0:T(8,128)(2,1)S(1)}, u32[]{:S(2)}, u32[]{:S(2)}) collective-permute-start(bf16[128,128]{1,0:T(8,128)(2,1)S(1)} %get-tuple-element.33), channel_id=1, source_target_pairs={{0,6},{2,4},{4,2},{6,0},{8,14},{10,12},{12,10},{14,8},{1,7},{3,5},... | collective-permute-start | bytes 98312 | tf_op jit(solution)/shard_map/ppermute | solution.py:196
  38.4 7.7 %collective-permute-start.15 = (bf16[128,128]{1,0:T(8,128)(2,1)S(1)}, bf16[128,128]{1,0:T(8,128)(2,1)S(1)}, u32[]{:S(2)}, u32[]{:S(2)}) collective-permute-start(bf16[128,128]{1,0:T(8,128)(2,1)S(1)} %get-tuple-element.34), channel_id=1, source_target_pairs={{0,8},{2,10},{4,12},{6,14},{8,0},{10,2},{12,4},{14,6},{1,9},{3,11}... | collective-permute-start | bytes 98312 | tf_op jit(solution)/shard_map/ppermute | solution.py:196
  38.9 7.1 %collective-permute-start.16 = (bf16[128,128]{1,0:T(8,128)(2,1)S(1)}, bf16[128,128]{1,0:T(8,128)(2,1)S(1)}, u32[]{:S(2)}, u32[]{:S(2)}) collective-permute-start(bf16[128,128]{1,0:T(8,128)(2,1)S(1)} %get-tuple-element.35), channel_id=1, source_target_pairs={{0,10},{2,8},{4,14},{6,12},{8,2},{10,0},{12,6},{14,4},{1,11},{3,9}... | collective-permute-start | bytes 98312 | tf_op jit(solution)/shard_map/ppermute | solution.py:196
  41.6 6.0 %collective-permute-start.17 = (bf16[128,128]{1,0:T(8,128)(2,1)S(1)}, bf16[128,128]{1,0:T(8,128)(2,1)S(1)}, u32[]{:S(2)}, u32[]{:S(2)}) collective-permute-start(bf16[128,128]{1,0:T(8,128)(2,1)S(1)} %get-tuple-element.36), channel_id=1, source_target_pairs={{0,12},{2,14},{4,8},{6,10},{8,4},{10,6},{12,0},{14,2},{1,13},{3,15... | collective-permute-start | bytes 98312 | tf_op jit(solution)/shard_map/ppermute | solution.py:196
  42.0 6.6 %collective-permute-start.18 = (bf16[128,128]{1,0:T(8,128)(2,1)S(1)}, bf16[128,128]{1,0:T(8,128)(2,1)S(1)}, u32[]{:S(2)}, u32[]{:S(2)}) collective-permute-start(bf16[128,128]{1,0:T(8,128)(2,1)S(1)} %get-tuple-element.37), channel_id=1, source_target_pairs={{0,14},{2,12},{4,10},{6,8},{8,6},{10,4},{12,2},{14,0},{1,15},{3,13... | collective-permute-start | bytes 98312 | tf_op jit(solution)/shard_map/ppermute | solution.py:196
  49.3 9.3 %collective-permute-start.25 = (bf16[128,128]{1,0:T(8,128)(2,1)S(1)}, bf16[128,128]{1,0:T(8,128)(2,1)S(1)}, u32[]{:S(2)}, u32[]{:S(2)}) collective-permute-start(bf16[128,128]{1,0:T(8,128)(2,1)S(1)} %get-tuple-element.40.refs_0_), channel_id=1, source_target_pairs={{0,14},{2,12},{4,10},{6,8},{8,6},{10,4},{12,2},{14,0},{1,15},{3,13... | collective-permute-start | bytes 98312 | tf_op jit(solution)/shard_map/ppermute | solution.py:196
  53.4 6.4 %collective-permute-start.24 = (bf16[128,128]{1,0:T(8,128)(2,1)S(1)}, bf16[128,128]{1,0:T(8,128)(2,1)S(1)}, u32[]{:S(2)}, u32[]{:S(2)}) collective-permute-start(bf16[128,128]{1,0:T(8,128)(2,1)S(1)} %get-tuple-element.40.refs_0_), channel_id=1, source_target_pairs={{0,12},{2,14},{4,8},{6,10},{8,4},{10,6},{12,0},{14,2},{1,13},{3,15... | collective-permute-start | bytes 98312 | tf_op jit(solution)/shard_map/ppermute | solution.py:196
  53.9 6.6 %collective-permute-start.23 = (bf16[128,128]{1,0:T(8,128)(2,1)S(1)}, bf16[128,128]{1,0:T(8,128)(2,1)S(1)}, u32[]{:S(2)}, u32[]{:S(2)}) collective-permute-start(bf16[128,128]{1,0:T(8,128)(2,1)S(1)} %get-tuple-element.40.refs_0_), channel_id=1, source_target_pairs={{0,10},{2,8},{4,14},{6,12},{8,2},{10,0},{12,6},{14,4},{1,11},{3,9}... | collective-permute-start | bytes 98312 | tf_op jit(solution)/shard_map/ppermute | solution.py:196
  53.9 6.6 %collective-permute-start.22 = (bf16[128,128]{1,0:T(8,128)(2,1)S(1)}, bf16[128,128]{1,0:T(8,128)(2,1)S(1)}, u32[]{:S(2)}, u32[]{:S(2)}) collective-permute-start(bf16[128,128]{1,0:T(8,128)(2,1)S(1)} %get-tuple-element.40.refs_0_), channel_id=1, source_target_pairs={{0,8},{2,10},{4,12},{6,14},{8,0},{10,2},{12,4},{14,6},{1,9},{3,11}... | collective-permute-start | bytes 98312 | tf_op jit(solution)/shard_map/ppermute | solution.py:196
  57.0 4.8 %collective-permute-start.21 = (bf16[128,128]{1,0:T(8,128)(2,1)S(1)}, bf16[128,128]{1,0:T(8,128)(2,1)S(1)}, u32[]{:S(2)}, u32[]{:S(2)}) collective-permute-start(bf16[128,128]{1,0:T(8,128)(2,1)S(1)} %get-tuple-element.40.refs_0_), channel_id=1, source_target_pairs={{0,6},{2,4},{4,2},{6,0},{8,14},{10,12},{12,10},{14,8},{1,7},{3,5},... | collective-permute-start | bytes 98312 | tf_op jit(solution)/shard_map/ppermute | solution.py:196
  58.7 3.9 %collective-permute-start.20 = (bf16[128,128]{1,0:T(8,128)(2,1)S(1)}, bf16[128,128]{1,0:T(8,128)(2,1)S(1)}, u32[]{:S(2)}, u32[]{:S(2)}) collective-permute-start(bf16[128,128]{1,0:T(8,128)(2,1)S(1)} %get-tuple-element.40.refs_0_), channel_id=1, source_target_pairs={{0,4},{2,6},{4,0},{6,2},{8,12},{10,14},{12,8},{14,10},{1,5},{3,7},... | collective-permute-start | bytes 98312 | tf_op jit(solution)/shard_map/ppermute | solution.py:196
  59.7 3.9 %collective-permute-start.19 = (bf16[128,128]{1,0:T(8,128)(2,1)S(1)}, bf16[128,128]{1,0:T(8,128)(2,1)S(1)}, u32[]{:S(2)}, u32[]{:S(2)}) collective-permute-start(bf16[128,128]{1,0:T(8,128)(2,1)S(1)} %get-tuple-element.40.refs_0_), channel_id=1, source_target_pairs={{0,2},{2,0},{4,6},{6,4},{8,10},{10,8},{12,14},{14,12},{1,3},{3,1},... | collective-permute-start | bytes 98312 | tf_op jit(solution)/shard_map/ppermute | solution.py:196

commit v2 on v1

--- a/solution.py
+++ b/solution.py
@@ -53,28 +53,38 @@
     return rows[0:1] + rows[1:2] + rows[2:3], rows[3:4] + rows[4:5] + rows[5:6]
 
 
-def prep_body(cost, rhs, y, out):
+def prep_body(cost_hbm, rhs_hbm, y_hbm, out, cost, rhs, y, sems):
+    copies = [
+        pltpu.make_async_copy(source, target, sems.at[k])
+        for k, (source, target) in enumerate(((y_hbm, y), (cost_hbm, cost), (rhs_hbm, rhs)))
+    ]
+    for copy in copies:
+        copy.start()
+    for copy in copies:
+        copy.wait()
     tile = y.shape[0]
     out[0:tile, :] = y[...].astype(BF16)
     c, r = cost[...], rhs[...]
     out[tile:, :] = pack_sums(jnp.sum(c * c, axis=0, keepdims=True), jnp.sum(r * r, axis=0, keepdims=True))
 
 
-def dense_body(n_blk, n_col, index, live, blocks, *outs):
+def dense_body(n_blk, n_col, index, live, blocks, bounded, *outs):
     tile = blocks.shape[-1]
     me_c = lax.axis_index("col")
-    for out in outs:
-        out[...] = jnp.zeros(out.shape, BF16)
+    *mats, limits = outs
+    limits[...] = jnp.broadcast_to(bounded[...], limits.shape).astype(F32)
+    for mat in mats:
+        mat[...] = jnp.zeros(mat.shape, BF16)
 
     def one(k, carry):
         position = index[0, 0, k]
         rel = (position // n_blk) ^ me_c
         col = position % n_blk
-        for s, out in enumerate(outs):
+        for s, mat in enumerate(mats):
 
             @pl.when(rel == s)
             def _():
-                out[:, pl.ds(pl.multiple_of(col * tile, tile), tile)] = blocks[0, 0, k]
+                mat[:, pl.ds(pl.multiple_of(col * tile, tile), tile)] = blocks[0, 0, k]
 
         return carry
 
@@ -87,9 +97,8 @@
 
 def first_terms_body(n_blk, n_col, *refs):
     payloads, mats = refs[:n_col], refs[n_col : 2 * n_col]
-    outs, scratch = refs[2 * n_col : 2 * n_col + n_blk], refs[-1]
+    out = refs[-1]
     tile = mats[0].shape[0]
-    me_b = lax.axis_index("blk")
     total = transposed_dot(mats[0][...], payloads[0][0:tile, :])
     cost_sum, rhs_sum = unpack_sums(payloads[0][tile:, :])
     for s in range(1, n_col):
@@ -97,30 +106,31 @@
         c, r = unpack_sums(payloads[s][tile:, :])
         cost_sum += c
         rhs_sum += r
-    scratch[...] = total
     packed = pack_sums(cost_sum, rhs_sum)
-    for t, out in enumerate(outs):
-        rows = pl.ds(pl.multiple_of((me_b ^ t) * tile, tile), tile)
-        out[0:tile, :] = scratch[rows, :].astype(BF16)
-        out[tile:, :] = packed
-
-
-def project(primal, grad, tau, upper, bounded):
+    for p in range(n_blk):
+        out[p, 0:tile, :] = total[p * tile : (p + 1) * tile, :].astype(BF16)
+        out[p, tile:, :] = packed
+
+
+def project(primal, grad, tau, upper, limited):
     value = primal - tau * grad
-    capped = jnp.where(bounded > 0, jnp.minimum(value, upper), value)
+    capped = jnp.where(limited > 0, jnp.minimum(value, upper), value)
     return jnp.maximum(capped, 0.0)
 
 
-def first_primal_body(n_blk, *refs):
-    terms = refs[:n_blk]
-    cost, primal, upper, bounded = refs[n_blk : n_blk + 4]
-    x_out, xbar_out, scales_out = refs[n_blk + 4 :]
+def write_bar(x_new, x, xbar_out):
+    xbar = (2.0 * x_new - x).astype(BF16)
+    for d in range(xbar_out.shape[0]):
+        xbar_out[d] = xbar
+
+
+def first_primal_body(terms, cost, primal, upper, limits, x_out, xbar_out, scales_out):
     tile = cost.shape[0]
-    kty = terms[0][0:tile, :].astype(F32)
-    cost_sum, rhs_sum = unpack_sums(terms[0][tile:, :])
-    for term in terms[1:]:
-        kty += term[0:tile, :].astype(F32)
-        c, r = unpack_sums(term[tile:, :])
+    kty = terms[0, 0:tile, :].astype(F32)
+    cost_sum, rhs_sum = unpack_sums(terms[0, tile:, :])
+    for p in range(1, terms.shape[0]):
+        kty += terms[p, 0:tile, :].astype(F32)
+        c, r = unpack_sums(terms[p, tile:, :])
         cost_sum += c
         rhs_sum += r
     weight = jnp.sqrt(cost_sum + EPS) / jnp.sqrt(rhs_sum + EPS)
@@ -128,49 +138,41 @@
     sigma = ETA * weight
     scales_out[...] = jnp.concatenate([tau, sigma, jnp.zeros((6, tau.shape[1]), F32)], axis=0)
     x = primal[...]
-    x_new = project(x, cost[...] - kty, tau, upper[...], bounded[...])
+    x_new = project(x, cost[...] - kty, tau, upper[...], limits[0:1, :])
     x_out[...] = x_new
-    xbar_out[...] = (2.0 * x_new - x).astype(BF16)
-
-
-def primal_body(n, last, *refs):
-    terms = refs[:n]
-    cost, primal, upper, bounded, scales = refs[n : n + 5]
-    x_out, xbar_out = refs[n + 5 :]
-    kty = terms[0][...].astype(F32)
-    for term in terms[1:]:
-        kty += term[...].astype(F32)
+    write_bar(x_new, x, xbar_out)
+
+
+def primal_body(terms, cost, primal, upper, limits, scales, x_out, xbar_out):
+    kty = terms[0].astype(F32)
+    for d in range(1, terms.shape[0]):
+        kty += terms[d].astype(F32)
     x = primal[...]
-    x_new = project(x, cost[...] - kty, scales[0:1, :], upper[...], bounded[...])
+    x_new = project(x, cost[...] - kty, scales[0:1, :], upper[...], limits[0:1, :])
     x_out[...] = x_new
-    xbar_out[...] = (2.0 * x_new - x).astype(BF16)
-
-
-def dual_body(n_blk, n_col, last, *refs):
-    n = n_blk * n_col
-    bars, slabs = refs[:n], refs[n : n + n_col]
-    dual, rhs, scales = refs[n + n_col : n + n_col + 3]
-    y_out = refs[n + n_col + 3]
+    write_bar(x_new, x, xbar_out)
+
+
+def dual_body(n_blk, n_col, last, bars, *refs):
+    slabs = refs[:n_col]
+    dual, rhs, scales, y_out = refs[n_col : n_col + 4]
     tile = dual.shape[0]
-    me_b = lax.axis_index("blk")
-    field = refs[-2]
-    scratch = refs[-1]
+    me_c = lax.axis_index("col")
+    field = refs[-1]
     kx = jnp.zeros(dual.shape, F32)
     for s in range(n_col):
-        for t in range(n_blk):
-            rows = pl.ds(pl.multiple_of((me_b ^ t) * tile, tile), tile)
-            field[s, rows, :] = bars[t * n_col + s][...]
+        for p in range(n_blk):
+            field[s, p * tile : (p + 1) * tile, :] = bars[p * n_col + (me_c ^ s)]
         kx += jnp.dot(slabs[s][...], field[s], preferred_element_type=F32)
     y_new = jnp.maximum(dual[...] + scales[1:2, :] * (rhs[...] - kx), 0.0)
     y_out[...] = y_new
     if not last:
-        outs = refs[n + n_col + 4 : n + n_col + 4 + n]
+        out = refs[n_col + 4]
         y_half = y_new.astype(BF16)
         for s in range(n_col):
-            scratch[...] = transposed_dot(slabs[s][...], y_half)
-            for t in range(n_blk):
-                rows = pl.ds(pl.multiple_of((me_b ^ t) * tile, tile), tile)
-                outs[t * n_col + s][...] = scratch[rows, :].astype(BF16)
+            total = transposed_dot(slabs[s][...], y_half)
+            for p in range(n_blk):
+                out[p * n_col + (me_c ^ s)] = total[p * tile : (p + 1) * tile, :].astype(BF16)
 
 
 def direct_plan(blocks, block_index, live, cost, rhs, upper, x_init, y_init, bounded):
@@ -181,69 +183,62 @@
     scn = cost.shape[1]
     like = jax.ShapeDtypeStruct
     field_f32 = like((tile, scn), F32)
-    field_half = like((tile, scn), BF16)
+    spread = like((n, tile, scn), BF16)
+    rows = like((8, scn), F32)
     payload = like((tile + SPLIT_ROWS, scn), BF16)
-    limits = bounded[None, :]
 
     def over_col(value, s):
         return lax.ppermute(value, "col", [(c, c ^ s) for c in range(n_col)])
 
-    def over_blk(value, t):
-        return lax.ppermute(value, "blk", [(b, b ^ t) for b in range(n_blk)])
-
-    def over_both(value, t, s):
-        pairs = [(b * n_col + c, (b ^ t) * n_col + (c ^ s)) for b in range(n_blk) for c in range(n_col)]
-        return lax.ppermute(value, ("blk", "col"), pairs)
-
-    shifts = [(t, s) for t in range(n_blk) for s in range(n_col)]
-
-    def spread(values):
-        return [v if (t, s) == (0, 0) else over_both(v, t, s) for v, (t, s) in zip(values, shifts)]
-
-    (own,) = call(prep_body, [payload], [VMEM] * 3, [cost, rhs, y_init])
+    def exchange(value, axes):
+        return lax.all_to_all(value, axes, 0, 0, tiled=True)
+
+    (own,) = call(
+        prep_body,
+        [payload],
+        [pl.BlockSpec(memory_space=pltpu.HBM)] * 3,
+        [cost, rhs, y_init],
+        scratch=[pltpu.VMEM((tile, scn), F32)] * 3 + [pltpu.SemaphoreType.DMA((3,))],
+    )
     payloads = [own] + [over_col(own, s) for s in range(1, n_col)]
-    mats = call(
+    *mats, limits = call(
         functools.partial(dense_body, n_blk, n_col),
-        [like((tile, n_blk * tile), BF16)] * n_col,
-        [SMEM, SMEM, VMEM],
-        [block_index, live, blocks],
+        [like((tile, n_blk * tile), BF16)] * n_col + [rows],
+        [SMEM, SMEM, VMEM, VMEM],
+        [block_index, live, blocks, bounded[None, :]],
     )
     slabs = [mats[0]] + [over_col(mats[s], s) for s in range(1, n_col)]
-    terms = call(
+    (terms,) = call(
         functools.partial(first_terms_body, n_blk, n_col),
-        [payload] * n_blk,
+        [like((n_blk, *payload.shape), BF16)],
         [VMEM] * (2 * n_col),
         payloads + list(mats),
-        scratch=[pltpu.VMEM((n_blk * tile, scn), F32)],
         flops=2 * n * tile * tile * scn,
     )
-    terms = [terms[0]] + [over_blk(terms[t], t) for t in range(1, n_blk)]
-    primal, xbar, scales = call(
-        functools.partial(first_primal_body, n_blk),
-        [field_f32, field_half, like((8, scn), F32)],
-        [VMEM] * (n_blk + 4),
-        terms + [cost, x_init, upper, limits],
+    primal, bars, scales = call(
+        first_primal_body,
+        [field_f32, spread, rows],
+        [VMEM] * 5,
+        [exchange(terms, "blk"), cost, x_init, upper, limits],
     )
     dual = y_init
     for step in range(ITERS):
         last = step == ITERS - 1
-        bars = spread([xbar] * n)
         outs = call(
             functools.partial(dual_body, n_blk, n_col, last),
-            [field_f32] + ([] if last else [field_half] * n),
-            [VMEM] * (n + n_col + 3),
-            bars + slabs + [dual, rhs, scales],
-            scratch=[pltpu.VMEM((n_col, n_blk * tile, scn), BF16), pltpu.VMEM((n_blk * tile, scn), F32)],
+            [field_f32] + ([] if last else [spread]),
+            [VMEM] * (n_col + 4),
+            [exchange(bars, ("blk", "col"))] + slabs + [dual, rhs, scales],
+            scratch=[pltpu.VMEM((n_col, n_blk * tile, scn), BF16)],
             flops=4 * n * tile * tile * scn,
         )
         dual = outs[0]
         if not last:
-            terms = spread(outs[1:])
-            primal, xbar = call(
-                functools.partial(primal_body, n, last),
-                [field_f32, field_half],
-                [VMEM] * (n + 5),
-                terms + [cost, primal, upper, limits, scales],
+            primal, bars = call(
+                primal_body,
+                [field_f32, spread],
+                [VMEM] * 6,
+                [exchange(outs[1], ("blk", "col")), cost, primal, upper, limits, scales],
             )
     return (primal, dual)
 

time: 64.8 us -> 57.8 us (0.89)
  blocking collectives: 0 us -> 33.9 us
  starting transfers between devices: 41.5 us -> 8.47 us
  waiting for transfers between devices: 15.3 us -> 6.24 us
  Pallas kernels: 3.15 us -> 4.02 us
    ppermute x24 -> x0, starting transfers between devices: 38.3 us -> none  [the longest x21 33.5 us: over_both(): return lax.ppermute(value, ('blk', 'col'), pairs)]
    all_to_all x0 -> x3, blocking collectives: none -> 33.9 us  [exchange(): return lax.all_to_all(value, axes, 0, 0, tiled=True)]
    ppermute x24 -> x0, waiting for transfers between devices: 14.9 us -> none  [the longest x21 9.17 us: over_both(): return lax.ppermute(value, ('blk', 'col'), pairs)]
    ppermute x2, waiting for transfers between devices: 0.32 us -> 4.56 us  [over_col(): return lax.ppermute(value, 'col', [(c, c ^ s) for c in range(n_col)])]
    all_to_all x0 -> x1, starting transfers between devices: none -> 3.54 us  [exchange(): return lax.all_to_all(value, axes, 0, 0, tiled=True)]
    ppermute x2, starting transfers between devices: 3.24 us -> 4.92 us  [over_col(): return lax.ppermute(value, 'col', [(c, c ^ s) for c in range(n_col)])]
    all_to_all x0 -> x1, waiting for transfers between devices: none -> 1.68 us  [exchange(): return lax.all_to_all(value, axes, 0, 0, tiled=True)]
    pallas_call x7, Pallas kernels: 3.15 us -> 4.02 us  [call(): pl.pallas_call(body, out_shape=list(outs), in_specs=ins_specs, out_specs=...]
  transfers between devices with their start and end apart: 26 -> 3, of which waited for: 11 -> 2; matrix products, arithmetic and copies ran while one was open for 0% -> 0% of each run, Pallas kernels for 2% -> 1%
where the time goes in v2:
time: 57.8 us; the launch traced here: 57.3 us
  blocking collectives  33.9 us (59%)
  starting transfers between devices  8.47 us (15%)
  waiting for transfers between devices  6.24 us (11%)
  Pallas kernels  4.02 us (7%)
  local copies, waits for them, and re-layouts  3.19 us (6%)
  between operations  1.4 us (2%)
    all_to_all x3, blocking collectives, exchange(): return lax.all_to_all(value, axes, 0, 0, tiled=True)  33.9 us
    ppermute x2, starting transfers between devices, over_col(): return lax.ppermute(value, 'col', [(c, c ^ s) for c in range(n_col)])  4.92 us
    ppermute x2, waiting for transfers between devices, over_col(): return lax.ppermute(value, 'col', [(c, c ^ s) for c in range(n_col)])  4.56 us
    pallas_call x7, Pallas kernels, call(): pl.pallas_call(body, out_shape=list(outs), in_specs=ins_specs, out_specs=...  4.02 us
    all_to_all x1, starting transfers between devices, exchange(): return lax.all_to_all(value, axes, 0, 0, tiled=True)  3.54 us
    unnamed x22, local copies, waits for them, and re-layouts  3.19 us
    all_to_all x1, waiting for transfers between devices, exchange(): return lax.all_to_all(value, axes, 0, 0, tiled=True)  1.68 us
  transfers between devices with their start and end apart: 3, of which 2 were waited for; matrix products, arithmetic and copies ran while one was open for 0% of the time, Pallas kernels for 1%

profile of v2, /device:TPU:0, one launch (start us, length us, event | category | flops | bytes accessed | tf_op | source)
XLA Modules:
  0.0 57.3 jit_solution(11488959235786687242)
XLA Ops:
  0.6 0.0 copy-start
  0.6 0.8 %copy-done = f32[128,128]{1,0:T(8,128)S(1)} copy-done((f32[128,128]{1,0:T(8,128)S(1)}, f32[128,128]{1,0:T(8,128)}, u32[]{:S(2)}) %copy-start) | copy-done | bytes 65560
  1.5 0.0 copy-start.2
  1.5 0.8 %copy-done.2 = f32[128,128]{1,0:T(8,128)S(1)} copy-done((f32[128,128]{1,0:T(8,128)S(1)}, f32[128,128]{1,0:T(8,128)}, u32[]{:S(2)}) %copy-start.2) | copy-done | bytes 65560
  2.3 0.0 copy-start.4
  2.3 0.8 %copy-done.4 = f32[128,128]{1,0:T(8,128)S(1)} copy-done((f32[128,128]{1,0:T(8,128)S(1)}, f32[128,128]{1,0:T(8,128)}, u32[]{:S(2)}) %copy-start.4) | copy-done | bytes 65560
  3.2 0.0 copy-start.7
  3.2 0.3 shard_map.104.refs_0_
  3.5 3.0 %collective-permute-start = (bf16[144,128]{1,0:T(8,128)(2,1)S(1)}, bf16[144,128]{1,0:T(8,128)(2,1)S(1)}, u32[]{:S(2)}, u32[]{:S(2)}) collective-permute-start(bf16[144,128]{1,0:T(8,128)(2,1)S(1)} %shard_map.104.refs_0_), channel_id=1, source_target_pairs={{0,2},{2,0},{1,3},{3,1},{4,6},{6,4},{5,7},{7,5},{8,10},{10,8},{9,1... | collective-permute-start | bytes 110600 | tf_op jit(solution)/shard_map/ppermute | solution.py:191
  7.1 0.0 copy-start.9
  7.1 0.0 copy-start.10
  7.1 0.0 copy-done.7
  7.1 0.6 %copy-done.9 = s32[1,1,6]{2,1,0:T(1,128)S(1)} copy-done((s32[1,1,6]{2,1,0:T(1,128)S(1)}, s32[1,1,6]{2,1,0:T(1,128)}, u32[]{:S(2)}) %copy-start.9) | copy-done | bytes 48
  7.8 0.0 copy-done.10
  7.8 0.7 %shard_map.105 = (bf16[128,512]{1,0:T(8,128)(2,1)S(1)}, bf16[128,512]{1,0:T(8,128)(2,1)S(1)}, f32[8,128]{1,0:T(8,128)S(1)}) custom-call(s32[1,1,6]{2,1,0:T(1,128)S(1)} %copy-done.9, s32[1,1]{1,0:T(1,128)S(6)} %copy.11.live, bf16[1,1,6,128,128]{4,3,2,1,0:T(8,128)(2,1)S(1)} %copy-done.7, s32[1,128]{1,0:T(1,128)S(1)} %bitcast.1), custom_call_target="tpu_custom_call" | custom-call | bytes 463388 | tf_op jit(solution)/shard_map/pallas_call | solution.py:26
  8.5 0.0 collective-permute-done.refs_1_
  8.5 0.3 shard_map.106
  8.7 0.0 copy-start.1
  8.8 0.0 copy-start.6
  8.8 0.0 copy-start.8
  8.8 11.9 %all_to_all.20.terms = bf16[4,144,128]{2,1,0:T(8,128)(2,1)S(1)} all-to-all(bf16[4,144,128]{2,1,0:T(8,128)(2,1)S(1)} %shard_map.106), channel_id=1, replica_groups=mesh['groups'=2,'blk'=4,'col'=2,'rep'=2] {'blk'}, dimensions={0} | all-to-all | bytes 294912 | tf_op jit(solution)/shard_map/all_to_all | solution.py:194
  20.7 0.0 copy-done.1
  20.7 0.0 copy-done.6
  20.7 0.0 copy-done.8
  20.7 0.8 %shard_map.107 = (f32[128,128]{1,0:T(8,128)S(1)}, bf16[8,128,128]{2,1,0:T(8,128)(2,1)}, f32[8,128]{1,0:T(8,128)S(1)}) custom-call(bf16[4,144,128]{2,1,0:T(8,128)(2,1)S(1)} %all_to_all.20.terms, f32[128,128]{1,0:T(8,128)S(1)} %copy-done.1, f32[128,128]{1,0:T(8,128)S(1)} %copy-done.8, f32[128,128]{1,0:T(8,128)S(1)} %copy-done.6, ...), custom_call_target="tpu_custom_call" | custom-call | bytes 679936 | tf_op jit(solution)/shard_map/pallas_call | solution.py:26
  21.5 0.0 copy-start.3
  21.5 0.0 copy-start.5
  21.5 3.5 %all-to-all-start.1 = ((bf16[8,128,128]{2,1,0:T(8,128)(2,1)}), bf16[8,128,128]{2,1,0:T(8,128)(2,1)S(1)}, u32[]{:S(2)}, u32[]{:S(2)}) async-start(bf16[8,128,128]{2,1,0:T(8,128)(2,1)} %get-tuple-element.15), calls=%async_computation.1 | async-start | bytes 524288 | tf_op jit(solution)/shard_map/all_to_all | solution.py:194
  25.0 1.9 %collective-permute-start.1 = (bf16[128,512]{1,0:T(8,128)(2,1)S(1)}, bf16[128,512]{1,0:T(8,128)(2,1)S(1)}, u32[]{:S(2)}, u32[]{:S(2)}) collective-permute-start(bf16[128,512]{1,0:T(8,128)(2,1)S(1)} %get-tuple-element.13.refs_3_), channel_id=1, source_target_pairs={{0,2},{2,0},{1,3},{3,1},{4,6},{6,4},{5,7},{7,5},{8,10},{10,8},{9,1... | collective-permute-start | bytes 393224 | tf_op jit(solution)/shard_map/ppermute | solution.py:191
  27.0 4.6 %collective-permute-done.1.refs_1_ = bf16[128,512]{1,0:T(8,128)(2,1)S(1)} collective-permute-done((bf16[128,512]{1,0:T(8,128)(2,1)S(1)}, bf16[128,512]{1,0:T(8,128)(2,1)S(1)}, u32[]{:S(2)}, u32[]{:S(2)}) %collective-permute-start.1) | collective-permute-done | bytes 131104 | tf_op jit(solution)/shard_map/ppermute | solution.py:191
  31.5 1.7 %all-to-all-done.1.bars = bf16[8,128,128]{2,1,0:T(8,128)(2,1)S(1)} async-done(((bf16[8,128,128]{2,1,0:T(8,128)(2,1)}), bf16[8,128,128]{2,1,0:T(8,128)(2,1)S(1)}, u32[]{:S(2)}, u32[]{:S(2)}) %all-to-all-start.1) | async-done | bytes 262176 | tf_op jit(solution)/shard_map/all_to_all | solution.py:194
  33.2 0.0 copy-done.3
  33.2 0.0 copy-done.5
  33.2 0.5 shard_map.108
  33.7 11.1 %all_to_all.21.terms = bf16[8,128,128]{2,1,0:T(8,128)(2,1)S(1)} all-to-all(bf16[8,128,128]{2,1,0:T(8,128)(2,1)S(1)} %get-tuple-element.17), channel_id=1, replica_groups=mesh['groups'=2,'blk'=4,'col'=2,'rep'=2] {'blk','col'}, dimensions={0} | all-to-all | bytes 524288 | tf_op jit(solution)/shard_map/all_to_all | solution.py:194
  44.8 0.7 %shard_map.109 = (f32[128,128]{1,0:T(8,128)}, bf16[8,128,128]{2,1,0:T(8,128)(2,1)S(1)}) custom-call(bf16[8,128,128]{2,1,0:T(8,128)(2,1)S(1)} %all_to_all.21.terms, f32[128,128]{1,0:T(8,128)S(1)} %copy-done.1, f32[128,128]{1,0:T(8,128)S(1)} %get-tuple-element.18.primal, f32[128,128]{1,0:T(8,128)S(1)} %copy-done.6, f32[8,128]{1,0:T(8,128)S(1)} %get-tuple-element.14.limits, ...), custom_call_target="tpu_custom_call" | custom-call | bytes 794624 | tf_op jit(solution)/shard_map/pallas_call | solution.py:26
  45.5 10.9 %all_to_all.22.bars = bf16[8,128,128]{2,1,0:T(8,128)(2,1)S(1)} all-to-all(bf16[8,128,128]{2,1,0:T(8,128)(2,1)S(1)} %get-tuple-element.20), channel_id=1, replica_groups=mesh['groups'=2,'blk'=4,'col'=2,'rep'=2] {'blk','col'}, dimensions={0} | all-to-all | bytes 524288 | tf_op jit(solution)/shard_map/all_to_all | solution.py:194
  56.4 0.9 %shard_map.110 = f32[128,128]{1,0:T(8,128)} custom-call(bf16[8,128,128]{2,1,0:T(8,128)(2,1)S(1)} %all_to_all.22.bars, bf16[128,512]{1,0:T(8,128)(2,1)S(1)} %get-tuple-element.12.refs_2_.refs_0_, bf16[128,512]{1,0:T(8,128)(2,1)S(1)} %collective-permute-done.1.refs_1_, f32[128,128]{1,0:T(8,128)S(1)} %get-tuple-element.21.refs_2_, f32[128,128]{1,0:T(8,128)S(1)} %copy-done.3, ...), custom_call_target="tpu_custom_call" | custom-call | flops 67108864 | bytes 724992 | tf_op jit(solution)/shard_map/pallas_call | solution.py:26
Async XLA Ops:
  0.6 0.8 %copy-start = (f32[128,128]{1,0:T(8,128)S(1)}, f32[128,128]{1,0:T(8,128)}, u32[]{:S(2)}) copy-start(f32[128,128]{1,0:T(8,128)} %cost.3) | copy-start | bytes 196612
  1.5 0.8 %copy-start.2 = (f32[128,128]{1,0:T(8,128)S(1)}, f32[128,128]{1,0:T(8,128)}, u32[]{:S(2)}) copy-start(f32[128,128]{1,0:T(8,128)} %refs_3_.3) | copy-start | bytes 196612
  2.3 0.8 %copy-start.4 = (f32[128,128]{1,0:T(8,128)S(1)}, f32[128,128]{1,0:T(8,128)}, u32[]{:S(2)}) copy-start(f32[128,128]{1,0:T(8,128)} %refs_2_.1) | copy-start | bytes 196612
  3.2 4.0 %copy-start.7 = (bf16[1,1,6,128,128]{4,3,2,1,0:T(8,128)(2,1)S(1)}, bf16[1,1,6,128,128]{4,3,2,1,0:T(8,128)(2,1)}, u32[]{:S(2)}) copy-start(bf16[1,1,6,128,128]{4,3,2,1,0:T(8,128)(2,1)} %blocks.1) | copy-start | bytes 589828
  3.5 5.0 %collective-permute-start = (bf16[144,128]{1,0:T(8,128)(2,1)S(1)}, bf16[144,128]{1,0:T(8,128)(2,1)S(1)}, u32[]{:S(2)}, u32[]{:S(2)}) collective-permute-start(bf16[144,128]{1,0:T(8,128)(2,1)S(1)} %shard_map.104.refs_0_), channel_id=1, source_target_pairs={{0,2},{2,0},{1,3},{3,1},{4,6},{6,4},{5,7},{7,5},{8,10},{10,8},{9,1... | collective-permute-start | bytes 110600 | tf_op jit(solution)/shard_map/ppermute | solution.py:191
  7.1 0.7 %copy-start.9 = (s32[1,1,6]{2,1,0:T(1,128)S(1)}, s32[1,1,6]{2,1,0:T(1,128)}, u32[]{:S(2)}) copy-start(s32[1,1,6]{2,1,0:T(1,128)} %index.1) | copy-start | bytes 76
  7.1 0.7 %copy-start.10 = (s32[128]{0:T(128)S(1)}, s32[128]{0:T(128)}, u32[]{:S(2)}) copy-start(s32[128]{0:T(128)} %param.17) | copy-start | bytes 1540
  8.7 12.0 %copy-start.1 = (f32[128,128]{1,0:T(8,128)S(1)}, f32[128,128]{1,0:T(8,128)}, u32[]{:S(2)}) copy-start(f32[128,128]{1,0:T(8,128)} %cost.3) | copy-start | bytes 196612
  8.8 11.9 %copy-start.6 = (f32[128,128]{1,0:T(8,128)S(1)}, f32[128,128]{1,0:T(8,128)}, u32[]{:S(2)}) copy-start(f32[128,128]{1,0:T(8,128)} %upper.3) | copy-start | bytes 196612
  8.8 11.9 %copy-start.8 = (f32[128,128]{1,0:T(8,128)S(1)}, f32[128,128]{1,0:T(8,128)}, u32[]{:S(2)}) copy-start(f32[128,128]{1,0:T(8,128)} %primal.1) | copy-start | bytes 196612
  21.5 11.7 %copy-start.3 = (f32[128,128]{1,0:T(8,128)S(1)}, f32[128,128]{1,0:T(8,128)}, u32[]{:S(2)}) copy-start(f32[128,128]{1,0:T(8,128)} %refs_3_.3) | copy-start | bytes 196612
  21.5 11.7 %copy-start.5 = (f32[128,128]{1,0:T(8,128)S(1)}, f32[128,128]{1,0:T(8,128)}, u32[]{:S(2)}) copy-start(f32[128,128]{1,0:T(8,128)} %refs_2_.1) | copy-start | bytes 196612
  21.5 11.7 %all-to-all-start.1 = ((bf16[8,128,128]{2,1,0:T(8,128)(2,1)}), bf16[8,128,128]{2,1,0:T(8,128)(2,1)S(1)}, u32[]{:S(2)}, u32[]{:S(2)}) async-start(bf16[8,128,128]{2,1,0:T(8,128)(2,1)} %get-tuple-element.15), calls=%async_computation.1 | async-start | bytes 524288 | tf_op jit(solution)/shard_map/all_to_all | solution.py:194
  25.0 6.5 %collective-permute-start.1 = (bf16[128,512]{1,0:T(8,128)(2,1)S(1)}, bf16[128,512]{1,0:T(8,128)(2,1)S(1)}, u32[]{:S(2)}, u32[]{:S(2)}) collective-permute-start(bf16[128,512]{1,0:T(8,128)(2,1)S(1)} %get-tuple-element.13.refs_3_), channel_id=1, source_target_pairs={{0,2},{2,0},{1,3},{3,1},{4,6},{6,4},{5,7},{7,5},{8,10},{10,8},{9,1... | collective-permute-start | bytes 393224 | tf_op jit(solution)/shard_map/ppermute | solution.py:191

commit v3 on v0

--- a/solution.py
+++ b/solution.py
@@ -1,6 +1,10 @@
+import functools
+
 import jax
 import jax.numpy as jnp
 from jax import lax
+from jax.experimental import pallas as pl
+from jax.experimental.pallas import tpu as pltpu
 from jax.sharding import PartitionSpec as P
 
 ITERS = 2
@@ -8,6 +12,224 @@
 
 ETA = 0.4
 EPS = 1e-06
+MAX_MATRIX = 8 * 1024 * 1024
+PARTS = 3
+FIELDS = 5
+SLOT_LANE = 2 * PARTS
+
+MIB = 1024 * 1024
+VMEM = pl.BlockSpec(memory_space=pltpu.VMEM)
+SMEM = pl.BlockSpec(memory_space=pltpu.SMEM)
+ANY = pl.BlockSpec(memory_space=pl.ANY)
+F32 = jnp.float32
+BF16 = jnp.bfloat16
+
+
+def call(body, outs, in_specs, args, scratch=(), flops=0, limit=32):
+    nbytes = sum(a.size * a.dtype.itemsize for a in list(args) + list(outs))
+    return pl.pallas_call(
+        body,
+        out_shape=list(outs),
+        in_specs=in_specs,
+        out_specs=[VMEM] * len(outs),
+        scratch_shapes=list(scratch),
+        compiler_params=pltpu.CompilerParams(vmem_limit_bytes=limit * MIB),
+        cost_estimate=pl.CostEstimate(flops=flops, bytes_accessed=nbytes, transcendentals=0),
+    )(*args)
+
+
+def split_parts(values):
+    high = values.astype(BF16).astype(F32)
+    rest = values - high
+    middle = rest.astype(BF16).astype(F32)
+    low = (rest - middle).astype(BF16).astype(F32)
+    return [high, middle, low]
+
+
+def project(primal, grad, tau, upper, limited):
+    value = primal - tau * grad
+    capped = jnp.where(limited > 0, jnp.minimum(value, upper), value)
+    return jnp.maximum(capped, 0.0)
+
+
+def share_body(blocks, out):
+    tile = blocks.shape[-1]
+    half = out.shape[0] // tile
+    first = lax.axis_index("rep") * half
+    for k in range(half):
+        out[k * tile : (k + 1) * tile, :] = blocks[0, 0, first + k]
+
+
+def prep_body(index, live, cost_in, rhs_in, upper_in, x_in, y_in, bounded, out, *scratch):
+    *fields, sems = scratch
+    copies = [
+        pltpu.make_async_copy(source, target, sems.at[k])
+        for k, (source, target) in enumerate(zip((cost_in, rhs_in, upper_in, x_in, y_in), fields))
+    ]
+    for copy in copies:
+        copy.start()
+    n, _, tile = out.shape
+    scn = fields[0].shape[1]
+    part = scn // n
+    nslots = index.shape[-1]
+    lane = lax.broadcasted_iota(jnp.int32, (scn, tile), 1)
+    info = jnp.zeros((scn, tile), F32)
+    for k in range(nslots):
+        info = jnp.where(lane == SLOT_LANE + k, index[0, 0, k].astype(F32), info)
+    info = jnp.where(lane == SLOT_LANE + nslots, live[0, 0].astype(F32), info)
+    limited = jnp.broadcast_to(bounded[...].astype(F32), (tile, scn)).T
+    info = jnp.where(lane == SLOT_LANE + nslots + 1, limited, info)
+    for j, (copy, field) in enumerate(zip(copies, fields)):
+        copy.wait()
+        turned = field[...].T
+        if j < 2:
+            for k, values in enumerate(split_parts(jnp.sum(turned * turned, axis=1, keepdims=True))):
+                info = jnp.where(lane == PARTS * j + k, values, info)
+        half = turned.astype(BF16)
+        for d in range(n):
+            out[d, j * part : (j + 1) * part, :] = half[d * part : (d + 1) * part, :]
+    half = info.astype(BF16)
+    for d in range(n):
+        out[d, FIELDS * part :, :] = half[d * part : (d + 1) * part, :]
+
+
+def main_body(n_blk, n_col, shifts, slots, recv, blocks, *refs):
+    n = n_blk * n_col
+    mine, theirs = refs[: n - 1], refs[n - 1 : 2 * (n - 1)]
+    out, mat = refs[2 * (n - 1) :]
+    tile = blocks.shape[-1]
+    nslots = blocks.shape[2]
+    half = mine[0].shape[0] // tile
+    part = recv.shape[1] // (FIELDS + 1)
+    me_b, me_c, me_r = lax.axis_index("blk"), lax.axis_index("col"), lax.axis_index("rep")
+    mat[...] = jnp.zeros(mat.shape, BF16)
+
+    def place(t, s, slot, block):
+        blk, col = me_b ^ t, me_c ^ s
+        owner = blk * n_col + col
+        position = slots[owner, slot]
+        row = pl.multiple_of((blk * n_col + position // n_blk) * tile, tile)
+        column = pl.multiple_of(((position % n_blk) * n_col + col) * tile, tile)
+
+        @pl.when(slot < slots[owner, nslots])
+        def _():
+            mat[pl.ds(row, tile), pl.ds(column, tile)] = block()
+
+    for k in range(nslots):
+        place(0, 0, k, lambda k=k: blocks[0, 0, k])
+    for (t, s), own_part, other_part in zip(shifts, mine, theirs):
+        for k in range(half):
+            place(t, s, me_r * half + k, lambda k=k, r=own_part: r[k * tile : (k + 1) * tile, :])
+            place(t, s, (1 - me_r) * half + k, lambda k=k, r=other_part: r[k * tile : (k + 1) * tile, :])
+
+    def field(j):
+        return jnp.concatenate([recv[d, j * part : (j + 1) * part, :] for d in range(n)], axis=1).astype(F32)
+
+    cost, rhs, upper, primal, dual = (field(j) for j in range(FIELDS))
+    info = recv[0, FIELDS * part :, :].astype(F32)
+    limited = info[:, SLOT_LANE + nslots + 1 : SLOT_LANE + nslots + 2]
+    sums = [jnp.zeros((part, 1), F32)] * 2
+    for d in range(n):
+        info = recv[d, FIELDS * part :, :].astype(F32)
+        for j in range(2):
+            sums[j] += (info[:, PARTS * j : PARTS * j + 1] + info[:, PARTS * j + 1 : PARTS * j + 2]) + info[
+                :, PARTS * j + 2 : PARTS * j + 3
+            ]
+    weight = jnp.sqrt(sums[0] + EPS) / jnp.sqrt(sums[1] + EPS)
+    tau = ETA / weight
+    sigma = ETA * weight
+
+    def store(j, values):
+        values = values.astype(BF16)
+        for d in range(n):
+            out[d, j * part : (j + 1) * part, :] = values[:, d * tile : (d + 1) * tile]
+
+    for step in range(ITERS):
+        kty = jnp.dot(dual.astype(BF16), mat[...], preferred_element_type=F32)
+        store(2 * step, kty)
+        x_new = project(primal, cost - kty, tau, upper, limited)
+        xbar = (2.0 * x_new - primal).astype(BF16)
+        primal = x_new
+        kx = lax.dot_general(xbar, mat[...], (((1,), (1,)), ((), ())), preferred_element_type=F32)
+        store(2 * step + 1, kx)
+        dual = jnp.maximum(dual + sigma * (rhs - kx), 0.0)
+    lane = lax.broadcasted_iota(jnp.int32, (part, tile), 1)
+    packed = jnp.zeros((part, tile), F32)
+    for k, values in enumerate(split_parts(weight)):
+        packed = jnp.where(lane == k, values, packed)
+    for d in range(n):
+        out[d, 2 * ITERS * part :, :] = packed.astype(BF16)
+
+
+def final_body(recv, cost, rhs, upper, x_in, y_in, bounded, x_out, y_out):
+    n, rows, tile = recv.shape
+    part = rows // (2 * ITERS + 1)
+
+    def turned(j):
+        return recv[:, j * part : (j + 1) * part, :].reshape(n * part, tile).astype(F32).T
+
+    packed = turned(2 * ITERS)
+    weight = packed[0:1] + packed[1:2] + packed[2:3]
+    tau = ETA / weight
+    sigma = ETA * weight
+    primal, dual = x_in[...], y_in[...]
+    for step in range(ITERS):
+        primal = project(primal, cost[...] - turned(2 * step), tau, upper[...], bounded[...])
+        dual = jnp.maximum(dual + sigma * (rhs[...] - turned(2 * step + 1)), 0.0)
+    x_out[...] = primal
+    y_out[...] = dual
+
+
+def local_plan(blocks, block_index, live, cost, rhs, upper, x_init, y_init, bounded):
+    n_blk, n_col = lax.axis_size("blk"), lax.axis_size("col")
+    n = n_blk * n_col
+    tile, nslots = blocks.shape[-1], blocks.shape[2]
+    scn = cost.shape[1]
+    part = scn // n
+    like = jax.ShapeDtypeStruct
+    limits = bounded[None, :]
+
+    def spread(value):
+        return lax.all_to_all(value, ("blk", "col"), 0, 0, tiled=True)
+
+    def move(value, t, s):
+        pairs = [(b * n_col + c, (b ^ t) * n_col + (c ^ s)) for b in range(n_blk) for c in range(n_col)]
+        return lax.ppermute(value, ("blk", "col"), pairs)
+
+    (share,) = call(share_body, [like((nslots // 2 * tile, tile), BF16)], [VMEM], [blocks])
+    (sent,) = call(
+        prep_body,
+        [like((n, (FIELDS + 1) * part, tile), BF16)],
+        [SMEM, SMEM] + [ANY] * FIELDS + [VMEM],
+        [block_index, live, cost, rhs, upper, x_init, y_init, limits],
+        scratch=[pltpu.VMEM((tile, scn), F32)] * FIELDS + [pltpu.SemaphoreType.DMA((FIELDS,))],
+        limit=60,
+    )
+    far = n_blk // 2
+    near = [(t, s) for t in range(far) for s in range(n_col) if (t, s) != (0, 0)]
+    mine = {(far, 0): move(share, far, 0)}
+    for t, s in near:
+        mine[t, s] = move(share, t, s)
+    recv = spread(sent)
+    for t, s in near:
+        mine[far + t, s] = move(mine[far, 0], t, s)
+    shifts = list(mine)
+    theirs = [lax.ppermute(mine[shift], "rep", [(0, 1), (1, 0)]) for shift in shifts]
+    slots = recv[:, FIELDS * part, SLOT_LANE : SLOT_LANE + nslots + 1].astype(jnp.int32)
+    (products,) = call(
+        functools.partial(main_body, n_blk, n_col, shifts),
+        [like((n, (2 * ITERS + 1) * part, tile), BF16)],
+        [SMEM] + [VMEM] * (2 * n),
+        [slots, recv, blocks] + [mine[shift] for shift in shifts] + theirs,
+        scratch=[pltpu.VMEM((n * tile, n * tile), BF16)],
+        flops=4 * ITERS * n * n * tile * tile * part,
+    )
+    return call(
+        final_body,
+        [like((tile, scn), F32)] * 2,
+        [VMEM] * (FIELDS + 2),
+        [spread(products), cost, rhs, upper, x_init, y_init, limits],
+    )
 
 
 def project_box(value, upper, bounded):
@@ -15,7 +237,7 @@
     return jnp.maximum(capped, 0.0)
 
 
-def shards(blocks, block_index, live, cost, rhs, upper, x_init, y_init, bounded):
+def collectives_plan(blocks, block_index, live, cost, rhs, upper, x_init, y_init, bounded):
     block_mats = blocks[0, 0]
     slots = block_index[0, 0]
     n_blk = lax.axis_size("blk")
@@ -63,6 +285,16 @@
     return (primal, dual)
 
 
+def shards(*args):
+    n_blk, n_col, n_rep = (lax.axis_size(axis) for axis in ("blk", "col", "rep"))
+    blocks, cost = args[0], args[3]
+    n, tile, nslots = n_blk * n_col, blocks.shape[-1], blocks.shape[2]
+    fits = 2 * (n * tile) ** 2 <= MAX_MATRIX and cost.shape[1] % (16 * n) == 0
+    even = n_blk & (n_blk - 1) == 0 and n_col & (n_col - 1) == 0 and n_blk > 1 and n_rep == 2 and nslots % 2 == 0
+    x, y = (local_plan if fits and even else collectives_plan)(*args)
+    return x, y
+
+
 def solution(mesh):
     in_specs = (
         P("blk", "col", None, None, None),

time: 128 us -> 48.6 us (0.38)
  blocking collectives: 59 us -> 11.7 us
  waiting for transfers between devices: 34.9 us -> 9.53 us
  starting transfers between devices: 0.16 us -> 18.4 us
  between operations: 14.7 us -> 1.39 us
  other arithmetic: 12.9 us -> 0.08 us
  Pallas kernels: 0 us -> 7.07 us
  local copies, waits for them, and re-layouts: 4.49 us -> 0.05 us
    all_gather x4 -> x0, blocking collectives: 36.8 us -> none  [the longest x2 26.7 us: shards(): whole = lax.all_gather(xbar, 'blk', axis=0, tiled=True)]
    reduce_scatter x4 -> x0, waiting for transfers between devices: 34.9 us -> none  [the longest x2 19.2 us: shards(): lax.psum_scatter(cols.reshape(n_blk * tile_size, scn_count).astype(jnp.bf...]
    psum x1 -> x0, blocking collectives: 22.2 us -> none  [shards(): lax.psum((jnp.sum(cost * cost, axis=0), jnp.sum(rhs * rhs, axis=0)), ('bl...]
    all_to_all x0 -> x1, blocking collectives: none -> 11.7 us  [spread(): return lax.all_to_all(value, ('blk', 'col'), 0, 0, tiled=True)]
    ppermute x0 -> x14, starting transfers between devices: none -> 11 us  [the longest x7 9.95 us: move(): return lax.ppermute(value, ('blk', 'col'), pairs)]
    ppermute x0 -> x14, waiting for transfers between devices: none -> 9.53 us  [the longest x7 8.39 us: move(): return lax.ppermute(value, ('blk', 'col'), pairs)]
    all_to_all x0 -> x1, starting transfers between devices: none -> 7.4 us  [spread(): return lax.all_to_all(value, ('blk', 'col'), 0, 0, tiled=True)]
    pallas_call x0 -> x4, Pallas kernels: none -> 7.07 us  [call(): pl.pallas_call(body, out_shape=list(outs), in_specs=in_specs, out_specs=[...]
  transfers between devices with their start and end apart: 4 -> 15, of which waited for: 3 -> 7; matrix products, arithmetic and copies ran while one was open for 0% -> 0% of each run, Pallas kernels for 0% -> 0%
where the time goes in v3:
time: 48.6 us; the launch traced here: 48.2 us
  starting transfers between devices  18.4 us (38%)
  blocking collectives  11.7 us (24%)
  waiting for transfers between devices  9.53 us (20%)
  Pallas kernels  7.07 us (15%)
  between operations  1.39 us (3%)
    all_to_all x1, blocking collectives, spread(): return lax.all_to_all(value, ('blk', 'col'), 0, 0, tiled=True)  11.7 us
    ppermute x7, starting transfers between devices, move(): return lax.ppermute(value, ('blk', 'col'), pairs)  9.95 us
    ppermute x7, waiting for transfers between devices, move(): return lax.ppermute(value, ('blk', 'col'), pairs)  8.39 us
    all_to_all x1, starting transfers between devices, spread(): return lax.all_to_all(value, ('blk', 'col'), 0, 0, tiled=True)  7.4 us
    pallas_call x4, Pallas kernels, call(): pl.pallas_call(body, out_shape=list(outs), in_specs=in_specs, out_specs=[...  7.07 us
    ppermute x7, waiting for transfers between devices, local_plan(): lax.ppermute(mine[shift], 'rep', [(0, 1), (1, 0)])  1.14 us
    ppermute x7, starting transfers between devices, local_plan(): lax.ppermute(mine[shift], 'rep', [(0, 1), (1, 0)])  1.09 us
  transfers between devices with their start and end apart: 15, of which 7 were waited for; matrix products, arithmetic and copies ran while one was open for 0% of the time, Pallas kernels for 0%

profile of v3, /device:TPU:0, one launch (start us, length us, event | category | flops | bytes accessed | tf_op | source)
XLA Modules:
  0.0 48.2 jit_solution(2064957658536118432)
XLA Ops:
  1.3 2.9 %shard_map.104 = bf16[8,96,128]{2,1,0:T(8,128)(2,1)} custom-call(s32[1,1,6]{2,1,0:T(1,128)} %index.1, s32[1,1]{1,0:T(1,128)S(6)} %copy.11.live, f32[128,128]{1,0:T(8,128)} %cost.1, f32[128,128]{1,0:T(8,128)} %rhs.1, f32[128,128]{1,0:T(8,128)} %upper.1, f32[128,128]{1,0:T(8,128)} %x_in.3, f32[128,128]{1,0:T(8,128)} %y_in.3, s32[1,128]{1,0:T(1,128)} %bitcast.3), custom_call_target="tpu_custom_call" | custom-call | bytes 524828 | tf_op jit(solution)/shard_map/pallas_call | solution.py:30
  4.2 0.0 copy-start
  4.2 7.4 %all-to-all-start = ((bf16[8,96,128]{2,1,0:T(8,128)(2,1)}), bf16[8,96,128]{2,1,0:T(8,128)(2,1)S(1)}, u32[]{:S(2)}, u32[]{:S(2)}) async-start(bf16[8,96,128]{2,1,0:T(8,128)(2,1)} %shard_map.104), calls=%async_computation | async-start | bytes 393216 | tf_op jit(solution)/shard_map/all_to_all | solution.py:193
  11.6 0.0 copy-done
  11.6 3.0 %collective-permute-start = (bf16[384,128]{1,0:T(8,128)(2,1)S(1)}, bf16[384,128]{1,0:T(8,128)(2,1)S(1)}, u32[]{:S(2)}, u32[]{:S(2)}) collective-permute-start(bf16[384,128]{1,0:T(8,128)(2,1)S(1)} %shard_map.105), channel_id=1, source_target_pairs={{0,8},{2,10},{4,12},{6,14},{8,0},{10,2},{12,4},{14,6},{1,9},{3,11}... | collective-permute-start | bytes 294920 | tf_op jit(solution)/shard_map/ppermute | solution.py:197
  14.6 1.5 %collective-permute-start.1 = (bf16[384,128]{1,0:T(8,128)(2,1)S(1)}, bf16[384,128]{1,0:T(8,128)(2,1)S(1)}, u32[]{:S(2)}, u32[]{:S(2)}) collective-permute-start(bf16[384,128]{1,0:T(8,128)(2,1)S(1)} %shard_map.105), channel_id=1, source_target_pairs={{0,2},{2,0},{4,6},{6,4},{8,10},{10,8},{12,14},{14,12},{1,3},{3,1},... | collective-permute-start | bytes 294920 | tf_op jit(solution)/shard_map/ppermute | solution.py:197
  16.1 1.5 %collective-permute-start.2 = (bf16[384,128]{1,0:T(8,128)(2,1)S(1)}, bf16[384,128]{1,0:T(8,128)(2,1)S(1)}, u32[]{:S(2)}, u32[]{:S(2)}) collective-permute-start(bf16[384,128]{1,0:T(8,128)(2,1)S(1)} %shard_map.105), channel_id=1, source_target_pairs={{0,4},{2,6},{4,0},{6,2},{8,12},{10,14},{12,8},{14,10},{1,5},{3,7},... | collective-permute-start | bytes 294920 | tf_op jit(solution)/shard_map/ppermute | solution.py:197
  17.5 0.6 %collective-permute-start.3 = (bf16[384,128]{1,0:T(8,128)(2,1)S(1)}, bf16[384,128]{1,0:T(8,128)(2,1)S(1)}, u32[]{:S(2)}, u32[]{:S(2)}) collective-permute-start(bf16[384,128]{1,0:T(8,128)(2,1)S(1)} %shard_map.105), channel_id=1, source_target_pairs={{0,6},{2,4},{4,2},{6,0},{8,14},{10,12},{12,10},{14,8},{1,7},{3,5},... | collective-permute-start | bytes 294920 | tf_op jit(solution)/shard_map/ppermute | solution.py:197
  18.1 5.3 %collective-permute-done.refs_0_ = bf16[384,128]{1,0:T(8,128)(2,1)S(1)} collective-permute-done((bf16[384,128]{1,0:T(8,128)(2,1)S(1)}, bf16[384,128]{1,0:T(8,128)(2,1)S(1)}, u32[]{:S(2)}, u32[]{:S(2)}) %collective-permute-start) | collective-permute-done | bytes 98336 | tf_op jit(solution)/shard_map/ppermute | solution.py:197
  23.3 1.4 %collective-permute-start.4 = (bf16[384,128]{1,0:T(8,128)(2,1)S(1)}, bf16[384,128]{1,0:T(8,128)(2,1)S(1)}, u32[]{:S(2)}, u32[]{:S(2)}) collective-permute-start(bf16[384,128]{1,0:T(8,128)(2,1)S(1)} %collective-permute-done.refs_0_), channel_id=1, source_target_pairs={{0,2},{2,0},{4,6},{6,4},{8,10},{10,8},{12,14},{14,12},{1,3},{3,1},... | collective-permute-start | bytes 294920 | tf_op jit(solution)/shard_map/ppermute | solution.py:197
  24.7 0.0 collective-permute-start.5
  24.7 0.0 collective-permute-done.1.refs_1_
  24.7 2.1 %collective-permute-start.6 = (bf16[384,128]{1,0:T(8,128)(2,1)S(1)}, bf16[384,128]{1,0:T(8,128)(2,1)S(1)}, u32[]{:S(2)}, u32[]{:S(2)}) collective-permute-start(bf16[384,128]{1,0:T(8,128)(2,1)S(1)} %collective-permute-done.refs_0_), channel_id=1, source_target_pairs={{0,6},{2,4},{4,2},{6,0},{8,14},{10,12},{12,10},{14,8},{1,7},{3,5},... | collective-permute-start | bytes 294920 | tf_op jit(solution)/shard_map/ppermute | solution.py:197
  26.8 0.0 collective-permute-done.2.refs_2_
  26.8 0.0 collective-permute-start.7
  26.8 0.0 collective-permute-done.3.refs_3_
  26.9 0.5 %collective-permute-start.8 = (bf16[384,128]{1,0:T(8,128)(2,1)S(1)}, bf16[384,128]{1,0:T(8,128)(2,1)S(1)}, u32[]{:S(2)}, u32[]{:S(2)}) collective-permute-start(bf16[384,128]{1,0:T(8,128)(2,1)S(1)} %collective-permute-done.1.refs_1_), channel_id=1, source_target_pairs={{0,1},{1,0},{2,3},{3,2},{4,5},{5,4},{6,7},{7,6},{8,9},{9,8},{10,11... | collective-permute-start | bytes 294920 | tf_op jit(solution)/shard_map/ppermute | solution.py:217
  27.4 1.2 %collective-permute-done.4.refs_4_ = bf16[384,128]{1,0:T(8,128)(2,1)S(1)} collective-permute-done((bf16[384,128]{1,0:T(8,128)(2,1)S(1)}, bf16[384,128]{1,0:T(8,128)(2,1)S(1)}, u32[]{:S(2)}, u32[]{:S(2)}) %collective-permute-start.4) | collective-permute-done | bytes 98336 | tf_op jit(solution)/shard_map/ppermute | solution.py:197
  28.5 0.0 collective-permute-start.9
  28.5 0.8 %collective-permute-done.5.refs_5_ = bf16[384,128]{1,0:T(8,128)(2,1)S(1)} collective-permute-done((bf16[384,128]{1,0:T(8,128)(2,1)S(1)}, bf16[384,128]{1,0:T(8,128)(2,1)S(1)}, u32[]{:S(2)}, u32[]{:S(2)}) %collective-permute-start.5) | collective-permute-done | bytes 98336 | tf_op jit(solution)/shard_map/ppermute | solution.py:197
  29.3 0.0 collective-permute-start.10
  29.4 1.1 %collective-permute-done.6.refs_6_ = bf16[384,128]{1,0:T(8,128)(2,1)S(1)} collective-permute-done((bf16[384,128]{1,0:T(8,128)(2,1)S(1)}, bf16[384,128]{1,0:T(8,128)(2,1)S(1)}, u32[]{:S(2)}, u32[]{:S(2)}) %collective-permute-start.6) | collective-permute-done | bytes 98336 | tf_op jit(solution)/shard_map/ppermute | solution.py:197
  30.5 0.0 collective-permute-start.11
  30.5 0.0 collective-permute-done.7.refs_7_
  30.5 0.5 %collective-permute-start.12 = (bf16[384,128]{1,0:T(8,128)(2,1)S(1)}, bf16[384,128]{1,0:T(8,128)(2,1)S(1)}, u32[]{:S(2)}, u32[]{:S(2)}) collective-permute-start(bf16[384,128]{1,0:T(8,128)(2,1)S(1)} %collective-permute-done.5.refs_5_), channel_id=1, source_target_pairs={{0,1},{1,0},{2,3},{3,2},{4,5},{5,4},{6,7},{7,6},{8,9},{9,8},{10,11... | collective-permute-start | bytes 294920 | tf_op jit(solution)/shard_map/ppermute | solution.py:217
  31.0 0.0 collective-permute-done.8.refs_8_
  31.0 0.1 collective-permute-start.13
  31.1 0.0 all-to-all-done.recv
  31.1 0.1 slice_convert_fusion
  31.2 0.0 collective-permute-done.9.refs_9_
  31.2 0.0 collective-permute-done.10.refs_10_
  31.2 0.6 %collective-permute-done.11.refs_11_ = bf16[384,128]{1,0:T(8,128)(2,1)S(1)} collective-permute-done((bf16[384,128]{1,0:T(8,128)(2,1)S(1)}, bf16[384,128]{1,0:T(8,128)(2,1)S(1)}, u32[]{:S(2)}, u32[]{:S(2)}) %collective-permute-start.11) | collective-permute-done | bytes 98336 | tf_op jit(solution)/shard_map/ppermute | solution.py:217
  31.8 0.2 collective-permute-done.12.refs_12_
  31.9 0.4 collective-permute-done.13.refs_13_
  32.3 0.0 copy-start.6
  32.3 3.4 %shard_map.106 = bf16[8,80,128]{2,1,0:T(8,128)(2,1)S(1)} custom-call(s32[8,7]{1,0:T(8,128)S(1)} %bitcast.2, bf16[8,96,128]{2,1,0:T(8,128)(2,1)S(1)} %all-to-all-done.recv, bf16[1,1,6,128,128]{4,3,2,1,0:T(8,128)(2,1)S(1)} %copy-done, bf16[384,128]{1,0:T(8,128)(2,1)S(1)} %collective-permute-done.refs_0_, bf16[384,128]{1,0:T(8,128)(2,1)S(1)} %collective-permute-done.1.refs_1_, ...), custom_call_target="tpu_custom_call" | custom-call | flops 134217728 | bytes 1933536 | tf_op jit(solution)/shard_map/pallas_call | solution.py:30
  35.7 0.0 copy-start.1
  35.7 0.0 copy-start.2
  35.7 0.0 copy-start.3
  35.7 0.0 copy-start.4
  35.7 0.0 copy-start.5
  35.7 11.7 %all_to_all.10.recv = bf16[8,80,128]{2,1,0:T(8,128)(2,1)S(1)} all-to-all(bf16[8,80,128]{2,1,0:T(8,128)(2,1)S(1)} %shard_map.106), channel_id=1, replica_groups=mesh['groups'=2,'blk'=4,'col'=2,'rep'=2] {'blk','col'}, dimensions={0} | all-to-all | bytes 327680 | tf_op jit(solution)/shard_map/all_to_all | solution.py:193
  47.4 0.0 copy-done.6
  47.4 0.0 copy-done.1
  47.4 0.0 copy-done.2
  47.4 0.0 copy-done.3
  47.4 0.0 copy-done.4
  47.4 0.0 copy-done.5
  47.4 0.8 %shard_map.107 = (f32[128,128]{1,0:T(8,128)}, f32[128,128]{1,0:T(8,128)}) custom-call(bf16[8,80,128]{2,1,0:T(8,128)(2,1)S(1)} %all_to_all.10.recv, f32[128,128]{1,0:T(8,128)S(1)} %copy-done.1, f32[128,128]{1,0:T(8,128)S(1)} %copy-done.2, f32[128,128]{1,0:T(8,128)S(1)} %copy-done.3, f32[128,128]{1,0:T(8,128)S(1)} %copy-done.4, f32[128,128]{1,0:T(8,128)S(1)} %copy-done.5, ...), custom_call_target="tpu_custom_call" | custom-call | bytes 623104 | tf_op jit(solution)/shard_map/pallas_call | solution.py:30
  (1 shorter events, 0.0 us)
Async XLA Ops:
  4.2 7.4 %copy-start = (bf16[1,1,6,128,128]{4,3,2,1,0:T(8,128)(2,1)S(1)}, bf16[1,1,6,128,128]{4,3,2,1,0:T(8,128)(2,1)}, u32[]{:S(2)}) copy-start(bf16[1,1,6,128,128]{4,3,2,1,0:T(8,128)(2,1)} %blocks.3) | copy-start | bytes 589828
  4.2 26.9 %all-to-all-start = ((bf16[8,96,128]{2,1,0:T(8,128)(2,1)}), bf16[8,96,128]{2,1,0:T(8,128)(2,1)S(1)}, u32[]{:S(2)}, u32[]{:S(2)}) async-start(bf16[8,96,128]{2,1,0:T(8,128)(2,1)} %shard_map.104), calls=%async_computation | async-start | bytes 393216 | tf_op jit(solution)/shard_map/all_to_all | solution.py:193
  11.6 11.7 %collective-permute-start = (bf16[384,128]{1,0:T(8,128)(2,1)S(1)}, bf16[384,128]{1,0:T(8,128)(2,1)S(1)}, u32[]{:S(2)}, u32[]{:S(2)}) collective-permute-start(bf16[384,128]{1,0:T(8,128)(2,1)S(1)} %shard_map.105), channel_id=1, source_target_pairs={{0,8},{2,10},{4,12},{6,14},{8,0},{10,2},{12,4},{14,6},{1,9},{3,11}... | collective-permute-start | bytes 294920 | tf_op jit(solution)/shard_map/ppermute | solution.py:197
  14.6 10.1 %collective-permute-start.1 = (bf16[384,128]{1,0:T(8,128)(2,1)S(1)}, bf16[384,128]{1,0:T(8,128)(2,1)S(1)}, u32[]{:S(2)}, u32[]{:S(2)}) collective-permute-start(bf16[384,128]{1,0:T(8,128)(2,1)S(1)} %shard_map.105), channel_id=1, source_target_pairs={{0,2},{2,0},{4,6},{6,4},{8,10},{10,8},{12,14},{14,12},{1,3},{3,1},... | collective-permute-start | bytes 294920 | tf_op jit(solution)/shard_map/ppermute | solution.py:197
  16.1 10.8 %collective-permute-start.2 = (bf16[384,128]{1,0:T(8,128)(2,1)S(1)}, bf16[384,128]{1,0:T(8,128)(2,1)S(1)}, u32[]{:S(2)}, u32[]{:S(2)}) collective-permute-start(bf16[384,128]{1,0:T(8,128)(2,1)S(1)} %shard_map.105), channel_id=1, source_target_pairs={{0,4},{2,6},{4,0},{6,2},{8,12},{10,14},{12,8},{14,10},{1,5},{3,7},... | collective-permute-start | bytes 294920 | tf_op jit(solution)/shard_map/ppermute | solution.py:197
  17.5 9.3 %collective-permute-start.3 = (bf16[384,128]{1,0:T(8,128)(2,1)S(1)}, bf16[384,128]{1,0:T(8,128)(2,1)S(1)}, u32[]{:S(2)}, u32[]{:S(2)}) collective-permute-start(bf16[384,128]{1,0:T(8,128)(2,1)S(1)} %shard_map.105), channel_id=1, source_target_pairs={{0,6},{2,4},{4,2},{6,0},{8,14},{10,12},{12,10},{14,8},{1,7},{3,5},... | collective-permute-start | bytes 294920 | tf_op jit(solution)/shard_map/ppermute | solution.py:197
  23.3 5.2 %collective-permute-start.4 = (bf16[384,128]{1,0:T(8,128)(2,1)S(1)}, bf16[384,128]{1,0:T(8,128)(2,1)S(1)}, u32[]{:S(2)}, u32[]{:S(2)}) collective-permute-start(bf16[384,128]{1,0:T(8,128)(2,1)S(1)} %collective-permute-done.refs_0_), channel_id=1, source_target_pairs={{0,2},{2,0},{4,6},{6,4},{8,10},{10,8},{12,14},{14,12},{1,3},{3,1},... | collective-permute-start | bytes 294920 | tf_op jit(solution)/shard_map/ppermute | solution.py:197
  24.7 4.6 %collective-permute-start.5 = (bf16[384,128]{1,0:T(8,128)(2,1)S(1)}, bf16[384,128]{1,0:T(8,128)(2,1)S(1)}, u32[]{:S(2)}, u32[]{:S(2)}) collective-permute-start(bf16[384,128]{1,0:T(8,128)(2,1)S(1)} %collective-permute-done.refs_0_), channel_id=1, source_target_pairs={{0,4},{2,6},{4,0},{6,2},{8,12},{10,14},{12,8},{14,10},{1,5},{3,7},... | collective-permute-start | bytes 294920 | tf_op jit(solution)/shard_map/ppermute | solution.py:197
  24.7 5.7 %collective-permute-start.6 = (bf16[384,128]{1,0:T(8,128)(2,1)S(1)}, bf16[384,128]{1,0:T(8,128)(2,1)S(1)}, u32[]{:S(2)}, u32[]{:S(2)}) collective-permute-start(bf16[384,128]{1,0:T(8,128)(2,1)S(1)} %collective-permute-done.refs_0_), channel_id=1, source_target_pairs={{0,6},{2,4},{4,2},{6,0},{8,14},{10,12},{12,10},{14,8},{1,7},{3,5},... | collective-permute-start | bytes 294920 | tf_op jit(solution)/shard_map/ppermute | solution.py:197
  26.8 3.6 %collective-permute-start.7 = (bf16[384,128]{1,0:T(8,128)(2,1)S(1)}, bf16[384,128]{1,0:T(8,128)(2,1)S(1)}, u32[]{:S(2)}, u32[]{:S(2)}) collective-permute-start(bf16[384,128]{1,0:T(8,128)(2,1)S(1)} %collective-permute-done.refs_0_), channel_id=1, source_target_pairs={{0,1},{1,0},{2,3},{3,2},{4,5},{5,4},{6,7},{7,6},{8,9},{9,8},{10,11... | collective-permute-start | bytes 294920 | tf_op jit(solution)/shard_map/ppermute | solution.py:217
  26.9 4.1 %collective-permute-start.8 = (bf16[384,128]{1,0:T(8,128)(2,1)S(1)}, bf16[384,128]{1,0:T(8,128)(2,1)S(1)}, u32[]{:S(2)}, u32[]{:S(2)}) collective-permute-start(bf16[384,128]{1,0:T(8,128)(2,1)S(1)} %collective-permute-done.1.refs_1_), channel_id=1, source_target_pairs={{0,1},{1,0},{2,3},{3,2},{4,5},{5,4},{6,7},{7,6},{8,9},{9,8},{10,11... | collective-permute-start | bytes 294920 | tf_op jit(solution)/shard_map/ppermute | solution.py:217
  28.5 2.6 %collective-permute-start.9 = (bf16[384,128]{1,0:T(8,128)(2,1)S(1)}, bf16[384,128]{1,0:T(8,128)(2,1)S(1)}, u32[]{:S(2)}, u32[]{:S(2)}) collective-permute-start(bf16[384,128]{1,0:T(8,128)(2,1)S(1)} %collective-permute-done.2.refs_2_), channel_id=1, source_target_pairs={{0,1},{1,0},{2,3},{3,2},{4,5},{5,4},{6,7},{7,6},{8,9},{9,8},{10,11... | collective-permute-start | bytes 294920 | tf_op jit(solution)/shard_map/ppermute | solution.py:217
  29.3 1.8 %collective-permute-start.10 = (bf16[384,128]{1,0:T(8,128)(2,1)S(1)}, bf16[384,128]{1,0:T(8,128)(2,1)S(1)}, u32[]{:S(2)}, u32[]{:S(2)}) collective-permute-start(bf16[384,128]{1,0:T(8,128)(2,1)S(1)} %collective-permute-done.3.refs_3_), channel_id=1, source_target_pairs={{0,1},{1,0},{2,3},{3,2},{4,5},{5,4},{6,7},{7,6},{8,9},{9,8},{10,11... | collective-permute-start | bytes 294920 | tf_op jit(solution)/shard_map/ppermute | solution.py:217
  30.5 1.3 %collective-permute-start.11 = (bf16[384,128]{1,0:T(8,128)(2,1)S(1)}, bf16[384,128]{1,0:T(8,128)(2,1)S(1)}, u32[]{:S(2)}, u32[]{:S(2)}) collective-permute-start(bf16[384,128]{1,0:T(8,128)(2,1)S(1)} %collective-permute-done.4.refs_4_), channel_id=1, source_target_pairs={{0,1},{1,0},{2,3},{3,2},{4,5},{5,4},{6,7},{7,6},{8,9},{9,8},{10,11... | collective-permute-start | bytes 294920 | tf_op jit(solution)/shard_map/ppermute | solution.py:217
  30.5 1.5 %collective-permute-start.12 = (bf16[384,128]{1,0:T(8,128)(2,1)S(1)}, bf16[384,128]{1,0:T(8,128)(2,1)S(1)}, u32[]{:S(2)}, u32[]{:S(2)}) collective-permute-start(bf16[384,128]{1,0:T(8,128)(2,1)S(1)} %collective-permute-done.5.refs_5_), channel_id=1, source_target_pairs={{0,1},{1,0},{2,3},{3,2},{4,5},{5,4},{6,7},{7,6},{8,9},{9,8},{10,11... | collective-permute-start | bytes 294920 | tf_op jit(solution)/shard_map/ppermute | solution.py:217
  31.0 1.3 %collective-permute-start.13 = (bf16[384,128]{1,0:T(8,128)(2,1)S(1)}, bf16[384,128]{1,0:T(8,128)(2,1)S(1)}, u32[]{:S(2)}, u32[]{:S(2)}) collective-permute-start(bf16[384,128]{1,0:T(8,128)(2,1)S(1)} %collective-permute-done.6.refs_6_), channel_id=1, source_target_pairs={{0,1},{1,0},{2,3},{3,2},{4,5},{5,4},{6,7},{7,6},{8,9},{9,8},{10,11... | collective-permute-start | bytes 294920 | tf_op jit(solution)/shard_map/ppermute | solution.py:217
  32.3 15.1 %copy-start.6 = (s32[128]{0:T(128)S(1)}, s32[128]{0:T(128)}, u32[]{:S(2)}) copy-start(s32[128]{0:T(128)} %param.17) | copy-start | bytes 1540
  35.7 11.7 %copy-start.1 = (f32[128,128]{1,0:T(8,128)S(1)}, f32[128,128]{1,0:T(8,128)}, u32[]{:S(2)}) copy-start(f32[128,128]{1,0:T(8,128)} %cost.1) | copy-start | bytes 196612
  35.7 11.7 %copy-start.2 = (f32[128,128]{1,0:T(8,128)S(1)}, f32[128,128]{1,0:T(8,128)}, u32[]{:S(2)}) copy-start(f32[128,128]{1,0:T(8,128)} %rhs.1) | copy-start | bytes 196612
  35.7 11.7 %copy-start.3 = (f32[128,128]{1,0:T(8,128)S(1)}, f32[128,128]{1,0:T(8,128)}, u32[]{:S(2)}) copy-start(f32[128,128]{1,0:T(8,128)} %upper.1) | copy-start | bytes 196612
  35.7 11.7 %copy-start.4 = (f32[128,128]{1,0:T(8,128)S(1)}, f32[128,128]{1,0:T(8,128)}, u32[]{:S(2)}) copy-start(f32[128,128]{1,0:T(8,128)} %x_in.3) | copy-start | bytes 196612
  35.7 11.7 %copy-start.5 = (f32[128,128]{1,0:T(8,128)S(1)}, f32[128,128]{1,0:T(8,128)}, u32[]{:S(2)}) copy-start(f32[128,128]{1,0:T(8,128)} %y_in.3) | copy-start | bytes 196612

commit v4 on v3

--- a/solution.py
+++ b/solution.py
@@ -15,7 +15,7 @@
 MAX_MATRIX = 8 * 1024 * 1024
 PARTS = 3
 FIELDS = 5
-SLOT_LANE = 2 * PARTS
+SLOT_ROW = 2 * PARTS
 
 MIB = 1024 * 1024
 VMEM = pl.BlockSpec(memory_space=pltpu.VMEM)
@@ -60,11 +60,18 @@
         out[k * tile : (k + 1) * tile, :] = blocks[0, 0, first + k]
 
 
-def prep_body(index, live, cost_in, rhs_in, upper_in, x_in, y_in, bounded, out, *scratch):
-    *fields, sems = scratch
+def touch_body(part, after, out):
+    del part, after, out
+
+
+def prep_body(index_in, live_in, cost_in, rhs_in, upper_in, x_in, y_in, after, out, token, *scratch):
+    del after
+    token[...] = jnp.zeros(token.shape, F32)
+    *fields, index, live, sems = scratch
+    sources = (cost_in, rhs_in, upper_in, x_in, y_in, index_in, live_in)
     copies = [
         pltpu.make_async_copy(source, target, sems.at[k])
-        for k, (source, target) in enumerate(zip((cost_in, rhs_in, upper_in, x_in, y_in), fields))
+        for k, (source, target) in enumerate(zip(sources, (*fields, index, live)))
     ]
     for copy in copies:
         copy.start()
@@ -72,31 +79,31 @@
     scn = fields[0].shape[1]
     part = scn // n
     nslots = index.shape[-1]
-    lane = lax.broadcasted_iota(jnp.int32, (scn, tile), 1)
-    info = jnp.zeros((scn, tile), F32)
-    for k in range(nslots):
-        info = jnp.where(lane == SLOT_LANE + k, index[0, 0, k].astype(F32), info)
-    info = jnp.where(lane == SLOT_LANE + nslots, live[0, 0].astype(F32), info)
-    limited = jnp.broadcast_to(bounded[...].astype(F32), (tile, scn)).T
-    info = jnp.where(lane == SLOT_LANE + nslots + 1, limited, info)
-    for j, (copy, field) in enumerate(zip(copies, fields)):
-        copy.wait()
-        turned = field[...].T
+    rows = []
+    for j, field in enumerate(fields):
+        copies[j].wait()
+        values = field[...]
         if j < 2:
-            for k, values in enumerate(split_parts(jnp.sum(turned * turned, axis=1, keepdims=True))):
-                info = jnp.where(lane == PARTS * j + k, values, info)
-        half = turned.astype(BF16)
+            rows += split_parts(jnp.sum(values * values, axis=0, keepdims=True))
+        half = values.T.astype(BF16)
         for d in range(n):
             out[d, j * part : (j + 1) * part, :] = half[d * part : (d + 1) * part, :]
-    half = info.astype(BF16)
+    copies[FIELDS].wait()
+    copies[FIELDS + 1].wait()
+    lane = lax.broadcasted_iota(jnp.int32, (1, tile), 1)
+    row = jnp.where(lane == nslots, live[0, 0].astype(F32), 0.0)
+    for k in range(nslots):
+        row = jnp.where(lane == k, index[0, 0, k].astype(F32), row)
+    rows += [row, jnp.zeros((part - len(rows) - 1, tile), F32)]
+    half = jnp.concatenate(rows, axis=0).astype(BF16)
     for d in range(n):
-        out[d, FIELDS * part :, :] = half[d * part : (d + 1) * part, :]
-
-
-def main_body(n_blk, n_col, shifts, slots, recv, blocks, *refs):
+        out[d, FIELDS * part :, :] = half
+
+
+def main_body(n_blk, n_col, shifts, slots, recv, bounded, blocks, *refs):
     n = n_blk * n_col
     mine, theirs = refs[: n - 1], refs[n - 1 : 2 * (n - 1)]
-    out, mat = refs[2 * (n - 1) :]
+    out, scales, mat, turned = refs[2 * (n - 1) :]
     tile = blocks.shape[-1]
     nslots = blocks.shape[2]
     half = mine[0].shape[0] // tile
@@ -126,18 +133,18 @@
         return jnp.concatenate([recv[d, j * part : (j + 1) * part, :] for d in range(n)], axis=1).astype(F32)
 
     cost, rhs, upper, primal, dual = (field(j) for j in range(FIELDS))
-    info = recv[0, FIELDS * part :, :].astype(F32)
-    limited = info[:, SLOT_LANE + nslots + 1 : SLOT_LANE + nslots + 2]
-    sums = [jnp.zeros((part, 1), F32)] * 2
+    sums = [jnp.zeros((1, tile), F32)] * 2
     for d in range(n):
         info = recv[d, FIELDS * part :, :].astype(F32)
         for j in range(2):
-            sums[j] += (info[:, PARTS * j : PARTS * j + 1] + info[:, PARTS * j + 1 : PARTS * j + 2]) + info[
-                :, PARTS * j + 2 : PARTS * j + 3
-            ]
+            first, second, third = (info[PARTS * j + k : PARTS * j + k + 1] for k in range(PARTS))
+            sums[j] += (first + second) + third
     weight = jnp.sqrt(sums[0] + EPS) / jnp.sqrt(sums[1] + EPS)
-    tau = ETA / weight
-    sigma = ETA * weight
+    rows = jnp.concatenate([ETA / weight, ETA * weight, bounded[...].astype(F32), jnp.zeros((5, tile), F32)], axis=0)
+    scales[...] = rows
+    turned[...] = jnp.concatenate([rows, jnp.zeros((tile - 8, tile), F32)], axis=0).T
+    own = turned[pl.ds(pl.multiple_of((me_b * n_col + me_c) * part, part), part), :]
+    tau, sigma, limited = own[:, 0:1], own[:, 1:2], own[:, 2:3]
 
     def store(j, values):
         values = values.astype(BF16)
@@ -153,25 +160,16 @@
         kx = lax.dot_general(xbar, mat[...], (((1,), (1,)), ((), ())), preferred_element_type=F32)
         store(2 * step + 1, kx)
         dual = jnp.maximum(dual + sigma * (rhs - kx), 0.0)
-    lane = lax.broadcasted_iota(jnp.int32, (part, tile), 1)
-    packed = jnp.zeros((part, tile), F32)
-    for k, values in enumerate(split_parts(weight)):
-        packed = jnp.where(lane == k, values, packed)
-    for d in range(n):
-        out[d, 2 * ITERS * part :, :] = packed.astype(BF16)
-
-
-def final_body(recv, cost, rhs, upper, x_in, y_in, bounded, x_out, y_out):
+
+
+def final_body(recv, scales, cost, rhs, upper, x_in, y_in, bounded, x_out, y_out):
     n, rows, tile = recv.shape
-    part = rows // (2 * ITERS + 1)
+    part = rows // (2 * ITERS)
 
     def turned(j):
         return recv[:, j * part : (j + 1) * part, :].reshape(n * part, tile).astype(F32).T
 
-    packed = turned(2 * ITERS)
-    weight = packed[0:1] + packed[1:2] + packed[2:3]
-    tau = ETA / weight
-    sigma = ETA * weight
+    tau, sigma = scales[0:1, :], scales[1:2, :]
     primal, dual = x_in[...], y_in[...]
     for step in range(ITERS):
         primal = project(primal, cost[...] - turned(2 * step), tau, upper[...], bounded[...])
@@ -197,38 +195,47 @@
         return lax.ppermute(value, ("blk", "col"), pairs)
 
     (share,) = call(share_body, [like((nslots // 2 * tile, tile), BF16)], [VMEM], [blocks])
-    (sent,) = call(
-        prep_body,
-        [like((n, (FIELDS + 1) * part, tile), BF16)],
-        [SMEM, SMEM] + [ANY] * FIELDS + [VMEM],
-        [block_index, live, cost, rhs, upper, x_init, y_init, limits],
-        scratch=[pltpu.VMEM((tile, scn), F32)] * FIELDS + [pltpu.SemaphoreType.DMA((FIELDS,))],
-        limit=60,
-    )
     far = n_blk // 2
     near = [(t, s) for t in range(far) for s in range(n_col) if (t, s) != (0, 0)]
     mine = {(far, 0): move(share, far, 0)}
     for t, s in near:
         mine[t, s] = move(share, t, s)
+    sent, token = call(
+        prep_body,
+        [like((n, (FIELDS + 1) * part, tile), BF16), like((8, 128), F32)],
+        [ANY] * (FIELDS + 3),
+        [block_index, live, cost, rhs, upper, x_init, y_init, mine[near[0]][:16]],
+        scratch=[pltpu.VMEM((tile, scn), F32)] * FIELDS
+        + [pltpu.SMEM(block_index.shape, jnp.int32), pltpu.SMEM(live.shape, jnp.int32)]
+        + [pltpu.SemaphoreType.DMA((FIELDS + 2,))],
+        limit=60,
+    )
     recv = spread(sent)
+    mine[far, 0] = pl.pallas_call(
+        touch_body,
+        out_shape=like(share.shape, share.dtype),
+        in_specs=[ANY, ANY],
+        out_specs=ANY,
+        input_output_aliases={0: 0},
+    )(mine[far, 0], token)
     for t, s in near:
         mine[far + t, s] = move(mine[far, 0], t, s)
     shifts = list(mine)
     theirs = [lax.ppermute(mine[shift], "rep", [(0, 1), (1, 0)]) for shift in shifts]
-    slots = recv[:, FIELDS * part, SLOT_LANE : SLOT_LANE + nslots + 1].astype(jnp.int32)
-    (products,) = call(
+    slots = recv[:, FIELDS * part + SLOT_ROW, : nslots + 1].astype(jnp.int32)
+    products, scales = call(
         functools.partial(main_body, n_blk, n_col, shifts),
-        [like((n, (2 * ITERS + 1) * part, tile), BF16)],
-        [SMEM] + [VMEM] * (2 * n),
-        [slots, recv, blocks] + [mine[shift] for shift in shifts] + theirs,
-        scratch=[pltpu.VMEM((n * tile, n * tile), BF16)],
+        [like((n, 2 * ITERS * part, tile), BF16), like((8, scn), F32)],
+        [SMEM] + [VMEM] * (2 * n + 1),
+        [slots, recv, limits, blocks] + [mine[shift] for shift in shifts] + theirs,
+        scratch=[pltpu.VMEM((n * tile, n * tile), BF16), pltpu.VMEM((tile, scn), F32)],
         flops=4 * ITERS * n * n * tile * tile * part,
     )
     return call(
         final_body,
         [like((tile, scn), F32)] * 2,
-        [VMEM] * (FIELDS + 2),
-        [spread(products), cost, rhs, upper, x_init, y_init, limits],
+        [VMEM] * (FIELDS + 3),
+        [spread(products), scales, cost, rhs, upper, x_init, y_init, limits],
     )
 
 
@@ -289,7 +296,7 @@
     n_blk, n_col, n_rep = (lax.axis_size(axis) for axis in ("blk", "col", "rep"))
     blocks, cost = args[0], args[3]
     n, tile, nslots = n_blk * n_col, blocks.shape[-1], blocks.shape[2]
-    fits = 2 * (n * tile) ** 2 <= MAX_MATRIX and cost.shape[1] % (16 * n) == 0
+    fits = 2 * (n * tile) ** 2 <= MAX_MATRIX and cost.shape[1] % (16 * n) == 0 and cost.shape[1] == tile
     even = n_blk & (n_blk - 1) == 0 and n_col & (n_col - 1) == 0 and n_blk > 1 and n_rep == 2 and nslots % 2 == 0
     x, y = (local_plan if fits and even else collectives_plan)(*args)
     return x, y

time: 48.6 us -> 55.3 us (1.14)
  local copies, waits for them, and re-layouts: 0.05 us -> 3.74 us
  waiting for transfers between devices: 9.53 us -> 13 us
  Pallas kernels: 7.07 us -> 6.3 us
  starting transfers between devices: 18.4 us -> 19.1 us
    ppermute x7, waiting for transfers between devices: 8.39 us -> 11.8 us  [move(): return lax.ppermute(value, ('blk', 'col'), pairs)]
    unnamed x14 -> x20, local copies, waits for them, and re-layouts: 0.05 us -> 3.15 us
    ppermute x7, starting transfers between devices: 9.95 us -> 12.3 us  [move(): return lax.ppermute(value, ('blk', 'col'), pairs)]
    all_to_all x1, starting transfers between devices: 7.4 us -> 6.15 us  [spread(): return lax.all_to_all(value, ('blk', 'col'), 0, 0, tiled=True)]
    pallas_call x4, Pallas kernels: 7.07 us -> 6.3 us  [call(): pl.pallas_call(body, out_shape=list(outs), in_specs=in_specs, out_specs=[...]
    slice x0 -> x1, local copies, waits for them, and re-layouts: none -> 0.59 us  [local_plan(): mine[near[0]][:16]]
  transfers between devices with their start and end apart: 15 -> 15, of which waited for: 7 -> 8; matrix products, arithmetic and copies ran while one was open for 0% -> 0% of each run, Pallas kernels for 0% -> 0%
where the time goes in v4:
time: 55.3 us; the launch traced here: 54.9 us
  starting transfers between devices  19.1 us (35%)
  waiting for transfers between devices  13 us (24%)
  blocking collectives  11.4 us (21%)
  Pallas kernels  6.3 us (11%)
  local copies, waits for them, and re-layouts  3.74 us (7%)
  between operations  1.39 us (3%)
    ppermute x7, starting transfers between devices, move(): return lax.ppermute(value, ('blk', 'col'), pairs)  12.3 us
    ppermute x7, waiting for transfers between devices, move(): return lax.ppermute(value, ('blk', 'col'), pairs)  11.8 us
    all_to_all x1, blocking collectives, spread(): return lax.all_to_all(value, ('blk', 'col'), 0, 0, tiled=True)  11.4 us
    pallas_call x4, Pallas kernels, call(): pl.pallas_call(body, out_shape=list(outs), in_specs=in_specs, out_specs=[...  6.3 us
    all_to_all x1, starting transfers between devices, spread(): return lax.all_to_all(value, ('blk', 'col'), 0, 0, tiled=True)  6.15 us
    unnamed x20, local copies, waits for them, and re-layouts  3.15 us
    ppermute x7, waiting for transfers between devices, local_plan(): lax.ppermute(mine[shift], 'rep', [(0, 1), (1, 0)])  1.2 us
  transfers between devices with their start and end apart: 15, of which 8 were waited for; matrix products, arithmetic and copies ran while one was open for 0% of the time, Pallas kernels for 0%

profile of v4, /device:TPU:0, one launch (start us, length us, event | category | flops | bytes accessed | tf_op | source)
XLA Modules:
  0.0 54.9 jit_solution(17963582299534137430)
XLA Ops:
  0.6 0.0 copy-start
  0.6 0.9 %copy-done = bf16[1,1,6,128,128]{4,3,2,1,0:T(8,128)(2,1)S(1)} copy-done((bf16[1,1,6,128,128]{4,3,2,1,0:T(8,128)(2,1)S(1)}, bf16[1,1,6,128,128]{4,3,2,1,0:T(8,128)(2,1)}, u32[]{:S(2)}) %copy-start) | copy-done | bytes 196632
  1.6 3.0 %collective-permute-start = (bf16[384,128]{1,0:T(8,128)(2,1)S(1)}, bf16[384,128]{1,0:T(8,128)(2,1)S(1)}, u32[]{:S(2)}, u32[]{:S(2)}) collective-permute-start(bf16[384,128]{1,0:T(8,128)(2,1)S(1)} %shard_map.104), channel_id=1, source_target_pairs={{0,2},{2,0},{4,6},{6,4},{8,10},{10,8},{12,14},{14,12},{1,3},{3,1},... | collective-permute-start | bytes 294920 | tf_op jit(solution)/shard_map/ppermute | solution.py:195
  5.2 2.1 %collective-permute-done.refs_1_ = bf16[384,128]{1,0:T(8,128)(2,1)S(1)} collective-permute-done((bf16[384,128]{1,0:T(8,128)(2,1)S(1)}, bf16[384,128]{1,0:T(8,128)(2,1)S(1)}, u32[]{:S(2)}, u32[]{:S(2)}) %collective-permute-start) | collective-permute-done | bytes 98336 | tf_op jit(solution)/shard_map/ppermute | solution.py:195
  7.4 0.6 %slice.8.after = bf16[16,128]{1,0:T(8,128)(2,1)} slice(bf16[384,128]{1,0:T(8,128)(2,1)S(1)} %collective-permute-done.refs_1_), slice={[0:16], [0:128]} | slice | bytes 8192 | tf_op jit(solution)/shard_map/slice | solution.py:207
  8.0 2.1 %shard_map.105 = (bf16[8,96,128]{2,1,0:T(8,128)(2,1)}, f32[8,128]{1,0:T(8,128)}) custom-call(s32[1,1,6]{2,1,0:T(1,128)} %index_in.1, s32[1,1]{1,0:T(1,128)S(6)} %copy.13.live_in, f32[128,128]{1,0:T(8,128)} %cost.1, f32[128,128]{1,0:T(8,128)} %rhs.1, f32[128,128]{1,0:T(8,128)} %upper.1, f32[128,128]{1,0:T(8,128)} %x_in.3, f32[128,128]{1,0:T(8,128)} %y_in.3, ...), custom_call_target="tpu_custom_call" | custom-call | bytes 532508 | tf_op jit(solution)/shard_map/pallas_call | solution.py:30
  10.1 6.1 %all-to-all-start = ((bf16[8,96,128]{2,1,0:T(8,128)(2,1)}), bf16[8,96,128]{2,1,0:T(8,128)(2,1)S(1)}, u32[]{:S(2)}, u32[]{:S(2)}) async-start(bf16[8,96,128]{2,1,0:T(8,128)(2,1)} %get-tuple-element.6), calls=%async_computation | async-start | bytes 393216 | tf_op jit(solution)/shard_map/all_to_all | solution.py:191
  16.2 0.0 copy-start.1
  16.2 2.9 %collective-permute-start.3 = (bf16[384,128]{1,0:T(8,128)(2,1)S(1)}, bf16[384,128]{1,0:T(8,128)(2,1)S(1)}, u32[]{:S(2)}, u32[]{:S(2)}) collective-permute-start(bf16[384,128]{1,0:T(8,128)(2,1)S(1)} %shard_map.104), channel_id=1, source_target_pairs={{0,6},{2,4},{4,2},{6,0},{8,14},{10,12},{12,10},{14,8},{1,7},{3,5},... | collective-permute-start | bytes 294920 | tf_op jit(solution)/shard_map/ppermute | solution.py:195
  19.2 0.6 %collective-permute-start.2 = (bf16[384,128]{1,0:T(8,128)(2,1)S(1)}, bf16[384,128]{1,0:T(8,128)(2,1)S(1)}, u32[]{:S(2)}, u32[]{:S(2)}) collective-permute-start(bf16[384,128]{1,0:T(8,128)(2,1)S(1)} %shard_map.104), channel_id=1, source_target_pairs={{0,4},{2,6},{4,0},{6,2},{8,12},{10,14},{12,8},{14,10},{1,5},{3,7},... | collective-permute-start | bytes 294920 | tf_op jit(solution)/shard_map/ppermute | solution.py:195
  19.7 2.4 %collective-permute-start.1 = (bf16[384,128]{1,0:T(8,128)(2,1)S(1)}, bf16[384,128]{1,0:T(8,128)(2,1)S(1)}, u32[]{:S(2)}, u32[]{:S(2)}) collective-permute-start(bf16[384,128]{1,0:T(8,128)(2,1)S(1)} %shard_map.104), channel_id=1, source_target_pairs={{0,8},{2,10},{4,12},{6,14},{8,0},{10,2},{12,4},{14,6},{1,9},{3,11}... | collective-permute-start | bytes 294920 | tf_op jit(solution)/shard_map/ppermute | solution.py:195
  22.1 4.7 %collective-permute-done.3.refs_3_ = bf16[384,128]{1,0:T(8,128)(2,1)S(1)} collective-permute-done((bf16[384,128]{1,0:T(8,128)(2,1)S(1)}, bf16[384,128]{1,0:T(8,128)(2,1)S(1)}, u32[]{:S(2)}, u32[]{:S(2)}) %collective-permute-start.3) | collective-permute-done | bytes 98336 | tf_op jit(solution)/shard_map/ppermute | solution.py:195
  26.8 0.0 collective-permute-start.10
  26.8 0.6 %collective-permute-done.2.refs_2_ = bf16[384,128]{1,0:T(8,128)(2,1)S(1)} collective-permute-done((bf16[384,128]{1,0:T(8,128)(2,1)S(1)}, bf16[384,128]{1,0:T(8,128)(2,1)S(1)}, u32[]{:S(2)}, u32[]{:S(2)}) %collective-permute-start.2) | collective-permute-done | bytes 98336 | tf_op jit(solution)/shard_map/ppermute | solution.py:195
  27.4 0.0 collective-permute-start.9
  27.4 0.0 collective-permute-done.1.part
  27.4 0.0 copy-start.2
  27.4 0.6 %copy-done.2 = bf16[384,128]{1,0:T(8,128)(2,1)} copy-done((bf16[384,128]{1,0:T(8,128)(2,1)}, bf16[384,128]{1,0:T(8,128)(2,1)S(1)}, u32[]{:S(2)}) %copy-start.2) | copy-done | bytes 98328
  28.0 2.9 %collective-permute-start.6 = (bf16[384,128]{1,0:T(8,128)(2,1)}, bf16[384,128]{1,0:T(8,128)(2,1)S(1)}, u32[]{:S(2)}, u32[]{:S(2)}) collective-permute-start(bf16[384,128]{1,0:T(8,128)(2,1)} %shard_map.106.refs_0_), channel_id=1, source_target_pairs={{0,6},{2,4},{4,2},{6,0},{8,14},{10,12},{12,10},{14,8},{1,7},{3,5},... | collective-permute-start | bytes 294920 | tf_op jit(solution)/shard_map/ppermute | solution.py:195
  30.9 0.0 collective-permute-start.5
  30.9 0.6 %collective-permute-start.4 = (bf16[384,128]{1,0:T(8,128)(2,1)}, bf16[384,128]{1,0:T(8,128)(2,1)S(1)}, u32[]{:S(2)}, u32[]{:S(2)}) collective-permute-start(bf16[384,128]{1,0:T(8,128)(2,1)} %shard_map.106.refs_0_), channel_id=1, source_target_pairs={{0,2},{2,0},{4,6},{6,4},{8,10},{10,8},{12,14},{14,12},{1,3},{3,1},... | collective-permute-start | bytes 294920 | tf_op jit(solution)/shard_map/ppermute | solution.py:195
  31.5 0.0 collective-permute-done.10.refs_10_
  31.5 0.0 collective-permute-start.7
  31.5 0.0 collective-permute-done.9.refs_9_
  31.5 0.5 collective-permute-start.8
  32.0 2.7 %collective-permute-done.6.refs_6_ = bf16[384,128]{1,0:T(8,128)(2,1)S(1)} collective-permute-done((bf16[384,128]{1,0:T(8,128)(2,1)}, bf16[384,128]{1,0:T(8,128)(2,1)S(1)}, u32[]{:S(2)}, u32[]{:S(2)}) %collective-permute-start.6) | collective-permute-done | bytes 98336 | tf_op jit(solution)/shard_map/ppermute | solution.py:195
  34.7 0.0 collective-permute-start.13
  34.7 1.3 %collective-permute-done.5.refs_5_ = bf16[384,128]{1,0:T(8,128)(2,1)S(1)} collective-permute-done((bf16[384,128]{1,0:T(8,128)(2,1)}, bf16[384,128]{1,0:T(8,128)(2,1)S(1)}, u32[]{:S(2)}, u32[]{:S(2)}) %collective-permute-start.5) | collective-permute-done | bytes 98336 | tf_op jit(solution)/shard_map/ppermute | solution.py:195
  36.0 0.0 collective-permute-start.12
  36.0 0.4 collective-permute-done.4.refs_4_
  36.4 0.1 collective-permute-start.11
  36.5 0.0 all-to-all-done.recv
  36.5 0.0 collective-permute-done.8.refs_8_
  36.5 0.0 collective-permute-done.7.refs_7_
  36.5 0.0 collective-permute-done.13.refs_13_
  36.5 0.7 %collective-permute-done.12.refs_12_ = bf16[384,128]{1,0:T(8,128)(2,1)S(1)} collective-permute-done((bf16[384,128]{1,0:T(8,128)(2,1)S(1)}, bf16[384,128]{1,0:T(8,128)(2,1)S(1)}, u32[]{:S(2)}, u32[]{:S(2)}) %collective-permute-start.12) | collective-permute-done | bytes 98336 | tf_op jit(solution)/shard_map/ppermute | solution.py:224
  37.3 0.4 collective-permute-done.11.refs_11_
  37.7 0.0 copy-start.9
  37.7 0.0 copy-done.1
  37.7 0.7 %copy-done.9 = s32[128]{0:T(128)S(1)} copy-done((s32[128]{0:T(128)S(1)}, s32[128]{0:T(128)}, u32[]{:S(2)}) %copy-start.9) | copy-done | bytes 536
  38.4 0.0 copy-start.3
  38.4 0.9 %copy-done.3 = bf16[384,128]{1,0:T(8,128)(2,1)S(1)} copy-done((bf16[384,128]{1,0:T(8,128)(2,1)S(1)}, bf16[384,128]{1,0:T(8,128)(2,1)}, u32[]{:S(2)}) %copy-start.3) | copy-done | bytes 98328
  39.3 0.0 copy-start.8
  39.3 3.4 %shard_map.107 = (bf16[8,64,128]{2,1,0:T(8,128)(2,1)S(1)}, f32[8,128]{1,0:T(8,128)S(1)}) custom-call(s32[8,7]{1,0:T(8,128)S(1)} %bitcast.2, bf16[8,96,128]{2,1,0:T(8,128)(2,1)S(1)} %all-to-all-done.recv, s32[1,128]{1,0:T(1,128)S(1)} %bitcast.3, bf16[1,1,6,128,128]{4,3,2,1,0:T(8,128)(2,1)S(1)} %copy-done.1, bf16[384,128]{1,0:T(8,128)(2,1)S(1)} %copy-done.3, ...), custom_call_target="tpu_custom_call" | custom-call | flops 134217728 | bytes 1905376 | tf_op jit(solution)/shard_map/pallas_call | solution.py:30
  42.7 0.0 copy-start.4
  42.7 0.0 copy-start.5
  42.7 0.0 copy-start.6
  42.7 0.0 copy-start.7
  42.7 11.4 %all_to_all.10.recv = bf16[8,64,128]{2,1,0:T(8,128)(2,1)S(1)} all-to-all(bf16[8,64,128]{2,1,0:T(8,128)(2,1)S(1)} %get-tuple-element.8), channel_id=1, replica_groups=mesh['groups'=2,'blk'=4,'col'=2,'rep'=2] {'blk','col'}, dimensions={0} | all-to-all | bytes 262144 | tf_op jit(solution)/shard_map/all_to_all | solution.py:191
  54.1 0.0 copy-done.8
  54.1 0.0 copy-done.4
  54.1 0.0 copy-done.5
  54.1 0.0 copy-done.6
  54.1 0.0 copy-done.7
  54.1 0.8 %shard_map.108 = (f32[128,128]{1,0:T(8,128)}, f32[128,128]{1,0:T(8,128)}) custom-call(bf16[8,64,128]{2,1,0:T(8,128)(2,1)S(1)} %all_to_all.10.recv, f32[8,128]{1,0:T(8,128)S(1)} %get-tuple-element.9.scales, f32[128,128]{1,0:T(8,128)S(1)} %copy-done.4, f32[128,128]{1,0:T(8,128)S(1)} %copy-done.5, f32[128,128]{1,0:T(8,128)S(1)} %copy-done.6, ...), custom_call_target="tpu_custom_call" | custom-call | bytes 594432 | tf_op jit(solution)/shard_map/pallas_call | solution.py:30
  (3 shorter events, 0.0 us)
Async XLA Ops:
  0.6 0.9 %copy-start = (bf16[1,1,6,128,128]{4,3,2,1,0:T(8,128)(2,1)S(1)}, bf16[1,1,6,128,128]{4,3,2,1,0:T(8,128)(2,1)}, u32[]{:S(2)}) copy-start(bf16[1,1,6,128,128]{4,3,2,1,0:T(8,128)(2,1)} %blocks.3) | copy-start | bytes 589828
  1.6 5.8 %collective-permute-start = (bf16[384,128]{1,0:T(8,128)(2,1)S(1)}, bf16[384,128]{1,0:T(8,128)(2,1)S(1)}, u32[]{:S(2)}, u32[]{:S(2)}) collective-permute-start(bf16[384,128]{1,0:T(8,128)(2,1)S(1)} %shard_map.104), channel_id=1, source_target_pairs={{0,2},{2,0},{4,6},{6,4},{8,10},{10,8},{12,14},{14,12},{1,3},{3,1},... | collective-permute-start | bytes 294920 | tf_op jit(solution)/shard_map/ppermute | solution.py:195
  10.1 26.4 %all-to-all-start = ((bf16[8,96,128]{2,1,0:T(8,128)(2,1)}), bf16[8,96,128]{2,1,0:T(8,128)(2,1)S(1)}, u32[]{:S(2)}, u32[]{:S(2)}) async-start(bf16[8,96,128]{2,1,0:T(8,128)(2,1)} %get-tuple-element.6), calls=%async_computation | async-start | bytes 393216 | tf_op jit(solution)/shard_map/all_to_all | solution.py:191
  16.2 21.5 %copy-start.1 = (bf16[1,1,6,128,128]{4,3,2,1,0:T(8,128)(2,1)S(1)}, bf16[1,1,6,128,128]{4,3,2,1,0:T(8,128)(2,1)}, u32[]{:S(2)}) copy-start(bf16[1,1,6,128,128]{4,3,2,1,0:T(8,128)(2,1)} %blocks.3) | copy-start | bytes 589828
  16.2 10.5 %collective-permute-start.3 = (bf16[384,128]{1,0:T(8,128)(2,1)S(1)}, bf16[384,128]{1,0:T(8,128)(2,1)S(1)}, u32[]{:S(2)}, u32[]{:S(2)}) collective-permute-start(bf16[384,128]{1,0:T(8,128)(2,1)S(1)} %shard_map.104), channel_id=1, source_target_pairs={{0,6},{2,4},{4,2},{6,0},{8,14},{10,12},{12,10},{14,8},{1,7},{3,5},... | collective-permute-start | bytes 294920 | tf_op jit(solution)/shard_map/ppermute | solution.py:195
  19.2 8.2 %collective-permute-start.2 = (bf16[384,128]{1,0:T(8,128)(2,1)S(1)}, bf16[384,128]{1,0:T(8,128)(2,1)S(1)}, u32[]{:S(2)}, u32[]{:S(2)}) collective-permute-start(bf16[384,128]{1,0:T(8,128)(2,1)S(1)} %shard_map.104), channel_id=1, source_target_pairs={{0,4},{2,6},{4,0},{6,2},{8,12},{10,14},{12,8},{14,10},{1,5},{3,7},... | collective-permute-start | bytes 294920 | tf_op jit(solution)/shard_map/ppermute | solution.py:195
  19.7 7.7 %collective-permute-start.1 = (bf16[384,128]{1,0:T(8,128)(2,1)S(1)}, bf16[384,128]{1,0:T(8,128)(2,1)S(1)}, u32[]{:S(2)}, u32[]{:S(2)}) collective-permute-start(bf16[384,128]{1,0:T(8,128)(2,1)S(1)} %shard_map.104), channel_id=1, source_target_pairs={{0,8},{2,10},{4,12},{6,14},{8,0},{10,2},{12,4},{14,6},{1,9},{3,11}... | collective-permute-start | bytes 294920 | tf_op jit(solution)/shard_map/ppermute | solution.py:195
  26.8 4.7 %collective-permute-start.10 = (bf16[384,128]{1,0:T(8,128)(2,1)S(1)}, bf16[384,128]{1,0:T(8,128)(2,1)S(1)}, u32[]{:S(2)}, u32[]{:S(2)}) collective-permute-start(bf16[384,128]{1,0:T(8,128)(2,1)S(1)} %collective-permute-done.3.refs_3_), channel_id=1, source_target_pairs={{0,1},{1,0},{2,3},{3,2},{4,5},{5,4},{6,7},{7,6},{8,9},{9,8},{10,11... | collective-permute-start | bytes 294920 | tf_op jit(solution)/shard_map/ppermute | solution.py:224
  27.4 4.1 %collective-permute-start.9 = (bf16[384,128]{1,0:T(8,128)(2,1)S(1)}, bf16[384,128]{1,0:T(8,128)(2,1)S(1)}, u32[]{:S(2)}, u32[]{:S(2)}) collective-permute-start(bf16[384,128]{1,0:T(8,128)(2,1)S(1)} %collective-permute-done.2.refs_2_), channel_id=1, source_target_pairs={{0,1},{1,0},{2,3},{3,2},{4,5},{5,4},{6,7},{7,6},{8,9},{9,8},{10,11... | collective-permute-start | bytes 294920 | tf_op jit(solution)/shard_map/ppermute | solution.py:224
  27.4 0.6 %copy-start.2 = (bf16[384,128]{1,0:T(8,128)(2,1)}, bf16[384,128]{1,0:T(8,128)(2,1)S(1)}, u32[]{:S(2)}) copy-start(bf16[384,128]{1,0:T(8,128)(2,1)S(1)} %collective-permute-done.1.part) | copy-start | bytes 294916
  28.0 6.7 %collective-permute-start.6 = (bf16[384,128]{1,0:T(8,128)(2,1)}, bf16[384,128]{1,0:T(8,128)(2,1)S(1)}, u32[]{:S(2)}, u32[]{:S(2)}) collective-permute-start(bf16[384,128]{1,0:T(8,128)(2,1)} %shard_map.106.refs_0_), channel_id=1, source_target_pairs={{0,6},{2,4},{4,2},{6,0},{8,14},{10,12},{12,10},{14,8},{1,7},{3,5},... | collective-permute-start | bytes 294920 | tf_op jit(solution)/shard_map/ppermute | solution.py:195
  30.9 5.1 %collective-permute-start.5 = (bf16[384,128]{1,0:T(8,128)(2,1)}, bf16[384,128]{1,0:T(8,128)(2,1)S(1)}, u32[]{:S(2)}, u32[]{:S(2)}) collective-permute-start(bf16[384,128]{1,0:T(8,128)(2,1)} %shard_map.106.refs_0_), channel_id=1, source_target_pairs={{0,4},{2,6},{4,0},{6,2},{8,12},{10,14},{12,8},{14,10},{1,5},{3,7},... | collective-permute-start | bytes 294920 | tf_op jit(solution)/shard_map/ppermute | solution.py:195
  30.9 5.6 %collective-permute-start.4 = (bf16[384,128]{1,0:T(8,128)(2,1)}, bf16[384,128]{1,0:T(8,128)(2,1)S(1)}, u32[]{:S(2)}, u32[]{:S(2)}) collective-permute-start(bf16[384,128]{1,0:T(8,128)(2,1)} %shard_map.106.refs_0_), channel_id=1, source_target_pairs={{0,2},{2,0},{4,6},{6,4},{8,10},{10,8},{12,14},{14,12},{1,3},{3,1},... | collective-permute-start | bytes 294920 | tf_op jit(solution)/shard_map/ppermute | solution.py:195
  31.5 5.0 %collective-permute-start.7 = (bf16[384,128]{1,0:T(8,128)(2,1)}, bf16[384,128]{1,0:T(8,128)(2,1)S(1)}, u32[]{:S(2)}, u32[]{:S(2)}) collective-permute-start(bf16[384,128]{1,0:T(8,128)(2,1)} %shard_map.106.refs_0_), channel_id=1, source_target_pairs={{0,1},{1,0},{2,3},{3,2},{4,5},{5,4},{6,7},{7,6},{8,9},{9,8},{10,11... | collective-permute-start | bytes 294920 | tf_op jit(solution)/shard_map/ppermute | solution.py:224
  31.5 5.0 %collective-permute-start.8 = (bf16[384,128]{1,0:T(8,128)(2,1)S(1)}, bf16[384,128]{1,0:T(8,128)(2,1)S(1)}, u32[]{:S(2)}, u32[]{:S(2)}) collective-permute-start(bf16[384,128]{1,0:T(8,128)(2,1)S(1)} %collective-permute-done.refs_1_), channel_id=1, source_target_pairs={{0,1},{1,0},{2,3},{3,2},{4,5},{5,4},{6,7},{7,6},{8,9},{9,8},{10,11... | collective-permute-start | bytes 294920 | tf_op jit(solution)/shard_map/ppermute | solution.py:224
  34.7 1.8 %collective-permute-start.13 = (bf16[384,128]{1,0:T(8,128)(2,1)S(1)}, bf16[384,128]{1,0:T(8,128)(2,1)S(1)}, u32[]{:S(2)}, u32[]{:S(2)}) collective-permute-start(bf16[384,128]{1,0:T(8,128)(2,1)S(1)} %collective-permute-done.6.refs_6_), channel_id=1, source_target_pairs={{0,1},{1,0},{2,3},{3,2},{4,5},{5,4},{6,7},{7,6},{8,9},{9,8},{10,11... | collective-permute-start | bytes 294920 | tf_op jit(solution)/shard_map/ppermute | solution.py:224
  36.0 1.3 %collective-permute-start.12 = (bf16[384,128]{1,0:T(8,128)(2,1)S(1)}, bf16[384,128]{1,0:T(8,128)(2,1)S(1)}, u32[]{:S(2)}, u32[]{:S(2)}) collective-permute-start(bf16[384,128]{1,0:T(8,128)(2,1)S(1)} %collective-permute-done.5.refs_5_), channel_id=1, source_target_pairs={{0,1},{1,0},{2,3},{3,2},{4,5},{5,4},{6,7},{7,6},{8,9},{9,8},{10,11... | collective-permute-start | bytes 294920 | tf_op jit(solution)/shard_map/ppermute | solution.py:224
  36.4 1.3 %collective-permute-start.11 = (bf16[384,128]{1,0:T(8,128)(2,1)S(1)}, bf16[384,128]{1,0:T(8,128)(2,1)S(1)}, u32[]{:S(2)}, u32[]{:S(2)}) collective-permute-start(bf16[384,128]{1,0:T(8,128)(2,1)S(1)} %collective-permute-done.4.refs_4_), channel_id=1, source_target_pairs={{0,1},{1,0},{2,3},{3,2},{4,5},{5,4},{6,7},{7,6},{8,9},{9,8},{10,11... | collective-permute-start | bytes 294920 | tf_op jit(solution)/shard_map/ppermute | solution.py:224
  37.7 0.7 %copy-start.9 = (s32[128]{0:T(128)S(1)}, s32[128]{0:T(128)}, u32[]{:S(2)}) copy-start(s32[128]{0:T(128)} %param.17) | copy-start | bytes 1540
  38.4 0.9 %copy-start.3 = (bf16[384,128]{1,0:T(8,128)(2,1)S(1)}, bf16[384,128]{1,0:T(8,128)(2,1)}, u32[]{:S(2)}) copy-start(bf16[384,128]{1,0:T(8,128)(2,1)} %shard_map.106.refs_0_) | copy-start | bytes 294916
  39.3 14.8 %copy-start.8 = (f32[128,128]{1,0:T(8,128)S(1)}, f32[128,128]{1,0:T(8,128)}, u32[]{:S(2)}) copy-start(f32[128,128]{1,0:T(8,128)} %y_in.3) | copy-start | bytes 196612
  42.7 11.4 %copy-start.4 = (f32[128,128]{1,0:T(8,128)S(1)}, f32[128,128]{1,0:T(8,128)}, u32[]{:S(2)}) copy-start(f32[128,128]{1,0:T(8,128)} %cost.1) | copy-start | bytes 196612
  42.7 11.4 %copy-start.5 = (f32[128,128]{1,0:T(8,128)S(1)}, f32[128,128]{1,0:T(8,128)}, u32[]{:S(2)}) copy-start(f32[128,128]{1,0:T(8,128)} %rhs.1) | copy-start | bytes 196612
  42.7 11.4 %copy-start.6 = (f32[128,128]{1,0:T(8,128)S(1)}, f32[128,128]{1,0:T(8,128)}, u32[]{:S(2)}) copy-start(f32[128,128]{1,0:T(8,128)} %upper.1) | copy-start | bytes 196612
  42.7 11.4 %copy-start.7 = (f32[128,128]{1,0:T(8,128)S(1)}, f32[128,128]{1,0:T(8,128)}, u32[]{:S(2)}) copy-start(f32[128,128]{1,0:T(8,128)} %x_in.3) | copy-start | bytes 196612

commit v5 on v4

--- a/solution.py
+++ b/solution.py
@@ -1,4 +1,5 @@
 import functools
+import math
 
 import jax
 import jax.numpy as jnp
@@ -25,8 +26,16 @@
 BF16 = jnp.bfloat16
 
 
+def held(shape, dtype):
+    return pltpu.VMEM(shape, dtype)
+
+
+def pinned(values):
+    return [pltpu.with_memory_space_constraint(v, pltpu.HBM) for v in values]
+
+
 def call(body, outs, in_specs, args, scratch=(), flops=0, limit=32):
-    nbytes = sum(a.size * a.dtype.itemsize for a in list(args) + list(outs))
+    nbytes = sum(math.prod(a.shape) * jnp.dtype(a.dtype).itemsize for a in list(args) + list(outs))
     return pl.pallas_call(
         body,
         out_shape=list(outs),
@@ -52,32 +61,21 @@
     return jnp.maximum(capped, 0.0)
 
 
-def share_body(blocks, out):
-    tile = blocks.shape[-1]
-    half = out.shape[0] // tile
+def prep_body(n_col, far, near, *refs):
+    live, *sources = refs[: FIELDS + 3]
+    far_out, *near_outs, own_out = refs[FIELDS + 3 : FIELDS + 5 + len(near)]
+    *fields, share, index, turned, sems = refs[FIELDS + 5 + len(near) :]
+    half, tile = share.shape[0], share.shape[1]
     first = lax.axis_index("rep") * half
-    for k in range(half):
-        out[k * tile : (k + 1) * tile, :] = blocks[0, 0, first + k]
-
-
-def touch_body(part, after, out):
-    del part, after, out
-
-
-def prep_body(index_in, live_in, cost_in, rhs_in, upper_in, x_in, y_in, after, out, token, *scratch):
-    del after
-    token[...] = jnp.zeros(token.shape, F32)
-    *fields, index, live, sems = scratch
-    sources = (cost_in, rhs_in, upper_in, x_in, y_in, index_in, live_in)
+    targets = (*fields, index)
     copies = [
         pltpu.make_async_copy(source, target, sems.at[k])
-        for k, (source, target) in enumerate(zip(sources, (*fields, index, live)))
+        for k, (source, target) in enumerate(zip(sources[:-1], targets))
     ]
+    copies.append(pltpu.make_async_copy(sources[-1].at[0, 0, pl.ds(first, half)], share, sems.at[FIELDS + 1]))
     for copy in copies:
         copy.start()
-    n, _, tile = out.shape
-    scn = fields[0].shape[1]
-    part = scn // n
+    part = own_out.shape[0] // (FIELDS + 1)
     nslots = index.shape[-1]
     rows = []
     for j, field in enumerate(fields):
@@ -85,60 +83,83 @@
         values = field[...]
         if j < 2:
             rows += split_parts(jnp.sum(values * values, axis=0, keepdims=True))
-        half = values.T.astype(BF16)
-        for d in range(n):
-            out[d, j * part : (j + 1) * part, :] = half[d * part : (d + 1) * part, :]
-    copies[FIELDS].wait()
-    copies[FIELDS + 1].wait()
+        turned[j] = values.T.astype(BF16)
+    for copy in copies[FIELDS:]:
+        copy.wait()
     lane = lax.broadcasted_iota(jnp.int32, (1, tile), 1)
     row = jnp.where(lane == nslots, live[0, 0].astype(F32), 0.0)
     for k in range(nslots):
         row = jnp.where(lane == k, index[0, 0, k].astype(F32), row)
     rows += [row, jnp.zeros((part - len(rows) - 1, tile), F32)]
-    half = jnp.concatenate(rows, axis=0).astype(BF16)
-    for d in range(n):
-        out[d, FIELDS * part :, :] = half
-
-
-def main_body(n_blk, n_col, shifts, slots, recv, bounded, blocks, *refs):
+    info = jnp.concatenate(rows, axis=0).astype(BF16)
+    me_b, me_c = lax.axis_index("blk"), lax.axis_index("col")
+
+    def piece(out, at, t, s):
+        peer = pl.ds(pl.multiple_of(((me_b ^ t) * n_col + (me_c ^ s)) * part, part), part)
+        for j in range(FIELDS):
+            out[at + j * part : at + (j + 1) * part, :] = turned[j, peer, :]
+
+    top = half * tile
+    for out in (far_out, *near_outs):
+        for k in range(half):
+            out[k * tile : (k + 1) * tile, :] = share[k]
+        out[out.shape[0] - part :, :] = info
+    for m, (t, s) in enumerate([(0, 0), *near]):
+        piece(far_out, top + m * FIELDS * part, far + t, s)
+        if m > 0:
+            piece(near_outs[m - 1], top, t, s)
+    piece(own_out, 0, 0, 0)
+    own_out[FIELDS * part :, :] = info
+
+
+def relay_body(top, part, came, *outs):
+    for m, out in enumerate(outs):
+        out[0:top, :] = came[0:top, :]
+        at = top + (m + 1) * FIELDS * part
+        out[top : top + FIELDS * part, :] = came[at : at + FIELDS * part, :]
+        out[top + FIELDS * part :, :] = came[came.shape[0] - part :, :]
+
+
+def main_body(n_blk, n_col, shifts, part, slots, bounded, blocks, own, *refs):
     n = n_blk * n_col
     mine, theirs = refs[: n - 1], refs[n - 1 : 2 * (n - 1)]
-    out, scales, mat, turned = refs[2 * (n - 1) :]
+    out, scales, mat, fields, turned = refs[2 * (n - 1) :]
     tile = blocks.shape[-1]
     nslots = blocks.shape[2]
-    half = mine[0].shape[0] // tile
-    part = recv.shape[1] // (FIELDS + 1)
+    half = nslots // 2
     me_b, me_c, me_r = lax.axis_index("blk"), lax.axis_index("col"), lax.axis_index("rep")
     mat[...] = jnp.zeros(mat.shape, BF16)
 
-    def place(t, s, slot, block):
+    def place(source, t, s, slot, block):
         blk, col = me_b ^ t, me_c ^ s
-        owner = blk * n_col + col
-        position = slots[owner, slot]
+        position = slots[source, slot]
         row = pl.multiple_of((blk * n_col + position // n_blk) * tile, tile)
         column = pl.multiple_of(((position % n_blk) * n_col + col) * tile, tile)
 
-        @pl.when(slot < slots[owner, nslots])
+        @pl.when(slot < slots[source, nslots])
         def _():
             mat[pl.ds(row, tile), pl.ds(column, tile)] = block()
 
-    for k in range(nslots):
-        place(0, 0, k, lambda k=k: blocks[0, 0, k])
-    for (t, s), own_part, other_part in zip(shifts, mine, theirs):
-        for k in range(half):
-            place(t, s, me_r * half + k, lambda k=k, r=own_part: r[k * tile : (k + 1) * tile, :])
-            place(t, s, (1 - me_r) * half + k, lambda k=k, r=other_part: r[k * tile : (k + 1) * tile, :])
-
-    def field(j):
-        return jnp.concatenate([recv[d, j * part : (j + 1) * part, :] for d in range(n)], axis=1).astype(F32)
-
-    cost, rhs, upper, primal, dual = (field(j) for j in range(FIELDS))
     sums = [jnp.zeros((1, tile), F32)] * 2
-    for d in range(n):
-        info = recv[d, FIELDS * part :, :].astype(F32)
+
+    def take(t, s, ref, at):
+        lanes = pl.ds(pl.multiple_of(((me_b ^ t) * n_col + (me_c ^ s)) * tile, tile), tile)
+        for j in range(FIELDS):
+            fields[j, :, lanes] = ref[at + j * part : at + (j + 1) * part, :]
+        info = ref[ref.shape[0] - part :, :].astype(F32)
         for j in range(2):
             first, second, third = (info[PARTS * j + k : PARTS * j + k + 1] for k in range(PARTS))
             sums[j] += (first + second) + third
+
+    for k in range(nslots):
+        place(0, 0, 0, k, lambda k=k: blocks[0, 0, k])
+    take(0, 0, own, 0)
+    for m, ((t, s), own_part, other_part) in enumerate(zip(shifts, mine, theirs)):
+        for k in range(half):
+            place(m + 1, t, s, me_r * half + k, lambda k=k, r=own_part: r[k * tile : (k + 1) * tile, :])
+            place(m + 1, t, s, (1 - me_r) * half + k, lambda k=k, r=other_part: r[k * tile : (k + 1) * tile, :])
+        take(t, s, own_part, half * tile)
+    cost, rhs, upper, primal, dual = (fields[j].astype(F32) for j in range(FIELDS))
     weight = jnp.sqrt(sums[0] + EPS) / jnp.sqrt(sums[1] + EPS)
     rows = jnp.concatenate([ETA / weight, ETA * weight, bounded[...].astype(F32), jnp.zeros((5, tile), F32)], axis=0)
     scales[...] = rows
@@ -194,41 +215,48 @@
         pairs = [(b * n_col + c, (b ^ t) * n_col + (c ^ s)) for b in range(n_blk) for c in range(n_col)]
         return lax.ppermute(value, ("blk", "col"), pairs)
 
-    (share,) = call(share_body, [like((nslots // 2 * tile, tile), BF16)], [VMEM], [blocks])
     far = n_blk // 2
     near = [(t, s) for t in range(far) for s in range(n_col) if (t, s) != (0, 0)]
-    mine = {(far, 0): move(share, far, 0)}
-    for t, s in near:
-        mine[t, s] = move(share, t, s)
-    sent, token = call(
-        prep_body,
-        [like((n, (FIELDS + 1) * part, tile), BF16), like((8, 128), F32)],
-        [ANY] * (FIELDS + 3),
-        [block_index, live, cost, rhs, upper, x_init, y_init, mine[near[0]][:16]],
+    half = nslots // 2
+    top = half * tile
+    size = top + (FIELDS + 1) * part
+    far_out, *near_outs, own = call(
+        functools.partial(prep_body, n_col, far, near),
+        [held((top + (FIELDS * (len(near) + 1) + 1) * part, tile), BF16)]
+        + [held((size, tile), BF16)] * len(near)
+        + [held(((FIELDS + 1) * part, tile), BF16)],
+        [SMEM] + [ANY] * (FIELDS + 2),
+        [live] + pinned([cost, rhs, upper, x_init, y_init, block_index, blocks]),
         scratch=[pltpu.VMEM((tile, scn), F32)] * FIELDS
-        + [pltpu.SMEM(block_index.shape, jnp.int32), pltpu.SMEM(live.shape, jnp.int32)]
-        + [pltpu.SemaphoreType.DMA((FIELDS + 2,))],
-        limit=60,
-    )
-    recv = spread(sent)
-    mine[far, 0] = pl.pallas_call(
-        touch_body,
-        out_shape=like(share.shape, share.dtype),
-        in_specs=[ANY, ANY],
-        out_specs=ANY,
-        input_output_aliases={0: 0},
-    )(mine[far, 0], token)
-    for t, s in near:
-        mine[far + t, s] = move(mine[far, 0], t, s)
+        + [pltpu.VMEM((half, tile, tile), BF16)]
+        + [pltpu.SMEM(block_index.shape, jnp.int32)]
+        + [pltpu.VMEM((FIELDS, scn, tile), BF16), pltpu.SemaphoreType.DMA((FIELDS + 2,))],
+    )
+    mine = {(far, 0): move(far_out, far, 0)}
+    for (t, s), out in zip(near, near_outs):
+        mine[t, s] = move(out, t, s)
+    relayed = call(
+        functools.partial(relay_body, top, part),
+        [held((size, tile), BF16)] * len(near),
+        [VMEM],
+        [mine[far, 0]],
+    )
+    for (t, s), out in zip(near, relayed):
+        mine[far + t, s] = move(out, t, s)
     shifts = list(mine)
     theirs = [lax.ppermute(mine[shift], "rep", [(0, 1), (1, 0)]) for shift in shifts]
-    slots = recv[:, FIELDS * part + SLOT_ROW, : nslots + 1].astype(jnp.int32)
+    rows = [v[v.shape[0] - part + SLOT_ROW, : nslots + 1] for v in [own] + list(mine.values())]
+    slots = jnp.stack(rows).astype(jnp.int32)
     products, scales = call(
-        functools.partial(main_body, n_blk, n_col, shifts),
+        functools.partial(main_body, n_blk, n_col, shifts, part),
         [like((n, 2 * ITERS * part, tile), BF16), like((8, scn), F32)],
         [SMEM] + [VMEM] * (2 * n + 1),
-        [slots, recv, limits, blocks] + [mine[shift] for shift in shifts] + theirs,
-        scratch=[pltpu.VMEM((n * tile, n * tile), BF16), pltpu.VMEM((tile, scn), F32)],
+        [slots, limits, blocks, own] + [mine[shift] for shift in shifts] + theirs,
+        scratch=[
+            pltpu.VMEM((n * tile, n * tile), BF16),
+            pltpu.VMEM((FIELDS, part, n * tile), BF16),
+            pltpu.VMEM((tile, scn), F32),
+        ],
         flops=4 * ITERS * n * n * tile * tile * part,
     )
     return call(

time: 55.3 us -> 43.5 us (0.79)
  starting transfers between devices: 19.1 us -> 11.7 us
  local copies, waits for them, and re-layouts: 3.74 us -> 0.14 us
  Pallas kernels: 6.3 us -> 5.72 us
    all_to_all x1 -> x0, starting transfers between devices: 6.15 us -> none  [spread(): return lax.all_to_all(value, ('blk', 'col'), 0, 0, tiled=True)]
    unnamed x20 -> x14, local copies, waits for them, and re-layouts: 3.15 us -> 0.05 us
    ppermute x7, starting transfers between devices: 12.3 us -> 11.1 us  [move(): return lax.ppermute(value, ('blk', 'col'), pairs)]
    pallas_call x4, Pallas kernels: 6.3 us -> 5.72 us  [call(): pl.pallas_call(body, out_shape=list(outs), in_specs=in_specs, out_specs=[...]
  transfers between devices with their start and end apart: 15 -> 14, of which waited for: 8 -> 6; matrix products, arithmetic and copies ran while one was open for 0% -> 0% of each run, Pallas kernels for 0% -> 0%
where the time goes in v5:
time: 43.5 us; the launch traced here: 43.3 us
  waiting for transfers between devices  13.3 us (31%)
  starting transfers between devices  11.7 us (27%)
  blocking collectives  11.1 us (26%)
  Pallas kernels  5.72 us (13%)
  between operations  1.44 us (3%)
    ppermute x7, waiting for transfers between devices, move(): return lax.ppermute(value, ('blk', 'col'), pairs)  12.1 us
    ppermute x7, starting transfers between devices, move(): return lax.ppermute(value, ('blk', 'col'), pairs)  11.1 us
    all_to_all x1, blocking collectives, spread(): return lax.all_to_all(value, ('blk', 'col'), 0, 0, tiled=True)  11.1 us
    pallas_call x4, Pallas kernels, call(): pl.pallas_call(body, out_shape=list(outs), in_specs=in_specs, out_specs=[...  5.72 us
    ppermute x7, waiting for transfers between devices, local_plan(): lax.ppermute(mine[shift], 'rep', [(0, 1), (1, 0)])  1.16 us
  transfers between devices with their start and end apart: 14, of which 6 were waited for; matrix products, arithmetic and copies ran while one was open for 0% of the time, Pallas kernels for 0%

profile of v5, /device:TPU:0, one launch (start us, length us, event | category | flops | bytes accessed | tf_op | source)
XLA Modules:
  0.0 43.3 jit_solution(2393924895208012686)
XLA Ops:
  1.3 1.5 %shard_map.104 = (bf16[720,128]{1,0:T(8,128)(2,1)S(1)}, bf16[480,128]{1,0:T(8,128)(2,1)S(1)}, bf16[480,128]{1,0:T(8,128)(2,1)S(1)}, bf16[480,128]{1,0:T(8,128)(2,1)S(1)}, bf16[96,128]{1,0:T(8,128)(2,1)S(1)}) custom-call(s32[1,1]{1,0:T(1,128)S(6)} %copy.11.refs_0_, f32[128,128]{1,0:T(8,128)} %cost.1, f32[128,128]{1,0:T(8,128)} %rhs.1, f32[128,128]{1,0:T(8,128)} %upper.1, ...), custom_call_target="tpu_custom_call" | custom-call | bytes 1101852 | tf_op jit(solution)/shard_map/pallas_call | solution.py:39
  2.8 0.0 copy-start
  2.8 4.1 %collective-permute-start = (bf16[720,128]{1,0:T(8,128)(2,1)S(1)}, bf16[720,128]{1,0:T(8,128)(2,1)S(1)}, u32[]{:S(2)}, u32[]{:S(2)}) collective-permute-start(bf16[720,128]{1,0:T(8,128)(2,1)S(1)} %get-tuple-element.13), channel_id=1, source_target_pairs={{0,8},{2,10},{4,12},{6,14},{8,0},{10,2},{12,4},{14,6},{1,9},{3,11}... | collective-permute-start | bytes 552968 | tf_op jit(solution)/shard_map/ppermute | solution.py:216
  6.9 1.5 %collective-permute-start.1 = (bf16[480,128]{1,0:T(8,128)(2,1)S(1)}, bf16[480,128]{1,0:T(8,128)(2,1)S(1)}, u32[]{:S(2)}, u32[]{:S(2)}) collective-permute-start(bf16[480,128]{1,0:T(8,128)(2,1)S(1)} %get-tuple-element.14), channel_id=1, source_target_pairs={{0,2},{2,0},{4,6},{6,4},{8,10},{10,8},{12,14},{14,12},{1,3},{3,1},... | collective-permute-start | bytes 368648 | tf_op jit(solution)/shard_map/ppermute | solution.py:216
  8.4 1.6 %collective-permute-start.2 = (bf16[480,128]{1,0:T(8,128)(2,1)S(1)}, bf16[480,128]{1,0:T(8,128)(2,1)S(1)}, u32[]{:S(2)}, u32[]{:S(2)}) collective-permute-start(bf16[480,128]{1,0:T(8,128)(2,1)S(1)} %get-tuple-element.15), channel_id=1, source_target_pairs={{0,4},{2,6},{4,0},{6,2},{8,12},{10,14},{12,8},{14,10},{1,5},{3,7},... | collective-permute-start | bytes 368648 | tf_op jit(solution)/shard_map/ppermute | solution.py:216
  10.0 0.4 collective-permute-start.3
  10.4 1.4 %collective-permute-done.1.refs_1_ = bf16[480,128]{1,0:T(8,128)(2,1)S(1)} collective-permute-done((bf16[480,128]{1,0:T(8,128)(2,1)S(1)}, bf16[480,128]{1,0:T(8,128)(2,1)S(1)}, u32[]{:S(2)}, u32[]{:S(2)}) %collective-permute-start.1) | collective-permute-done | bytes 122912 | tf_op jit(solution)/shard_map/ppermute | solution.py:216
  11.8 0.0 collective-permute-start.8
  11.8 5.2 %collective-permute-done.2.refs_2_ = bf16[480,128]{1,0:T(8,128)(2,1)S(1)} collective-permute-done((bf16[480,128]{1,0:T(8,128)(2,1)S(1)}, bf16[480,128]{1,0:T(8,128)(2,1)S(1)}, u32[]{:S(2)}, u32[]{:S(2)}) %collective-permute-start.2) | collective-permute-done | bytes 122912 | tf_op jit(solution)/shard_map/ppermute | solution.py:216
  17.0 0.0 collective-permute-start.9
  17.0 0.0 collective-permute-done.came.refs_0_
  17.0 0.6 %collective-permute-start.4 = (bf16[480,128]{1,0:T(8,128)(2,1)S(1)}, bf16[480,128]{1,0:T(8,128)(2,1)S(1)}, u32[]{:S(2)}, u32[]{:S(2)}) collective-permute-start(bf16[480,128]{1,0:T(8,128)(2,1)S(1)} %get-tuple-element.17), channel_id=1, source_target_pairs={{0,2},{2,0},{4,6},{6,4},{8,10},{10,8},{12,14},{14,12},{1,3},{3,1},... | collective-permute-start | bytes 368648 | tf_op jit(solution)/shard_map/ppermute | solution.py:216
  17.6 1.1 %collective-permute-start.5 = (bf16[480,128]{1,0:T(8,128)(2,1)S(1)}, bf16[480,128]{1,0:T(8,128)(2,1)S(1)}, u32[]{:S(2)}, u32[]{:S(2)}) collective-permute-start(bf16[480,128]{1,0:T(8,128)(2,1)S(1)} %get-tuple-element.18), channel_id=1, source_target_pairs={{0,4},{2,6},{4,0},{6,2},{8,12},{10,14},{12,8},{14,10},{1,5},{3,7},... | collective-permute-start | bytes 368648 | tf_op jit(solution)/shard_map/ppermute | solution.py:216
  18.7 0.0 collective-permute-done.3.refs_3_
  18.7 1.9 %collective-permute-start.6 = (bf16[480,128]{1,0:T(8,128)(2,1)S(1)}, bf16[480,128]{1,0:T(8,128)(2,1)S(1)}, u32[]{:S(2)}, u32[]{:S(2)}) collective-permute-start(bf16[480,128]{1,0:T(8,128)(2,1)S(1)} %get-tuple-element.19), channel_id=1, source_target_pairs={{0,6},{2,4},{4,2},{6,0},{8,14},{10,12},{12,10},{14,8},{1,7},{3,5},... | collective-permute-start | bytes 368648 | tf_op jit(solution)/shard_map/ppermute | solution.py:216
  20.6 0.0 collective-permute-done.8.refs_8_
  20.6 0.0 collective-permute-start.7
  20.6 0.0 collective-permute-done.9.refs_9_
  20.6 0.5 %collective-permute-start.10 = (bf16[480,128]{1,0:T(8,128)(2,1)S(1)}, bf16[480,128]{1,0:T(8,128)(2,1)S(1)}, u32[]{:S(2)}, u32[]{:S(2)}) collective-permute-start(bf16[480,128]{1,0:T(8,128)(2,1)S(1)} %collective-permute-done.3.refs_3_), channel_id=1, source_target_pairs={{0,1},{1,0},{2,3},{3,2},{4,5},{5,4},{6,7},{7,6},{8,9},{9,8},{10,11... | collective-permute-start | bytes 368648 | tf_op jit(solution)/shard_map/ppermute | solution.py:247
  21.1 1.7 %collective-permute-done.4.refs_4_ = bf16[480,128]{1,0:T(8,128)(2,1)S(1)} collective-permute-done((bf16[480,128]{1,0:T(8,128)(2,1)S(1)}, bf16[480,128]{1,0:T(8,128)(2,1)S(1)}, u32[]{:S(2)}, u32[]{:S(2)}) %collective-permute-start.4) | collective-permute-done | bytes 122912 | tf_op jit(solution)/shard_map/ppermute | solution.py:216
  22.8 0.0 collective-permute-start.11
  22.8 0.9 %collective-permute-done.5.refs_5_ = bf16[480,128]{1,0:T(8,128)(2,1)S(1)} collective-permute-done((bf16[480,128]{1,0:T(8,128)(2,1)S(1)}, bf16[480,128]{1,0:T(8,128)(2,1)S(1)}, u32[]{:S(2)}, u32[]{:S(2)}) %collective-permute-start.5) | collective-permute-done | bytes 122912 | tf_op jit(solution)/shard_map/ppermute | solution.py:216
  23.8 0.0 collective-permute-start.12
  23.8 2.9 %collective-permute-done.6.refs_6_ = bf16[480,128]{1,0:T(8,128)(2,1)S(1)} collective-permute-done((bf16[480,128]{1,0:T(8,128)(2,1)S(1)}, bf16[480,128]{1,0:T(8,128)(2,1)S(1)}, u32[]{:S(2)}, u32[]{:S(2)}) %collective-permute-start.6) | collective-permute-done | bytes 122912 | tf_op jit(solution)/shard_map/ppermute | solution.py:216
  26.7 0.0 collective-permute-start.13
  26.8 0.0 copy-start.6
  26.8 0.0 collective-permute-done.10.refs_10_
  26.8 0.0 collective-permute-done.7.refs_7_
  26.8 0.0 collective-permute-done.11.refs_11_
  26.8 0.0 collective-permute-done.12.refs_12_
  26.9 1.1 %collective-permute-done.13.refs_13_ = bf16[480,128]{1,0:T(8,128)(2,1)S(1)} collective-permute-done((bf16[480,128]{1,0:T(8,128)(2,1)S(1)}, bf16[480,128]{1,0:T(8,128)(2,1)S(1)}, u32[]{:S(2)}, u32[]{:S(2)}) %collective-permute-start.13) | collective-permute-done | bytes 122912 | tf_op jit(solution)/shard_map/ppermute | solution.py:247
  28.0 0.0 copy-done
  28.0 0.0 copy-done.6
  28.0 0.0 copy-start.5
  28.0 3.4 %shard_map.106 = (bf16[8,64,128]{2,1,0:T(8,128)(2,1)S(1)}, f32[8,128]{1,0:T(8,128)S(1)}) custom-call(s32[8,7]{1,0:T(8,128)S(1)} %convert_element_type.3.slots, s32[1,128]{1,0:T(1,128)S(1)} %bitcast.1, bf16[1,1,6,128,128]{4,3,2,1,0:T(8,128)(2,1)S(1)} %copy-done, bf16[96,128]{1,0:T(8,128)(2,1)S(1)} %get-tuple-element.12.own, ...), custom_call_target="tpu_custom_call" | custom-call | flops 134217728 | bytes 2200288 | tf_op jit(solution)/shard_map/pallas_call | solution.py:39
  31.4 0.0 copy-start.1
  31.4 0.0 copy-start.2
  31.4 0.0 copy-start.3
  31.4 0.0 copy-start.4
  31.5 11.1 %all_to_all.5.recv = bf16[8,64,128]{2,1,0:T(8,128)(2,1)S(1)} all-to-all(bf16[8,64,128]{2,1,0:T(8,128)(2,1)S(1)} %get-tuple-element.20), channel_id=1, replica_groups=mesh['groups'=2,'blk'=4,'col'=2,'rep'=2] {'blk','col'}, dimensions={0} | all-to-all | bytes 262144 | tf_op jit(solution)/shard_map/all_to_all | solution.py:212
  42.5 0.0 copy-done.5
  42.5 0.0 copy-done.1
  42.5 0.0 copy-done.2
  42.5 0.0 copy-done.3
  42.5 0.0 copy-done.4
  42.5 0.8 %shard_map.107 = (f32[128,128]{1,0:T(8,128)}, f32[128,128]{1,0:T(8,128)}) custom-call(bf16[8,64,128]{2,1,0:T(8,128)(2,1)S(1)} %all_to_all.5.recv, f32[8,128]{1,0:T(8,128)S(1)} %get-tuple-element.21.scales, f32[128,128]{1,0:T(8,128)S(1)} %copy-done.1, f32[128,128]{1,0:T(8,128)S(1)} %copy-done.2, f32[128,128]{1,0:T(8,128)S(1)} %copy-done.3, ...), custom_call_target="tpu_custom_call" | custom-call | bytes 594432 | tf_op jit(solution)/shard_map/pallas_call | solution.py:39
  (11 shorter events, 0.1 us)
Async XLA Ops:
  2.8 25.2 %copy-start = (bf16[1,1,6,128,128]{4,3,2,1,0:T(8,128)(2,1)S(1)}, bf16[1,1,6,128,128]{4,3,2,1,0:T(8,128)(2,1)}, u32[]{:S(2)}) copy-start(bf16[1,1,6,128,128]{4,3,2,1,0:T(8,128)(2,1)} %blocks.1) | copy-start | bytes 589828
  2.8 14.2 %collective-permute-start = (bf16[720,128]{1,0:T(8,128)(2,1)S(1)}, bf16[720,128]{1,0:T(8,128)(2,1)S(1)}, u32[]{:S(2)}, u32[]{:S(2)}) collective-permute-start(bf16[720,128]{1,0:T(8,128)(2,1)S(1)} %get-tuple-element.13), channel_id=1, source_target_pairs={{0,8},{2,10},{4,12},{6,14},{8,0},{10,2},{12,4},{14,6},{1,9},{3,11}... | collective-permute-start | bytes 552968 | tf_op jit(solution)/shard_map/ppermute | solution.py:216
  6.9 4.9 %collective-permute-start.1 = (bf16[480,128]{1,0:T(8,128)(2,1)S(1)}, bf16[480,128]{1,0:T(8,128)(2,1)S(1)}, u32[]{:S(2)}, u32[]{:S(2)}) collective-permute-start(bf16[480,128]{1,0:T(8,128)(2,1)S(1)} %get-tuple-element.14), channel_id=1, source_target_pairs={{0,2},{2,0},{4,6},{6,4},{8,10},{10,8},{12,14},{14,12},{1,3},{3,1},... | collective-permute-start | bytes 368648 | tf_op jit(solution)/shard_map/ppermute | solution.py:216
  8.4 8.6 %collective-permute-start.2 = (bf16[480,128]{1,0:T(8,128)(2,1)S(1)}, bf16[480,128]{1,0:T(8,128)(2,1)S(1)}, u32[]{:S(2)}, u32[]{:S(2)}) collective-permute-start(bf16[480,128]{1,0:T(8,128)(2,1)S(1)} %get-tuple-element.15), channel_id=1, source_target_pairs={{0,4},{2,6},{4,0},{6,2},{8,12},{10,14},{12,8},{14,10},{1,5},{3,7},... | collective-permute-start | bytes 368648 | tf_op jit(solution)/shard_map/ppermute | solution.py:216
  10.0 8.7 %collective-permute-start.3 = (bf16[480,128]{1,0:T(8,128)(2,1)S(1)}, bf16[480,128]{1,0:T(8,128)(2,1)S(1)}, u32[]{:S(2)}, u32[]{:S(2)}) collective-permute-start(bf16[480,128]{1,0:T(8,128)(2,1)S(1)} %get-tuple-element.16), channel_id=1, source_target_pairs={{0,6},{2,4},{4,2},{6,0},{8,14},{10,12},{12,10},{14,8},{1,7},{3,5},... | collective-permute-start | bytes 368648 | tf_op jit(solution)/shard_map/ppermute | solution.py:216
  11.8 8.8 %collective-permute-start.8 = (bf16[480,128]{1,0:T(8,128)(2,1)S(1)}, bf16[480,128]{1,0:T(8,128)(2,1)S(1)}, u32[]{:S(2)}, u32[]{:S(2)}) collective-permute-start(bf16[480,128]{1,0:T(8,128)(2,1)S(1)} %collective-permute-done.1.refs_1_), channel_id=1, source_target_pairs={{0,1},{1,0},{2,3},{3,2},{4,5},{5,4},{6,7},{7,6},{8,9},{9,8},{10,11... | collective-permute-start | bytes 368648 | tf_op jit(solution)/shard_map/ppermute | solution.py:247
  17.0 3.6 %collective-permute-start.9 = (bf16[480,128]{1,0:T(8,128)(2,1)S(1)}, bf16[480,128]{1,0:T(8,128)(2,1)S(1)}, u32[]{:S(2)}, u32[]{:S(2)}) collective-permute-start(bf16[480,128]{1,0:T(8,128)(2,1)S(1)} %collective-permute-done.2.refs_2_), channel_id=1, source_target_pairs={{0,1},{1,0},{2,3},{3,2},{4,5},{5,4},{6,7},{7,6},{8,9},{9,8},{10,11... | collective-permute-start | bytes 368648 | tf_op jit(solution)/shard_map/ppermute | solution.py:247
  17.0 5.8 %collective-permute-start.4 = (bf16[480,128]{1,0:T(8,128)(2,1)S(1)}, bf16[480,128]{1,0:T(8,128)(2,1)S(1)}, u32[]{:S(2)}, u32[]{:S(2)}) collective-permute-start(bf16[480,128]{1,0:T(8,128)(2,1)S(1)} %get-tuple-element.17), channel_id=1, source_target_pairs={{0,2},{2,0},{4,6},{6,4},{8,10},{10,8},{12,14},{14,12},{1,3},{3,1},... | collective-permute-start | bytes 368648 | tf_op jit(solution)/shard_map/ppermute | solution.py:216
  17.6 6.2 %collective-permute-start.5 = (bf16[480,128]{1,0:T(8,128)(2,1)S(1)}, bf16[480,128]{1,0:T(8,128)(2,1)S(1)}, u32[]{:S(2)}, u32[]{:S(2)}) collective-permute-start(bf16[480,128]{1,0:T(8,128)(2,1)S(1)} %get-tuple-element.18), channel_id=1, source_target_pairs={{0,4},{2,6},{4,0},{6,2},{8,12},{10,14},{12,8},{14,10},{1,5},{3,7},... | collective-permute-start | bytes 368648 | tf_op jit(solution)/shard_map/ppermute | solution.py:216
  18.7 8.0 %collective-permute-start.6 = (bf16[480,128]{1,0:T(8,128)(2,1)S(1)}, bf16[480,128]{1,0:T(8,128)(2,1)S(1)}, u32[]{:S(2)}, u32[]{:S(2)}) collective-permute-start(bf16[480,128]{1,0:T(8,128)(2,1)S(1)} %get-tuple-element.19), channel_id=1, source_target_pairs={{0,6},{2,4},{4,2},{6,0},{8,14},{10,12},{12,10},{14,8},{1,7},{3,5},... | collective-permute-start | bytes 368648 | tf_op jit(solution)/shard_map/ppermute | solution.py:216
  20.6 6.2 %collective-permute-start.7 = (bf16[720,128]{1,0:T(8,128)(2,1)S(1)}, bf16[720,128]{1,0:T(8,128)(2,1)S(1)}, u32[]{:S(2)}, u32[]{:S(2)}) collective-permute-start(bf16[720,128]{1,0:T(8,128)(2,1)S(1)} %collective-permute-done.came.refs_0_), channel_id=1, source_target_pairs={{0,1},{1,0},{2,3},{3,2},{4,5},{5,4},{6,7},{7,6},{8,9},{9,8},{10,11... | collective-permute-start | bytes 552968 | tf_op jit(solution)/shard_map/ppermute | solution.py:247
  20.6 6.2 %collective-permute-start.10 = (bf16[480,128]{1,0:T(8,128)(2,1)S(1)}, bf16[480,128]{1,0:T(8,128)(2,1)S(1)}, u32[]{:S(2)}, u32[]{:S(2)}) collective-permute-start(bf16[480,128]{1,0:T(8,128)(2,1)S(1)} %collective-permute-done.3.refs_3_), channel_id=1, source_target_pairs={{0,1},{1,0},{2,3},{3,2},{4,5},{5,4},{6,7},{7,6},{8,9},{9,8},{10,11... | collective-permute-start | bytes 368648 | tf_op jit(solution)/shard_map/ppermute | solution.py:247
  22.8 4.0 %collective-permute-start.11 = (bf16[480,128]{1,0:T(8,128)(2,1)S(1)}, bf16[480,128]{1,0:T(8,128)(2,1)S(1)}, u32[]{:S(2)}, u32[]{:S(2)}) collective-permute-start(bf16[480,128]{1,0:T(8,128)(2,1)S(1)} %collective-permute-done.4.refs_4_), channel_id=1, source_target_pairs={{0,1},{1,0},{2,3},{3,2},{4,5},{5,4},{6,7},{7,6},{8,9},{9,8},{10,11... | collective-permute-start | bytes 368648 | tf_op jit(solution)/shard_map/ppermute | solution.py:247
  23.8 3.1 %collective-permute-start.12 = (bf16[480,128]{1,0:T(8,128)(2,1)S(1)}, bf16[480,128]{1,0:T(8,128)(2,1)S(1)}, u32[]{:S(2)}, u32[]{:S(2)}) collective-permute-start(bf16[480,128]{1,0:T(8,128)(2,1)S(1)} %collective-permute-done.5.refs_5_), channel_id=1, source_target_pairs={{0,1},{1,0},{2,3},{3,2},{4,5},{5,4},{6,7},{7,6},{8,9},{9,8},{10,11... | collective-permute-start | bytes 368648 | tf_op jit(solution)/shard_map/ppermute | solution.py:247
  26.7 1.3 %collective-permute-start.13 = (bf16[480,128]{1,0:T(8,128)(2,1)S(1)}, bf16[480,128]{1,0:T(8,128)(2,1)S(1)}, u32[]{:S(2)}, u32[]{:S(2)}) collective-permute-start(bf16[480,128]{1,0:T(8,128)(2,1)S(1)} %collective-permute-done.6.refs_6_), channel_id=1, source_target_pairs={{0,1},{1,0},{2,3},{3,2},{4,5},{5,4},{6,7},{7,6},{8,9},{9,8},{10,11... | collective-permute-start | bytes 368648 | tf_op jit(solution)/shard_map/ppermute | solution.py:247
  26.8 1.2 %copy-start.6 = (s32[128]{0:T(128)S(1)}, s32[128]{0:T(128)}, u32[]{:S(2)}) copy-start(s32[128]{0:T(128)} %param.17) | copy-start | bytes 1540
  28.0 14.5 %copy-start.5 = (f32[128,128]{1,0:T(8,128)S(1)}, f32[128,128]{1,0:T(8,128)}, u32[]{:S(2)}) copy-start(f32[128,128]{1,0:T(8,128)} %y_in.1) | copy-start | bytes 196612
  31.4 11.1 %copy-start.1 = (f32[128,128]{1,0:T(8,128)S(1)}, f32[128,128]{1,0:T(8,128)}, u32[]{:S(2)}) copy-start(f32[128,128]{1,0:T(8,128)} %cost.1) | copy-start | bytes 196612
  31.4 11.1 %copy-start.2 = (f32[128,128]{1,0:T(8,128)S(1)}, f32[128,128]{1,0:T(8,128)}, u32[]{:S(2)}) copy-start(f32[128,128]{1,0:T(8,128)} %rhs.1) | copy-start | bytes 196612
  31.4 11.1 %copy-start.3 = (f32[128,128]{1,0:T(8,128)S(1)}, f32[128,128]{1,0:T(8,128)}, u32[]{:S(2)}) copy-start(f32[128,128]{1,0:T(8,128)} %upper.1) | copy-start | bytes 196612
  31.4 11.1 %copy-start.4 = (f32[128,128]{1,0:T(8,128)S(1)}, f32[128,128]{1,0:T(8,128)}, u32[]{:S(2)}) copy-start(f32[128,128]{1,0:T(8,128)} %x_in.1) | copy-start | bytes 196612

commit v6 on v5

--- a/solution.py
+++ b/solution.py
@@ -63,8 +63,8 @@
 
 def prep_body(n_col, far, near, *refs):
     live, *sources = refs[: FIELDS + 3]
-    far_out, *near_outs, own_out = refs[FIELDS + 3 : FIELDS + 5 + len(near)]
-    *fields, share, index, turned, sems = refs[FIELDS + 5 + len(near) :]
+    far_share, far_out, *near_outs, own_out = refs[FIELDS + 3 : FIELDS + 6 + len(near)]
+    *fields, share, index, turned, sems = refs[FIELDS + 6 + len(near) :]
     half, tile = share.shape[0], share.shape[1]
     first = lax.axis_index("rep") * half
     targets = (*fields, index)
@@ -100,30 +100,29 @@
             out[at + j * part : at + (j + 1) * part, :] = turned[j, peer, :]
 
     top = half * tile
-    for out in (far_out, *near_outs):
+    for out in (far_share, *near_outs):
         for k in range(half):
             out[k * tile : (k + 1) * tile, :] = share[k]
-        out[out.shape[0] - part :, :] = info
     for m, (t, s) in enumerate([(0, 0), *near]):
-        piece(far_out, top + m * FIELDS * part, far + t, s)
+        piece(far_out, m * FIELDS * part, far + t, s)
         if m > 0:
             piece(near_outs[m - 1], top, t, s)
     piece(own_out, 0, 0, 0)
-    own_out[FIELDS * part :, :] = info
-
-
-def relay_body(top, part, came, *outs):
+    for out in (far_out, *near_outs, own_out):
+        out[out.shape[0] - part :, :] = info
+
+
+def relay_body(part, came, *outs):
     for m, out in enumerate(outs):
-        out[0:top, :] = came[0:top, :]
-        at = top + (m + 1) * FIELDS * part
-        out[top : top + FIELDS * part, :] = came[at : at + FIELDS * part, :]
-        out[top + FIELDS * part :, :] = came[came.shape[0] - part :, :]
+        at = (m + 1) * FIELDS * part
+        out[0 : FIELDS * part, :] = came[at : at + FIELDS * part, :]
+        out[FIELDS * part :, :] = came[came.shape[0] - part :, :]
 
 
 def main_body(n_blk, n_col, shifts, part, slots, bounded, blocks, own, *refs):
     n = n_blk * n_col
-    mine, theirs = refs[: n - 1], refs[n - 1 : 2 * (n - 1)]
-    out, scales, mat, fields, turned = refs[2 * (n - 1) :]
+    mine, theirs, pieces = refs[: n - 1], refs[n - 1 : 2 * (n - 1)], refs[2 * (n - 1) : 3 * (n - 1)]
+    out, scales, mat, fields, turned = refs[3 * (n - 1) :]
     tile = blocks.shape[-1]
     nslots = blocks.shape[2]
     half = nslots // 2
@@ -154,11 +153,11 @@
     for k in range(nslots):
         place(0, 0, 0, k, lambda k=k: blocks[0, 0, k])
     take(0, 0, own, 0)
-    for m, ((t, s), own_part, other_part) in enumerate(zip(shifts, mine, theirs)):
+    for m, ((t, s), own_part, other_part, piece) in enumerate(zip(shifts, mine, theirs, pieces)):
         for k in range(half):
             place(m + 1, t, s, me_r * half + k, lambda k=k, r=own_part: r[k * tile : (k + 1) * tile, :])
             place(m + 1, t, s, (1 - me_r) * half + k, lambda k=k, r=other_part: r[k * tile : (k + 1) * tile, :])
-        take(t, s, own_part, half * tile)
+        take(t, s, piece, half * tile if piece.shape[0] > half * tile else 0)
     cost, rhs, upper, primal, dual = (fields[j].astype(F32) for j in range(FIELDS))
     weight = jnp.sqrt(sums[0] + EPS) / jnp.sqrt(sums[1] + EPS)
     rows = jnp.concatenate([ETA / weight, ETA * weight, bounded[...].astype(F32), jnp.zeros((5, tile), F32)], axis=0)
@@ -220,11 +219,11 @@
     half = nslots // 2
     top = half * tile
     size = top + (FIELDS + 1) * part
-    far_out, *near_outs, own = call(
+    far_share, far_out, *near_outs, own = call(
         functools.partial(prep_body, n_col, far, near),
-        [held((top + (FIELDS * (len(near) + 1) + 1) * part, tile), BF16)]
+        [held((top, tile), BF16), held(((FIELDS * (len(near) + 1) + 1) * part, tile), BF16)]
         + [held((size, tile), BF16)] * len(near)
-        + [held(((FIELDS + 1) * part, tile), BF16)],
+        + [held((size - top, tile), BF16)],
         [SMEM] + [ANY] * (FIELDS + 2),
         [live] + pinned([cost, rhs, upper, x_init, y_init, block_index, blocks]),
         scratch=[pltpu.VMEM((tile, scn), F32)] * FIELDS
@@ -232,26 +231,31 @@
         + [pltpu.SMEM(block_index.shape, jnp.int32)]
         + [pltpu.VMEM((FIELDS, scn, tile), BF16), pltpu.SemaphoreType.DMA((FIELDS + 2,))],
     )
-    mine = {(far, 0): move(far_out, far, 0)}
+    mine = {(far, 0): move(far_share, far, 0)}
     for (t, s), out in zip(near, near_outs):
         mine[t, s] = move(out, t, s)
+    pieces = dict(mine)
+    pieces[far, 0] = move(far_out, far, 0)
+    for t, s in near:
+        mine[far + t, s] = move(mine[far, 0], t, s)
     relayed = call(
-        functools.partial(relay_body, top, part),
-        [held((size, tile), BF16)] * len(near),
+        functools.partial(relay_body, part),
+        [held((size - top, tile), BF16)] * len(near),
         [VMEM],
-        [mine[far, 0]],
+        [pieces[far, 0]],
     )
     for (t, s), out in zip(near, relayed):
-        mine[far + t, s] = move(out, t, s)
+        pieces[far + t, s] = move(out, t, s)
     shifts = list(mine)
     theirs = [lax.ppermute(mine[shift], "rep", [(0, 1), (1, 0)]) for shift in shifts]
-    rows = [v[v.shape[0] - part + SLOT_ROW, : nslots + 1] for v in [own] + list(mine.values())]
+    pieces = [pieces[shift] for shift in shifts]
+    rows = [v[v.shape[0] - part + SLOT_ROW, : nslots + 1] for v in [own] + pieces]
     slots = jnp.stack(rows).astype(jnp.int32)
     products, scales = call(
         functools.partial(main_body, n_blk, n_col, shifts, part),
         [like((n, 2 * ITERS * part, tile), BF16), like((8, scn), F32)],
-        [SMEM] + [VMEM] * (2 * n + 1),
-        [slots, limits, blocks, own] + [mine[shift] for shift in shifts] + theirs,
+        [SMEM] + [VMEM] * (3 * n),
+        [slots, limits, blocks, own] + [mine[shift] for shift in shifts] + theirs + pieces,
         scratch=[
             pltpu.VMEM((n * tile, n * tile), BF16),
             pltpu.VMEM((FIELDS, part, n * tile), BF16),

time: 43.5 us -> 49.4 us (1.14)
  starting transfers between devices: 11.7 us -> 15.7 us
  blocking collectives: 11.1 us -> 12 us
  waiting for transfers between devices: 13.3 us -> 14.2 us
    ppermute x7 -> x11, starting transfers between devices: 11.1 us -> 15.1 us  [move(): return lax.ppermute(value, ('blk', 'col'), pairs)]
    ppermute x7 -> x11, waiting for transfers between devices: 12.1 us -> 13.4 us  [move(): return lax.ppermute(value, ('blk', 'col'), pairs)]
    all_to_all x1, blocking collectives: 11.1 us -> 12 us  [spread(): return lax.all_to_all(value, ('blk', 'col'), 0, 0, tiled=True)]
  transfers between devices with their start and end apart: 14 -> 18, of which waited for: 6 -> 8; matrix products, arithmetic and copies ran while one was open for 0% -> 0% of each run, Pallas kernels for 0% -> 0%
where the time goes in v6:
time: 49.4 us; the launch traced here: 49.2 us
  starting transfers between devices  15.7 us (32%)
  waiting for transfers between devices  14.2 us (29%)
  blocking collectives  12 us (24%)
  Pallas kernels  5.7 us (12%)
  between operations  1.42 us (3%)
    ppermute x11, starting transfers between devices, move(): return lax.ppermute(value, ('blk', 'col'), pairs)  15.1 us
    ppermute x11, waiting for transfers between devices, move(): return lax.ppermute(value, ('blk', 'col'), pairs)  13.4 us
    all_to_all x1, blocking collectives, spread(): return lax.all_to_all(value, ('blk', 'col'), 0, 0, tiled=True)  12 us
    pallas_call x4, Pallas kernels, call(): pl.pallas_call(body, out_shape=list(outs), in_specs=in_specs, out_specs=[...  5.7 us
  transfers between devices with their start and end apart: 18, of which 8 were waited for; matrix products, arithmetic and copies ran while one was open for 0% of the time, Pallas kernels for 0%

profile of v6, /device:TPU:0, one launch (start us, length us, event | category | flops | bytes accessed | tf_op | source)
XLA Modules:
  0.0 49.2 jit_solution(2154826308081007025)
XLA Ops:
  1.3 0.0 copy-start
  1.3 1.5 %shard_map.104 = (bf16[384,128]{1,0:T(8,128)(2,1)S(1)}, bf16[336,128]{1,0:T(8,128)(2,1)S(1)}, bf16[480,128]{1,0:T(8,128)(2,1)S(1)}, bf16[480,128]{1,0:T(8,128)(2...) custom-call(s32[1,1]{1,0:T(1,128)S(6)} %copy.11.refs_0_, f32[128,128]{1,0:T(8,128)} %cost.1, ...), custom_call_target="tpu_custom_call" | custom-call | bytes 1101852 | tf_op jit(solution)/shard_map/pallas_call | solution.py:39
  2.8 4.1 %collective-permute-start = (bf16[336,128]{1,0:T(8,128)(2,1)S(1)}, bf16[336,128]{1,0:T(8,128)(2,1)S(1)}, u32[]{:S(2)}, u32[]{:S(2)}) collective-permute-start(bf16[336,128]{1,0:T(8,128)(2,1)S(1)} %get-tuple-element.14), channel_id=1, source_target_pairs={{0,8},{2,10},{4,12},{6,14},{8,0},{10,2},{12,4},{14,6},{1,9},{3,11}... | collective-permute-start | bytes 258056 | tf_op jit(solution)/shard_map/ppermute | solution.py:215
  6.9 0.1 collective-permute-start.7
  7.0 1.7 %collective-permute-start.1 = (bf16[480,128]{1,0:T(8,128)(2,1)S(1)}, bf16[480,128]{1,0:T(8,128)(2,1)S(1)}, u32[]{:S(2)}, u32[]{:S(2)}) collective-permute-start(bf16[480,128]{1,0:T(8,128)(2,1)S(1)} %get-tuple-element.15), channel_id=1, source_target_pairs={{0,2},{2,0},{4,6},{6,4},{8,10},{10,8},{12,14},{14,12},{1,3},{3,1},... | collective-permute-start | bytes 368648 | tf_op jit(solution)/shard_map/ppermute | solution.py:215
  8.8 1.6 %collective-permute-start.2 = (bf16[480,128]{1,0:T(8,128)(2,1)S(1)}, bf16[480,128]{1,0:T(8,128)(2,1)S(1)}, u32[]{:S(2)}, u32[]{:S(2)}) collective-permute-start(bf16[480,128]{1,0:T(8,128)(2,1)S(1)} %get-tuple-element.16), channel_id=1, source_target_pairs={{0,4},{2,6},{4,0},{6,2},{8,12},{10,14},{12,8},{14,10},{1,5},{3,7},... | collective-permute-start | bytes 368648 | tf_op jit(solution)/shard_map/ppermute | solution.py:215
  10.3 0.2 collective-permute-start.3
  10.5 2.8 %collective-permute-done.came.refs_14_ = bf16[336,128]{1,0:T(8,128)(2,1)S(1)} collective-permute-done((bf16[336,128]{1,0:T(8,128)(2,1)S(1)}, bf16[336,128]{1,0:T(8,128)(2,1)S(1)}, u32[]{:S(2)}, u32[]{:S(2)}) %collective-permute-start) | collective-permute-done | bytes 86048 | tf_op jit(solution)/shard_map/ppermute | solution.py:215
  13.3 2.2 %collective-permute-start.4 = (bf16[96,128]{1,0:T(8,128)(2,1)S(1)}, bf16[96,128]{1,0:T(8,128)(2,1)S(1)}, u32[]{:S(2)}, u32[]{:S(2)}) collective-permute-start(bf16[96,128]{1,0:T(8,128)(2,1)S(1)} %get-tuple-element.18), channel_id=1, source_target_pairs={{0,2},{2,0},{4,6},{6,4},{8,10},{10,8},{12,14},{14,12},{1,3},{3,1},... | collective-permute-start | bytes 73736 | tf_op jit(solution)/shard_map/ppermute | solution.py:215
  15.5 0.0 collective-permute-done.7.refs_0_
  15.5 0.8 %collective-permute-start.5 = (bf16[96,128]{1,0:T(8,128)(2,1)S(1)}, bf16[96,128]{1,0:T(8,128)(2,1)S(1)}, u32[]{:S(2)}, u32[]{:S(2)}) collective-permute-start(bf16[96,128]{1,0:T(8,128)(2,1)S(1)} %get-tuple-element.19), channel_id=1, source_target_pairs={{0,4},{2,6},{4,0},{6,2},{8,12},{10,14},{12,8},{14,10},{1,5},{3,7},... | collective-permute-start | bytes 73736 | tf_op jit(solution)/shard_map/ppermute | solution.py:215
  16.3 2.6 %collective-permute-done.4.refs_18_ = bf16[96,128]{1,0:T(8,128)(2,1)S(1)} collective-permute-done((bf16[96,128]{1,0:T(8,128)(2,1)S(1)}, bf16[96,128]{1,0:T(8,128)(2,1)S(1)}, u32[]{:S(2)}, u32[]{:S(2)}) %collective-permute-start.4) | collective-permute-done | bytes 24608 | tf_op jit(solution)/shard_map/ppermute | solution.py:215
  18.8 1.0 %collective-permute-start.6 = (bf16[96,128]{1,0:T(8,128)(2,1)S(1)}, bf16[96,128]{1,0:T(8,128)(2,1)S(1)}, u32[]{:S(2)}, u32[]{:S(2)}) collective-permute-start(bf16[96,128]{1,0:T(8,128)(2,1)S(1)} %get-tuple-element.20), channel_id=1, source_target_pairs={{0,6},{2,4},{4,2},{6,0},{8,14},{10,12},{12,10},{14,8},{1,7},{3,5},... | collective-permute-start | bytes 73736 | tf_op jit(solution)/shard_map/ppermute | solution.py:215
  19.8 0.0 collective-permute-done.5.refs_19_
  19.8 0.0 collective-permute-start.11
  19.8 3.8 %collective-permute-done.6.refs_20_ = bf16[96,128]{1,0:T(8,128)(2,1)S(1)} collective-permute-done((bf16[96,128]{1,0:T(8,128)(2,1)S(1)}, bf16[96,128]{1,0:T(8,128)(2,1)S(1)}, u32[]{:S(2)}, u32[]{:S(2)}) %collective-permute-start.6) | collective-permute-done | bytes 24608 | tf_op jit(solution)/shard_map/ppermute | solution.py:215
  23.6 1.0 %collective-permute-start.10 = (bf16[384,128]{1,0:T(8,128)(2,1)S(1)}, bf16[384,128]{1,0:T(8,128)(2,1)S(1)}, u32[]{:S(2)}, u32[]{:S(2)}) collective-permute-start(bf16[384,128]{1,0:T(8,128)(2,1)S(1)} %collective-permute-done.7.refs_0_), channel_id=1, source_target_pairs={{0,6},{2,4},{4,2},{6,0},{8,14},{10,12},{12,10},{14,8},{1,7},{3,5},... | collective-permute-start | bytes 294920 | tf_op jit(solution)/shard_map/ppermute | solution.py:215
  24.5 0.0 collective-permute-done.1.refs_1_.refs_15_
  24.5 0.0 collective-permute-start.12
  24.5 0.0 collective-permute-done.2.refs_2_.refs_16_
  24.5 1.5 %collective-permute-start.9 = (bf16[384,128]{1,0:T(8,128)(2,1)S(1)}, bf16[384,128]{1,0:T(8,128)(2,1)S(1)}, u32[]{:S(2)}, u32[]{:S(2)}) collective-permute-start(bf16[384,128]{1,0:T(8,128)(2,1)S(1)} %collective-permute-done.7.refs_0_), channel_id=1, source_target_pairs={{0,4},{2,6},{4,0},{6,2},{8,12},{10,14},{12,8},{14,10},{1,5},{3,7},... | collective-permute-start | bytes 294920 | tf_op jit(solution)/shard_map/ppermute | solution.py:215
  26.0 0.0 collective-permute-done.3.refs_3_.refs_17_
  26.0 1.1 %collective-permute-start.8 = (bf16[384,128]{1,0:T(8,128)(2,1)S(1)}, bf16[384,128]{1,0:T(8,128)(2,1)S(1)}, u32[]{:S(2)}, u32[]{:S(2)}) collective-permute-start(bf16[384,128]{1,0:T(8,128)(2,1)S(1)} %collective-permute-done.7.refs_0_), channel_id=1, source_target_pairs={{0,2},{2,0},{4,6},{6,4},{8,10},{10,8},{12,14},{14,12},{1,3},{3,1},... | collective-permute-start | bytes 294920 | tf_op jit(solution)/shard_map/ppermute | solution.py:215
  27.1 0.0 collective-permute-done.11.refs_7_
  27.1 0.0 collective-permute-start.13
  27.1 2.7 %collective-permute-done.10.refs_6_ = bf16[384,128]{1,0:T(8,128)(2,1)S(1)} collective-permute-done((bf16[384,128]{1,0:T(8,128)(2,1)S(1)}, bf16[384,128]{1,0:T(8,128)(2,1)S(1)}, u32[]{:S(2)}, u32[]{:S(2)}) %collective-permute-start.10) | collective-permute-done | bytes 98336 | tf_op jit(solution)/shard_map/ppermute | solution.py:215
  29.8 0.0 collective-permute-start.14
  29.8 0.8 %collective-permute-done.9.refs_5_ = bf16[384,128]{1,0:T(8,128)(2,1)S(1)} collective-permute-done((bf16[384,128]{1,0:T(8,128)(2,1)S(1)}, bf16[384,128]{1,0:T(8,128)(2,1)S(1)}, u32[]{:S(2)}, u32[]{:S(2)}) %collective-permute-start.9) | collective-permute-done | bytes 98336 | tf_op jit(solution)/shard_map/ppermute | solution.py:215
  30.7 0.0 collective-permute-start.17
  30.7 0.8 %collective-permute-done.8.refs_4_ = bf16[384,128]{1,0:T(8,128)(2,1)S(1)} collective-permute-done((bf16[384,128]{1,0:T(8,128)(2,1)S(1)}, bf16[384,128]{1,0:T(8,128)(2,1)S(1)}, u32[]{:S(2)}, u32[]{:S(2)}) %collective-permute-start.8) | collective-permute-done | bytes 98336 | tf_op jit(solution)/shard_map/ppermute | solution.py:215
  31.4 0.0 collective-permute-start.16
  31.4 0.0 collective-permute-done.12.refs_8_
  31.4 0.5 %collective-permute-start.15 = (bf16[384,128]{1,0:T(8,128)(2,1)S(1)}, bf16[384,128]{1,0:T(8,128)(2,1)S(1)}, u32[]{:S(2)}, u32[]{:S(2)}) collective-permute-start(bf16[384,128]{1,0:T(8,128)(2,1)S(1)} %collective-permute-done.8.refs_4_), channel_id=1, source_target_pairs={{0,1},{1,0},{2,3},{3,2},{4,5},{5,4},{6,7},{7,6},{8,9},{9,8},{10,11... | collective-permute-start | bytes 294920 | tf_op jit(solution)/shard_map/ppermute | solution.py:250
  32.1 0.0 copy-start.6
  32.1 0.0 collective-permute-done.13.refs_9_
  32.1 0.0 collective-permute-done.14.refs_10_
  32.1 0.0 collective-permute-done.17.refs_13_
  32.1 0.6 %collective-permute-done.16.refs_12_ = bf16[384,128]{1,0:T(8,128)(2,1)S(1)} collective-permute-done((bf16[384,128]{1,0:T(8,128)(2,1)S(1)}, bf16[384,128]{1,0:T(8,128)(2,1)S(1)}, u32[]{:S(2)}, u32[]{:S(2)}) %collective-permute-start.16) | collective-permute-done | bytes 98336 | tf_op jit(solution)/shard_map/ppermute | solution.py:250
  32.7 0.2 collective-permute-done.15.refs_11_
  32.9 0.0 copy-done
  32.9 0.0 copy-done.6
  32.9 0.0 copy-start.5
  32.9 3.4 %shard_map.106 = (bf16[8,64,128]{2,1,0:T(8,128)(2,1)S(1)}, f32[8,128]{1,0:T(8,128)S(1)}) custom-call(s32[8,7]{1,0:T(8,128)S(1)} %convert_element_type.3.slots, s32[1,128]{1,0:T(1,128)S(1)} %bitcast.1, bf16[1,1,6,128,128]{4,3,2,1,0:T(8,128)(2,1)S(1)} %copy-done, bf16[96,128]{1,0:T(8,128)(2,1)S(1)} %get-tuple-element.13.own, ...), custom_call_target="tpu_custom_call" | custom-call | flops 134217728 | bytes 2409184 | tf_op jit(solution)/shard_map/pallas_call | solution.py:39
  36.3 0.0 copy-start.1
  36.3 0.0 copy-start.2
  36.3 0.0 copy-start.3
  36.3 0.0 copy-start.4
  36.3 12.0 %all_to_all.5.recv = bf16[8,64,128]{2,1,0:T(8,128)(2,1)S(1)} all-to-all(bf16[8,64,128]{2,1,0:T(8,128)(2,1)S(1)} %get-tuple-element.22), channel_id=1, replica_groups=mesh['groups'=2,'blk'=4,'col'=2,'rep'=2] {'blk','col'}, dimensions={0} | all-to-all | bytes 262144 | tf_op jit(solution)/shard_map/all_to_all | solution.py:211
  48.4 0.0 copy-done.5
  48.4 0.0 copy-done.1
  48.4 0.0 copy-done.2
  48.4 0.0 copy-done.3
  48.4 0.0 copy-done.4
  48.4 0.8 %shard_map.107 = (f32[128,128]{1,0:T(8,128)}, f32[128,128]{1,0:T(8,128)}) custom-call(bf16[8,64,128]{2,1,0:T(8,128)(2,1)S(1)} %all_to_all.5.recv, f32[8,128]{1,0:T(8,128)S(1)} %get-tuple-element.23.scales, f32[128,128]{1,0:T(8,128)S(1)} %copy-done.1, f32[128,128]{1,0:T(8,128)S(1)} %copy-done.2, f32[128,128]{1,0:T(8,128)S(1)} %copy-done.3, ...), custom_call_target="tpu_custom_call" | custom-call | bytes 594432 | tf_op jit(solution)/shard_map/pallas_call | solution.py:39
  (11 shorter events, 0.1 us)
Async XLA Ops:
  1.3 31.6 %copy-start = (bf16[1,1,6,128,128]{4,3,2,1,0:T(8,128)(2,1)S(1)}, bf16[1,1,6,128,128]{4,3,2,1,0:T(8,128)(2,1)}, u32[]{:S(2)}) copy-start(bf16[1,1,6,128,128]{4,3,2,1,0:T(8,128)(2,1)} %blocks.1) | copy-start | bytes 589828
  2.8 10.5 %collective-permute-start = (bf16[336,128]{1,0:T(8,128)(2,1)S(1)}, bf16[336,128]{1,0:T(8,128)(2,1)S(1)}, u32[]{:S(2)}, u32[]{:S(2)}) collective-permute-start(bf16[336,128]{1,0:T(8,128)(2,1)S(1)} %get-tuple-element.14), channel_id=1, source_target_pairs={{0,8},{2,10},{4,12},{6,14},{8,0},{10,2},{12,4},{14,6},{1,9},{3,11}... | collective-permute-start | bytes 258056 | tf_op jit(solution)/shard_map/ppermute | solution.py:215
  6.9 8.6 %collective-permute-start.7 = (bf16[384,128]{1,0:T(8,128)(2,1)S(1)}, bf16[384,128]{1,0:T(8,128)(2,1)S(1)}, u32[]{:S(2)}, u32[]{:S(2)}) collective-permute-start(bf16[384,128]{1,0:T(8,128)(2,1)S(1)} %get-tuple-element.21), channel_id=1, source_target_pairs={{0,8},{2,10},{4,12},{6,14},{8,0},{10,2},{12,4},{14,6},{1,9},{3,11}... | collective-permute-start | bytes 294920 | tf_op jit(solution)/shard_map/ppermute | solution.py:215
  7.0 17.5 %collective-permute-start.1 = (bf16[480,128]{1,0:T(8,128)(2,1)S(1)}, bf16[480,128]{1,0:T(8,128)(2,1)S(1)}, u32[]{:S(2)}, u32[]{:S(2)}) collective-permute-start(bf16[480,128]{1,0:T(8,128)(2,1)S(1)} %get-tuple-element.15), channel_id=1, source_target_pairs={{0,2},{2,0},{4,6},{6,4},{8,10},{10,8},{12,14},{14,12},{1,3},{3,1},... | collective-permute-start | bytes 368648 | tf_op jit(solution)/shard_map/ppermute | solution.py:215
  8.8 15.8 %collective-permute-start.2 = (bf16[480,128]{1,0:T(8,128)(2,1)S(1)}, bf16[480,128]{1,0:T(8,128)(2,1)S(1)}, u32[]{:S(2)}, u32[]{:S(2)}) collective-permute-start(bf16[480,128]{1,0:T(8,128)(2,1)S(1)} %get-tuple-element.16), channel_id=1, source_target_pairs={{0,4},{2,6},{4,0},{6,2},{8,12},{10,14},{12,8},{14,10},{1,5},{3,7},... | collective-permute-start | bytes 368648 | tf_op jit(solution)/shard_map/ppermute | solution.py:215
  10.3 15.7 %collective-permute-start.3 = (bf16[480,128]{1,0:T(8,128)(2,1)S(1)}, bf16[480,128]{1,0:T(8,128)(2,1)S(1)}, u32[]{:S(2)}, u32[]{:S(2)}) collective-permute-start(bf16[480,128]{1,0:T(8,128)(2,1)S(1)} %get-tuple-element.17), channel_id=1, source_target_pairs={{0,6},{2,4},{4,2},{6,0},{8,14},{10,12},{12,10},{14,8},{1,7},{3,5},... | collective-permute-start | bytes 368648 | tf_op jit(solution)/shard_map/ppermute | solution.py:215
  13.3 5.5 %collective-permute-start.4 = (bf16[96,128]{1,0:T(8,128)(2,1)S(1)}, bf16[96,128]{1,0:T(8,128)(2,1)S(1)}, u32[]{:S(2)}, u32[]{:S(2)}) collective-permute-start(bf16[96,128]{1,0:T(8,128)(2,1)S(1)} %get-tuple-element.18), channel_id=1, source_target_pairs={{0,2},{2,0},{4,6},{6,4},{8,10},{10,8},{12,14},{14,12},{1,3},{3,1},... | collective-permute-start | bytes 73736 | tf_op jit(solution)/shard_map/ppermute | solution.py:215
  15.5 4.3 %collective-permute-start.5 = (bf16[96,128]{1,0:T(8,128)(2,1)S(1)}, bf16[96,128]{1,0:T(8,128)(2,1)S(1)}, u32[]{:S(2)}, u32[]{:S(2)}) collective-permute-start(bf16[96,128]{1,0:T(8,128)(2,1)S(1)} %get-tuple-element.19), channel_id=1, source_target_pairs={{0,4},{2,6},{4,0},{6,2},{8,12},{10,14},{12,8},{14,10},{1,5},{3,7},... | collective-permute-start | bytes 73736 | tf_op jit(solution)/shard_map/ppermute | solution.py:215
  18.8 4.7 %collective-permute-start.6 = (bf16[96,128]{1,0:T(8,128)(2,1)S(1)}, bf16[96,128]{1,0:T(8,128)(2,1)S(1)}, u32[]{:S(2)}, u32[]{:S(2)}) collective-permute-start(bf16[96,128]{1,0:T(8,128)(2,1)S(1)} %get-tuple-element.20), channel_id=1, source_target_pairs={{0,6},{2,4},{4,2},{6,0},{8,14},{10,12},{12,10},{14,8},{1,7},{3,5},... | collective-permute-start | bytes 73736 | tf_op jit(solution)/shard_map/ppermute | solution.py:215
  19.8 7.3 %collective-permute-start.11 = (bf16[384,128]{1,0:T(8,128)(2,1)S(1)}, bf16[384,128]{1,0:T(8,128)(2,1)S(1)}, u32[]{:S(2)}, u32[]{:S(2)}) collective-permute-start(bf16[384,128]{1,0:T(8,128)(2,1)S(1)} %collective-permute-done.7.refs_0_), channel_id=1, source_target_pairs={{0,1},{1,0},{2,3},{3,2},{4,5},{5,4},{6,7},{7,6},{8,9},{9,8},{10,11... | collective-permute-start | bytes 294920 | tf_op jit(solution)/shard_map/ppermute | solution.py:250
  23.6 6.3 %collective-permute-start.10 = (bf16[384,128]{1,0:T(8,128)(2,1)S(1)}, bf16[384,128]{1,0:T(8,128)(2,1)S(1)}, u32[]{:S(2)}, u32[]{:S(2)}) collective-permute-start(bf16[384,128]{1,0:T(8,128)(2,1)S(1)} %collective-permute-done.7.refs_0_), channel_id=1, source_target_pairs={{0,6},{2,4},{4,2},{6,0},{8,14},{10,12},{12,10},{14,8},{1,7},{3,5},... | collective-permute-start | bytes 294920 | tf_op jit(solution)/shard_map/ppermute | solution.py:215
  24.5 6.9 %collective-permute-start.12 = (bf16[480,128]{1,0:T(8,128)(2,1)S(1)}, bf16[480,128]{1,0:T(8,128)(2,1)S(1)}, u32[]{:S(2)}, u32[]{:S(2)}) collective-permute-start(bf16[480,128]{1,0:T(8,128)(2,1)S(1)} %collective-permute-done.1.refs_1_.refs_15_), channel_id=1, source_target_pairs={{0,1},{1,0},{2,3},{3,2},{4,5},{5,4},{6,7},{7,6},{8,9},{9,8},{10,11... | collective-permute-start | bytes 368648 | tf_op jit(solution)/shard_map/ppermute | solution.py:250
  24.5 6.1 %collective-permute-start.9 = (bf16[384,128]{1,0:T(8,128)(2,1)S(1)}, bf16[384,128]{1,0:T(8,128)(2,1)S(1)}, u32[]{:S(2)}, u32[]{:S(2)}) collective-permute-start(bf16[384,128]{1,0:T(8,128)(2,1)S(1)} %collective-permute-done.7.refs_0_), channel_id=1, source_target_pairs={{0,4},{2,6},{4,0},{6,2},{8,12},{10,14},{12,8},{14,10},{1,5},{3,7},... | collective-permute-start | bytes 294920 | tf_op jit(solution)/shard_map/ppermute | solution.py:215
  26.0 5.4 %collective-permute-start.8 = (bf16[384,128]{1,0:T(8,128)(2,1)S(1)}, bf16[384,128]{1,0:T(8,128)(2,1)S(1)}, u32[]{:S(2)}, u32[]{:S(2)}) collective-permute-start(bf16[384,128]{1,0:T(8,128)(2,1)S(1)} %collective-permute-done.7.refs_0_), channel_id=1, source_target_pairs={{0,2},{2,0},{4,6},{6,4},{8,10},{10,8},{12,14},{14,12},{1,3},{3,1},... | collective-permute-start | bytes 294920 | tf_op jit(solution)/shard_map/ppermute | solution.py:215
  27.1 4.9 %collective-permute-start.13 = (bf16[480,128]{1,0:T(8,128)(2,1)S(1)}, bf16[480,128]{1,0:T(8,128)(2,1)S(1)}, u32[]{:S(2)}, u32[]{:S(2)}) collective-permute-start(bf16[480,128]{1,0:T(8,128)(2,1)S(1)} %collective-permute-done.2.refs_2_.refs_16_), channel_id=1, source_target_pairs={{0,1},{1,0},{2,3},{3,2},{4,5},{5,4},{6,7},{7,6},{8,9},{9,8},{10,11... | collective-permute-start | bytes 368648 | tf_op jit(solution)/shard_map/ppermute | solution.py:250
  29.8 2.3 %collective-permute-start.14 = (bf16[480,128]{1,0:T(8,128)(2,1)S(1)}, bf16[480,128]{1,0:T(8,128)(2,1)S(1)}, u32[]{:S(2)}, u32[]{:S(2)}) collective-permute-start(bf16[480,128]{1,0:T(8,128)(2,1)S(1)} %collective-permute-done.3.refs_3_.refs_17_), channel_id=1, source_target_pairs={{0,1},{1,0},{2,3},{3,2},{4,5},{5,4},{6,7},{7,6},{8,9},{9,8},{10,11... | collective-permute-start | bytes 368648 | tf_op jit(solution)/shard_map/ppermute | solution.py:250
  30.7 1.4 %collective-permute-start.17 = (bf16[384,128]{1,0:T(8,128)(2,1)S(1)}, bf16[384,128]{1,0:T(8,128)(2,1)S(1)}, u32[]{:S(2)}, u32[]{:S(2)}) collective-permute-start(bf16[384,128]{1,0:T(8,128)(2,1)S(1)} %collective-permute-done.10.refs_6_), channel_id=1, source_target_pairs={{0,1},{1,0},{2,3},{3,2},{4,5},{5,4},{6,7},{7,6},{8,9},{9,8},{10,11... | collective-permute-start | bytes 294920 | tf_op jit(solution)/shard_map/ppermute | solution.py:250
  31.4 1.3 %collective-permute-start.16 = (bf16[384,128]{1,0:T(8,128)(2,1)S(1)}, bf16[384,128]{1,0:T(8,128)(2,1)S(1)}, u32[]{:S(2)}, u32[]{:S(2)}) collective-permute-start(bf16[384,128]{1,0:T(8,128)(2,1)S(1)} %collective-permute-done.9.refs_5_), channel_id=1, source_target_pairs={{0,1},{1,0},{2,3},{3,2},{4,5},{5,4},{6,7},{7,6},{8,9},{9,8},{10,11... | collective-permute-start | bytes 294920 | tf_op jit(solution)/shard_map/ppermute | solution.py:250
  31.4 1.5 %collective-permute-start.15 = (bf16[384,128]{1,0:T(8,128)(2,1)S(1)}, bf16[384,128]{1,0:T(8,128)(2,1)S(1)}, u32[]{:S(2)}, u32[]{:S(2)}) collective-permute-start(bf16[384,128]{1,0:T(8,128)(2,1)S(1)} %collective-permute-done.8.refs_4_), channel_id=1, source_target_pairs={{0,1},{1,0},{2,3},{3,2},{4,5},{5,4},{6,7},{7,6},{8,9},{9,8},{10,11... | collective-permute-start | bytes 294920 | tf_op jit(solution)/shard_map/ppermute | solution.py:250
  32.1 0.8 %copy-start.6 = (s32[128]{0:T(128)S(1)}, s32[128]{0:T(128)}, u32[]{:S(2)}) copy-start(s32[128]{0:T(128)} %param.17) | copy-start | bytes 1540
  32.9 15.5 %copy-start.5 = (f32[128,128]{1,0:T(8,128)S(1)}, f32[128,128]{1,0:T(8,128)}, u32[]{:S(2)}) copy-start(f32[128,128]{1,0:T(8,128)} %y_in.1) | copy-start | bytes 196612
  36.3 12.1 %copy-start.1 = (f32[128,128]{1,0:T(8,128)S(1)}, f32[128,128]{1,0:T(8,128)}, u32[]{:S(2)}) copy-start(f32[128,128]{1,0:T(8,128)} %cost.1) | copy-start | bytes 196612
  36.3 12.1 %copy-start.2 = (f32[128,128]{1,0:T(8,128)S(1)}, f32[128,128]{1,0:T(8,128)}, u32[]{:S(2)}) copy-start(f32[128,128]{1,0:T(8,128)} %rhs.1) | copy-start | bytes 196612
  36.3 12.1 %copy-start.3 = (f32[128,128]{1,0:T(8,128)S(1)}, f32[128,128]{1,0:T(8,128)}, u32[]{:S(2)}) copy-start(f32[128,128]{1,0:T(8,128)} %upper.1) | copy-start | bytes 196612
  36.3 12.1 %copy-start.4 = (f32[128,128]{1,0:T(8,128)S(1)}, f32[128,128]{1,0:T(8,128)}, u32[]{:S(2)}) copy-start(f32[128,128]{1,0:T(8,128)} %x_in.1) | copy-start | bytes 196612

commit v7 on v5

--- a/solution.py
+++ b/solution.py
@@ -34,7 +34,7 @@
     return [pltpu.with_memory_space_constraint(v, pltpu.HBM) for v in values]
 
 
-def call(body, outs, in_specs, args, scratch=(), flops=0, limit=32):
+def call(body, outs, in_specs, args, scratch=(), flops=0, limit=32, aliases=None):
     nbytes = sum(math.prod(a.shape) * jnp.dtype(a.dtype).itemsize for a in list(args) + list(outs))
     return pl.pallas_call(
         body,
@@ -42,6 +42,7 @@
         in_specs=in_specs,
         out_specs=[VMEM] * len(outs),
         scratch_shapes=list(scratch),
+        input_output_aliases=aliases or {},
         compiler_params=pltpu.CompilerParams(vmem_limit_bytes=limit * MIB),
         cost_estimate=pl.CostEstimate(flops=flops, bytes_accessed=nbytes, transcendentals=0),
     )(*args)
@@ -61,10 +62,10 @@
     return jnp.maximum(capped, 0.0)
 
 
-def prep_body(n_col, far, near, *refs):
+def prep_body(n_col, far, near, first_near, *refs):
     live, *sources = refs[: FIELDS + 3]
-    far_out, *near_outs, own_out = refs[FIELDS + 3 : FIELDS + 5 + len(near)]
-    *fields, share, index, turned, sems = refs[FIELDS + 5 + len(near) :]
+    far_out, *near_outs, own_out = refs[FIELDS + 3 : FIELDS + 5 + len(first_near)]
+    *fields, share, index, turned, sems = refs[FIELDS + 5 + len(first_near) :]
     half, tile = share.shape[0], share.shape[1]
     first = lax.axis_index("rep") * half
     targets = (*fields, index)
@@ -106,8 +107,9 @@
         out[out.shape[0] - part :, :] = info
     for m, (t, s) in enumerate([(0, 0), *near]):
         piece(far_out, top + m * FIELDS * part, far + t, s)
-        if m > 0:
-            piece(near_outs[m - 1], top, t, s)
+    for out, (t, s) in zip(near_outs, first_near):
+        for m in range(1 if t == 0 else n_col):
+            piece(out, top + m * FIELDS * part, t, s ^ m)
     piece(own_out, 0, 0, 0)
     own_out[FIELDS * part :, :] = info
 
@@ -120,45 +122,74 @@
         out[top + FIELDS * part :, :] = came[came.shape[0] - part :, :]
 
 
-def main_body(n_blk, n_col, shifts, part, slots, bounded, blocks, own, *refs):
+def place(n_blk, n_col, mat, slots, source, shift, slot, block, nslots):
+    tile = block.shape[-1]
+    blk, col = lax.axis_index("blk") ^ shift[0], lax.axis_index("col") ^ shift[1]
+    position = slots[source, slot]
+    row = pl.multiple_of((blk * n_col + position // n_blk) * tile, tile)
+    column = pl.multiple_of(((position % n_blk) * n_col + col) * tile, tile)
+
+    @pl.when(slot < slots[source, nslots])
+    def _():
+        mat[pl.ds(row, tile), pl.ds(column, tile)] = block[...]
+
+
+def place_shares(n_blk, n_col, mat, slots, source, shift, own_part, other_part, nslots):
+    half = nslots // 2
+    tile = own_part.shape[1]
+    core = lax.axis_index("rep")
+    for part, which in ((own_part, core), (other_part, 1 - core)):
+        for k in range(half):
+            block = part.at[k * tile : (k + 1) * tile, :]
+            place(n_blk, n_col, mat, slots, source, shift, which * half + k, block, nslots)
+
+
+def take(n_col, fields, shift, ref, at):
+    part, tile = fields.shape[1], ref.shape[1]
+    blk, col = lax.axis_index("blk") ^ shift[0], lax.axis_index("col") ^ shift[1]
+    lanes = pl.ds(pl.multiple_of((blk * n_col + col) * tile, tile), tile)
+    for j in range(FIELDS):
+        fields[j, :, lanes] = ref[at + j * part : at + (j + 1) * part, :]
+    info = ref[ref.shape[0] - part :, :].astype(F32)
+    sums = []
+    for j in range(2):
+        first, second, third = (info[PARTS * j + k : PARTS * j + k + 1] for k in range(PARTS))
+        sums.append((first + second) + third)
+    return sums
+
+
+def early_body(n_blk, n_col, shifts, slots, blocks_in, own, *refs):
+    count = len(shifts)
+    mine, theirs = refs[:count], refs[count : 2 * count]
+    mat, fields, sums_out, blocks, sem = refs[2 * count :]
+    copy = pltpu.make_async_copy(blocks_in, blocks, sem)
+    copy.start()
+    nslots = blocks.shape[2]
+    mat[...] = jnp.zeros(mat.shape, BF16)
+    fields[...] = jnp.zeros(fields.shape, BF16)
+    sums = take(n_col, fields, (0, 0), own, 0)
+    for m, (shift, own_part, other_part) in enumerate(zip(shifts, mine, theirs)):
+        place_shares(n_blk, n_col, mat, slots, m + 1, shift, own_part, other_part, nslots)
+        more = take(n_col, fields, shift, own_part, nslots // 2 * own_part.shape[1])
+        sums = [a + b for a, b in zip(sums, more)]
+    copy.wait()
+    for k in range(nslots):
+        place(n_blk, n_col, mat, slots, 0, (0, 0), k, blocks.at[0, 0, k], nslots)
+    sums_out[...] = jnp.concatenate(sums + [jnp.zeros((6, own.shape[1]), F32)], axis=0)
+
+
+def main_body(n_blk, n_col, shifts, nslots, slots, bounded, mat, fields, sums_in, *refs):
     n = n_blk * n_col
-    mine, theirs = refs[: n - 1], refs[n - 1 : 2 * (n - 1)]
-    out, scales, mat, fields, turned = refs[2 * (n - 1) :]
-    tile = blocks.shape[-1]
-    nslots = blocks.shape[2]
-    half = nslots // 2
-    me_b, me_c, me_r = lax.axis_index("blk"), lax.axis_index("col"), lax.axis_index("rep")
-    mat[...] = jnp.zeros(mat.shape, BF16)
-
-    def place(source, t, s, slot, block):
-        blk, col = me_b ^ t, me_c ^ s
-        position = slots[source, slot]
-        row = pl.multiple_of((blk * n_col + position // n_blk) * tile, tile)
-        column = pl.multiple_of(((position % n_blk) * n_col + col) * tile, tile)
-
-        @pl.when(slot < slots[source, nslots])
-        def _():
-            mat[pl.ds(row, tile), pl.ds(column, tile)] = block()
-
-    sums = [jnp.zeros((1, tile), F32)] * 2
-
-    def take(t, s, ref, at):
-        lanes = pl.ds(pl.multiple_of(((me_b ^ t) * n_col + (me_c ^ s)) * tile, tile), tile)
-        for j in range(FIELDS):
-            fields[j, :, lanes] = ref[at + j * part : at + (j + 1) * part, :]
-        info = ref[ref.shape[0] - part :, :].astype(F32)
-        for j in range(2):
-            first, second, third = (info[PARTS * j + k : PARTS * j + k + 1] for k in range(PARTS))
-            sums[j] += (first + second) + third
-
-    for k in range(nslots):
-        place(0, 0, 0, k, lambda k=k: blocks[0, 0, k])
-    take(0, 0, own, 0)
-    for m, ((t, s), own_part, other_part) in enumerate(zip(shifts, mine, theirs)):
-        for k in range(half):
-            place(m + 1, t, s, me_r * half + k, lambda k=k, r=own_part: r[k * tile : (k + 1) * tile, :])
-            place(m + 1, t, s, (1 - me_r) * half + k, lambda k=k, r=other_part: r[k * tile : (k + 1) * tile, :])
-        take(t, s, own_part, half * tile)
+    count = len(shifts)
+    mine, theirs = refs[:count], refs[count : 2 * count]
+    out, scales, _, _, turned = refs[2 * count :]
+    part, tile = fields.shape[1], mine[0].shape[1]
+    me_b, me_c = lax.axis_index("blk"), lax.axis_index("col")
+    sums = [sums_in[0:1, :], sums_in[1:2, :]]
+    for m, (shift, own_part, other_part) in enumerate(zip(shifts, mine, theirs)):
+        place_shares(n_blk, n_col, mat, slots, m, shift, own_part, other_part, nslots)
+        more = take(n_col, fields, shift, own_part, nslots // 2 * tile)
+        sums = [a + b for a, b in zip(sums, more)]
     cost, rhs, upper, primal, dual = (fields[j].astype(F32) for j in range(FIELDS))
     weight = jnp.sqrt(sums[0] + EPS) / jnp.sqrt(sums[1] + EPS)
     rows = jnp.concatenate([ETA / weight, ETA * weight, bounded[...].astype(F32), jnp.zeros((5, tile), F32)], axis=0)
@@ -220,10 +251,11 @@
     half = nslots // 2
     top = half * tile
     size = top + (FIELDS + 1) * part
+    first_near = [(0, s) for s in range(1, n_col)] + [(t, 0) for t in range(1, far)]
     far_out, *near_outs, own = call(
-        functools.partial(prep_body, n_col, far, near),
+        functools.partial(prep_body, n_col, far, near, first_near),
         [held((top + (FIELDS * (len(near) + 1) + 1) * part, tile), BF16)]
-        + [held((size, tile), BF16)] * len(near)
+        + [held((size + (n_col - 1) * FIELDS * part * (t > 0), tile), BF16) for t, s in first_near]
         + [held(((FIELDS + 1) * part, tile), BF16)],
         [SMEM] + [ANY] * (FIELDS + 2),
         [live] + pinned([cost, rhs, upper, x_init, y_init, block_index, blocks]),
@@ -232,32 +264,44 @@
         + [pltpu.SMEM(block_index.shape, jnp.int32)]
         + [pltpu.VMEM((FIELDS, scn, tile), BF16), pltpu.SemaphoreType.DMA((FIELDS + 2,))],
     )
-    mine = {(far, 0): move(far_out, far, 0)}
-    for (t, s), out in zip(near, near_outs):
-        mine[t, s] = move(out, t, s)
-    relayed = call(
-        functools.partial(relay_body, top, part),
-        [held((size, tile), BF16)] * len(near),
-        [VMEM],
-        [mine[far, 0]],
-    )
-    for (t, s), out in zip(near, relayed):
-        mine[far + t, s] = move(out, t, s)
-    shifts = list(mine)
-    theirs = [lax.ppermute(mine[shift], "rep", [(0, 1), (1, 0)]) for shift in shifts]
-    rows = [v[v.shape[0] - part + SLOT_ROW, : nslots + 1] for v in [own] + list(mine.values())]
-    slots = jnp.stack(rows).astype(jnp.int32)
-    products, scales = call(
-        functools.partial(main_body, n_blk, n_col, shifts, part),
-        [like((n, 2 * ITERS * part, tile), BF16), like((8, scn), F32)],
-        [SMEM] + [VMEM] * (2 * n + 1),
-        [slots, limits, blocks, own] + [mine[shift] for shift in shifts] + theirs,
-        scratch=[
-            pltpu.VMEM((n * tile, n * tile), BF16),
-            pltpu.VMEM((FIELDS, part, n * tile), BF16),
-            pltpu.VMEM((tile, scn), F32),
-        ],
+
+    def relay(came, count):
+        return call(functools.partial(relay_body, top, part), [held((size, tile), BF16)] * count, [VMEM], [came])
+
+    def other_core(values):
+        return [lax.ppermute(v, "rep", [(0, 1), (1, 0)]) for v in values]
+
+    def slots_of(values):
+        rows = [v[v.shape[0] - part + SLOT_ROW, : nslots + 1] for v in values]
+        return jnp.stack(rows).astype(jnp.int32)
+
+    early = {(far, 0): move(far_out, far, 0)}
+    for (t, s), out in zip(first_near, near_outs):
+        early[t, s] = move(out, t, s)
+    for t in range(1, far):
+        for s, out in zip(range(1, n_col), relay(early[t, 0], n_col - 1)):
+            early[t, s] = move(out, 0, s)
+    late = {}
+    for (t, s), out in zip(near, relay(early[far, 0], len(near))):
+        late[far + t, s] = move(out, t, s)
+    shifts, mine = list(early), list(early.values())
+    mat, fields, sums = call(
+        functools.partial(early_body, n_blk, n_col, shifts),
+        [held((n * tile, n * tile), BF16), held((FIELDS, part, n * tile), BF16), held((8, scn), F32)],
+        [SMEM, ANY] + [VMEM] * (1 + 2 * len(mine)),
+        [slots_of([own] + mine), *pinned([blocks]), own] + mine + other_core(mine),
+        scratch=[pltpu.VMEM(blocks.shape, BF16), pltpu.SemaphoreType.DMA],
+    )
+    shifts, mine = list(late), list(late.values())
+    products, scales, _, _ = call(
+        functools.partial(main_body, n_blk, n_col, shifts, nslots),
+        [like((n, 2 * ITERS * part, tile), BF16), like((8, scn), F32)]
+        + [held(mat.shape, BF16), held(fields.shape, BF16)],
+        [SMEM] + [VMEM] * (4 + 2 * len(mine)),
+        [slots_of(mine), limits, mat, fields, sums] + mine + other_core(mine),
+        scratch=[pltpu.VMEM((tile, scn), F32)],
         flops=4 * ITERS * n * n * tile * tile * part,
+        aliases={2: 2, 3: 3},
     )
     return call(
         final_body,

time: 43.5 us -> 42.8 us (0.984)
  waiting for transfers between devices: 13.3 us -> 11.5 us
  Pallas kernels: 5.72 us -> 6.58 us
    ppermute x7, waiting for transfers between devices: 1.16 us -> 0.02 us  [other_core(): return [lax.ppermute(v, 'rep', [(0, 1), (1, 0)]) for v in values]]
    pallas_call x4 -> x6, Pallas kernels: 5.72 us -> 6.58 us  [call(): pl.pallas_call(body, out_shape=list(outs), in_specs=in_specs, out_specs=[...]
    ppermute x7, waiting for transfers between devices: 12.1 us -> 11.5 us  [move(): return lax.ppermute(value, ('blk', 'col'), pairs)]
  transfers between devices with their start and end apart: 14 -> 14, of which waited for: 6 -> 5; matrix products, arithmetic and copies ran while one was open for 0% -> 0% of each run, Pallas kernels for 0% -> 4%
where the time goes in v7:
time: 42.8 us; the launch traced here: 42.6 us
  starting transfers between devices  11.5 us (27%)
  waiting for transfers between devices  11.5 us (27%)
  blocking collectives  11.4 us (27%)
  Pallas kernels  6.58 us (15%)
  between operations  1.49 us (3%)
    ppermute x7, waiting for transfers between devices, move(): return lax.ppermute(value, ('blk', 'col'), pairs)  11.5 us
    all_to_all x1, blocking collectives, spread(): return lax.all_to_all(value, ('blk', 'col'), 0, 0, tiled=True)  11.4 us
    ppermute x7, starting transfers between devices, move(): return lax.ppermute(value, ('blk', 'col'), pairs)  11 us
    pallas_call x6, Pallas kernels, call(): pl.pallas_call(body, out_shape=list(outs), in_specs=in_specs, out_specs=[...  6.58 us
  transfers between devices with their start and end apart: 14, of which 5 were waited for; matrix products, arithmetic and copies ran while one was open for 0% of the time, Pallas kernels for 4%

profile of v7, /device:TPU:0, one launch (start us, length us, event | category | flops | bytes accessed | tf_op | source)
XLA Modules:
  0.0 42.6 jit_solution(3530633692433827840)
XLA Ops:
  0.6 0.0 copy-start.5
  1.3 1.5 %shard_map.104 = (bf16[720,128]{1,0:T(8,128)(2,1)S(1)}, bf16[480,128]{1,0:T(8,128)(2,1)S(1)}, bf16[560,128]{1,0:T(8,128)(2,1)S(1)}, bf16[96,128]{1,0:T(8,128)(2,1)S(1)}) custom-call(s32[1,1]{1,0:T(1,128)S(6)} %copy.15.refs_0_, f32[128,128]{1,0:T(8,128)} %cost.1, f32[128,128]{1,0:T(8,128)} %rhs.1, f32[128,128]{1,0:T(8,128)} %upper.1, f32[128,128]{1,0:T(8,128)} %x_in.1, ...), custom_call_target="tpu_custom_call" | custom-call | bytes 999452 | tf_op jit(solution)/shard_map/pallas_call | solution.py:39
  2.8 3.0 %collective-permute-start.4 = (bf16[480,128]{1,0:T(8,128)(2,1)S(1)}, bf16[480,128]{1,0:T(8,128)(2,1)S(1)}, u32[]{:S(2)}, u32[]{:S(2)}) collective-permute-start(bf16[480,128]{1,0:T(8,128)(2,1)S(1)} %get-tuple-element.19), channel_id=1, source_target_pairs={{0,2},{2,0},{4,6},{6,4},{8,10},{10,8},{12,14},{14,12},{1,3},{3,1},... | collective-permute-start | bytes 368648 | tf_op jit(solution)/shard_map/ppermute | solution.py:247
  5.8 1.6 %collective-permute-start.5 = (bf16[560,128]{1,0:T(8,128)(2,1)S(1)}, bf16[560,128]{1,0:T(8,128)(2,1)S(1)}, u32[]{:S(2)}, u32[]{:S(2)}) collective-permute-start(bf16[560,128]{1,0:T(8,128)(2,1)S(1)} %get-tuple-element.20), channel_id=1, source_target_pairs={{0,4},{2,6},{4,0},{6,2},{8,12},{10,14},{12,8},{14,10},{1,5},{3,7},... | collective-permute-start | bytes 430088 | tf_op jit(solution)/shard_map/ppermute | solution.py:247
  7.4 2.6 %collective-permute-start = (bf16[720,128]{1,0:T(8,128)(2,1)S(1)}, bf16[720,128]{1,0:T(8,128)(2,1)S(1)}, u32[]{:S(2)}, u32[]{:S(2)}) collective-permute-start(bf16[720,128]{1,0:T(8,128)(2,1)S(1)} %get-tuple-element.14), channel_id=1, source_target_pairs={{0,8},{2,10},{4,12},{6,14},{8,0},{10,2},{12,4},{14,6},{1,9},{3,11}... | collective-permute-start | bytes 552968 | tf_op jit(solution)/shard_map/ppermute | solution.py:247
  10.0 0.0 collective-permute-done.4.refs_1_
  10.0 0.0 collective-permute-start.8
  10.0 3.3 %collective-permute-done.5.came.refs_2_ = bf16[560,128]{1,0:T(8,128)(2,1)S(1)} collective-permute-done((bf16[560,128]{1,0:T(8,128)(2,1)S(1)}, bf16[560,128]{1,0:T(8,128)(2,1)S(1)}, u32[]{:S(2)}, u32[]{:S(2)}) %collective-permute-start.5) | collective-permute-done | bytes 143392 | tf_op jit(solution)/shard_map/ppermute | solution.py:247
  13.2 0.3 collective-permute-start.6
  13.5 0.0 collective-permute-start.9
  13.5 4.6 %collective-permute-done.came.refs_0_ = bf16[720,128]{1,0:T(8,128)(2,1)S(1)} collective-permute-done((bf16[720,128]{1,0:T(8,128)(2,1)S(1)}, bf16[720,128]{1,0:T(8,128)(2,1)S(1)}, u32[]{:S(2)}, u32[]{:S(2)}) %collective-permute-start) | collective-permute-done | bytes 184352 | tf_op jit(solution)/shard_map/ppermute | solution.py:247
  18.1 0.6 %collective-permute-start.1 = (bf16[480,128]{1,0:T(8,128)(2,1)S(1)}, bf16[480,128]{1,0:T(8,128)(2,1)S(1)}, u32[]{:S(2)}, u32[]{:S(2)}) collective-permute-start(bf16[480,128]{1,0:T(8,128)(2,1)S(1)} %get-tuple-element.15), channel_id=1, source_target_pairs={{0,2},{2,0},{4,6},{6,4},{8,10},{10,8},{12,14},{14,12},{1,3},{3,1},... | collective-permute-start | bytes 368648 | tf_op jit(solution)/shard_map/ppermute | solution.py:247
  18.7 0.0 collective-permute-start.2
  18.7 0.0 collective-permute-done.8.refs_5_
  18.7 3.0 %collective-permute-start.3 = (bf16[480,128]{1,0:T(8,128)(2,1)S(1)}, bf16[480,128]{1,0:T(8,128)(2,1)S(1)}, u32[]{:S(2)}, u32[]{:S(2)}) collective-permute-start(bf16[480,128]{1,0:T(8,128)(2,1)S(1)} %get-tuple-element.17), channel_id=1, source_target_pairs={{0,6},{2,4},{4,2},{6,0},{8,14},{10,12},{12,10},{14,8},{1,7},{3,5},... | collective-permute-start | bytes 368648 | tf_op jit(solution)/shard_map/ppermute | solution.py:247
  21.7 0.0 collective-permute-done.6.refs_3_
  21.7 0.0 collective-permute-start.7
  21.7 0.0 collective-permute-done.9.refs_6_
  21.7 0.5 %collective-permute-start.10 = (bf16[480,128]{1,0:T(8,128)(2,1)S(1)}, bf16[480,128]{1,0:T(8,128)(2,1)S(1)}, u32[]{:S(2)}, u32[]{:S(2)}) collective-permute-start(bf16[480,128]{1,0:T(8,128)(2,1)S(1)} %collective-permute-done.6.refs_3_), channel_id=1, source_target_pairs={{0,1},{1,0},{2,3},{3,2},{4,5},{5,4},{6,7},{7,6},{8,9},{9,8},{10,11... | collective-permute-start | bytes 368648 | tf_op jit(solution)/shard_map/ppermute | solution.py:272
  22.2 0.9 %collective-permute-done.1.refs_0_ = bf16[480,128]{1,0:T(8,128)(2,1)S(1)} collective-permute-done((bf16[480,128]{1,0:T(8,128)(2,1)S(1)}, bf16[480,128]{1,0:T(8,128)(2,1)S(1)}, u32[]{:S(2)}, u32[]{:S(2)}) %collective-permute-start.1) | collective-permute-done | bytes 122912 | tf_op jit(solution)/shard_map/ppermute | solution.py:247
  23.1 0.0 collective-permute-start.11
  23.1 0.5 %collective-permute-done.2.refs_1_ = bf16[480,128]{1,0:T(8,128)(2,1)S(1)} collective-permute-done((bf16[480,128]{1,0:T(8,128)(2,1)S(1)}, bf16[480,128]{1,0:T(8,128)(2,1)S(1)}, u32[]{:S(2)}, u32[]{:S(2)}) %collective-permute-start.2) | collective-permute-done | bytes 122912 | tf_op jit(solution)/shard_map/ppermute | solution.py:247
  23.6 0.0 collective-permute-start.12
  23.6 2.2 %collective-permute-done.3.refs_2_ = bf16[480,128]{1,0:T(8,128)(2,1)S(1)} collective-permute-done((bf16[480,128]{1,0:T(8,128)(2,1)S(1)}, bf16[480,128]{1,0:T(8,128)(2,1)S(1)}, u32[]{:S(2)}, u32[]{:S(2)}) %collective-permute-start.3) | collective-permute-done | bytes 122912 | tf_op jit(solution)/shard_map/ppermute | solution.py:247
  25.9 0.0 collective-permute-start.13
  26.0 0.0 copy-start
  26.0 0.0 copy-start.1
  26.0 0.0 copy-start.2
  26.0 0.0 copy-start.3
  26.1 0.0 copy-start.4
  26.1 0.0 collective-permute-done.7.refs_4_
  26.1 0.0 collective-permute-done.10.refs_7_
  26.1 1.6 %shard_map.107 = (bf16[1024,1024]{1,0:T(8,128)(2,1)S(1)}, bf16[5,16,1024]{2,1,0:T(8,128)(2,1)S(1)}, f32[8,128]{1,0:T(8,128)S(1)}) custom-call(s32[5,7]{1,0:T(8,128)S(1)} %convert_element_type.7.slots, bf16[1,1,6,128,128]{4,3,2,1,0:T(8,128)(2,1)} %blocks_in.1, bf16[96,128]{1,0:T(8,128)(2,1)S(1)} %get-tuple-element.18.own, ...), custom_call_target="tpu_custom_call" | custom-call | bytes 3633292 | tf_op jit(solution)/shard_map/pallas_call | solution.py:39
  27.7 0.0 collective-permute-done.11.refs_3_
  27.7 0.0 collective-permute-done.12.refs_4_
  27.7 0.0 collective-permute-done.13.refs_5_
  27.7 0.0 copy-done.5
  27.7 2.7 %shard_map.108 = (bf16[8,64,128]{2,1,0:T(8,128)(2,1)S(1)}, f32[8,128]{1,0:T(8,128)S(1)}, bf16[1024,1024]{1,0:T(8,128)(2,1)S(1)}, bf16[5,16,1024]{2,1,0:T(8,128)(2,1)S(1)}) custom-call(s32[3,7]{1,0:T(4,128)S(1)} %maximum_convert_fusion.slots, s32[1,128]{1,0:T(1,128)S(1)} %bitcast.1, ...), custom_call_target="tpu_custom_call", output_to_operand_aliasing={{2}: (2, {}), {3}: (3, {})} | custom-call | flops 134217728 | bytes 5399124 | tf_op jit(solution)/shard_map/pallas_call | solution.py:39
  30.4 11.4 %all_to_all.5.recv = bf16[8,64,128]{2,1,0:T(8,128)(2,1)S(1)} all-to-all(bf16[8,64,128]{2,1,0:T(8,128)(2,1)S(1)} %get-tuple-element.24), channel_id=1, replica_groups=mesh['groups'=2,'blk'=4,'col'=2,'rep'=2] {'blk','col'}, dimensions={0} | all-to-all | bytes 262144 | tf_op jit(solution)/shard_map/all_to_all | solution.py:243
  41.8 0.0 copy-done
  41.8 0.0 copy-done.1
  41.8 0.0 copy-done.2
  41.8 0.0 copy-done.3
  41.8 0.0 copy-done.4
  41.8 0.8 %shard_map.109 = (f32[128,128]{1,0:T(8,128)}, f32[128,128]{1,0:T(8,128)}) custom-call(bf16[8,64,128]{2,1,0:T(8,128)(2,1)S(1)} %all_to_all.5.recv, f32[8,128]{1,0:T(8,128)S(1)} %get-tuple-element.25.scales, f32[128,128]{1,0:T(8,128)S(1)} %copy-done, f32[128,128]{1,0:T(8,128)S(1)} %copy-done.1, f32[128,128]{1,0:T(8,128)S(1)} %copy-done.2, ...), custom_call_target="tpu_custom_call" | custom-call | bytes 594432 | tf_op jit(solution)/shard_map/pallas_call | solution.py:39
  (13 shorter events, 0.2 us)
Async XLA Ops:
  0.6 27.1 %copy-start.5 = (s32[128]{0:T(128)S(1)}, s32[128]{0:T(128)}, u32[]{:S(2)}) copy-start(s32[128]{0:T(128)} %param.17) | copy-start | bytes 1540
  2.8 7.2 %collective-permute-start.4 = (bf16[480,128]{1,0:T(8,128)(2,1)S(1)}, bf16[480,128]{1,0:T(8,128)(2,1)S(1)}, u32[]{:S(2)}, u32[]{:S(2)}) collective-permute-start(bf16[480,128]{1,0:T(8,128)(2,1)S(1)} %get-tuple-element.19), channel_id=1, source_target_pairs={{0,2},{2,0},{4,6},{6,4},{8,10},{10,8},{12,14},{14,12},{1,3},{3,1},... | collective-permute-start | bytes 368648 | tf_op jit(solution)/shard_map/ppermute | solution.py:247
  5.8 7.4 %collective-permute-start.5 = (bf16[560,128]{1,0:T(8,128)(2,1)S(1)}, bf16[560,128]{1,0:T(8,128)(2,1)S(1)}, u32[]{:S(2)}, u32[]{:S(2)}) collective-permute-start(bf16[560,128]{1,0:T(8,128)(2,1)S(1)} %get-tuple-element.20), channel_id=1, source_target_pairs={{0,4},{2,6},{4,0},{6,2},{8,12},{10,14},{12,8},{14,10},{1,5},{3,7},... | collective-permute-start | bytes 430088 | tf_op jit(solution)/shard_map/ppermute | solution.py:247
  7.4 10.7 %collective-permute-start = (bf16[720,128]{1,0:T(8,128)(2,1)S(1)}, bf16[720,128]{1,0:T(8,128)(2,1)S(1)}, u32[]{:S(2)}, u32[]{:S(2)}) collective-permute-start(bf16[720,128]{1,0:T(8,128)(2,1)S(1)} %get-tuple-element.14), channel_id=1, source_target_pairs={{0,8},{2,10},{4,12},{6,14},{8,0},{10,2},{12,4},{14,6},{1,9},{3,11}... | collective-permute-start | bytes 552968 | tf_op jit(solution)/shard_map/ppermute | solution.py:247
  10.0 8.8 %collective-permute-start.8 = (bf16[480,128]{1,0:T(8,128)(2,1)S(1)}, bf16[480,128]{1,0:T(8,128)(2,1)S(1)}, u32[]{:S(2)}, u32[]{:S(2)}) collective-permute-start(bf16[480,128]{1,0:T(8,128)(2,1)S(1)} %collective-permute-done.4.refs_1_), channel_id=1, source_target_pairs={{0,1},{1,0},{2,3},{3,2},{4,5},{5,4},{6,7},{7,6},{8,9},{9,8},{10,11... | collective-permute-start | bytes 368648 | tf_op jit(solution)/shard_map/ppermute | solution.py:272
  13.2 8.5 %collective-permute-start.6 = (bf16[480,128]{1,0:T(8,128)(2,1)S(1)}, bf16[480,128]{1,0:T(8,128)(2,1)S(1)}, u32[]{:S(2)}, u32[]{:S(2)}) collective-permute-start(bf16[480,128]{1,0:T(8,128)(2,1)S(1)} %shard_map.106), channel_id=1, source_target_pairs={{0,2},{2,0},{4,6},{6,4},{8,10},{10,8},{12,14},{14,12},{1,3},{3,1},... | collective-permute-start | bytes 368648 | tf_op jit(solution)/shard_map/ppermute | solution.py:247
  13.5 8.2 %collective-permute-start.9 = (bf16[560,128]{1,0:T(8,128)(2,1)S(1)}, bf16[560,128]{1,0:T(8,128)(2,1)S(1)}, u32[]{:S(2)}, u32[]{:S(2)}) collective-permute-start(bf16[560,128]{1,0:T(8,128)(2,1)S(1)} %collective-permute-done.5.came.refs_2_), channel_id=1, source_target_pairs={{0,1},{1,0},{2,3},{3,2},{4,5},{5,4},{6,7},{7,6},{8,9},{9,8},{10,11... | collective-permute-start | bytes 430088 | tf_op jit(solution)/shard_map/ppermute | solution.py:272
  18.1 4.9 %collective-permute-start.1 = (bf16[480,128]{1,0:T(8,128)(2,1)S(1)}, bf16[480,128]{1,0:T(8,128)(2,1)S(1)}, u32[]{:S(2)}, u32[]{:S(2)}) collective-permute-start(bf16[480,128]{1,0:T(8,128)(2,1)S(1)} %get-tuple-element.15), channel_id=1, source_target_pairs={{0,2},{2,0},{4,6},{6,4},{8,10},{10,8},{12,14},{14,12},{1,3},{3,1},... | collective-permute-start | bytes 368648 | tf_op jit(solution)/shard_map/ppermute | solution.py:247
  18.7 4.9 %collective-permute-start.2 = (bf16[480,128]{1,0:T(8,128)(2,1)S(1)}, bf16[480,128]{1,0:T(8,128)(2,1)S(1)}, u32[]{:S(2)}, u32[]{:S(2)}) collective-permute-start(bf16[480,128]{1,0:T(8,128)(2,1)S(1)} %get-tuple-element.16), channel_id=1, source_target_pairs={{0,4},{2,6},{4,0},{6,2},{8,12},{10,14},{12,8},{14,10},{1,5},{3,7},... | collective-permute-start | bytes 368648 | tf_op jit(solution)/shard_map/ppermute | solution.py:247
  18.7 7.1 %collective-permute-start.3 = (bf16[480,128]{1,0:T(8,128)(2,1)S(1)}, bf16[480,128]{1,0:T(8,128)(2,1)S(1)}, u32[]{:S(2)}, u32[]{:S(2)}) collective-permute-start(bf16[480,128]{1,0:T(8,128)(2,1)S(1)} %get-tuple-element.17), channel_id=1, source_target_pairs={{0,6},{2,4},{4,2},{6,0},{8,14},{10,12},{12,10},{14,8},{1,7},{3,5},... | collective-permute-start | bytes 368648 | tf_op jit(solution)/shard_map/ppermute | solution.py:247
  21.7 4.4 %collective-permute-start.7 = (bf16[720,128]{1,0:T(8,128)(2,1)S(1)}, bf16[720,128]{1,0:T(8,128)(2,1)S(1)}, u32[]{:S(2)}, u32[]{:S(2)}) collective-permute-start(bf16[720,128]{1,0:T(8,128)(2,1)S(1)} %collective-permute-done.came.refs_0_), channel_id=1, source_target_pairs={{0,1},{1,0},{2,3},{3,2},{4,5},{5,4},{6,7},{7,6},{8,9},{9,8},{10,11... | collective-permute-start | bytes 552968 | tf_op jit(solution)/shard_map/ppermute | solution.py:272
  21.7 4.4 %collective-permute-start.10 = (bf16[480,128]{1,0:T(8,128)(2,1)S(1)}, bf16[480,128]{1,0:T(8,128)(2,1)S(1)}, u32[]{:S(2)}, u32[]{:S(2)}) collective-permute-start(bf16[480,128]{1,0:T(8,128)(2,1)S(1)} %collective-permute-done.6.refs_3_), channel_id=1, source_target_pairs={{0,1},{1,0},{2,3},{3,2},{4,5},{5,4},{6,7},{7,6},{8,9},{9,8},{10,11... | collective-permute-start | bytes 368648 | tf_op jit(solution)/shard_map/ppermute | solution.py:272
  23.1 4.6 %collective-permute-start.11 = (bf16[480,128]{1,0:T(8,128)(2,1)S(1)}, bf16[480,128]{1,0:T(8,128)(2,1)S(1)}, u32[]{:S(2)}, u32[]{:S(2)}) collective-permute-start(bf16[480,128]{1,0:T(8,128)(2,1)S(1)} %collective-permute-done.1.refs_0_), channel_id=1, source_target_pairs={{0,1},{1,0},{2,3},{3,2},{4,5},{5,4},{6,7},{7,6},{8,9},{9,8},{10,11... | collective-permute-start | bytes 368648 | tf_op jit(solution)/shard_map/ppermute | solution.py:272
  23.6 4.1 %collective-permute-start.12 = (bf16[480,128]{1,0:T(8,128)(2,1)S(1)}, bf16[480,128]{1,0:T(8,128)(2,1)S(1)}, u32[]{:S(2)}, u32[]{:S(2)}) collective-permute-start(bf16[480,128]{1,0:T(8,128)(2,1)S(1)} %collective-permute-done.2.refs_1_), channel_id=1, source_target_pairs={{0,1},{1,0},{2,3},{3,2},{4,5},{5,4},{6,7},{7,6},{8,9},{9,8},{10,11... | collective-permute-start | bytes 368648 | tf_op jit(solution)/shard_map/ppermute | solution.py:272
  25.9 1.9 %collective-permute-start.13 = (bf16[480,128]{1,0:T(8,128)(2,1)S(1)}, bf16[480,128]{1,0:T(8,128)(2,1)S(1)}, u32[]{:S(2)}, u32[]{:S(2)}) collective-permute-start(bf16[480,128]{1,0:T(8,128)(2,1)S(1)} %collective-permute-done.3.refs_2_), channel_id=1, source_target_pairs={{0,1},{1,0},{2,3},{3,2},{4,5},{5,4},{6,7},{7,6},{8,9},{9,8},{10,11... | collective-permute-start | bytes 368648 | tf_op jit(solution)/shard_map/ppermute | solution.py:272
  26.0 15.8 %copy-start = (f32[128,128]{1,0:T(8,128)S(1)}, f32[128,128]{1,0:T(8,128)}, u32[]{:S(2)}) copy-start(f32[128,128]{1,0:T(8,128)} %cost.1) | copy-start | bytes 196612
  26.0 15.8 %copy-start.1 = (f32[128,128]{1,0:T(8,128)S(1)}, f32[128,128]{1,0:T(8,128)}, u32[]{:S(2)}) copy-start(f32[128,128]{1,0:T(8,128)} %rhs.1) | copy-start | bytes 196612
  26.0 15.8 %copy-start.2 = (f32[128,128]{1,0:T(8,128)S(1)}, f32[128,128]{1,0:T(8,128)}, u32[]{:S(2)}) copy-start(f32[128,128]{1,0:T(8,128)} %upper.1) | copy-start | bytes 196612
  26.0 15.7 %copy-start.3 = (f32[128,128]{1,0:T(8,128)S(1)}, f32[128,128]{1,0:T(8,128)}, u32[]{:S(2)}) copy-start(f32[128,128]{1,0:T(8,128)} %x_in.1) | copy-start | bytes 196612
  26.1 15.7 %copy-start.4 = (f32[128,128]{1,0:T(8,128)S(1)}, f32[128,128]{1,0:T(8,128)}, u32[]{:S(2)}) copy-start(f32[128,128]{1,0:T(8,128)} %y_in.1) | copy-start | bytes 196612

commit v8 on v7

--- a/solution.py
+++ b/solution.py
@@ -34,13 +34,13 @@
     return [pltpu.with_memory_space_constraint(v, pltpu.HBM) for v in values]
 
 
-def call(body, outs, in_specs, args, scratch=(), flops=0, limit=32, aliases=None):
+def call(body, outs, in_specs, args, scratch=(), flops=0, limit=32, aliases=None, spec=VMEM):
     nbytes = sum(math.prod(a.shape) * jnp.dtype(a.dtype).itemsize for a in list(args) + list(outs))
     return pl.pallas_call(
         body,
         out_shape=list(outs),
         in_specs=in_specs,
-        out_specs=[VMEM] * len(outs),
+        out_specs=[spec] * len(outs),
         scratch_shapes=list(scratch),
         input_output_aliases=aliases or {},
         compiler_params=pltpu.CompilerParams(vmem_limit_bytes=limit * MIB),
@@ -114,6 +114,10 @@
     own_out[FIELDS * part :, :] = info
 
 
+def touch_body(part, after, out):
+    del part, after, out
+
+
 def relay_body(top, part, came, *outs):
     for m, out in enumerate(outs):
         out[0:top, :] = came[0:top, :]
@@ -265,8 +269,9 @@
         + [pltpu.VMEM((FIELDS, scn, tile), BF16), pltpu.SemaphoreType.DMA((FIELDS + 2,))],
     )
 
-    def relay(came, count):
-        return call(functools.partial(relay_body, top, part), [held((size, tile), BF16)] * count, [VMEM], [came])
+    def relay(came, count, flops=0):
+        outs = [held((size, tile), BF16)] * count
+        return call(functools.partial(relay_body, top, part), outs, [VMEM], [came], flops=flops)
 
     def other_core(values):
         return [lax.ppermute(v, "rep", [(0, 1), (1, 0)]) for v in values]
@@ -282,7 +287,7 @@
         for s, out in zip(range(1, n_col), relay(early[t, 0], n_col - 1)):
             early[t, s] = move(out, 0, s)
     late = {}
-    for (t, s), out in zip(near, relay(early[far, 0], len(near))):
+    for (t, s), out in zip(near, relay(early[far, 0], len(near), flops=10**10)):
         late[far + t, s] = move(out, t, s)
     shifts, mine = list(early), list(early.values())
     mat, fields, sums = call(
@@ -292,6 +297,8 @@
         [slots_of([own] + mine), *pinned([blocks]), own] + mine + other_core(mine),
         scratch=[pltpu.VMEM(blocks.shape, BF16), pltpu.SemaphoreType.DMA],
     )
+    last = near[-1][0] + far, near[-1][1]
+    late[last] = call(touch_body, [held(late[last].shape, BF16)], [ANY, ANY], [late[last], sums], aliases={0: 0}, spec=ANY)[0]
     shifts, mine = list(late), list(late.values())
     products, scales, _, _ = call(
         functools.partial(main_body, n_blk, n_col, shifts, nslots),

time: 42.8 us -> 43.5 us (1.016)
  starting transfers between devices: 11.5 us -> 16.7 us
  waiting for transfers between devices: 11.5 us -> 7.35 us
    ppermute x7, waiting for transfers between devices: 11.5 us -> 6.07 us  [move(): return lax.ppermute(value, ('blk', 'col'), pairs)]
    ppermute x7, starting transfers between devices: 11 us -> 15.6 us  [move(): return lax.ppermute(value, ('blk', 'col'), pairs)]
    ppermute x7, waiting for transfers between devices: 0.02 us -> 1.28 us  [other_core(): return [lax.ppermute(v, 'rep', [(0, 1), (1, 0)]) for v in values]]
    ppermute x7, starting transfers between devices: 0.52 us -> 1.09 us  [other_core(): return [lax.ppermute(v, 'rep', [(0, 1), (1, 0)]) for v in values]]
    pallas_call x6 -> x7, Pallas kernels: 6.58 us -> 6.59 us  [call(): pl.pallas_call(body, out_shape=list(outs), in_specs=in_specs, out_specs=[...]
where the time goes in v8:
time: 43.5 us; the launch traced here: 43.3 us
  starting transfers between devices  16.7 us (38%)
  blocking collectives  11.1 us (26%)
  waiting for transfers between devices  7.35 us (17%)
  Pallas kernels  6.59 us (15%)
  between operations  1.44 us (3%)
    ppermute x7, starting transfers between devices, move(): return lax.ppermute(value, ('blk', 'col'), pairs)  15.6 us
    all_to_all x1, blocking collectives, spread(): return lax.all_to_all(value, ('blk', 'col'), 0, 0, tiled=True)  11.1 us
    pallas_call x7, Pallas kernels, call(): pl.pallas_call(body, out_shape=list(outs), in_specs=in_specs, out_specs=[...  6.59 us
    ppermute x7, waiting for transfers between devices, move(): return lax.ppermute(value, ('blk', 'col'), pairs)  6.07 us
    ppermute x7, waiting for transfers between devices, other_core(): return [lax.ppermute(v, 'rep', [(0, 1), (1, 0)]) for v in values]  1.28 us
    ppermute x7, starting transfers between devices, other_core(): return [lax.ppermute(v, 'rep', [(0, 1), (1, 0)]) for v in values]  1.09 us
  transfers between devices with their start and end apart: 14, of which 5 were waited for; matrix products, arithmetic and copies ran while one was open for 0% of the time, Pallas kernels for 4%

profile of v8, /device:TPU:0, one launch (start us, length us, event | category | flops | bytes accessed | tf_op | source)
XLA Modules:
  0.0 43.3 jit_solution(1973379834687304370)
XLA Ops:
  1.3 1.5 %shard_map.104 = (bf16[720,128]{1,0:T(8,128)(2,1)S(1)}, bf16[480,128]{1,0:T(8,128)(2,1)S(1)}, bf16[560,128]{1,0:T(8,128)(2,1)S(1)}, bf16[96,128]{1,0:T(8,128)(2,1)S(1)}) custom-call(s32[1,1]{1,0:T(1,128)S(6)} %copy.17.refs_0_, f32[128,128]{1,0:T(8,128)} %cost.1, f32[128,128]{1,0:T(8,128)} %rhs.1, f32[128,128]{1,0:T(8,128)} %upper.1, f32[128,128]{1,0:T(8,128)} %x_in.1, ...), custom_call_target="tpu_custom_call" | custom-call | bytes 999452 | tf_op jit(solution)/shard_map/pallas_call | solution.py:39
  2.8 4.1 %collective-permute-start = (bf16[720,128]{1,0:T(8,128)(2,1)S(1)}, bf16[720,128]{1,0:T(8,128)(2,1)S(1)}, u32[]{:S(2)}, u32[]{:S(2)}) collective-permute-start(bf16[720,128]{1,0:T(8,128)(2,1)S(1)} %get-tuple-element.14), channel_id=1, source_target_pairs={{0,8},{2,10},{4,12},{6,14},{8,0},{10,2},{12,4},{14,6},{1,9},{3,11}... | collective-permute-start | bytes 552968 | tf_op jit(solution)/shard_map/ppermute | solution.py:251
  6.9 1.6 %collective-permute-start.5 = (bf16[560,128]{1,0:T(8,128)(2,1)S(1)}, bf16[560,128]{1,0:T(8,128)(2,1)S(1)}, u32[]{:S(2)}, u32[]{:S(2)}) collective-permute-start(bf16[560,128]{1,0:T(8,128)(2,1)S(1)} %get-tuple-element.20), channel_id=1, source_target_pairs={{0,4},{2,6},{4,0},{6,2},{8,12},{10,14},{12,8},{14,10},{1,5},{3,7},... | collective-permute-start | bytes 430088 | tf_op jit(solution)/shard_map/ppermute | solution.py:251
  8.4 1.5 %collective-permute-start.4 = (bf16[480,128]{1,0:T(8,128)(2,1)S(1)}, bf16[480,128]{1,0:T(8,128)(2,1)S(1)}, u32[]{:S(2)}, u32[]{:S(2)}) collective-permute-start(bf16[480,128]{1,0:T(8,128)(2,1)S(1)} %get-tuple-element.19), channel_id=1, source_target_pairs={{0,2},{2,0},{4,6},{6,4},{8,10},{10,8},{12,14},{14,12},{1,3},{3,1},... | collective-permute-start | bytes 368648 | tf_op jit(solution)/shard_map/ppermute | solution.py:251
  9.9 3.4 %collective-permute-done.4.refs_1_ = bf16[480,128]{1,0:T(8,128)(2,1)S(1)} collective-permute-done((bf16[480,128]{1,0:T(8,128)(2,1)S(1)}, bf16[480,128]{1,0:T(8,128)(2,1)S(1)}, u32[]{:S(2)}, u32[]{:S(2)}) %collective-permute-start.4) | collective-permute-done | bytes 122912 | tf_op jit(solution)/shard_map/ppermute | solution.py:251
  13.3 0.0 collective-permute-start.8
  13.3 0.6 %collective-permute-done.5.came.refs_2_ = bf16[560,128]{1,0:T(8,128)(2,1)S(1)} collective-permute-done((bf16[560,128]{1,0:T(8,128)(2,1)S(1)}, bf16[560,128]{1,0:T(8,128)(2,1)S(1)}, u32[]{:S(2)}, u32[]{:S(2)}) %collective-permute-start.5) | collective-permute-done | bytes 143392 | tf_op jit(solution)/shard_map/ppermute | solution.py:251
  13.9 0.0 copy-start.5
  13.9 1.6 %collective-permute-start.6 = (bf16[480,128]{1,0:T(8,128)(2,1)S(1)}, bf16[480,128]{1,0:T(8,128)(2,1)S(1)}, u32[]{:S(2)}, u32[]{:S(2)}) collective-permute-start(bf16[480,128]{1,0:T(8,128)(2,1)S(1)} %shard_map.106), channel_id=1, source_target_pairs={{0,2},{2,0},{4,6},{6,4},{8,10},{10,8},{12,14},{14,12},{1,3},{3,1},... | collective-permute-start | bytes 368648 | tf_op jit(solution)/shard_map/ppermute | solution.py:251
  15.5 0.0 collective-permute-start.9
  15.5 0.0 collective-permute-done.came.refs_0_
  15.5 0.5 %collective-permute-start.7 = (bf16[720,128]{1,0:T(8,128)(2,1)S(1)}, bf16[720,128]{1,0:T(8,128)(2,1)S(1)}, u32[]{:S(2)}, u32[]{:S(2)}) collective-permute-start(bf16[720,128]{1,0:T(8,128)(2,1)S(1)} %collective-permute-done.came.refs_0_), channel_id=1, source_target_pairs={{0,1},{1,0},{2,3},{3,2},{4,5},{5,4},{6,7},{7,6},{8,9},{9,8},{10,11... | collective-permute-start | bytes 552968 | tf_op jit(solution)/shard_map/ppermute | solution.py:277
  16.0 1.1 %collective-permute-start.1 = (bf16[480,128]{1,0:T(8,128)(2,1)S(1)}, bf16[480,128]{1,0:T(8,128)(2,1)S(1)}, u32[]{:S(2)}, u32[]{:S(2)}) collective-permute-start(bf16[480,128]{1,0:T(8,128)(2,1)S(1)} %get-tuple-element.15), channel_id=1, source_target_pairs={{0,2},{2,0},{4,6},{6,4},{8,10},{10,8},{12,14},{14,12},{1,3},{3,1},... | collective-permute-start | bytes 368648 | tf_op jit(solution)/shard_map/ppermute | solution.py:251
  17.1 0.0 collective-permute-done.8.refs_5_
  17.1 2.0 %collective-permute-start.2 = (bf16[480,128]{1,0:T(8,128)(2,1)S(1)}, bf16[480,128]{1,0:T(8,128)(2,1)S(1)}, u32[]{:S(2)}, u32[]{:S(2)}) collective-permute-start(bf16[480,128]{1,0:T(8,128)(2,1)S(1)} %get-tuple-element.16), channel_id=1, source_target_pairs={{0,4},{2,6},{4,0},{6,2},{8,12},{10,14},{12,8},{14,10},{1,5},{3,7},... | collective-permute-start | bytes 368648 | tf_op jit(solution)/shard_map/ppermute | solution.py:251
  19.1 0.5 %collective-permute-done.6.refs_3_ = bf16[480,128]{1,0:T(8,128)(2,1)S(1)} collective-permute-done((bf16[480,128]{1,0:T(8,128)(2,1)S(1)}, bf16[480,128]{1,0:T(8,128)(2,1)S(1)}, u32[]{:S(2)}, u32[]{:S(2)}) %collective-permute-start.6) | collective-permute-done | bytes 122912 | tf_op jit(solution)/shard_map/ppermute | solution.py:251
  19.6 0.0 collective-permute-start.10
  19.6 0.0 collective-permute-done.9.refs_6_
  19.6 3.8 %collective-permute-start.3 = (bf16[480,128]{1,0:T(8,128)(2,1)S(1)}, bf16[480,128]{1,0:T(8,128)(2,1)S(1)}, u32[]{:S(2)}, u32[]{:S(2)}) collective-permute-start(bf16[480,128]{1,0:T(8,128)(2,1)S(1)} %get-tuple-element.17), channel_id=1, source_target_pairs={{0,6},{2,4},{4,2},{6,0},{8,14},{10,12},{12,10},{14,8},{1,7},{3,5},... | collective-permute-start | bytes 368648 | tf_op jit(solution)/shard_map/ppermute | solution.py:251
  23.5 0.0 collective-permute-done.1.refs_0_
  23.5 0.3 collective-permute-start.11
  23.8 0.0 collective-permute-done.2.refs_1_
  23.8 0.3 collective-permute-start.12
  24.1 0.0 collective-permute-done.7.refs_4_
  24.1 0.0 collective-permute-done.10.refs_7_
  24.1 1.6 %shard_map.107 = (bf16[1024,1024]{1,0:T(8,128)(2,1)S(1)}, bf16[5,16,1024]{2,1,0:T(8,128)(2,1)S(1)}, f32[8,128]{1,0:T(8,128)S(1)}) custom-call(s32[5,7]{1,0:T(8,128)S(1)} %convert_element_type.6.slots, bf16[1,1,6,128,128]{4,3,2,1,0:T(8,128)(2,1)} %blocks_in.1, bf16[96,128]{1,0:T(8,128)(2,1)S(1)} %get-tuple-element.18.own, ...), custom_call_target="tpu_custom_call" | custom-call | bytes 3633292 | tf_op jit(solution)/shard_map/pallas_call | solution.py:39
  25.7 0.0 copy-start
  25.7 0.0 copy-start.1
  25.7 0.0 copy-start.2
  25.7 0.0 copy-start.3
  25.7 0.0 copy-start.4
  25.8 1.6 %collective-permute-done.3.part = bf16[480,128]{1,0:T(8,128)(2,1)S(1)} collective-permute-done((bf16[480,128]{1,0:T(8,128)(2,1)S(1)}, bf16[480,128]{1,0:T(8,128)(2,1)S(1)}, u32[]{:S(2)}, u32[]{:S(2)}) %collective-permute-start.3) | collective-permute-done | bytes 122912 | tf_op jit(solution)/shard_map/ppermute | solution.py:251
  27.4 0.0 collective-permute-start.13
  27.4 0.0 collective-permute-done.11.refs_3_
  27.4 0.0 collective-permute-done.12.refs_4_
  27.5 1.3 %collective-permute-done.13.refs_5_ = bf16[480,128]{1,0:T(8,128)(2,1)S(1)} collective-permute-done((bf16[480,128]{1,0:T(8,128)(2,1)S(1)}, bf16[480,128]{1,0:T(8,128)(2,1)S(1)}, u32[]{:S(2)}, u32[]{:S(2)}) %collective-permute-start.13) | collective-permute-done | bytes 122912 | tf_op jit(solution)/shard_map/ppermute | solution.py:277
  28.7 0.0 copy-done.5
  28.7 2.7 %shard_map.109 = (bf16[8,64,128]{2,1,0:T(8,128)(2,1)S(1)}, f32[8,128]{1,0:T(8,128)S(1)}, bf16[1024,1024]{1,0:T(8,128)(2,1)S(1)}, bf16[5,16,1024]{2,1,0:T(8,128)(2,1)S(1)}) custom-call(s32[3,7]{1,0:T(4,128)S(1)} %maximum_convert_fusion.slots, s32[1,128]{1,0:T(1,128)S(1)} %bitcast.1, ...), custom_call_target="tpu_custom_call", output_to_operand_aliasing={{2}: (2, {}), {3}: (3, {})} | custom-call | flops 134217728 | bytes 5399124 | tf_op jit(solution)/shard_map/pallas_call | solution.py:39
  31.4 11.1 %all_to_all.5.recv = bf16[8,64,128]{2,1,0:T(8,128)(2,1)S(1)} all-to-all(bf16[8,64,128]{2,1,0:T(8,128)(2,1)S(1)} %get-tuple-element.24), channel_id=1, replica_groups=mesh['groups'=2,'blk'=4,'col'=2,'rep'=2] {'blk','col'}, dimensions={0} | all-to-all | bytes 262144 | tf_op jit(solution)/shard_map/all_to_all | solution.py:247
  42.5 0.0 copy-done
  42.5 0.0 copy-done.1
  42.5 0.0 copy-done.2
  42.5 0.0 copy-done.3
  42.5 0.0 copy-done.4
  42.5 0.8 %shard_map.110 = (f32[128,128]{1,0:T(8,128)}, f32[128,128]{1,0:T(8,128)}) custom-call(bf16[8,64,128]{2,1,0:T(8,128)(2,1)S(1)} %all_to_all.5.recv, f32[8,128]{1,0:T(8,128)S(1)} %get-tuple-element.25.scales, f32[128,128]{1,0:T(8,128)S(1)} %copy-done, f32[128,128]{1,0:T(8,128)S(1)} %copy-done.1, f32[128,128]{1,0:T(8,128)S(1)} %copy-done.2, ...), custom_call_target="tpu_custom_call" | custom-call | bytes 594432 | tf_op jit(solution)/shard_map/pallas_call | solution.py:39
  (14 shorter events, 0.2 us)
Async XLA Ops:
  2.8 12.7 %collective-permute-start = (bf16[720,128]{1,0:T(8,128)(2,1)S(1)}, bf16[720,128]{1,0:T(8,128)(2,1)S(1)}, u32[]{:S(2)}, u32[]{:S(2)}) collective-permute-start(bf16[720,128]{1,0:T(8,128)(2,1)S(1)} %get-tuple-element.14), channel_id=1, source_target_pairs={{0,8},{2,10},{4,12},{6,14},{8,0},{10,2},{12,4},{14,6},{1,9},{3,11}... | collective-permute-start | bytes 552968 | tf_op jit(solution)/shard_map/ppermute | solution.py:251
  6.9 7.0 %collective-permute-start.5 = (bf16[560,128]{1,0:T(8,128)(2,1)S(1)}, bf16[560,128]{1,0:T(8,128)(2,1)S(1)}, u32[]{:S(2)}, u32[]{:S(2)}) collective-permute-start(bf16[560,128]{1,0:T(8,128)(2,1)S(1)} %get-tuple-element.20), channel_id=1, source_target_pairs={{0,4},{2,6},{4,0},{6,2},{8,12},{10,14},{12,8},{14,10},{1,5},{3,7},... | collective-permute-start | bytes 430088 | tf_op jit(solution)/shard_map/ppermute | solution.py:251
  8.4 4.9 %collective-permute-start.4 = (bf16[480,128]{1,0:T(8,128)(2,1)S(1)}, bf16[480,128]{1,0:T(8,128)(2,1)S(1)}, u32[]{:S(2)}, u32[]{:S(2)}) collective-permute-start(bf16[480,128]{1,0:T(8,128)(2,1)S(1)} %get-tuple-element.19), channel_id=1, source_target_pairs={{0,2},{2,0},{4,6},{6,4},{8,10},{10,8},{12,14},{14,12},{1,3},{3,1},... | collective-permute-start | bytes 368648 | tf_op jit(solution)/shard_map/ppermute | solution.py:251
  13.3 3.8 %collective-permute-start.8 = (bf16[480,128]{1,0:T(8,128)(2,1)S(1)}, bf16[480,128]{1,0:T(8,128)(2,1)S(1)}, u32[]{:S(2)}, u32[]{:S(2)}) collective-permute-start(bf16[480,128]{1,0:T(8,128)(2,1)S(1)} %collective-permute-done.4.refs_1_), channel_id=1, source_target_pairs={{0,1},{1,0},{2,3},{3,2},{4,5},{5,4},{6,7},{7,6},{8,9},{9,8},{10,11... | collective-permute-start | bytes 368648 | tf_op jit(solution)/shard_map/ppermute | solution.py:277
  13.9 14.8 %copy-start.5 = (s32[128]{0:T(128)S(1)}, s32[128]{0:T(128)}, u32[]{:S(2)}) copy-start(s32[128]{0:T(128)} %param.17) | copy-start | bytes 1540
  13.9 5.7 %collective-permute-start.6 = (bf16[480,128]{1,0:T(8,128)(2,1)S(1)}, bf16[480,128]{1,0:T(8,128)(2,1)S(1)}, u32[]{:S(2)}, u32[]{:S(2)}) collective-permute-start(bf16[480,128]{1,0:T(8,128)(2,1)S(1)} %shard_map.106), channel_id=1, source_target_pairs={{0,2},{2,0},{4,6},{6,4},{8,10},{10,8},{12,14},{14,12},{1,3},{3,1},... | collective-permute-start | bytes 368648 | tf_op jit(solution)/shard_map/ppermute | solution.py:251
  15.5 4.2 %collective-permute-start.9 = (bf16[560,128]{1,0:T(8,128)(2,1)S(1)}, bf16[560,128]{1,0:T(8,128)(2,1)S(1)}, u32[]{:S(2)}, u32[]{:S(2)}) collective-permute-start(bf16[560,128]{1,0:T(8,128)(2,1)S(1)} %collective-permute-done.5.came.refs_2_), channel_id=1, source_target_pairs={{0,1},{1,0},{2,3},{3,2},{4,5},{5,4},{6,7},{7,6},{8,9},{9,8},{10,11... | collective-permute-start | bytes 430088 | tf_op jit(solution)/shard_map/ppermute | solution.py:277
  15.5 8.6 %collective-permute-start.7 = (bf16[720,128]{1,0:T(8,128)(2,1)S(1)}, bf16[720,128]{1,0:T(8,128)(2,1)S(1)}, u32[]{:S(2)}, u32[]{:S(2)}) collective-permute-start(bf16[720,128]{1,0:T(8,128)(2,1)S(1)} %collective-permute-done.came.refs_0_), channel_id=1, source_target_pairs={{0,1},{1,0},{2,3},{3,2},{4,5},{5,4},{6,7},{7,6},{8,9},{9,8},{10,11... | collective-permute-start | bytes 552968 | tf_op jit(solution)/shard_map/ppermute | solution.py:277
  16.0 7.5 %collective-permute-start.1 = (bf16[480,128]{1,0:T(8,128)(2,1)S(1)}, bf16[480,128]{1,0:T(8,128)(2,1)S(1)}, u32[]{:S(2)}, u32[]{:S(2)}) collective-permute-start(bf16[480,128]{1,0:T(8,128)(2,1)S(1)} %get-tuple-element.15), channel_id=1, source_target_pairs={{0,2},{2,0},{4,6},{6,4},{8,10},{10,8},{12,14},{14,12},{1,3},{3,1},... | collective-permute-start | bytes 368648 | tf_op jit(solution)/shard_map/ppermute | solution.py:251
  17.1 6.7 %collective-permute-start.2 = (bf16[480,128]{1,0:T(8,128)(2,1)S(1)}, bf16[480,128]{1,0:T(8,128)(2,1)S(1)}, u32[]{:S(2)}, u32[]{:S(2)}) collective-permute-start(bf16[480,128]{1,0:T(8,128)(2,1)S(1)} %get-tuple-element.16), channel_id=1, source_target_pairs={{0,4},{2,6},{4,0},{6,2},{8,12},{10,14},{12,8},{14,10},{1,5},{3,7},... | collective-permute-start | bytes 368648 | tf_op jit(solution)/shard_map/ppermute | solution.py:251
  19.6 4.5 %collective-permute-start.10 = (bf16[480,128]{1,0:T(8,128)(2,1)S(1)}, bf16[480,128]{1,0:T(8,128)(2,1)S(1)}, u32[]{:S(2)}, u32[]{:S(2)}) collective-permute-start(bf16[480,128]{1,0:T(8,128)(2,1)S(1)} %collective-permute-done.6.refs_3_), channel_id=1, source_target_pairs={{0,1},{1,0},{2,3},{3,2},{4,5},{5,4},{6,7},{7,6},{8,9},{9,8},{10,11... | collective-permute-start | bytes 368648 | tf_op jit(solution)/shard_map/ppermute | solution.py:277
  19.6 7.8 %collective-permute-start.3 = (bf16[480,128]{1,0:T(8,128)(2,1)S(1)}, bf16[480,128]{1,0:T(8,128)(2,1)S(1)}, u32[]{:S(2)}, u32[]{:S(2)}) collective-permute-start(bf16[480,128]{1,0:T(8,128)(2,1)S(1)} %get-tuple-element.17), channel_id=1, source_target_pairs={{0,6},{2,4},{4,2},{6,0},{8,14},{10,12},{12,10},{14,8},{1,7},{3,5},... | collective-permute-start | bytes 368648 | tf_op jit(solution)/shard_map/ppermute | solution.py:251
  23.5 4.0 %collective-permute-start.11 = (bf16[480,128]{1,0:T(8,128)(2,1)S(1)}, bf16[480,128]{1,0:T(8,128)(2,1)S(1)}, u32[]{:S(2)}, u32[]{:S(2)}) collective-permute-start(bf16[480,128]{1,0:T(8,128)(2,1)S(1)} %collective-permute-done.1.refs_0_), channel_id=1, source_target_pairs={{0,1},{1,0},{2,3},{3,2},{4,5},{5,4},{6,7},{7,6},{8,9},{9,8},{10,11... | collective-permute-start | bytes 368648 | tf_op jit(solution)/shard_map/ppermute | solution.py:277
  23.8 3.7 %collective-permute-start.12 = (bf16[480,128]{1,0:T(8,128)(2,1)S(1)}, bf16[480,128]{1,0:T(8,128)(2,1)S(1)}, u32[]{:S(2)}, u32[]{:S(2)}) collective-permute-start(bf16[480,128]{1,0:T(8,128)(2,1)S(1)} %collective-permute-done.2.refs_1_), channel_id=1, source_target_pairs={{0,1},{1,0},{2,3},{3,2},{4,5},{5,4},{6,7},{7,6},{8,9},{9,8},{10,11... | collective-permute-start | bytes 368648 | tf_op jit(solution)/shard_map/ppermute | solution.py:277
  25.7 16.8 %copy-start = (f32[128,128]{1,0:T(8,128)S(1)}, f32[128,128]{1,0:T(8,128)}, u32[]{:S(2)}) copy-start(f32[128,128]{1,0:T(8,128)} %cost.1) | copy-start | bytes 196612
  25.7 16.8 %copy-start.1 = (f32[128,128]{1,0:T(8,128)S(1)}, f32[128,128]{1,0:T(8,128)}, u32[]{:S(2)}) copy-start(f32[128,128]{1,0:T(8,128)} %rhs.1) | copy-start | bytes 196612
  25.7 16.7 %copy-start.2 = (f32[128,128]{1,0:T(8,128)S(1)}, f32[128,128]{1,0:T(8,128)}, u32[]{:S(2)}) copy-start(f32[128,128]{1,0:T(8,128)} %upper.1) | copy-start | bytes 196612
  25.7 16.7 %copy-start.3 = (f32[128,128]{1,0:T(8,128)S(1)}, f32[128,128]{1,0:T(8,128)}, u32[]{:S(2)}) copy-start(f32[128,128]{1,0:T(8,128)} %x_in.1) | copy-start | bytes 196612
  25.7 16.7 %copy-start.4 = (f32[128,128]{1,0:T(8,128)S(1)}, f32[128,128]{1,0:T(8,128)}, u32[]{:S(2)}) copy-start(f32[128,128]{1,0:T(8,128)} %y_in.1) | copy-start | bytes 196612
  27.4 1.3 %collective-permute-start.13 = (bf16[480,128]{1,0:T(8,128)(2,1)S(1)}, bf16[480,128]{1,0:T(8,128)(2,1)S(1)}, u32[]{:S(2)}, u32[]{:S(2)}) collective-permute-start(bf16[480,128]{1,0:T(8,128)(2,1)S(1)} %shard_map.108.refs_2_), channel_id=1, source_target_pairs={{0,1},{1,0},{2,3},{3,2},{4,5},{5,4},{6,7},{7,6},{8,9},{9,8},{10,11... | collective-permute-start | bytes 368648 | tf_op jit(solution)/shard_map/ppermute | solution.py:277

commit v9 on v8

--- a/solution.py
+++ b/solution.py
@@ -126,6 +126,12 @@
         out[top + FIELDS * part :, :] = came[came.shape[0] - part :, :]
 
 
+def pack_body(top, *refs):
+    *parts, out = refs
+    for k, part in enumerate(parts):
+        out[k * top : (k + 1) * top, :] = part[0:top, :]
+
+
 def place(n_blk, n_col, mat, slots, source, shift, slot, block, nslots):
     tile = block.shape[-1]
     blk, col = lax.axis_index("blk") ^ shift[0], lax.axis_index("col") ^ shift[1]
@@ -138,13 +144,13 @@
         mat[pl.ds(row, tile), pl.ds(column, tile)] = block[...]
 
 
-def place_shares(n_blk, n_col, mat, slots, source, shift, own_part, other_part, nslots):
+def place_shares(n_blk, n_col, mat, slots, source, shift, own_part, other_parts, at, nslots):
     half = nslots // 2
     tile = own_part.shape[1]
     core = lax.axis_index("rep")
-    for part, which in ((own_part, core), (other_part, 1 - core)):
+    for part, start, which in ((own_part, 0, core), (other_parts, at * half * tile, 1 - core)):
         for k in range(half):
-            block = part.at[k * tile : (k + 1) * tile, :]
+            block = part.at[start + k * tile : start + (k + 1) * tile, :]
             place(n_blk, n_col, mat, slots, source, shift, which * half + k, block, nslots)
 
 
@@ -164,16 +170,16 @@
 
 def early_body(n_blk, n_col, shifts, slots, blocks_in, own, *refs):
     count = len(shifts)
-    mine, theirs = refs[:count], refs[count : 2 * count]
-    mat, fields, sums_out, blocks, sem = refs[2 * count :]
+    mine, theirs = refs[:count], refs[count]
+    mat, fields, sums_out, blocks, sem = refs[count + 1 :]
     copy = pltpu.make_async_copy(blocks_in, blocks, sem)
     copy.start()
     nslots = blocks.shape[2]
     mat[...] = jnp.zeros(mat.shape, BF16)
     fields[...] = jnp.zeros(fields.shape, BF16)
     sums = take(n_col, fields, (0, 0), own, 0)
-    for m, (shift, own_part, other_part) in enumerate(zip(shifts, mine, theirs)):
-        place_shares(n_blk, n_col, mat, slots, m + 1, shift, own_part, other_part, nslots)
+    for m, (shift, own_part) in enumerate(zip(shifts, mine)):
+        place_shares(n_blk, n_col, mat, slots, m + 1, shift, own_part, theirs, m, nslots)
         more = take(n_col, fields, shift, own_part, nslots // 2 * own_part.shape[1])
         sums = [a + b for a, b in zip(sums, more)]
     copy.wait()
@@ -191,7 +197,7 @@
     me_b, me_c = lax.axis_index("blk"), lax.axis_index("col")
     sums = [sums_in[0:1, :], sums_in[1:2, :]]
     for m, (shift, own_part, other_part) in enumerate(zip(shifts, mine, theirs)):
-        place_shares(n_blk, n_col, mat, slots, m, shift, own_part, other_part, nslots)
+        place_shares(n_blk, n_col, mat, slots, m, shift, own_part, other_part, 0, nslots)
         more = take(n_col, fields, shift, own_part, nslots // 2 * tile)
         sums = [a + b for a, b in zip(sums, more)]
     cost, rhs, upper, primal, dual = (fields[j].astype(F32) for j in range(FIELDS))
@@ -283,18 +289,20 @@
     early = {(far, 0): move(far_out, far, 0)}
     for (t, s), out in zip(first_near, near_outs):
         early[t, s] = move(out, t, s)
+    late = {}
     for t in range(1, far):
         for s, out in zip(range(1, n_col), relay(early[t, 0], n_col - 1)):
-            early[t, s] = move(out, 0, s)
-    late = {}
+            late[t, s] = move(out, 0, s)
     for (t, s), out in zip(near, relay(early[far, 0], len(near), flops=10**10)):
         late[far + t, s] = move(out, t, s)
     shifts, mine = list(early), list(early.values())
+    packed_shape = held((len(mine) * top, tile), BF16)
+    (packed,) = call(functools.partial(pack_body, top), [packed_shape], [VMEM] * len(mine), mine)
     mat, fields, sums = call(
         functools.partial(early_body, n_blk, n_col, shifts),
         [held((n * tile, n * tile), BF16), held((FIELDS, part, n * tile), BF16), held((8, scn), F32)],
-        [SMEM, ANY] + [VMEM] * (1 + 2 * len(mine)),
-        [slots_of([own] + mine), *pinned([blocks]), own] + mine + other_core(mine),
+        [SMEM, ANY] + [VMEM] * (2 + len(mine)),
+        [slots_of([own] + mine), *pinned([blocks]), own] + mine + other_core([packed]),
         scratch=[pltpu.VMEM(blocks.shape, BF16), pltpu.SemaphoreType.DMA],
     )
     last = near[-1][0] + far, near[-1][1]

time: 43.5 us -> 43.3 us (level)
  starting transfers between devices: 16.7 us -> 12.9 us
  waiting for transfers between devices: 7.35 us -> 9.73 us
  blocking collectives: 11.1 us -> 12.1 us
    ppermute x7, starting transfers between devices: 15.6 us -> 12.7 us  [move(): return lax.ppermute(value, ('blk', 'col'), pairs)]
    ppermute x7, waiting for transfers between devices: 6.07 us -> 8.48 us  [move(): return lax.ppermute(value, ('blk', 'col'), pairs)]
    all_to_all x1, blocking collectives: 11.1 us -> 12.1 us  [spread(): return lax.all_to_all(value, ('blk', 'col'), 0, 0, tiled=True)]
    ppermute x7 -> x5, starting transfers between devices: 1.09 us -> 0.15 us  [other_core(): return [lax.ppermute(v, 'rep', [(0, 1), (1, 0)]) for v in values]]
    pallas_call x7 -> x8, Pallas kernels: 6.59 us -> 6.68 us  [call(): pl.pallas_call(body, out_shape=list(outs), in_specs=in_specs, out_specs=[...]
    ppermute x7 -> x5, waiting for transfers between devices: 1.28 us -> 1.25 us  [other_core(): return [lax.ppermute(v, 'rep', [(0, 1), (1, 0)]) for v in values]]
  transfers between devices with their start and end apart: 14 -> 12, of which waited for: 5 -> 5; matrix products, arithmetic and copies ran while one was open for 0% -> 0% of each run, Pallas kernels for 4% -> 4%
where the time goes in v9:
time: 43.3 us; the launch traced here: 43 us
  starting transfers between devices  12.9 us (30%)
  blocking collectives  12.1 us (28%)
  waiting for transfers between devices  9.73 us (22%)
  Pallas kernels  6.68 us (15%)
  between operations  1.48 us (3%)
    ppermute x7, starting transfers between devices, move(): return lax.ppermute(value, ('blk', 'col'), pairs)  12.7 us
    all_to_all x1, blocking collectives, spread(): return lax.all_to_all(value, ('blk', 'col'), 0, 0, tiled=True)  12.1 us
    ppermute x7, waiting for transfers between devices, move(): return lax.ppermute(value, ('blk', 'col'), pairs)  8.48 us
    pallas_call x8, Pallas kernels, call(): pl.pallas_call(body, out_shape=list(outs), in_specs=in_specs, out_specs=[...  6.68 us
    ppermute x5, waiting for transfers between devices, other_core(): return [lax.ppermute(v, 'rep', [(0, 1), (1, 0)]) for v in values]  1.25 us
  transfers between devices with their start and end apart: 12, of which 5 were waited for; matrix products, arithmetic and copies ran while one was open for 0% of the time, Pallas kernels for 4%

profile of v9, /device:TPU:0, one launch (start us, length us, event | category | flops | bytes accessed | tf_op | source)
XLA Modules:
  0.0 43.0 jit_solution(2875897024503269255)
XLA Ops:
  1.3 1.5 %shard_map.104 = (bf16[720,128]{1,0:T(8,128)(2,1)S(1)}, bf16[480,128]{1,0:T(8,128)(2,1)S(1)}, bf16[560,128]{1,0:T(8,128)(2,1)S(1)}, bf16[96,128]{1,0:T(8,128)(2,1)S(1)}) custom-call(s32[1,1]{1,0:T(1,128)S(6)} %copy.17.refs_0_, f32[128,128]{1,0:T(8,128)} %cost.1, f32[128,128]{1,0:T(8,128)} %rhs.1, f32[128,128]{1,0:T(8,128)} %upper.1, f32[128,128]{1,0:T(8,128)} %x_in.1, ...), custom_call_target="tpu_custom_call" | custom-call | bytes 999452 | tf_op jit(solution)/shard_map/pallas_call | solution.py:39
  2.8 4.1 %collective-permute-start.2 = (bf16[720,128]{1,0:T(8,128)(2,1)S(1)}, bf16[720,128]{1,0:T(8,128)(2,1)S(1)}, u32[]{:S(2)}, u32[]{:S(2)}) collective-permute-start(bf16[720,128]{1,0:T(8,128)(2,1)S(1)} %get-tuple-element.15), channel_id=1, source_target_pairs={{0,8},{2,10},{4,12},{6,14},{8,0},{10,2},{12,4},{14,6},{1,9},{3,11}... | collective-permute-start | bytes 552968 | tf_op jit(solution)/shard_map/ppermute | solution.py:257
  6.9 1.6 %collective-permute-start = (bf16[560,128]{1,0:T(8,128)(2,1)S(1)}, bf16[560,128]{1,0:T(8,128)(2,1)S(1)}, u32[]{:S(2)}, u32[]{:S(2)}) collective-permute-start(bf16[560,128]{1,0:T(8,128)(2,1)S(1)} %get-tuple-element.14), channel_id=1, source_target_pairs={{0,4},{2,6},{4,0},{6,2},{8,12},{10,14},{12,8},{14,10},{1,5},{3,7},... | collective-permute-start | bytes 430088 | tf_op jit(solution)/shard_map/ppermute | solution.py:257
  8.4 1.5 %collective-permute-start.6 = (bf16[480,128]{1,0:T(8,128)(2,1)S(1)}, bf16[480,128]{1,0:T(8,128)(2,1)S(1)}, u32[]{:S(2)}, u32[]{:S(2)}) collective-permute-start(bf16[480,128]{1,0:T(8,128)(2,1)S(1)} %get-tuple-element.20), channel_id=1, source_target_pairs={{0,2},{2,0},{4,6},{6,4},{8,10},{10,8},{12,14},{14,12},{1,3},{3,1},... | collective-permute-start | bytes 368648 | tf_op jit(solution)/shard_map/ppermute | solution.py:257
  9.9 3.9 %collective-permute-done.came.refs_2_ = bf16[560,128]{1,0:T(8,128)(2,1)S(1)} collective-permute-done((bf16[560,128]{1,0:T(8,128)(2,1)S(1)}, bf16[560,128]{1,0:T(8,128)(2,1)S(1)}, u32[]{:S(2)}, u32[]{:S(2)}) %collective-permute-start) | collective-permute-done | bytes 143392 | tf_op jit(solution)/shard_map/ppermute | solution.py:257
  13.9 1.6 %collective-permute-start.1 = (bf16[480,128]{1,0:T(8,128)(2,1)S(1)}, bf16[480,128]{1,0:T(8,128)(2,1)S(1)}, u32[]{:S(2)}, u32[]{:S(2)}) collective-permute-start(bf16[480,128]{1,0:T(8,128)(2,1)S(1)} %shard_map.105), channel_id=1, source_target_pairs={{0,2},{2,0},{4,6},{6,4},{8,10},{10,8},{12,14},{14,12},{1,3},{3,1},... | collective-permute-start | bytes 368648 | tf_op jit(solution)/shard_map/ppermute | solution.py:257
  15.4 0.0 collective-permute-done.6.refs_1_
  15.5 0.0 collective-permute-done.2.came.refs_0_
  15.5 0.0 copy-start.5
  15.5 0.1 collective-permute-start.7
  15.6 1.6 %collective-permute-start.3 = (bf16[480,128]{1,0:T(8,128)(2,1)S(1)}, bf16[480,128]{1,0:T(8,128)(2,1)S(1)}, u32[]{:S(2)}, u32[]{:S(2)}) collective-permute-start(bf16[480,128]{1,0:T(8,128)(2,1)S(1)} %get-tuple-element.16), channel_id=1, source_target_pairs={{0,2},{2,0},{4,6},{6,4},{8,10},{10,8},{12,14},{14,12},{1,3},{3,1},... | collective-permute-start | bytes 368648 | tf_op jit(solution)/shard_map/ppermute | solution.py:257
  17.2 1.5 %collective-permute-start.4 = (bf16[480,128]{1,0:T(8,128)(2,1)S(1)}, bf16[480,128]{1,0:T(8,128)(2,1)S(1)}, u32[]{:S(2)}, u32[]{:S(2)}) collective-permute-start(bf16[480,128]{1,0:T(8,128)(2,1)S(1)} %get-tuple-element.17), channel_id=1, source_target_pairs={{0,4},{2,6},{4,0},{6,2},{8,12},{10,14},{12,8},{14,10},{1,5},{3,7},... | collective-permute-start | bytes 368648 | tf_op jit(solution)/shard_map/ppermute | solution.py:257
  18.7 0.9 %collective-permute-start.5 = (bf16[480,128]{1,0:T(8,128)(2,1)S(1)}, bf16[480,128]{1,0:T(8,128)(2,1)S(1)}, u32[]{:S(2)}, u32[]{:S(2)}) collective-permute-start(bf16[480,128]{1,0:T(8,128)(2,1)S(1)} %get-tuple-element.18), channel_id=1, source_target_pairs={{0,6},{2,4},{4,2},{6,0},{8,14},{10,12},{12,10},{14,8},{1,7},{3,5},... | collective-permute-start | bytes 368648 | tf_op jit(solution)/shard_map/ppermute | solution.py:257
  19.7 0.0 collective-permute-done.1.refs_0_
  19.7 0.1 collective-permute-start.8
  19.8 1.7 %collective-permute-done.3.refs_1_ = bf16[480,128]{1,0:T(8,128)(2,1)S(1)} collective-permute-done((bf16[480,128]{1,0:T(8,128)(2,1)S(1)}, bf16[480,128]{1,0:T(8,128)(2,1)S(1)}, u32[]{:S(2)}, u32[]{:S(2)}) %collective-permute-start.3) | collective-permute-done | bytes 122912 | tf_op jit(solution)/shard_map/ppermute | solution.py:257
  21.5 0.0 collective-permute-start.9
  21.5 1.6 %collective-permute-done.4.refs_2_ = bf16[480,128]{1,0:T(8,128)(2,1)S(1)} collective-permute-done((bf16[480,128]{1,0:T(8,128)(2,1)S(1)}, bf16[480,128]{1,0:T(8,128)(2,1)S(1)}, u32[]{:S(2)}, u32[]{:S(2)}) %collective-permute-start.4) | collective-permute-done | bytes 122912 | tf_op jit(solution)/shard_map/ppermute | solution.py:257
  23.1 0.0 collective-permute-start.10
  23.1 0.0 collective-permute-done.7.refs_3_
  23.1 1.6 %shard_map.108 = (bf16[1024,1024]{1,0:T(8,128)(2,1)S(1)}, bf16[5,16,1024]{2,1,0:T(8,128)(2,1)S(1)}, f32[8,128]{1,0:T(8,128)S(1)}) custom-call(s32[4,7]{1,0:T(4,128)S(1)} %maximum_convert_fusion.slots, bf16[1,1,6,128,128]{4,3,2,1,0:T(8,128)(2,1)} %blocks_in.1, bf16[96,128]{1,0:T(8,128)(2,1)S(1)} %get-tuple-element.19.own, ...), custom_call_target="tpu_custom_call" | custom-call | bytes 3231856 | tf_op jit(solution)/shard_map/pallas_call | solution.py:39
  24.7 0.0 copy-start
  24.7 0.0 copy-start.1
  24.7 0.0 copy-start.2
  24.7 0.0 copy-start.3
  24.8 0.0 copy-start.4
  24.8 1.2 %collective-permute-done.5.part = bf16[480,128]{1,0:T(8,128)(2,1)S(1)} collective-permute-done((bf16[480,128]{1,0:T(8,128)(2,1)S(1)}, bf16[480,128]{1,0:T(8,128)(2,1)S(1)}, u32[]{:S(2)}, u32[]{:S(2)}) %collective-permute-start.5) | collective-permute-done | bytes 122912 | tf_op jit(solution)/shard_map/ppermute | solution.py:257
  26.0 0.0 collective-permute-start.11
  26.0 0.0 collective-permute-done.8.refs_4_
  26.0 0.0 collective-permute-done.9.refs_5_
  26.1 0.0 collective-permute-done.10.refs_6_
  26.1 1.2 %collective-permute-done.11.refs_7_ = bf16[480,128]{1,0:T(8,128)(2,1)S(1)} collective-permute-done((bf16[480,128]{1,0:T(8,128)(2,1)S(1)}, bf16[480,128]{1,0:T(8,128)(2,1)S(1)}, u32[]{:S(2)}, u32[]{:S(2)}) %collective-permute-start.11) | collective-permute-done | bytes 122912 | tf_op jit(solution)/shard_map/ppermute | solution.py:283
  27.3 0.0 copy-done.5
  27.3 2.8 %shard_map.110 = (bf16[8,64,128]{2,1,0:T(8,128)(2,1)S(1)}, f32[8,128]{1,0:T(8,128)S(1)}, bf16[1024,1024]{1,0:T(8,128)(2,1)S(1)}, bf16[5,16,1024]{2,1,0:T(8,128)(2,1)S(1)}) custom-call(s32[4,7]{1,0:T(4,128)S(1)} %maximum_convert_fusion.1.slots, s32[1,128]{1,0:T(1,128)S(1)} %bitcast.1, ...), custom_call_target="tpu_custom_call", output_to_operand_aliasing={{2}: (2, {}), {3}: (3, {})} | custom-call | flops 134217728 | bytes 5644912 | tf_op jit(solution)/shard_map/pallas_call | solution.py:39
  30.1 12.1 %all_to_all.5.recv = bf16[8,64,128]{2,1,0:T(8,128)(2,1)S(1)} all-to-all(bf16[8,64,128]{2,1,0:T(8,128)(2,1)S(1)} %get-tuple-element.24), channel_id=1, replica_groups=mesh['groups'=2,'blk'=4,'col'=2,'rep'=2] {'blk','col'}, dimensions={0} | all-to-all | bytes 262144 | tf_op jit(solution)/shard_map/all_to_all | solution.py:253
  42.2 0.0 copy-done
  42.2 0.0 copy-done.1
  42.2 0.0 copy-done.2
  42.2 0.0 copy-done.3
  42.2 0.0 copy-done.4
  42.3 0.8 %shard_map.111 = (f32[128,128]{1,0:T(8,128)}, f32[128,128]{1,0:T(8,128)}) custom-call(bf16[8,64,128]{2,1,0:T(8,128)(2,1)S(1)} %all_to_all.5.recv, f32[8,128]{1,0:T(8,128)S(1)} %get-tuple-element.25.scales, f32[128,128]{1,0:T(8,128)S(1)} %copy-done, f32[128,128]{1,0:T(8,128)S(1)} %copy-done.1, f32[128,128]{1,0:T(8,128)S(1)} %copy-done.2, ...), custom_call_target="tpu_custom_call" | custom-call | bytes 594432 | tf_op jit(solution)/shard_map/pallas_call | solution.py:39
  (14 shorter events, 0.2 us)
Async XLA Ops:
  2.8 12.7 %collective-permute-start.2 = (bf16[720,128]{1,0:T(8,128)(2,1)S(1)}, bf16[720,128]{1,0:T(8,128)(2,1)S(1)}, u32[]{:S(2)}, u32[]{:S(2)}) collective-permute-start(bf16[720,128]{1,0:T(8,128)(2,1)S(1)} %get-tuple-element.15), channel_id=1, source_target_pairs={{0,8},{2,10},{4,12},{6,14},{8,0},{10,2},{12,4},{14,6},{1,9},{3,11}... | collective-permute-start | bytes 552968 | tf_op jit(solution)/shard_map/ppermute | solution.py:257
  6.9 7.0 %collective-permute-start = (bf16[560,128]{1,0:T(8,128)(2,1)S(1)}, bf16[560,128]{1,0:T(8,128)(2,1)S(1)}, u32[]{:S(2)}, u32[]{:S(2)}) collective-permute-start(bf16[560,128]{1,0:T(8,128)(2,1)S(1)} %get-tuple-element.14), channel_id=1, source_target_pairs={{0,4},{2,6},{4,0},{6,2},{8,12},{10,14},{12,8},{14,10},{1,5},{3,7},... | collective-permute-start | bytes 430088 | tf_op jit(solution)/shard_map/ppermute | solution.py:257
  8.4 7.0 %collective-permute-start.6 = (bf16[480,128]{1,0:T(8,128)(2,1)S(1)}, bf16[480,128]{1,0:T(8,128)(2,1)S(1)}, u32[]{:S(2)}, u32[]{:S(2)}) collective-permute-start(bf16[480,128]{1,0:T(8,128)(2,1)S(1)} %get-tuple-element.20), channel_id=1, source_target_pairs={{0,2},{2,0},{4,6},{6,4},{8,10},{10,8},{12,14},{14,12},{1,3},{3,1},... | collective-permute-start | bytes 368648 | tf_op jit(solution)/shard_map/ppermute | solution.py:257
  13.9 5.8 %collective-permute-start.1 = (bf16[480,128]{1,0:T(8,128)(2,1)S(1)}, bf16[480,128]{1,0:T(8,128)(2,1)S(1)}, u32[]{:S(2)}, u32[]{:S(2)}) collective-permute-start(bf16[480,128]{1,0:T(8,128)(2,1)S(1)} %shard_map.105), channel_id=1, source_target_pairs={{0,2},{2,0},{4,6},{6,4},{8,10},{10,8},{12,14},{14,12},{1,3},{3,1},... | collective-permute-start | bytes 368648 | tf_op jit(solution)/shard_map/ppermute | solution.py:257
  15.5 11.8 %copy-start.5 = (s32[128]{0:T(128)S(1)}, s32[128]{0:T(128)}, u32[]{:S(2)}) copy-start(s32[128]{0:T(128)} %param.17) | copy-start | bytes 1540
  15.5 7.6 %collective-permute-start.7 = (bf16[1152,128]{1,0:T(8,128)(2,1)S(1)}, bf16[1152,128]{1,0:T(8,128)(2,1)S(1)}, u32[]{:S(2)}, u32[]{:S(2)}) collective-permute-start(bf16[1152,128]{1,0:T(8,128)(2,1)S(1)} %shard_map.107), channel_id=1, source_target_pairs={{0,1},{1,0},{2,3},{3,2},{4,5},{5,4},{6,7},{7,6},{8,9},{9,8},{10,11... | collective-permute-start | bytes 884744 | tf_op jit(solution)/shard_map/ppermute | solution.py:283
  15.6 5.8 %collective-permute-start.3 = (bf16[480,128]{1,0:T(8,128)(2,1)S(1)}, bf16[480,128]{1,0:T(8,128)(2,1)S(1)}, u32[]{:S(2)}, u32[]{:S(2)}) collective-permute-start(bf16[480,128]{1,0:T(8,128)(2,1)S(1)} %get-tuple-element.16), channel_id=1, source_target_pairs={{0,2},{2,0},{4,6},{6,4},{8,10},{10,8},{12,14},{14,12},{1,3},{3,1},... | collective-permute-start | bytes 368648 | tf_op jit(solution)/shard_map/ppermute | solution.py:257
  17.2 5.9 %collective-permute-start.4 = (bf16[480,128]{1,0:T(8,128)(2,1)S(1)}, bf16[480,128]{1,0:T(8,128)(2,1)S(1)}, u32[]{:S(2)}, u32[]{:S(2)}) collective-permute-start(bf16[480,128]{1,0:T(8,128)(2,1)S(1)} %get-tuple-element.17), channel_id=1, source_target_pairs={{0,4},{2,6},{4,0},{6,2},{8,12},{10,14},{12,8},{14,10},{1,5},{3,7},... | collective-permute-start | bytes 368648 | tf_op jit(solution)/shard_map/ppermute | solution.py:257
  18.7 7.3 %collective-permute-start.5 = (bf16[480,128]{1,0:T(8,128)(2,1)S(1)}, bf16[480,128]{1,0:T(8,128)(2,1)S(1)}, u32[]{:S(2)}, u32[]{:S(2)}) collective-permute-start(bf16[480,128]{1,0:T(8,128)(2,1)S(1)} %get-tuple-element.18), channel_id=1, source_target_pairs={{0,6},{2,4},{4,2},{6,0},{8,14},{10,12},{12,10},{14,8},{1,7},{3,5},... | collective-permute-start | bytes 368648 | tf_op jit(solution)/shard_map/ppermute | solution.py:257
  19.7 6.3 %collective-permute-start.8 = (bf16[480,128]{1,0:T(8,128)(2,1)S(1)}, bf16[480,128]{1,0:T(8,128)(2,1)S(1)}, u32[]{:S(2)}, u32[]{:S(2)}) collective-permute-start(bf16[480,128]{1,0:T(8,128)(2,1)S(1)} %collective-permute-done.1.refs_0_), channel_id=1, source_target_pairs={{0,1},{1,0},{2,3},{3,2},{4,5},{5,4},{6,7},{7,6},{8,9},{9,8},{10,11... | collective-permute-start | bytes 368648 | tf_op jit(solution)/shard_map/ppermute | solution.py:283
  21.5 4.6 %collective-permute-start.9 = (bf16[480,128]{1,0:T(8,128)(2,1)S(1)}, bf16[480,128]{1,0:T(8,128)(2,1)S(1)}, u32[]{:S(2)}, u32[]{:S(2)}) collective-permute-start(bf16[480,128]{1,0:T(8,128)(2,1)S(1)} %collective-permute-done.3.refs_1_), channel_id=1, source_target_pairs={{0,1},{1,0},{2,3},{3,2},{4,5},{5,4},{6,7},{7,6},{8,9},{9,8},{10,11... | collective-permute-start | bytes 368648 | tf_op jit(solution)/shard_map/ppermute | solution.py:283
  23.1 2.9 %collective-permute-start.10 = (bf16[480,128]{1,0:T(8,128)(2,1)S(1)}, bf16[480,128]{1,0:T(8,128)(2,1)S(1)}, u32[]{:S(2)}, u32[]{:S(2)}) collective-permute-start(bf16[480,128]{1,0:T(8,128)(2,1)S(1)} %collective-permute-done.4.refs_2_), channel_id=1, source_target_pairs={{0,1},{1,0},{2,3},{3,2},{4,5},{5,4},{6,7},{7,6},{8,9},{9,8},{10,11... | collective-permute-start | bytes 368648 | tf_op jit(solution)/shard_map/ppermute | solution.py:283
  24.7 17.5 %copy-start = (f32[128,128]{1,0:T(8,128)S(1)}, f32[128,128]{1,0:T(8,128)}, u32[]{:S(2)}) copy-start(f32[128,128]{1,0:T(8,128)} %cost.1) | copy-start | bytes 196612
  24.7 17.5 %copy-start.1 = (f32[128,128]{1,0:T(8,128)S(1)}, f32[128,128]{1,0:T(8,128)}, u32[]{:S(2)}) copy-start(f32[128,128]{1,0:T(8,128)} %rhs.1) | copy-start | bytes 196612
  24.7 17.5 %copy-start.2 = (f32[128,128]{1,0:T(8,128)S(1)}, f32[128,128]{1,0:T(8,128)}, u32[]{:S(2)}) copy-start(f32[128,128]{1,0:T(8,128)} %upper.1) | copy-start | bytes 196612
  24.7 17.5 %copy-start.3 = (f32[128,128]{1,0:T(8,128)S(1)}, f32[128,128]{1,0:T(8,128)}, u32[]{:S(2)}) copy-start(f32[128,128]{1,0:T(8,128)} %x_in.1) | copy-start | bytes 196612
  24.8 17.5 %copy-start.4 = (f32[128,128]{1,0:T(8,128)S(1)}, f32[128,128]{1,0:T(8,128)}, u32[]{:S(2)}) copy-start(f32[128,128]{1,0:T(8,128)} %y_in.1) | copy-start | bytes 196612
  26.0 1.3 %collective-permute-start.11 = (bf16[480,128]{1,0:T(8,128)(2,1)S(1)}, bf16[480,128]{1,0:T(8,128)(2,1)S(1)}, u32[]{:S(2)}, u32[]{:S(2)}) collective-permute-start(bf16[480,128]{1,0:T(8,128)(2,1)S(1)} %shard_map.109.refs_3_), channel_id=1, source_target_pairs={{0,1},{1,0},{2,3},{3,2},{4,5},{5,4},{6,7},{7,6},{8,9},{9,8},{10,11... | collective-permute-start | bytes 368648 | tf_op jit(solution)/shard_map/ppermute | solution.py:283

commit v10 on v9

--- a/solution.py
+++ b/solution.py
@@ -275,7 +275,7 @@
         + [pltpu.VMEM((FIELDS, scn, tile), BF16), pltpu.SemaphoreType.DMA((FIELDS + 2,))],
     )
 
-    def relay(came, count, flops=0):
+    def relay(came, count, flops):
         outs = [held((size, tile), BF16)] * count
         return call(functools.partial(relay_body, top, part), outs, [VMEM], [came], flops=flops)
 
@@ -291,9 +291,9 @@
         early[t, s] = move(out, t, s)
     late = {}
     for t in range(1, far):
-        for s, out in zip(range(1, n_col), relay(early[t, 0], n_col - 1)):
+        for s, out in zip(range(1, n_col), relay(early[t, 0], n_col - 1, 10**10)):
             late[t, s] = move(out, 0, s)
-    for (t, s), out in zip(near, relay(early[far, 0], len(near), flops=10**10)):
+    for (t, s), out in zip(near, relay(early[far, 0], len(near), 5 * 10**9)):
         late[far + t, s] = move(out, t, s)
     shifts, mine = list(early), list(early.values())
     packed_shape = held((len(mine) * top, tile), BF16)

time: 43.3 us -> 44 us (1.016)
  starting transfers between devices: 12.9 us -> 14.3 us
  blocking collectives: 12.1 us -> 11.1 us
    ppermute x7, starting transfers between devices: 12.7 us -> 14.1 us  [move(): return lax.ppermute(value, ('blk', 'col'), pairs)]
    all_to_all x1, blocking collectives: 12.1 us -> 11.1 us  [spread(): return lax.all_to_all(value, ('blk', 'col'), 0, 0, tiled=True)]
where the time goes in v10:
time: 44 us; the launch traced here: 43.8 us
  starting transfers between devices  14.3 us (32%)
  blocking collectives  11.1 us (25%)
  waiting for transfers between devices  10.1 us (23%)
  Pallas kernels  6.69 us (15%)
  between operations  1.48 us (3%)
    ppermute x7, starting transfers between devices, move(): return lax.ppermute(value, ('blk', 'col'), pairs)  14.1 us
    all_to_all x1, blocking collectives, spread(): return lax.all_to_all(value, ('blk', 'col'), 0, 0, tiled=True)  11.1 us
    ppermute x7, waiting for transfers between devices, move(): return lax.ppermute(value, ('blk', 'col'), pairs)  8.89 us
    pallas_call x8, Pallas kernels, call(): pl.pallas_call(body, out_shape=list(outs), in_specs=in_specs, out_specs=[...  6.69 us
    ppermute x5, waiting for transfers between devices, other_core(): return [lax.ppermute(v, 'rep', [(0, 1), (1, 0)]) for v in values]  1.25 us
  transfers between devices with their start and end apart: 12, of which 5 were waited for; matrix products, arithmetic and copies ran while one was open for 0% of the time, Pallas kernels for 4%

profile of v10, /device:TPU:0, one launch (start us, length us, event | category | flops | bytes accessed | tf_op | source)
XLA Modules:
  0.0 43.8 jit_solution(6220692480669639316)
XLA Ops:
  1.3 1.5 %shard_map.104 = (bf16[720,128]{1,0:T(8,128)(2,1)S(1)}, bf16[480,128]{1,0:T(8,128)(2,1)S(1)}, bf16[560,128]{1,0:T(8,128)(2,1)S(1)}, bf16[96,128]{1,0:T(8,128)(2,1)S(1)}) custom-call(s32[1,1]{1,0:T(1,128)S(6)} %copy.17.refs_0_, f32[128,128]{1,0:T(8,128)} %cost.1, f32[128,128]{1,0:T(8,128)} %rhs.1, f32[128,128]{1,0:T(8,128)} %upper.1, f32[128,128]{1,0:T(8,128)} %x_in.1, ...), custom_call_target="tpu_custom_call" | custom-call | bytes 999452 | tf_op jit(solution)/shard_map/pallas_call | solution.py:39
  2.8 3.1 %collective-permute-start = (bf16[560,128]{1,0:T(8,128)(2,1)S(1)}, bf16[560,128]{1,0:T(8,128)(2,1)S(1)}, u32[]{:S(2)}, u32[]{:S(2)}) collective-permute-start(bf16[560,128]{1,0:T(8,128)(2,1)S(1)} %get-tuple-element.14), channel_id=1, source_target_pairs={{0,4},{2,6},{4,0},{6,2},{8,12},{10,14},{12,8},{14,10},{1,5},{3,7},... | collective-permute-start | bytes 430088 | tf_op jit(solution)/shard_map/ppermute | solution.py:257
  5.9 1.5 %collective-permute-start.6 = (bf16[480,128]{1,0:T(8,128)(2,1)S(1)}, bf16[480,128]{1,0:T(8,128)(2,1)S(1)}, u32[]{:S(2)}, u32[]{:S(2)}) collective-permute-start(bf16[480,128]{1,0:T(8,128)(2,1)S(1)} %get-tuple-element.20), channel_id=1, source_target_pairs={{0,2},{2,0},{4,6},{6,4},{8,10},{10,8},{12,14},{14,12},{1,3},{3,1},... | collective-permute-start | bytes 368648 | tf_op jit(solution)/shard_map/ppermute | solution.py:257
  7.3 2.6 %collective-permute-start.2 = (bf16[720,128]{1,0:T(8,128)(2,1)S(1)}, bf16[720,128]{1,0:T(8,128)(2,1)S(1)}, u32[]{:S(2)}, u32[]{:S(2)}) collective-permute-start(bf16[720,128]{1,0:T(8,128)(2,1)S(1)} %get-tuple-element.15), channel_id=1, source_target_pairs={{0,8},{2,10},{4,12},{6,14},{8,0},{10,2},{12,4},{14,6},{1,9},{3,11}... | collective-permute-start | bytes 552968 | tf_op jit(solution)/shard_map/ppermute | solution.py:257
  9.9 0.0 collective-permute-done.came.refs_2_
  10.0 3.4 %collective-permute-start.1 = (bf16[480,128]{1,0:T(8,128)(2,1)S(1)}, bf16[480,128]{1,0:T(8,128)(2,1)S(1)}, u32[]{:S(2)}, u32[]{:S(2)}) collective-permute-start(bf16[480,128]{1,0:T(8,128)(2,1)S(1)} %shard_map.105), channel_id=1, source_target_pairs={{0,2},{2,0},{4,6},{6,4},{8,10},{10,8},{12,14},{14,12},{1,3},{3,1},... | collective-permute-start | bytes 368648 | tf_op jit(solution)/shard_map/ppermute | solution.py:257
  13.4 0.0 collective-permute-done.6.refs_1_
  13.4 4.6 %collective-permute-done.2.came.refs_0_ = bf16[720,128]{1,0:T(8,128)(2,1)S(1)} collective-permute-done((bf16[720,128]{1,0:T(8,128)(2,1)S(1)}, bf16[720,128]{1,0:T(8,128)(2,1)S(1)}, u32[]{:S(2)}, u32[]{:S(2)}) %collective-permute-start.2) | collective-permute-done | bytes 184352 | tf_op jit(solution)/shard_map/ppermute | solution.py:257
  18.0 0.0 copy-start.5
  18.0 0.1 collective-permute-start.7
  18.2 0.6 %collective-permute-start.3 = (bf16[480,128]{1,0:T(8,128)(2,1)S(1)}, bf16[480,128]{1,0:T(8,128)(2,1)S(1)}, u32[]{:S(2)}, u32[]{:S(2)}) collective-permute-start(bf16[480,128]{1,0:T(8,128)(2,1)S(1)} %get-tuple-element.16), channel_id=1, source_target_pairs={{0,2},{2,0},{4,6},{6,4},{8,10},{10,8},{12,14},{14,12},{1,3},{3,1},... | collective-permute-start | bytes 368648 | tf_op jit(solution)/shard_map/ppermute | solution.py:257
  18.8 0.0 collective-permute-start.4
  18.8 2.9 %collective-permute-start.5 = (bf16[480,128]{1,0:T(8,128)(2,1)S(1)}, bf16[480,128]{1,0:T(8,128)(2,1)S(1)}, u32[]{:S(2)}, u32[]{:S(2)}) collective-permute-start(bf16[480,128]{1,0:T(8,128)(2,1)S(1)} %get-tuple-element.18), channel_id=1, source_target_pairs={{0,6},{2,4},{4,2},{6,0},{8,14},{10,12},{12,10},{14,8},{1,7},{3,5},... | collective-permute-start | bytes 368648 | tf_op jit(solution)/shard_map/ppermute | solution.py:257
  21.8 0.0 collective-permute-done.1.refs_0_
  21.8 0.1 collective-permute-start.8
  21.9 2.1 %collective-permute-done.3.refs_1_ = bf16[480,128]{1,0:T(8,128)(2,1)S(1)} collective-permute-done((bf16[480,128]{1,0:T(8,128)(2,1)S(1)}, bf16[480,128]{1,0:T(8,128)(2,1)S(1)}, u32[]{:S(2)}, u32[]{:S(2)}) %collective-permute-start.3) | collective-permute-done | bytes 122912 | tf_op jit(solution)/shard_map/ppermute | solution.py:257
  24.0 0.0 collective-permute-start.9
  24.0 1.0 %collective-permute-done.4.refs_2_ = bf16[480,128]{1,0:T(8,128)(2,1)S(1)} collective-permute-done((bf16[480,128]{1,0:T(8,128)(2,1)S(1)}, bf16[480,128]{1,0:T(8,128)(2,1)S(1)}, u32[]{:S(2)}, u32[]{:S(2)}) %collective-permute-start.4) | collective-permute-done | bytes 122912 | tf_op jit(solution)/shard_map/ppermute | solution.py:257
  25.0 0.0 collective-permute-start.10
  25.0 0.0 collective-permute-done.7.refs_3_
  25.0 1.6 %shard_map.108 = (bf16[1024,1024]{1,0:T(8,128)(2,1)S(1)}, bf16[5,16,1024]{2,1,0:T(8,128)(2,1)S(1)}, f32[8,128]{1,0:T(8,128)S(1)}) custom-call(s32[4,7]{1,0:T(4,128)S(1)} %maximum_convert_fusion.slots, bf16[1,1,6,128,128]{4,3,2,1,0:T(8,128)(2,1)} %blocks_in.1, bf16[96,128]{1,0:T(8,128)(2,1)S(1)} %get-tuple-element.19.own, ...), custom_call_target="tpu_custom_call" | custom-call | bytes 3231856 | tf_op jit(solution)/shard_map/pallas_call | solution.py:39
  26.6 0.0 copy-start
  26.6 0.0 copy-start.1
  26.6 0.0 copy-start.2
  26.6 0.0 copy-start.3
  26.6 0.0 copy-start.4
  26.6 1.1 %collective-permute-done.5.part = bf16[480,128]{1,0:T(8,128)(2,1)S(1)} collective-permute-done((bf16[480,128]{1,0:T(8,128)(2,1)S(1)}, bf16[480,128]{1,0:T(8,128)(2,1)S(1)}, u32[]{:S(2)}, u32[]{:S(2)}) %collective-permute-start.5) | collective-permute-done | bytes 122912 | tf_op jit(solution)/shard_map/ppermute | solution.py:257
  27.8 0.0 collective-permute-start.11
  27.9 0.0 collective-permute-done.8.refs_4_
  27.9 0.0 collective-permute-done.9.refs_5_
  27.9 0.0 collective-permute-done.10.refs_6_
  27.9 1.2 %collective-permute-done.11.refs_7_ = bf16[480,128]{1,0:T(8,128)(2,1)S(1)} collective-permute-done((bf16[480,128]{1,0:T(8,128)(2,1)S(1)}, bf16[480,128]{1,0:T(8,128)(2,1)S(1)}, u32[]{:S(2)}, u32[]{:S(2)}) %collective-permute-start.11) | collective-permute-done | bytes 122912 | tf_op jit(solution)/shard_map/ppermute | solution.py:283
  29.1 0.0 copy-done.5
  29.1 2.8 %shard_map.110 = (bf16[8,64,128]{2,1,0:T(8,128)(2,1)S(1)}, f32[8,128]{1,0:T(8,128)S(1)}, bf16[1024,1024]{1,0:T(8,128)(2,1)S(1)}, bf16[5,16,1024]{2,1,0:T(8,128)(2,1)S(1)}) custom-call(s32[4,7]{1,0:T(4,128)S(1)} %maximum_convert_fusion.1.slots, s32[1,128]{1,0:T(1,128)S(1)} %bitcast.1, ...), custom_call_target="tpu_custom_call", output_to_operand_aliasing={{2}: (2, {}), {3}: (3, {})} | custom-call | flops 134217728 | bytes 5644912 | tf_op jit(solution)/shard_map/pallas_call | solution.py:39
  31.9 11.1 %all_to_all.5.recv = bf16[8,64,128]{2,1,0:T(8,128)(2,1)S(1)} all-to-all(bf16[8,64,128]{2,1,0:T(8,128)(2,1)S(1)} %get-tuple-element.24), channel_id=1, replica_groups=mesh['groups'=2,'blk'=4,'col'=2,'rep'=2] {'blk','col'}, dimensions={0} | all-to-all | bytes 262144 | tf_op jit(solution)/shard_map/all_to_all | solution.py:253
  43.0 0.0 copy-done
  43.0 0.0 copy-done.1
  43.0 0.0 copy-done.2
  43.0 0.0 copy-done.3
  43.0 0.0 copy-done.4
  43.0 0.8 %shard_map.111 = (f32[128,128]{1,0:T(8,128)}, f32[128,128]{1,0:T(8,128)}) custom-call(bf16[8,64,128]{2,1,0:T(8,128)(2,1)S(1)} %all_to_all.5.recv, f32[8,128]{1,0:T(8,128)S(1)} %get-tuple-element.25.scales, f32[128,128]{1,0:T(8,128)S(1)} %copy-done, f32[128,128]{1,0:T(8,128)S(1)} %copy-done.1, f32[128,128]{1,0:T(8,128)S(1)} %copy-done.2, ...), custom_call_target="tpu_custom_call" | custom-call | bytes 594432 | tf_op jit(solution)/shard_map/pallas_call | solution.py:39
  (14 shorter events, 0.2 us)
Async XLA Ops:
  2.8 7.2 %collective-permute-start = (bf16[560,128]{1,0:T(8,128)(2,1)S(1)}, bf16[560,128]{1,0:T(8,128)(2,1)S(1)}, u32[]{:S(2)}, u32[]{:S(2)}) collective-permute-start(bf16[560,128]{1,0:T(8,128)(2,1)S(1)} %get-tuple-element.14), channel_id=1, source_target_pairs={{0,4},{2,6},{4,0},{6,2},{8,12},{10,14},{12,8},{14,10},{1,5},{3,7},... | collective-permute-start | bytes 430088 | tf_op jit(solution)/shard_map/ppermute | solution.py:257
  5.9 7.5 %collective-permute-start.6 = (bf16[480,128]{1,0:T(8,128)(2,1)S(1)}, bf16[480,128]{1,0:T(8,128)(2,1)S(1)}, u32[]{:S(2)}, u32[]{:S(2)}) collective-permute-start(bf16[480,128]{1,0:T(8,128)(2,1)S(1)} %get-tuple-element.20), channel_id=1, source_target_pairs={{0,2},{2,0},{4,6},{6,4},{8,10},{10,8},{12,14},{14,12},{1,3},{3,1},... | collective-permute-start | bytes 368648 | tf_op jit(solution)/shard_map/ppermute | solution.py:257
  7.3 10.7 %collective-permute-start.2 = (bf16[720,128]{1,0:T(8,128)(2,1)S(1)}, bf16[720,128]{1,0:T(8,128)(2,1)S(1)}, u32[]{:S(2)}, u32[]{:S(2)}) collective-permute-start(bf16[720,128]{1,0:T(8,128)(2,1)S(1)} %get-tuple-element.15), channel_id=1, source_target_pairs={{0,8},{2,10},{4,12},{6,14},{8,0},{10,2},{12,4},{14,6},{1,9},{3,11}... | collective-permute-start | bytes 552968 | tf_op jit(solution)/shard_map/ppermute | solution.py:257
  10.0 11.8 %collective-permute-start.1 = (bf16[480,128]{1,0:T(8,128)(2,1)S(1)}, bf16[480,128]{1,0:T(8,128)(2,1)S(1)}, u32[]{:S(2)}, u32[]{:S(2)}) collective-permute-start(bf16[480,128]{1,0:T(8,128)(2,1)S(1)} %shard_map.105), channel_id=1, source_target_pairs={{0,2},{2,0},{4,6},{6,4},{8,10},{10,8},{12,14},{14,12},{1,3},{3,1},... | collective-permute-start | bytes 368648 | tf_op jit(solution)/shard_map/ppermute | solution.py:257
  18.0 11.1 %copy-start.5 = (s32[128]{0:T(128)S(1)}, s32[128]{0:T(128)}, u32[]{:S(2)}) copy-start(s32[128]{0:T(128)} %param.17) | copy-start | bytes 1540
  18.0 6.9 %collective-permute-start.7 = (bf16[1152,128]{1,0:T(8,128)(2,1)S(1)}, bf16[1152,128]{1,0:T(8,128)(2,1)S(1)}, u32[]{:S(2)}, u32[]{:S(2)}) collective-permute-start(bf16[1152,128]{1,0:T(8,128)(2,1)S(1)} %shard_map.107), channel_id=1, source_target_pairs={{0,1},{1,0},{2,3},{3,2},{4,5},{5,4},{6,7},{7,6},{8,9},{9,8},{10,11... | collective-permute-start | bytes 884744 | tf_op jit(solution)/shard_map/ppermute | solution.py:283
  18.2 5.8 %collective-permute-start.3 = (bf16[480,128]{1,0:T(8,128)(2,1)S(1)}, bf16[480,128]{1,0:T(8,128)(2,1)S(1)}, u32[]{:S(2)}, u32[]{:S(2)}) collective-permute-start(bf16[480,128]{1,0:T(8,128)(2,1)S(1)} %get-tuple-element.16), channel_id=1, source_target_pairs={{0,2},{2,0},{4,6},{6,4},{8,10},{10,8},{12,14},{14,12},{1,3},{3,1},... | collective-permute-start | bytes 368648 | tf_op jit(solution)/shard_map/ppermute | solution.py:257
  18.8 6.2 %collective-permute-start.4 = (bf16[480,128]{1,0:T(8,128)(2,1)S(1)}, bf16[480,128]{1,0:T(8,128)(2,1)S(1)}, u32[]{:S(2)}, u32[]{:S(2)}) collective-permute-start(bf16[480,128]{1,0:T(8,128)(2,1)S(1)} %get-tuple-element.17), channel_id=1, source_target_pairs={{0,4},{2,6},{4,0},{6,2},{8,12},{10,14},{12,8},{14,10},{1,5},{3,7},... | collective-permute-start | bytes 368648 | tf_op jit(solution)/shard_map/ppermute | solution.py:257
  18.8 9.0 %collective-permute-start.5 = (bf16[480,128]{1,0:T(8,128)(2,1)S(1)}, bf16[480,128]{1,0:T(8,128)(2,1)S(1)}, u32[]{:S(2)}, u32[]{:S(2)}) collective-permute-start(bf16[480,128]{1,0:T(8,128)(2,1)S(1)} %get-tuple-element.18), channel_id=1, source_target_pairs={{0,6},{2,4},{4,2},{6,0},{8,14},{10,12},{12,10},{14,8},{1,7},{3,5},... | collective-permute-start | bytes 368648 | tf_op jit(solution)/shard_map/ppermute | solution.py:257
  21.8 6.0 %collective-permute-start.8 = (bf16[480,128]{1,0:T(8,128)(2,1)S(1)}, bf16[480,128]{1,0:T(8,128)(2,1)S(1)}, u32[]{:S(2)}, u32[]{:S(2)}) collective-permute-start(bf16[480,128]{1,0:T(8,128)(2,1)S(1)} %collective-permute-done.1.refs_0_), channel_id=1, source_target_pairs={{0,1},{1,0},{2,3},{3,2},{4,5},{5,4},{6,7},{7,6},{8,9},{9,8},{10,11... | collective-permute-start | bytes 368648 | tf_op jit(solution)/shard_map/ppermute | solution.py:283
  24.0 3.9 %collective-permute-start.9 = (bf16[480,128]{1,0:T(8,128)(2,1)S(1)}, bf16[480,128]{1,0:T(8,128)(2,1)S(1)}, u32[]{:S(2)}, u32[]{:S(2)}) collective-permute-start(bf16[480,128]{1,0:T(8,128)(2,1)S(1)} %collective-permute-done.3.refs_1_), channel_id=1, source_target_pairs={{0,1},{1,0},{2,3},{3,2},{4,5},{5,4},{6,7},{7,6},{8,9},{9,8},{10,11... | collective-permute-start | bytes 368648 | tf_op jit(solution)/shard_map/ppermute | solution.py:283
  25.0 2.9 %collective-permute-start.10 = (bf16[480,128]{1,0:T(8,128)(2,1)S(1)}, bf16[480,128]{1,0:T(8,128)(2,1)S(1)}, u32[]{:S(2)}, u32[]{:S(2)}) collective-permute-start(bf16[480,128]{1,0:T(8,128)(2,1)S(1)} %collective-permute-done.4.refs_2_), channel_id=1, source_target_pairs={{0,1},{1,0},{2,3},{3,2},{4,5},{5,4},{6,7},{7,6},{8,9},{9,8},{10,11... | collective-permute-start | bytes 368648 | tf_op jit(solution)/shard_map/ppermute | solution.py:283
  26.6 16.4 %copy-start = (f32[128,128]{1,0:T(8,128)S(1)}, f32[128,128]{1,0:T(8,128)}, u32[]{:S(2)}) copy-start(f32[128,128]{1,0:T(8,128)} %cost.1) | copy-start | bytes 196612
  26.6 16.4 %copy-start.1 = (f32[128,128]{1,0:T(8,128)S(1)}, f32[128,128]{1,0:T(8,128)}, u32[]{:S(2)}) copy-start(f32[128,128]{1,0:T(8,128)} %rhs.1) | copy-start | bytes 196612
  26.6 16.4 %copy-start.2 = (f32[128,128]{1,0:T(8,128)S(1)}, f32[128,128]{1,0:T(8,128)}, u32[]{:S(2)}) copy-start(f32[128,128]{1,0:T(8,128)} %upper.1) | copy-start | bytes 196612
  26.6 16.4 %copy-start.3 = (f32[128,128]{1,0:T(8,128)S(1)}, f32[128,128]{1,0:T(8,128)}, u32[]{:S(2)}) copy-start(f32[128,128]{1,0:T(8,128)} %x_in.1) | copy-start | bytes 196612
  26.6 16.4 %copy-start.4 = (f32[128,128]{1,0:T(8,128)S(1)}, f32[128,128]{1,0:T(8,128)}, u32[]{:S(2)}) copy-start(f32[128,128]{1,0:T(8,128)} %y_in.1) | copy-start | bytes 196612
  27.8 1.3 %collective-permute-start.11 = (bf16[480,128]{1,0:T(8,128)(2,1)S(1)}, bf16[480,128]{1,0:T(8,128)(2,1)S(1)}, u32[]{:S(2)}, u32[]{:S(2)}) collective-permute-start(bf16[480,128]{1,0:T(8,128)(2,1)S(1)} %shard_map.109.refs_3_), channel_id=1, source_target_pairs={{0,1},{1,0},{2,3},{3,2},{4,5},{5,4},{6,7},{7,6},{8,9},{9,8},{10,11... | collective-permute-start | bytes 368648 | tf_op jit(solution)/shard_map/ppermute | solution.py:283

commit v11 on v7

--- a/solution.py
+++ b/solution.py
@@ -17,6 +17,7 @@
 PARTS = 3
 FIELDS = 5
 SLOT_ROW = 2 * PARTS
+INFO = 16
 
 MIB = 1024 * 1024
 VMEM = pl.BlockSpec(memory_space=pltpu.VMEM)
@@ -62,7 +63,7 @@
     return jnp.maximum(capped, 0.0)
 
 
-def prep_body(n_col, far, near, first_near, *refs):
+def prep_body(far, first_near, *refs):
     live, *sources = refs[: FIELDS + 3]
     far_out, *near_outs, own_out = refs[FIELDS + 3 : FIELDS + 5 + len(first_near)]
     *fields, share, index, turned, sems = refs[FIELDS + 5 + len(first_near) :]
@@ -76,7 +77,7 @@
     copies.append(pltpu.make_async_copy(sources[-1].at[0, 0, pl.ds(first, half)], share, sems.at[FIELDS + 1]))
     for copy in copies:
         copy.start()
-    part = own_out.shape[0] // (FIELDS + 1)
+    part = (own_out.shape[0] - INFO) // FIELDS
     nslots = index.shape[-1]
     rows = []
     for j, field in enumerate(fields):
@@ -91,35 +92,34 @@
     row = jnp.where(lane == nslots, live[0, 0].astype(F32), 0.0)
     for k in range(nslots):
         row = jnp.where(lane == k, index[0, 0, k].astype(F32), row)
-    rows += [row, jnp.zeros((part - len(rows) - 1, tile), F32)]
+    rows += [row, jnp.zeros((INFO - len(rows) - 1, tile), F32)]
     info = jnp.concatenate(rows, axis=0).astype(BF16)
-    me_b, me_c = lax.axis_index("blk"), lax.axis_index("col")
-
-    def piece(out, at, t, s):
-        peer = pl.ds(pl.multiple_of(((me_b ^ t) * n_col + (me_c ^ s)) * part, part), part)
+    me_b = lax.axis_index("blk")
+
+    def piece(out, at, t):
+        rows = pl.ds(pl.multiple_of((me_b ^ t) * part, part), part)
         for j in range(FIELDS):
-            out[at + j * part : at + (j + 1) * part, :] = turned[j, peer, :]
+            out[at + j * part : at + (j + 1) * part, :] = turned[j, rows, :]
 
     top = half * tile
     for out in (far_out, *near_outs):
         for k in range(half):
             out[k * tile : (k + 1) * tile, :] = share[k]
-        out[out.shape[0] - part :, :] = info
-    for m, (t, s) in enumerate([(0, 0), *near]):
-        piece(far_out, top + m * FIELDS * part, far + t, s)
-    for out, (t, s) in zip(near_outs, first_near):
-        for m in range(1 if t == 0 else n_col):
-            piece(out, top + m * FIELDS * part, t, s ^ m)
-    piece(own_out, 0, 0, 0)
-    own_out[FIELDS * part :, :] = info
+    for t in range(far):
+        piece(far_out, top + t * FIELDS * part, far + t)
+    for out, (t, _) in zip(near_outs, first_near):
+        piece(out, top, t)
+    piece(own_out, 0, 0)
+    for out in (far_out, *near_outs, own_out):
+        out[out.shape[0] - INFO :, :] = info
 
 
 def relay_body(top, part, came, *outs):
-    for m, out in enumerate(outs):
+    for t, out in enumerate(outs):
         out[0:top, :] = came[0:top, :]
-        at = top + (m + 1) * FIELDS * part
+        at = top + t * FIELDS * part
         out[top : top + FIELDS * part, :] = came[at : at + FIELDS * part, :]
-        out[top + FIELDS * part :, :] = came[came.shape[0] - part :, :]
+        out[top + FIELDS * part :, :] = came[came.shape[0] - INFO :, :]
 
 
 def place(n_blk, n_col, mat, slots, source, shift, slot, block, nslots):
@@ -150,7 +150,7 @@
     lanes = pl.ds(pl.multiple_of((blk * n_col + col) * tile, tile), tile)
     for j in range(FIELDS):
         fields[j, :, lanes] = ref[at + j * part : at + (j + 1) * part, :]
-    info = ref[ref.shape[0] - part :, :].astype(F32)
+    info = ref[ref.shape[0] - INFO :, :].astype(F32)
     sums = []
     for j in range(2):
         first, second, third = (info[PARTS * j + k : PARTS * j + k + 1] for k in range(PARTS))
@@ -179,10 +179,9 @@
 
 
 def main_body(n_blk, n_col, shifts, nslots, slots, bounded, mat, fields, sums_in, *refs):
-    n = n_blk * n_col
     count = len(shifts)
     mine, theirs = refs[:count], refs[count : 2 * count]
-    out, scales, _, _, turned = refs[2 * count :]
+    *outs, scales, _, _, products, turned = refs[2 * count :]
     part, tile = fields.shape[1], mine[0].shape[1]
     me_b, me_c = lax.axis_index("blk"), lax.axis_index("col")
     sums = [sums_in[0:1, :], sums_in[1:2, :]]
@@ -195,31 +194,36 @@
     rows = jnp.concatenate([ETA / weight, ETA * weight, bounded[...].astype(F32), jnp.zeros((5, tile), F32)], axis=0)
     scales[...] = rows
     turned[...] = jnp.concatenate([rows, jnp.zeros((tile - 8, tile), F32)], axis=0).T
-    own = turned[pl.ds(pl.multiple_of((me_b * n_col + me_c) * part, part), part), :]
+    own = turned[pl.ds(pl.multiple_of(me_b * part, part), part), :]
     tau, sigma, limited = own[:, 0:1], own[:, 1:2], own[:, 2:3]
-
-    def store(j, values):
-        values = values.astype(BF16)
-        for d in range(n):
-            out[d, j * part : (j + 1) * part, :] = values[:, d * tile : (d + 1) * tile]
 
     for step in range(ITERS):
         kty = jnp.dot(dual.astype(BF16), mat[...], preferred_element_type=F32)
-        store(2 * step, kty)
+        products[2 * step] = kty.astype(BF16)
         x_new = project(primal, cost - kty, tau, upper, limited)
         xbar = (2.0 * x_new - primal).astype(BF16)
         primal = x_new
         kx = lax.dot_general(xbar, mat[...], (((1,), (1,)), ((), ())), preferred_element_type=F32)
-        store(2 * step + 1, kx)
+        products[2 * step + 1] = kx.astype(BF16)
         dual = jnp.maximum(dual + sigma * (rhs - kx), 0.0)
-
-
-def final_body(recv, scales, cost, rhs, upper, x_in, y_in, bounded, x_out, y_out):
-    n, rows, tile = recv.shape
-    part = rows // (2 * ITERS)
+    for t, out in enumerate(outs):
+        lanes = pl.ds(pl.multiple_of(((me_b ^ t) * n_col + me_c) * tile, tile), tile)
+        for j in range(2 * ITERS):
+            out[j * part : (j + 1) * part, :] = products[j, :, lanes]
+
+
+def final_body(order, *refs):
+    parts = refs[: len(order)]
+    scales, cost, rhs, upper, x_in, y_in, bounded, x_out, y_out, products = refs[len(order) :]
+    part = parts[0].shape[0] // (2 * ITERS)
+    me_b = lax.axis_index("blk")
+    for t, recv in zip(order, parts):
+        rows = pl.ds(pl.multiple_of((me_b ^ t) * part, part), part)
+        for j in range(2 * ITERS):
+            products[j, rows, :] = recv[j * part : (j + 1) * part, :]
 
     def turned(j):
-        return recv[:, j * part : (j + 1) * part, :].reshape(n * part, tile).astype(F32).T
+        return products[j].astype(F32).T
 
     tau, sigma = scales[0:1, :], scales[1:2, :]
     primal, dual = x_in[...], y_in[...]
@@ -235,12 +239,9 @@
     n = n_blk * n_col
     tile, nslots = blocks.shape[-1], blocks.shape[2]
     scn = cost.shape[1]
-    part = scn // n
+    part = scn // n_blk
     like = jax.ShapeDtypeStruct
     limits = bounded[None, :]
-
-    def spread(value):
-        return lax.all_to_all(value, ("blk", "col"), 0, 0, tiled=True)
 
     def move(value, t, s):
         pairs = [(b * n_col + c, (b ^ t) * n_col + (c ^ s)) for b in range(n_blk) for c in range(n_col)]
@@ -250,13 +251,13 @@
     near = [(t, s) for t in range(far) for s in range(n_col) if (t, s) != (0, 0)]
     half = nslots // 2
     top = half * tile
-    size = top + (FIELDS + 1) * part
+    size = top + FIELDS * part + INFO
     first_near = [(0, s) for s in range(1, n_col)] + [(t, 0) for t in range(1, far)]
     far_out, *near_outs, own = call(
-        functools.partial(prep_body, n_col, far, near, first_near),
-        [held((top + (FIELDS * (len(near) + 1) + 1) * part, tile), BF16)]
-        + [held((size + (n_col - 1) * FIELDS * part * (t > 0), tile), BF16) for t, s in first_near]
-        + [held(((FIELDS + 1) * part, tile), BF16)],
+        functools.partial(prep_body, far, first_near),
+        [held((top + FIELDS * far * part + INFO, tile), BF16)]
+        + [held((size, tile), BF16)] * len(first_near)
+        + [held((size - top, tile), BF16)],
         [SMEM] + [ANY] * (FIELDS + 2),
         [live] + pinned([cost, rhs, upper, x_init, y_init, block_index, blocks]),
         scratch=[pltpu.VMEM((tile, scn), F32)] * FIELDS
@@ -265,25 +266,23 @@
         + [pltpu.VMEM((FIELDS, scn, tile), BF16), pltpu.SemaphoreType.DMA((FIELDS + 2,))],
     )
 
-    def relay(came, count):
-        return call(functools.partial(relay_body, top, part), [held((size, tile), BF16)] * count, [VMEM], [came])
-
     def other_core(values):
-        return [lax.ppermute(v, "rep", [(0, 1), (1, 0)]) for v in values]
+        return [lax.ppermute(v[:top], "rep", [(0, 1), (1, 0)]) for v in values]
 
     def slots_of(values):
-        rows = [v[v.shape[0] - part + SLOT_ROW, : nslots + 1] for v in values]
+        rows = [v[v.shape[0] - INFO + SLOT_ROW, : nslots + 1] for v in values]
         return jnp.stack(rows).astype(jnp.int32)
 
     early = {(far, 0): move(far_out, far, 0)}
     for (t, s), out in zip(first_near, near_outs):
         early[t, s] = move(out, t, s)
     for t in range(1, far):
-        for s, out in zip(range(1, n_col), relay(early[t, 0], n_col - 1)):
-            early[t, s] = move(out, 0, s)
-    late = {}
-    for (t, s), out in zip(near, relay(early[far, 0], len(near))):
-        late[far + t, s] = move(out, t, s)
+        for s in range(1, n_col):
+            early[t, s] = move(early[t, 0], 0, s)
+    relayed = call(
+        functools.partial(relay_body, top, part), [held((size, tile), BF16)] * far, [VMEM], [early[far, 0]]
+    )
+    late = {(far + t, s): move(relayed[t], t, s) for t, s in near}
     shifts, mine = list(early), list(early.values())
     mat, fields, sums = call(
         functools.partial(early_body, n_blk, n_col, shifts),
@@ -293,21 +292,24 @@
         scratch=[pltpu.VMEM(blocks.shape, BF16), pltpu.SemaphoreType.DMA],
     )
     shifts, mine = list(late), list(late.values())
-    products, scales, _, _ = call(
+    *products, scales, _, _ = call(
         functools.partial(main_body, n_blk, n_col, shifts, nslots),
-        [like((n, 2 * ITERS * part, tile), BF16), like((8, scn), F32)]
-        + [held(mat.shape, BF16), held(fields.shape, BF16)],
+        [held((2 * ITERS * part, tile), BF16)] * n_blk
+        + [like((8, scn), F32), held(mat.shape, BF16), held(fields.shape, BF16)],
         [SMEM] + [VMEM] * (4 + 2 * len(mine)),
         [slots_of(mine), limits, mat, fields, sums] + mine + other_core(mine),
-        scratch=[pltpu.VMEM((tile, scn), F32)],
+        scratch=[pltpu.VMEM((2 * ITERS, part, n * tile), BF16), pltpu.VMEM((tile, scn), F32)],
         flops=4 * ITERS * n * n * tile * tile * part,
-        aliases={2: 2, 3: 3},
-    )
+        aliases={2: n_blk + 1, 3: n_blk + 2},
+    )
+    order = [0, *range(n_blk - 1, 0, -1)]
+    parts = [products[t] if t == 0 else move(products[t], t, 0) for t in order]
     return call(
-        final_body,
+        functools.partial(final_body, order),
         [like((tile, scn), F32)] * 2,
-        [VMEM] * (FIELDS + 3),
-        [spread(products), scales, cost, rhs, upper, x_init, y_init, limits],
+        [VMEM] * (n_blk + FIELDS + 2),
+        parts + [scales, cost, rhs, upper, x_init, y_init, limits],
+        scratch=[pltpu.VMEM((2 * ITERS, scn, tile), BF16)],
     )
 
 
@@ -368,7 +370,7 @@
     n_blk, n_col, n_rep = (lax.axis_size(axis) for axis in ("blk", "col", "rep"))
     blocks, cost = args[0], args[3]
     n, tile, nslots = n_blk * n_col, blocks.shape[-1], blocks.shape[2]
-    fits = 2 * (n * tile) ** 2 <= MAX_MATRIX and cost.shape[1] % (16 * n) == 0 and cost.shape[1] == tile
+    fits = 2 * (n * tile) ** 2 <= MAX_MATRIX and cost.shape[1] % (16 * n_blk) == 0 and cost.shape[1] == tile
     even = n_blk & (n_blk - 1) == 0 and n_col & (n_col - 1) == 0 and n_blk > 1 and n_rep == 2 and nslots % 2 == 0
     x, y = (local_plan if fits and even else collectives_plan)(*args)
     return x, y

time: 42.8 us -> 39.7 us (0.928)
  blocking collectives: 11.4 us -> 0 us
  starting transfers between devices: 11.5 us -> 18.3 us
  waiting for transfers between devices: 11.5 us -> 12.5 us
    all_to_all x1 -> x0, blocking collectives: 11.4 us -> none  [spread(): return lax.all_to_all(value, ('blk', 'col'), 0, 0, tiled=True)]
    ppermute x7 -> x10, starting transfers between devices: 11 us -> 17 us  [move(): return lax.ppermute(value, ('blk', 'col'), pairs)]
    ppermute x7 -> x10, waiting for transfers between devices: 11.5 us -> 12.5 us  [move(): return lax.ppermute(value, ('blk', 'col'), pairs)]
    ppermute x7, starting transfers between devices: 0.52 us -> 1.28 us  [other_core(): return [lax.ppermute(v[:top], 'rep', [(0, 1), (1, 0)]) for v in values]]
    pallas_call x6 -> x5, Pallas kernels: 6.58 us -> 6.99 us  [call(): pl.pallas_call(body, out_shape=list(outs), in_specs=in_specs, out_specs=[...]
  transfers between devices with their start and end apart: 14 -> 17, of which waited for: 5 -> 7; matrix products, arithmetic and copies ran while one was open for 0% -> 0% of each run, Pallas kernels for 4% -> 4%
where the time goes in v11:
time: 39.7 us; the launch traced here: 39.5 us
  starting transfers between devices  18.3 us (46%)
  waiting for transfers between devices  12.5 us (31%)
  Pallas kernels  6.99 us (18%)
  between operations  1.55 us (4%)
    ppermute x10, starting transfers between devices, move(): return lax.ppermute(value, ('blk', 'col'), pairs)  17 us
    ppermute x10, waiting for transfers between devices, move(): return lax.ppermute(value, ('blk', 'col'), pairs)  12.5 us
    pallas_call x5, Pallas kernels, call(): pl.pallas_call(body, out_shape=list(outs), in_specs=in_specs, out_specs=[...  6.99 us
    ppermute x7, starting transfers between devices, other_core(): return [lax.ppermute(v[:top], 'rep', [(0, 1), (1, 0)]) for v in values]  1.28 us
  transfers between devices with their start and end apart: 17, of which 7 were waited for; matrix products, arithmetic and copies ran while one was open for 0% of the time, Pallas kernels for 4%

profile of v11, /device:TPU:0, one launch (start us, length us, event | category | flops | bytes accessed | tf_op | source)
XLA Modules:
  0.0 39.5 jit_solution(3087631494011011077)
XLA Ops:
  0.6 0.0 copy-start.5
  1.3 1.5 %shard_map.104 = (bf16[720,128]{1,0:T(8,128)(2,1)S(1)}, bf16[560,128]{1,0:T(8,128)(2,1)S(1)}, bf16[560,128]{1,0:T(8,128)(2,1)S(1)}, bf16[176,128]{1,0:T(8,128)(2,1)S(1)}) custom-call(s32[1,1]{1,0:T(1,128)S(6)} %copy.15.refs_0_, f32[128,128]{1,0:T(8,128)} %refs_5_.3, f32[128,128]{1,0:T(8,128)} %refs_6_.3, f32[128,128]{1,0:T(8,128)} %refs_7_.3, ...), custom_call_target="tpu_custom_call" | custom-call | bytes 1040412 | tf_op jit(solution)/shard_map/pallas_call | solution.py:40
  2.8 3.1 %collective-permute-start.5 = (bf16[560,128]{1,0:T(8,128)(2,1)S(1)}, bf16[560,128]{1,0:T(8,128)(2,1)S(1)}, u32[]{:S(2)}, u32[]{:S(2)}) collective-permute-start(bf16[560,128]{1,0:T(8,128)(2,1)S(1)} %get-tuple-element.21), channel_id=1, source_target_pairs={{0,4},{2,6},{4,0},{6,2},{8,12},{10,14},{12,8},{14,10},{1,5},{3,7},... | collective-permute-start | bytes 430088 | tf_op jit(solution)/shard_map/ppermute | solution.py:248
  5.9 2.6 %collective-permute-start = (bf16[720,128]{1,0:T(8,128)(2,1)S(1)}, bf16[720,128]{1,0:T(8,128)(2,1)S(1)}, u32[]{:S(2)}, u32[]{:S(2)}) collective-permute-start(bf16[720,128]{1,0:T(8,128)(2,1)S(1)} %get-tuple-element.16), channel_id=1, source_target_pairs={{0,8},{2,10},{4,12},{6,14},{8,0},{10,2},{12,4},{14,6},{1,9},{3,11}... | collective-permute-start | bytes 552968 | tf_op jit(solution)/shard_map/ppermute | solution.py:248
  8.5 1.5 %collective-permute-start.4 = (bf16[560,128]{1,0:T(8,128)(2,1)S(1)}, bf16[560,128]{1,0:T(8,128)(2,1)S(1)}, u32[]{:S(2)}, u32[]{:S(2)}) collective-permute-start(bf16[560,128]{1,0:T(8,128)(2,1)S(1)} %get-tuple-element.20), channel_id=1, source_target_pairs={{0,2},{2,0},{4,6},{6,4},{8,10},{10,8},{12,14},{14,12},{1,3},{3,1},... | collective-permute-start | bytes 430088 | tf_op jit(solution)/shard_map/ppermute | solution.py:248
  10.0 2.0 %collective-permute-done.5.refs_2_ = bf16[560,128]{1,0:T(8,128)(2,1)S(1)} collective-permute-done((bf16[560,128]{1,0:T(8,128)(2,1)S(1)}, bf16[560,128]{1,0:T(8,128)(2,1)S(1)}, u32[]{:S(2)}, u32[]{:S(2)}) %collective-permute-start.5) | collective-permute-done | bytes 143392 | tf_op jit(solution)/shard_map/ppermute | solution.py:248
  12.0 1.8 %collective-permute-start.6 = (bf16[560,128]{1,0:T(8,128)(2,1)S(1)}, bf16[560,128]{1,0:T(8,128)(2,1)S(1)}, u32[]{:S(2)}, u32[]{:S(2)}) collective-permute-start(bf16[560,128]{1,0:T(8,128)(2,1)S(1)} %collective-permute-done.5.refs_2_), channel_id=1, source_target_pairs={{0,2},{2,0},{4,6},{6,4},{8,10},{10,8},{12,14},{14,12},{1,3},{3,1},... | collective-permute-start | bytes 430088 | tf_op jit(solution)/shard_map/ppermute | solution.py:248
  13.8 3.0 %collective-permute-done.came.refs_0_ = bf16[720,128]{1,0:T(8,128)(2,1)S(1)} collective-permute-done((bf16[720,128]{1,0:T(8,128)(2,1)S(1)}, bf16[720,128]{1,0:T(8,128)(2,1)S(1)}, u32[]{:S(2)}, u32[]{:S(2)}) %collective-permute-start) | collective-permute-done | bytes 184352 | tf_op jit(solution)/shard_map/ppermute | solution.py:248
  16.9 1.6 %collective-permute-start.1 = (bf16[560,128]{1,0:T(8,128)(2,1)S(1)}, bf16[560,128]{1,0:T(8,128)(2,1)S(1)}, u32[]{:S(2)}, u32[]{:S(2)}) collective-permute-start(bf16[560,128]{1,0:T(8,128)(2,1)S(1)} %get-tuple-element.17), channel_id=1, source_target_pairs={{0,2},{2,0},{4,6},{6,4},{8,10},{10,8},{12,14},{14,12},{1,3},{3,1},... | collective-permute-start | bytes 430088 | tf_op jit(solution)/shard_map/ppermute | solution.py:248
  18.5 0.0 collective-permute-start.3
  18.5 2.0 %collective-permute-start.2 = (bf16[560,128]{1,0:T(8,128)(2,1)S(1)}, bf16[560,128]{1,0:T(8,128)(2,1)S(1)}, u32[]{:S(2)}, u32[]{:S(2)}) collective-permute-start(bf16[560,128]{1,0:T(8,128)(2,1)S(1)} %get-tuple-element.18), channel_id=1, source_target_pairs={{0,4},{2,6},{4,0},{6,2},{8,12},{10,14},{12,8},{14,10},{1,5},{3,7},... | collective-permute-start | bytes 430088 | tf_op jit(solution)/shard_map/ppermute | solution.py:248
  20.5 0.0 collective-permute-done.4.refs_1_
  20.5 0.1 collective-permute-start.8
  20.6 0.0 collective-permute-done.6.refs_3_
  20.6 0.5 %collective-permute-start.9 = (bf16[384,128]{1,0:T(8,128)(2,1)S(1)}, bf16[384,128]{1,0:T(8,128)(2,1)S(1)}, u32[]{:S(2)}, u32[]{:S(2)}) collective-permute-start(bf16[384,128]{1,0:T(8,128)(2,1)S(1)} %slice.69), channel_id=1, source_target_pairs={{0,1},{1,0},{2,3},{3,2},{4,5},{5,4},{6,7},{7,6},{8,9},{9,8},{10,11... | collective-permute-start | bytes 294920 | tf_op jit(solution)/shard_map/ppermute | solution.py:270
  21.3 0.8 %collective-permute-done.1.refs_0_ = bf16[560,128]{1,0:T(8,128)(2,1)S(1)} collective-permute-done((bf16[560,128]{1,0:T(8,128)(2,1)S(1)}, bf16[560,128]{1,0:T(8,128)(2,1)S(1)}, u32[]{:S(2)}, u32[]{:S(2)}) %collective-permute-start.1) | collective-permute-done | bytes 143392 | tf_op jit(solution)/shard_map/ppermute | solution.py:248
  22.1 0.0 collective-permute-start.7
  22.1 2.4 %collective-permute-done.3.refs_2_ = bf16[560,128]{1,0:T(8,128)(2,1)S(1)} collective-permute-done((bf16[560,128]{1,0:T(8,128)(2,1)S(1)}, bf16[560,128]{1,0:T(8,128)(2,1)S(1)}, u32[]{:S(2)}, u32[]{:S(2)}) %collective-permute-start.3) | collective-permute-done | bytes 143392 | tf_op jit(solution)/shard_map/ppermute | solution.py:248
  24.5 0.0 collective-permute-start.10
  24.5 0.6 %collective-permute-done.2.refs_1_ = bf16[560,128]{1,0:T(8,128)(2,1)S(1)} collective-permute-done((bf16[560,128]{1,0:T(8,128)(2,1)S(1)}, bf16[560,128]{1,0:T(8,128)(2,1)S(1)}, u32[]{:S(2)}, u32[]{:S(2)}) %collective-permute-start.2) | collective-permute-done | bytes 143392 | tf_op jit(solution)/shard_map/ppermute | solution.py:248
  25.1 0.0 collective-permute-start.11
  25.2 0.0 collective-permute-done.8.refs_5_
  25.2 0.6 %collective-permute-start.13 = (bf16[384,128]{1,0:T(8,128)(2,1)S(1)}, bf16[384,128]{1,0:T(8,128)(2,1)S(1)}, u32[]{:S(2)}, u32[]{:S(2)}) collective-permute-start(bf16[384,128]{1,0:T(8,128)(2,1)S(1)} %slice.73), channel_id=1, source_target_pairs={{0,1},{1,0},{2,3},{3,2},{4,5},{5,4},{6,7},{7,6},{8,9},{9,8},{10,11... | collective-permute-start | bytes 294920 | tf_op jit(solution)/shard_map/ppermute | solution.py:270
  25.7 0.0 collective-permute-done.9.refs_6_
  25.7 0.1 collective-permute-start.12
  25.8 0.0 copy-start
  25.8 0.0 copy-start.1
  25.9 0.0 copy-start.2
  25.9 0.0 copy-start.3
  25.9 0.0 copy-start.4
  25.9 0.0 collective-permute-done.7.refs_4_
  25.9 0.0 collective-permute-done.10.refs_7_
  25.9 1.6 %shard_map.106 = (bf16[1024,1024]{1,0:T(8,128)(2,1)S(1)}, bf16[5,32,1024]{2,1,0:T(8,128)(2,1)S(1)}, f32[8,128]{1,0:T(8,128)S(1)}) custom-call(s32[5,7]{1,0:T(8,128)S(1)} %convert_element_type.7.slots, bf16[1,1,6,128,128]{4,3,2,1,0:T(8,128)(2,1)} %blocks_in.1, bf16[176,128]{1,0:T(8,128)(2,1)S(1)} %get-tuple-element.19.own, ...), custom_call_target="tpu_custom_call" | custom-call | bytes 3678348 | tf_op jit(solution)/shard_map/pallas_call | solution.py:40
  27.5 0.0 collective-permute-done.11.refs_3_
  27.6 0.0 collective-permute-done.13.refs_5_
  27.6 0.0 collective-permute-done.12.refs_4_
  27.6 0.0 copy-done.5
  27.6 3.0 %shard_map.107 = (bf16[128,128]{1,0:T(8,128)(2,1)S(1)}, bf16[128,128]{1,0:T(8,128)(2,1)S(1)}, bf16[128,128]{1,0:T(8,128)(2,1)S(1)}, bf16[128,128]{1,0:T(8,128)(2...) custom-call(s32[3,7]{1,0:T(4,128)S(1)} %maximum_convert_fusion.slots, ...), custom_call_target="tpu_custom_call", output_to_operand_aliasing={{5}: (2, {}), {6}: (3, {})} | custom-call | flops 268435456 | bytes 5714516 | tf_op jit(solution)/shard_map/pallas_call | solution.py:40
  30.6 3.2 %collective-permute-start.14 = (bf16[128,128]{1,0:T(8,128)(2,1)S(1)}, bf16[128,128]{1,0:T(8,128)(2,1)S(1)}, u32[]{:S(2)}, u32[]{:S(2)}) collective-permute-start(bf16[128,128]{1,0:T(8,128)(2,1)S(1)} %get-tuple-element.26), channel_id=1, source_target_pairs={{0,12},{2,14},{4,8},{6,10},{8,4},{10,6},{12,0},{14,2},{1,13},{3,15... | collective-permute-start | bytes 98312 | tf_op jit(solution)/shard_map/ppermute | solution.py:248
  33.9 0.0 collective-permute-start.15
  33.9 1.2 %collective-permute-start.16 = (bf16[128,128]{1,0:T(8,128)(2,1)S(1)}, bf16[128,128]{1,0:T(8,128)(2,1)S(1)}, u32[]{:S(2)}, u32[]{:S(2)}) collective-permute-start(bf16[128,128]{1,0:T(8,128)(2,1)S(1)} %get-tuple-element.28), channel_id=1, source_target_pairs={{0,4},{2,6},{4,0},{6,2},{8,12},{10,14},{12,8},{14,10},{1,5},{3,7},... | collective-permute-start | bytes 98312 | tf_op jit(solution)/shard_map/ppermute | solution.py:248
  35.1 1.4 %collective-permute-done.14.refs_1_ = bf16[128,128]{1,0:T(8,128)(2,1)S(1)} collective-permute-done((bf16[128,128]{1,0:T(8,128)(2,1)S(1)}, bf16[128,128]{1,0:T(8,128)(2,1)S(1)}, u32[]{:S(2)}, u32[]{:S(2)}) %collective-permute-start.14) | collective-permute-done | bytes 32800 | tf_op jit(solution)/shard_map/ppermute | solution.py:248
  36.5 2.2 %collective-permute-done.15.refs_2_ = bf16[128,128]{1,0:T(8,128)(2,1)S(1)} collective-permute-done((bf16[128,128]{1,0:T(8,128)(2,1)S(1)}, bf16[128,128]{1,0:T(8,128)(2,1)S(1)}, u32[]{:S(2)}, u32[]{:S(2)}) %collective-permute-start.15) | collective-permute-done | bytes 32800 | tf_op jit(solution)/shard_map/ppermute | solution.py:248
  38.7 0.0 collective-permute-done.16.refs_3_
  38.7 0.0 copy-done
  38.7 0.0 copy-done.1
  38.7 0.0 copy-done.2
  38.7 0.0 copy-done.3
  38.7 0.0 copy-done.4
  38.7 0.8 %shard_map.108 = (f32[128,128]{1,0:T(8,128)}, f32[128,128]{1,0:T(8,128)}) custom-call(bf16[128,128]{1,0:T(8,128)(2,1)S(1)} %get-tuple-element.25.refs_0_, bf16[128,128]{1,0:T(8,128)(2,1)S(1)} %collective-permute-done.14.refs_1_, bf16[128,128]{1,0:T(8,128)(2,1)S(1)} %collective-permute-done.15.refs_2_, bf16[128,128]{1,0:T(8,128)(2,1)S(1)} %collective-permute-done.16.refs_3_, ...), custom_call_target="tpu_custom_call" | custom-call | bytes 594432 | tf_op jit(solution)/shard_map/pallas_call | solution.py:40
  (19 shorter events, 0.2 us)
Async XLA Ops:
  0.6 26.9 %copy-start.5 = (s32[128]{0:T(128)S(1)}, s32[128]{0:T(128)}, u32[]{:S(2)}) copy-start(s32[128]{0:T(128)} %param.17) | copy-start | bytes 1540
  2.8 9.2 %collective-permute-start.5 = (bf16[560,128]{1,0:T(8,128)(2,1)S(1)}, bf16[560,128]{1,0:T(8,128)(2,1)S(1)}, u32[]{:S(2)}, u32[]{:S(2)}) collective-permute-start(bf16[560,128]{1,0:T(8,128)(2,1)S(1)} %get-tuple-element.21), channel_id=1, source_target_pairs={{0,4},{2,6},{4,0},{6,2},{8,12},{10,14},{12,8},{14,10},{1,5},{3,7},... | collective-permute-start | bytes 430088 | tf_op jit(solution)/shard_map/ppermute | solution.py:248
  5.9 11.0 %collective-permute-start = (bf16[720,128]{1,0:T(8,128)(2,1)S(1)}, bf16[720,128]{1,0:T(8,128)(2,1)S(1)}, u32[]{:S(2)}, u32[]{:S(2)}) collective-permute-start(bf16[720,128]{1,0:T(8,128)(2,1)S(1)} %get-tuple-element.16), channel_id=1, source_target_pairs={{0,8},{2,10},{4,12},{6,14},{8,0},{10,2},{12,4},{14,6},{1,9},{3,11}... | collective-permute-start | bytes 552968 | tf_op jit(solution)/shard_map/ppermute | solution.py:248
  8.5 12.0 %collective-permute-start.4 = (bf16[560,128]{1,0:T(8,128)(2,1)S(1)}, bf16[560,128]{1,0:T(8,128)(2,1)S(1)}, u32[]{:S(2)}, u32[]{:S(2)}) collective-permute-start(bf16[560,128]{1,0:T(8,128)(2,1)S(1)} %get-tuple-element.20), channel_id=1, source_target_pairs={{0,2},{2,0},{4,6},{6,4},{8,10},{10,8},{12,14},{14,12},{1,3},{3,1},... | collective-permute-start | bytes 430088 | tf_op jit(solution)/shard_map/ppermute | solution.py:248
  12.0 8.6 %collective-permute-start.6 = (bf16[560,128]{1,0:T(8,128)(2,1)S(1)}, bf16[560,128]{1,0:T(8,128)(2,1)S(1)}, u32[]{:S(2)}, u32[]{:S(2)}) collective-permute-start(bf16[560,128]{1,0:T(8,128)(2,1)S(1)} %collective-permute-done.5.refs_2_), channel_id=1, source_target_pairs={{0,2},{2,0},{4,6},{6,4},{8,10},{10,8},{12,14},{14,12},{1,3},{3,1},... | collective-permute-start | bytes 430088 | tf_op jit(solution)/shard_map/ppermute | solution.py:248
  16.9 5.2 %collective-permute-start.1 = (bf16[560,128]{1,0:T(8,128)(2,1)S(1)}, bf16[560,128]{1,0:T(8,128)(2,1)S(1)}, u32[]{:S(2)}, u32[]{:S(2)}) collective-permute-start(bf16[560,128]{1,0:T(8,128)(2,1)S(1)} %get-tuple-element.17), channel_id=1, source_target_pairs={{0,2},{2,0},{4,6},{6,4},{8,10},{10,8},{12,14},{14,12},{1,3},{3,1},... | collective-permute-start | bytes 430088 | tf_op jit(solution)/shard_map/ppermute | solution.py:248
  18.5 6.0 %collective-permute-start.3 = (bf16[560,128]{1,0:T(8,128)(2,1)S(1)}, bf16[560,128]{1,0:T(8,128)(2,1)S(1)}, u32[]{:S(2)}, u32[]{:S(2)}) collective-permute-start(bf16[560,128]{1,0:T(8,128)(2,1)S(1)} %get-tuple-element.18), channel_id=1, source_target_pairs={{0,6},{2,4},{4,2},{6,0},{8,14},{10,12},{12,10},{14,8},{1,7},{3,5},... | collective-permute-start | bytes 430088 | tf_op jit(solution)/shard_map/ppermute | solution.py:248
  18.5 6.6 %collective-permute-start.2 = (bf16[560,128]{1,0:T(8,128)(2,1)S(1)}, bf16[560,128]{1,0:T(8,128)(2,1)S(1)}, u32[]{:S(2)}, u32[]{:S(2)}) collective-permute-start(bf16[560,128]{1,0:T(8,128)(2,1)S(1)} %get-tuple-element.18), channel_id=1, source_target_pairs={{0,4},{2,6},{4,0},{6,2},{8,12},{10,14},{12,8},{14,10},{1,5},{3,7},... | collective-permute-start | bytes 430088 | tf_op jit(solution)/shard_map/ppermute | solution.py:248
  20.5 4.7 %collective-permute-start.8 = (bf16[384,128]{1,0:T(8,128)(2,1)S(1)}, bf16[384,128]{1,0:T(8,128)(2,1)S(1)}, u32[]{:S(2)}, u32[]{:S(2)}) collective-permute-start(bf16[384,128]{1,0:T(8,128)(2,1)S(1)} %slice.68), channel_id=1, source_target_pairs={{0,1},{1,0},{2,3},{3,2},{4,5},{5,4},{6,7},{7,6},{8,9},{9,8},{10,11... | collective-permute-start | bytes 294920 | tf_op jit(solution)/shard_map/ppermute | solution.py:270
  20.6 5.1 %collective-permute-start.9 = (bf16[384,128]{1,0:T(8,128)(2,1)S(1)}, bf16[384,128]{1,0:T(8,128)(2,1)S(1)}, u32[]{:S(2)}, u32[]{:S(2)}) collective-permute-start(bf16[384,128]{1,0:T(8,128)(2,1)S(1)} %slice.69), channel_id=1, source_target_pairs={{0,1},{1,0},{2,3},{3,2},{4,5},{5,4},{6,7},{7,6},{8,9},{9,8},{10,11... | collective-permute-start | bytes 294920 | tf_op jit(solution)/shard_map/ppermute | solution.py:270
  22.1 3.8 %collective-permute-start.7 = (bf16[384,128]{1,0:T(8,128)(2,1)S(1)}, bf16[384,128]{1,0:T(8,128)(2,1)S(1)}, u32[]{:S(2)}, u32[]{:S(2)}) collective-permute-start(bf16[384,128]{1,0:T(8,128)(2,1)S(1)} %slice.67), channel_id=1, source_target_pairs={{0,1},{1,0},{2,3},{3,2},{4,5},{5,4},{6,7},{7,6},{8,9},{9,8},{10,11... | collective-permute-start | bytes 294920 | tf_op jit(solution)/shard_map/ppermute | solution.py:270
  24.5 1.4 %collective-permute-start.10 = (bf16[384,128]{1,0:T(8,128)(2,1)S(1)}, bf16[384,128]{1,0:T(8,128)(2,1)S(1)}, u32[]{:S(2)}, u32[]{:S(2)}) collective-permute-start(bf16[384,128]{1,0:T(8,128)(2,1)S(1)} %slice.70), channel_id=1, source_target_pairs={{0,1},{1,0},{2,3},{3,2},{4,5},{5,4},{6,7},{7,6},{8,9},{9,8},{10,11... | collective-permute-start | bytes 294920 | tf_op jit(solution)/shard_map/ppermute | solution.py:270
  25.1 2.4 %collective-permute-start.11 = (bf16[384,128]{1,0:T(8,128)(2,1)S(1)}, bf16[384,128]{1,0:T(8,128)(2,1)S(1)}, u32[]{:S(2)}, u32[]{:S(2)}) collective-permute-start(bf16[384,128]{1,0:T(8,128)(2,1)S(1)} %slice.71), channel_id=1, source_target_pairs={{0,1},{1,0},{2,3},{3,2},{4,5},{5,4},{6,7},{7,6},{8,9},{9,8},{10,11... | collective-permute-start | bytes 294920 | tf_op jit(solution)/shard_map/ppermute | solution.py:270
  25.2 2.4 %collective-permute-start.13 = (bf16[384,128]{1,0:T(8,128)(2,1)S(1)}, bf16[384,128]{1,0:T(8,128)(2,1)S(1)}, u32[]{:S(2)}, u32[]{:S(2)}) collective-permute-start(bf16[384,128]{1,0:T(8,128)(2,1)S(1)} %slice.73), channel_id=1, source_target_pairs={{0,1},{1,0},{2,3},{3,2},{4,5},{5,4},{6,7},{7,6},{8,9},{9,8},{10,11... | collective-permute-start | bytes 294920 | tf_op jit(solution)/shard_map/ppermute | solution.py:270
  25.7 1.8 %collective-permute-start.12 = (bf16[384,128]{1,0:T(8,128)(2,1)S(1)}, bf16[384,128]{1,0:T(8,128)(2,1)S(1)}, u32[]{:S(2)}, u32[]{:S(2)}) collective-permute-start(bf16[384,128]{1,0:T(8,128)(2,1)S(1)} %slice.72), channel_id=1, source_target_pairs={{0,1},{1,0},{2,3},{3,2},{4,5},{5,4},{6,7},{7,6},{8,9},{9,8},{10,11... | collective-permute-start | bytes 294920 | tf_op jit(solution)/shard_map/ppermute | solution.py:270
  25.8 12.8 %copy-start = (f32[128,128]{1,0:T(8,128)S(1)}, f32[128,128]{1,0:T(8,128)}, u32[]{:S(2)}) copy-start(f32[128,128]{1,0:T(8,128)} %refs_5_.3) | copy-start | bytes 196612
  25.8 12.8 %copy-start.1 = (f32[128,128]{1,0:T(8,128)S(1)}, f32[128,128]{1,0:T(8,128)}, u32[]{:S(2)}) copy-start(f32[128,128]{1,0:T(8,128)} %refs_6_.3) | copy-start | bytes 196612
  25.9 12.8 %copy-start.2 = (f32[128,128]{1,0:T(8,128)S(1)}, f32[128,128]{1,0:T(8,128)}, u32[]{:S(2)}) copy-start(f32[128,128]{1,0:T(8,128)} %refs_7_.3) | copy-start | bytes 196612
  25.9 12.8 %copy-start.3 = (f32[128,128]{1,0:T(8,128)S(1)}, f32[128,128]{1,0:T(8,128)}, u32[]{:S(2)}) copy-start(f32[128,128]{1,0:T(8,128)} %refs_8_.1) | copy-start | bytes 196612
  25.9 12.8 %copy-start.4 = (f32[128,128]{1,0:T(8,128)S(1)}, f32[128,128]{1,0:T(8,128)}, u32[]{:S(2)}) copy-start(f32[128,128]{1,0:T(8,128)} %refs_9_.1) | copy-start | bytes 196612
  30.6 5.8 %collective-permute-start.14 = (bf16[128,128]{1,0:T(8,128)(2,1)S(1)}, bf16[128,128]{1,0:T(8,128)(2,1)S(1)}, u32[]{:S(2)}, u32[]{:S(2)}) collective-permute-start(bf16[128,128]{1,0:T(8,128)(2,1)S(1)} %get-tuple-element.26), channel_id=1, source_target_pairs={{0,12},{2,14},{4,8},{6,10},{8,4},{10,6},{12,0},{14,2},{1,13},{3,15... | collective-permute-start | bytes 98312 | tf_op jit(solution)/shard_map/ppermute | solution.py:248
  33.9 4.8 %collective-permute-start.15 = (bf16[128,128]{1,0:T(8,128)(2,1)S(1)}, bf16[128,128]{1,0:T(8,128)(2,1)S(1)}, u32[]{:S(2)}, u32[]{:S(2)}) collective-permute-start(bf16[128,128]{1,0:T(8,128)(2,1)S(1)} %get-tuple-element.27), channel_id=1, source_target_pairs={{0,8},{2,10},{4,12},{6,14},{8,0},{10,2},{12,4},{14,6},{1,9},{3,11}... | collective-permute-start | bytes 98312 | tf_op jit(solution)/shard_map/ppermute | solution.py:248
  33.9 4.8 %collective-permute-start.16 = (bf16[128,128]{1,0:T(8,128)(2,1)S(1)}, bf16[128,128]{1,0:T(8,128)(2,1)S(1)}, u32[]{:S(2)}, u32[]{:S(2)}) collective-permute-start(bf16[128,128]{1,0:T(8,128)(2,1)S(1)} %get-tuple-element.28), channel_id=1, source_target_pairs={{0,4},{2,6},{4,0},{6,2},{8,12},{10,14},{12,8},{14,10},{1,5},{3,7},... | collective-permute-start | bytes 98312 | tf_op jit(solution)/shard_map/ppermute | solution.py:248

commit v12 on v11

--- a/solution.py
+++ b/solution.py
@@ -35,13 +35,13 @@
     return [pltpu.with_memory_space_constraint(v, pltpu.HBM) for v in values]
 
 
-def call(body, outs, in_specs, args, scratch=(), flops=0, limit=32, aliases=None):
+def call(body, outs, in_specs, args, scratch=(), flops=0, limit=32, aliases=None, spec=VMEM):
     nbytes = sum(math.prod(a.shape) * jnp.dtype(a.dtype).itemsize for a in list(args) + list(outs))
     return pl.pallas_call(
         body,
         out_shape=list(outs),
         in_specs=in_specs,
-        out_specs=[VMEM] * len(outs),
+        out_specs=[spec] * len(outs),
         scratch_shapes=list(scratch),
         input_output_aliases=aliases or {},
         compiler_params=pltpu.CompilerParams(vmem_limit_bytes=limit * MIB),
@@ -61,6 +61,10 @@
     value = primal - tau * grad
     capped = jnp.where(limited > 0, jnp.minimum(value, upper), value)
     return jnp.maximum(capped, 0.0)
+
+
+def touch_body(part, after, out):
+    del part, after, out
 
 
 def prep_body(far, first_near, *refs):
@@ -134,14 +138,12 @@
         mat[pl.ds(row, tile), pl.ds(column, tile)] = block[...]
 
 
-def place_shares(n_blk, n_col, mat, slots, source, shift, own_part, other_part, nslots):
+def place_share(n_blk, n_col, mat, slots, source, shift, share, core, nslots):
     half = nslots // 2
-    tile = own_part.shape[1]
-    core = lax.axis_index("rep")
-    for part, which in ((own_part, core), (other_part, 1 - core)):
-        for k in range(half):
-            block = part.at[k * tile : (k + 1) * tile, :]
-            place(n_blk, n_col, mat, slots, source, shift, which * half + k, block, nslots)
+    tile = share.shape[1]
+    for k in range(half):
+        block = share.at[k * tile : (k + 1) * tile, :]
+        place(n_blk, n_col, mat, slots, source, shift, core * half + k, block, nslots)
 
 
 def take(n_col, fields, shift, ref, at):
@@ -165,11 +167,13 @@
     copy = pltpu.make_async_copy(blocks_in, blocks, sem)
     copy.start()
     nslots = blocks.shape[2]
+    core = lax.axis_index("rep")
     mat[...] = jnp.zeros(mat.shape, BF16)
     fields[...] = jnp.zeros(fields.shape, BF16)
     sums = take(n_col, fields, (0, 0), own, 0)
     for m, (shift, own_part, other_part) in enumerate(zip(shifts, mine, theirs)):
-        place_shares(n_blk, n_col, mat, slots, m + 1, shift, own_part, other_part, nslots)
+        place_share(n_blk, n_col, mat, slots, m + 1, shift, own_part, core, nslots)
+        place_share(n_blk, n_col, mat, slots, m + 1, shift, other_part, 1 - core, nslots)
         more = take(n_col, fields, shift, own_part, nslots // 2 * own_part.shape[1])
         sums = [a + b for a, b in zip(sums, more)]
     copy.wait()
@@ -178,25 +182,31 @@
     sums_out[...] = jnp.concatenate(sums + [jnp.zeros((6, own.shape[1]), F32)], axis=0)
 
 
-def main_body(n_blk, n_col, shifts, nslots, slots, bounded, mat, fields, sums_in, *refs):
-    count = len(shifts)
-    mine, theirs = refs[:count], refs[count : 2 * count]
-    *outs, scales, _, _, products, turned = refs[2 * count :]
+def relayed_body(n_blk, n_col, shifts, nslots, slots, bounded, mat, fields, sums_in, *refs):
+    mine = refs[: len(shifts)]
+    scales, own, _, _, turned = refs[len(shifts) :]
     part, tile = fields.shape[1], mine[0].shape[1]
-    me_b, me_c = lax.axis_index("blk"), lax.axis_index("col")
     sums = [sums_in[0:1, :], sums_in[1:2, :]]
-    for m, (shift, own_part, other_part) in enumerate(zip(shifts, mine, theirs)):
-        place_shares(n_blk, n_col, mat, slots, m, shift, own_part, other_part, nslots)
+    for m, (shift, own_part) in enumerate(zip(shifts, mine)):
+        place_share(n_blk, n_col, mat, slots, m, shift, own_part, lax.axis_index("rep"), nslots)
         more = take(n_col, fields, shift, own_part, nslots // 2 * tile)
         sums = [a + b for a, b in zip(sums, more)]
-    cost, rhs, upper, primal, dual = (fields[j].astype(F32) for j in range(FIELDS))
     weight = jnp.sqrt(sums[0] + EPS) / jnp.sqrt(sums[1] + EPS)
     rows = jnp.concatenate([ETA / weight, ETA * weight, bounded[...].astype(F32), jnp.zeros((5, tile), F32)], axis=0)
     scales[...] = rows
     turned[...] = jnp.concatenate([rows, jnp.zeros((tile - 8, tile), F32)], axis=0).T
-    own = turned[pl.ds(pl.multiple_of(me_b * part, part), part), :]
+    own[...] = turned[pl.ds(pl.multiple_of(lax.axis_index("blk") * part, part), part), :]
+
+
+def main_body(n_blk, n_col, shifts, nslots, slots, mat, fields, own, *refs):
+    theirs = refs[: len(shifts)]
+    *outs, _, products = refs[len(shifts) :]
+    part, tile = fields.shape[1], theirs[0].shape[1]
+    me_b, me_c = lax.axis_index("blk"), lax.axis_index("col")
+    for m, (shift, other_part) in enumerate(zip(shifts, theirs)):
+        place_share(n_blk, n_col, mat, slots, m, shift, other_part, 1 - lax.axis_index("rep"), nslots)
+    cost, rhs, upper, primal, dual = (fields[j].astype(F32) for j in range(FIELDS))
     tau, sigma, limited = own[:, 0:1], own[:, 1:2], own[:, 2:3]
-
     for step in range(ITERS):
         kty = jnp.dot(dual.astype(BF16), mat[...], preferred_element_type=F32)
         products[2 * step] = kty.astype(BF16)
@@ -291,16 +301,26 @@
         [slots_of([own] + mine), *pinned([blocks]), own] + mine + other_core(mine),
         scratch=[pltpu.VMEM(blocks.shape, BF16), pltpu.SemaphoreType.DMA],
     )
+    last = list(late)[-1]
+    late[last] = call(touch_body, [held(late[last].shape, BF16)], [ANY, ANY], [late[last], sums], aliases={0: 0}, spec=ANY)[0]
     shifts, mine = list(late), list(late.values())
-    *products, scales, _, _ = call(
+    slots = slots_of(mine)
+    scales, own_scales, mat, fields = call(
+        functools.partial(relayed_body, n_blk, n_col, shifts, nslots),
+        [held((8, scn), F32), held((part, tile), F32), held(mat.shape, BF16), held(fields.shape, BF16)],
+        [SMEM] + [VMEM] * (4 + len(mine)),
+        [slots, limits, mat, fields, sums] + mine,
+        scratch=[pltpu.VMEM((tile, scn), F32)],
+        aliases={2: 2, 3: 3},
+    )
+    *products, _ = call(
         functools.partial(main_body, n_blk, n_col, shifts, nslots),
-        [held((2 * ITERS * part, tile), BF16)] * n_blk
-        + [like((8, scn), F32), held(mat.shape, BF16), held(fields.shape, BF16)],
-        [SMEM] + [VMEM] * (4 + 2 * len(mine)),
-        [slots_of(mine), limits, mat, fields, sums] + mine + other_core(mine),
-        scratch=[pltpu.VMEM((2 * ITERS, part, n * tile), BF16), pltpu.VMEM((tile, scn), F32)],
+        [held((2 * ITERS * part, tile), BF16)] * n_blk + [held(mat.shape, BF16)],
+        [SMEM] + [VMEM] * (3 + len(mine)),
+        [slots, mat, fields, own_scales] + other_core(mine),
+        scratch=[pltpu.VMEM((2 * ITERS, part, n * tile), BF16)],
         flops=4 * ITERS * n * n * tile * tile * part,
-        aliases={2: n_blk + 1, 3: n_blk + 2},
+        aliases={1: n_blk},
     )
     order = [0, *range(n_blk - 1, 0, -1)]
     parts = [products[t] if t == 0 else move(products[t], t, 0) for t in order]

time: 39.7 us -> 40.8 us (1.028)
  Pallas kernels: 6.99 us -> 7.63 us
    ppermute x7, waiting for transfers between devices: 0.02 us -> 0.66 us  [other_core(): return [lax.ppermute(v[:top], 'rep', [(0, 1), (1, 0)]) for v in values]]
    pallas_call x5 -> x7, Pallas kernels: 6.99 us -> 7.63 us  [call(): pl.pallas_call(body, out_shape=list(outs), in_specs=in_specs, out_specs=[...]
    ppermute x10, waiting for transfers between devices: 12.5 us -> 12 us  [move(): return lax.ppermute(value, ('blk', 'col'), pairs)]
  transfers between devices with their start and end apart: 17 -> 17, of which waited for: 7 -> 9; matrix products, arithmetic and copies ran while one was open for 0% -> 0% of each run, Pallas kernels for 4% -> 6%
where the time goes in v12:
time: 40.8 us; the launch traced here: 40.6 us
  starting transfers between devices  18.6 us (46%)
  waiting for transfers between devices  12.6 us (31%)
  Pallas kernels  7.63 us (19%)
  between operations  1.56 us (4%)
    ppermute x10, starting transfers between devices, move(): return lax.ppermute(value, ('blk', 'col'), pairs)  17.1 us
    ppermute x10, waiting for transfers between devices, move(): return lax.ppermute(value, ('blk', 'col'), pairs)  12 us
    pallas_call x7, Pallas kernels, call(): pl.pallas_call(body, out_shape=list(outs), in_specs=in_specs, out_specs=[...  7.63 us
    ppermute x7, starting transfers between devices, other_core(): return [lax.ppermute(v[:top], 'rep', [(0, 1), (1, 0)]) for v in values]  1.49 us
  transfers between devices with their start and end apart: 17, of which 9 were waited for; matrix products, arithmetic and copies ran while one was open for 0% of the time, Pallas kernels for 6%

profile of v12, /device:TPU:0, one launch (start us, length us, event | category | flops | bytes accessed | tf_op | source)
XLA Modules:
  0.0 40.6 jit_solution(9279838358061762032)
XLA Ops:
  0.6 0.0 copy-start.5
  1.3 1.5 %shard_map.104 = (bf16[720,128]{1,0:T(8,128)(2,1)S(1)}, bf16[560,128]{1,0:T(8,128)(2,1)S(1)}, bf16[560,128]{1,0:T(8,128)(2,1)S(1)}, bf16[176,128]{1,0:T(8,128)(2,1)S(1)}) custom-call(s32[1,1]{1,0:T(1,128)S(6)} %copy.19.refs_0_, f32[128,128]{1,0:T(8,128)} %refs_5_.3, f32[128,128]{1,0:T(8,128)} %refs_6_.3, f32[128,128]{1,0:T(8,128)} %refs_7_.3, ...), custom_call_target="tpu_custom_call" | custom-call | bytes 1040412 | tf_op jit(solution)/shard_map/pallas_call | solution.py:40
  2.8 4.1 %collective-permute-start = (bf16[720,128]{1,0:T(8,128)(2,1)S(1)}, bf16[720,128]{1,0:T(8,128)(2,1)S(1)}, u32[]{:S(2)}, u32[]{:S(2)}) collective-permute-start(bf16[720,128]{1,0:T(8,128)(2,1)S(1)} %get-tuple-element.19), channel_id=1, source_target_pairs={{0,8},{2,10},{4,12},{6,14},{8,0},{10,2},{12,4},{14,6},{1,9},{3,11}... | collective-permute-start | bytes 552968 | tf_op jit(solution)/shard_map/ppermute | solution.py:258
  6.9 1.6 %collective-permute-start.5 = (bf16[560,128]{1,0:T(8,128)(2,1)S(1)}, bf16[560,128]{1,0:T(8,128)(2,1)S(1)}, u32[]{:S(2)}, u32[]{:S(2)}) collective-permute-start(bf16[560,128]{1,0:T(8,128)(2,1)S(1)} %get-tuple-element.24), channel_id=1, source_target_pairs={{0,4},{2,6},{4,0},{6,2},{8,12},{10,14},{12,8},{14,10},{1,5},{3,7},... | collective-permute-start | bytes 430088 | tf_op jit(solution)/shard_map/ppermute | solution.py:258
  8.5 1.5 %collective-permute-start.4 = (bf16[560,128]{1,0:T(8,128)(2,1)S(1)}, bf16[560,128]{1,0:T(8,128)(2,1)S(1)}, u32[]{:S(2)}, u32[]{:S(2)}) collective-permute-start(bf16[560,128]{1,0:T(8,128)(2,1)S(1)} %get-tuple-element.23), channel_id=1, source_target_pairs={{0,2},{2,0},{4,6},{6,4},{8,10},{10,8},{12,14},{14,12},{1,3},{3,1},... | collective-permute-start | bytes 430088 | tf_op jit(solution)/shard_map/ppermute | solution.py:258
  10.0 3.9 %collective-permute-done.5.refs_2_ = bf16[560,128]{1,0:T(8,128)(2,1)S(1)} collective-permute-done((bf16[560,128]{1,0:T(8,128)(2,1)S(1)}, bf16[560,128]{1,0:T(8,128)(2,1)S(1)}, u32[]{:S(2)}, u32[]{:S(2)}) %collective-permute-start.5) | collective-permute-done | bytes 143392 | tf_op jit(solution)/shard_map/ppermute | solution.py:258
  13.9 1.5 %collective-permute-start.6 = (bf16[560,128]{1,0:T(8,128)(2,1)S(1)}, bf16[560,128]{1,0:T(8,128)(2,1)S(1)}, u32[]{:S(2)}, u32[]{:S(2)}) collective-permute-start(bf16[560,128]{1,0:T(8,128)(2,1)S(1)} %collective-permute-done.5.refs_2_), channel_id=1, source_target_pairs={{0,2},{2,0},{4,6},{6,4},{8,10},{10,8},{12,14},{14,12},{1,3},{3,1},... | collective-permute-start | bytes 430088 | tf_op jit(solution)/shard_map/ppermute | solution.py:258
  15.4 0.1 collective-permute-done.came.refs_0_
  15.5 2.5 %collective-permute-start.2 = (bf16[560,128]{1,0:T(8,128)(2,1)S(1)}, bf16[560,128]{1,0:T(8,128)(2,1)S(1)}, u32[]{:S(2)}, u32[]{:S(2)}) collective-permute-start(bf16[560,128]{1,0:T(8,128)(2,1)S(1)} %get-tuple-element.21), channel_id=1, source_target_pairs={{0,4},{2,6},{4,0},{6,2},{8,12},{10,14},{12,8},{14,10},{1,5},{3,7},... | collective-permute-start | bytes 430088 | tf_op jit(solution)/shard_map/ppermute | solution.py:258
  18.0 0.5 %collective-permute-start.1 = (bf16[560,128]{1,0:T(8,128)(2,1)S(1)}, bf16[560,128]{1,0:T(8,128)(2,1)S(1)}, u32[]{:S(2)}, u32[]{:S(2)}) collective-permute-start(bf16[560,128]{1,0:T(8,128)(2,1)S(1)} %get-tuple-element.20), channel_id=1, source_target_pairs={{0,2},{2,0},{4,6},{6,4},{8,10},{10,8},{12,14},{14,12},{1,3},{3,1},... | collective-permute-start | bytes 430088 | tf_op jit(solution)/shard_map/ppermute | solution.py:258
  18.5 1.0 %collective-permute-start.3 = (bf16[560,128]{1,0:T(8,128)(2,1)S(1)}, bf16[560,128]{1,0:T(8,128)(2,1)S(1)}, u32[]{:S(2)}, u32[]{:S(2)}) collective-permute-start(bf16[560,128]{1,0:T(8,128)(2,1)S(1)} %get-tuple-element.21), channel_id=1, source_target_pairs={{0,6},{2,4},{4,2},{6,0},{8,14},{10,12},{12,10},{14,8},{1,7},{3,5},... | collective-permute-start | bytes 430088 | tf_op jit(solution)/shard_map/ppermute | solution.py:258
  19.5 0.0 collective-permute-done.4.refs_1_
  19.5 0.1 collective-permute-start.9
  19.7 0.0 collective-permute-done.6.refs_3_
  19.7 0.5 %collective-permute-start.8 = (bf16[384,128]{1,0:T(8,128)(2,1)S(1)}, bf16[384,128]{1,0:T(8,128)(2,1)S(1)}, u32[]{:S(2)}, u32[]{:S(2)}) collective-permute-start(bf16[384,128]{1,0:T(8,128)(2,1)S(1)} %slice.67), channel_id=1, source_target_pairs={{0,1},{1,0},{2,3},{3,2},{4,5},{5,4},{6,7},{7,6},{8,9},{9,8},{10,11... | collective-permute-start | bytes 294920 | tf_op jit(solution)/shard_map/ppermute | solution.py:280
  20.2 1.8 %collective-permute-done.2.refs_1_ = bf16[560,128]{1,0:T(8,128)(2,1)S(1)} collective-permute-done((bf16[560,128]{1,0:T(8,128)(2,1)S(1)}, bf16[560,128]{1,0:T(8,128)(2,1)S(1)}, u32[]{:S(2)}, u32[]{:S(2)}) %collective-permute-start.2) | collective-permute-done | bytes 143392 | tf_op jit(solution)/shard_map/ppermute | solution.py:258
  22.0 0.0 collective-permute-start.7
  22.0 3.7 %collective-permute-done.1.refs_0_ = bf16[560,128]{1,0:T(8,128)(2,1)S(1)} collective-permute-done((bf16[560,128]{1,0:T(8,128)(2,1)S(1)}, bf16[560,128]{1,0:T(8,128)(2,1)S(1)}, u32[]{:S(2)}, u32[]{:S(2)}) %collective-permute-start.1) | collective-permute-done | bytes 143392 | tf_op jit(solution)/shard_map/ppermute | solution.py:258
  25.7 0.0 collective-permute-start.10
  25.9 0.0 collective-permute-done.9.refs_6_
  25.9 0.6 %collective-permute-start.12 = (bf16[384,128]{1,0:T(8,128)(2,1)S(1)}, bf16[384,128]{1,0:T(8,128)(2,1)S(1)}, u32[]{:S(2)}, u32[]{:S(2)}) collective-permute-start(bf16[384,128]{1,0:T(8,128)(2,1)S(1)} %slice.72), channel_id=1, source_target_pairs={{0,1},{1,0},{2,3},{3,2},{4,5},{5,4},{6,7},{7,6},{8,9},{9,8},{10,11... | collective-permute-start | bytes 294920 | tf_op jit(solution)/shard_map/ppermute | solution.py:280
  26.5 0.0 collective-permute-done.8.refs_5_
  26.5 0.1 collective-permute-start.11
  26.6 0.0 collective-permute-done.7.refs_4_
  26.6 0.5 %collective-permute-done.10.refs_7_ = bf16[384,128]{1,0:T(8,128)(2,1)S(1)} collective-permute-done((bf16[384,128]{1,0:T(8,128)(2,1)S(1)}, bf16[384,128]{1,0:T(8,128)(2,1)S(1)}, u32[]{:S(2)}, u32[]{:S(2)}) %collective-permute-start.10) | collective-permute-done | bytes 98336 | tf_op jit(solution)/shard_map/ppermute | solution.py:280
  27.0 1.6 %shard_map.106 = (bf16[1024,1024]{1,0:T(8,128)(2,1)S(1)}, bf16[5,32,1024]{2,1,0:T(8,128)(2,1)S(1)}, f32[8,128]{1,0:T(8,128)S(1)}) custom-call(s32[5,7]{1,0:T(8,128)S(1)} %convert_element_type.6.slots, bf16[1,1,6,128,128]{4,3,2,1,0:T(8,128)(2,1)} %blocks_in.1, bf16[176,128]{1,0:T(8,128)(2,1)S(1)} %get-tuple-element.22.own, ...), custom_call_target="tpu_custom_call" | custom-call | bytes 3678348 | tf_op jit(solution)/shard_map/pallas_call | solution.py:40
  28.6 0.0 collective-permute-done.3.part
  28.7 0.2 collective-permute-start.13
  28.9 0.0 copy-done.5
  28.9 0.0 copy-start
  28.9 0.0 copy-start.1
  29.0 0.0 copy-start.2
  29.0 0.0 copy-start.3
  29.0 0.0 copy-start.4
  29.0 0.9 %shard_map.108 = (f32[8,128]{1,0:T(8,128)S(1)}, f32[32,128]{1,0:T(8,128)S(1)}, bf16[1024,1024]{1,0:T(8,128)(2,1)S(1)}, bf16[5,32,1024]{2,1,0:T(8,128)(2,1)S(1)}) custom-call(s32[3,7]{1,0:T(4,128)S(1)} %maximum_convert_fusion.slots, s32[1,128]{1,0:T(1,128)S(1)} %bitcast.1, ...), custom_call_target="tpu_custom_call", output_to_operand_aliasing={{2}: (2, {}), {3}: (3, {})} | custom-call | bytes 5304916 | tf_op jit(solution)/shard_map/pallas_call | solution.py:40
  29.9 0.0 collective-permute-done.12.refs_1_
  29.9 0.0 collective-permute-done.11.refs_0_
  29.9 0.2 collective-permute-done.13.refs_2_
  30.1 2.8 %shard_map.109 = (bf16[128,128]{1,0:T(8,128)(2,1)S(1)}, bf16[128,128]{1,0:T(8,128)(2,1)S(1)}, bf16[128,128]{1,0:T(8,128)(2,1)S(1)}, bf16[128,128]{1,0:T(8,128)(2,1)S(1)}, bf16[1024,1024]{1,0:T(8,128)(2,1)S(1)}) custom-call(s32[3,7]{1,0:T(4,128)S(1)} %maximum_convert_fusion.slots, ...), custom_call_target="tpu_custom_call", output_to_operand_aliasing={{4}: (1, {})} | custom-call | flops 268435456 | bytes 4964436 | tf_op jit(solution)/shard_map/pallas_call | solution.py:40
  32.9 0.3 collective-permute-start.14
  33.2 2.7 %collective-permute-start.15 = (bf16[128,128]{1,0:T(8,128)(2,1)S(1)}, bf16[128,128]{1,0:T(8,128)(2,1)S(1)}, u32[]{:S(2)}, u32[]{:S(2)}) collective-permute-start(bf16[128,128]{1,0:T(8,128)(2,1)S(1)} %get-tuple-element.33), channel_id=1, source_target_pairs={{0,8},{2,10},{4,12},{6,14},{8,0},{10,2},{12,4},{14,6},{1,9},{3,11}... | collective-permute-start | bytes 98312 | tf_op jit(solution)/shard_map/ppermute | solution.py:258
  35.9 1.5 %collective-permute-start.16 = (bf16[128,128]{1,0:T(8,128)(2,1)S(1)}, bf16[128,128]{1,0:T(8,128)(2,1)S(1)}, u32[]{:S(2)}, u32[]{:S(2)}) collective-permute-start(bf16[128,128]{1,0:T(8,128)(2,1)S(1)} %get-tuple-element.34), channel_id=1, source_target_pairs={{0,4},{2,6},{4,0},{6,2},{8,12},{10,14},{12,8},{14,10},{1,5},{3,7},... | collective-permute-start | bytes 98312 | tf_op jit(solution)/shard_map/ppermute | solution.py:258
  37.4 1.4 %collective-permute-done.14.refs_1_ = bf16[128,128]{1,0:T(8,128)(2,1)S(1)} collective-permute-done((bf16[128,128]{1,0:T(8,128)(2,1)S(1)}, bf16[128,128]{1,0:T(8,128)(2,1)S(1)}, u32[]{:S(2)}, u32[]{:S(2)}) %collective-permute-start.14) | collective-permute-done | bytes 32800 | tf_op jit(solution)/shard_map/ppermute | solution.py:258
  38.7 0.1 collective-permute-done.15.refs_2_
  38.9 0.9 %collective-permute-done.16.refs_3_ = bf16[128,128]{1,0:T(8,128)(2,1)S(1)} collective-permute-done((bf16[128,128]{1,0:T(8,128)(2,1)S(1)}, bf16[128,128]{1,0:T(8,128)(2,1)S(1)}, u32[]{:S(2)}, u32[]{:S(2)}) %collective-permute-start.16) | collective-permute-done | bytes 32800 | tf_op jit(solution)/shard_map/ppermute | solution.py:258
  39.8 0.0 copy-done
  39.8 0.0 copy-done.1
  39.8 0.0 copy-done.2
  39.8 0.0 copy-done.3
  39.8 0.0 copy-done.4
  39.8 0.8 %shard_map.110 = (f32[128,128]{1,0:T(8,128)}, f32[128,128]{1,0:T(8,128)}) custom-call(bf16[128,128]{1,0:T(8,128)(2,1)S(1)} %get-tuple-element.31.refs_0_, bf16[128,128]{1,0:T(8,128)(2,1)S(1)} %collective-permute-done.14.refs_1_, bf16[128,128]{1,0:T(8,128)(2,1)S(1)} %collective-permute-done.15.refs_2_, bf16[128,128]{1,0:T(8,128)(2,1)S(1)} %collective-permute-done.16.refs_3_, ...), custom_call_target="tpu_custom_call" | custom-call | bytes 594432 | tf_op jit(solution)/shard_map/pallas_call | solution.py:40
  (20 shorter events, 0.2 us)
Async XLA Ops:
  0.6 28.3 %copy-start.5 = (s32[128]{0:T(128)S(1)}, s32[128]{0:T(128)}, u32[]{:S(2)}) copy-start(s32[128]{0:T(128)} %param.17) | copy-start | bytes 1540
  2.8 12.7 %collective-permute-start = (bf16[720,128]{1,0:T(8,128)(2,1)S(1)}, bf16[720,128]{1,0:T(8,128)(2,1)S(1)}, u32[]{:S(2)}, u32[]{:S(2)}) collective-permute-start(bf16[720,128]{1,0:T(8,128)(2,1)S(1)} %get-tuple-element.19), channel_id=1, source_target_pairs={{0,8},{2,10},{4,12},{6,14},{8,0},{10,2},{12,4},{14,6},{1,9},{3,11}... | collective-permute-start | bytes 552968 | tf_op jit(solution)/shard_map/ppermute | solution.py:258
  6.9 7.0 %collective-permute-start.5 = (bf16[560,128]{1,0:T(8,128)(2,1)S(1)}, bf16[560,128]{1,0:T(8,128)(2,1)S(1)}, u32[]{:S(2)}, u32[]{:S(2)}) collective-permute-start(bf16[560,128]{1,0:T(8,128)(2,1)S(1)} %get-tuple-element.24), channel_id=1, source_target_pairs={{0,4},{2,6},{4,0},{6,2},{8,12},{10,14},{12,8},{14,10},{1,5},{3,7},... | collective-permute-start | bytes 430088 | tf_op jit(solution)/shard_map/ppermute | solution.py:258
  8.5 11.1 %collective-permute-start.4 = (bf16[560,128]{1,0:T(8,128)(2,1)S(1)}, bf16[560,128]{1,0:T(8,128)(2,1)S(1)}, u32[]{:S(2)}, u32[]{:S(2)}) collective-permute-start(bf16[560,128]{1,0:T(8,128)(2,1)S(1)} %get-tuple-element.23), channel_id=1, source_target_pairs={{0,2},{2,0},{4,6},{6,4},{8,10},{10,8},{12,14},{14,12},{1,3},{3,1},... | collective-permute-start | bytes 430088 | tf_op jit(solution)/shard_map/ppermute | solution.py:258
  13.9 5.7 %collective-permute-start.6 = (bf16[560,128]{1,0:T(8,128)(2,1)S(1)}, bf16[560,128]{1,0:T(8,128)(2,1)S(1)}, u32[]{:S(2)}, u32[]{:S(2)}) collective-permute-start(bf16[560,128]{1,0:T(8,128)(2,1)S(1)} %collective-permute-done.5.refs_2_), channel_id=1, source_target_pairs={{0,2},{2,0},{4,6},{6,4},{8,10},{10,8},{12,14},{14,12},{1,3},{3,1},... | collective-permute-start | bytes 430088 | tf_op jit(solution)/shard_map/ppermute | solution.py:258
  15.5 6.5 %collective-permute-start.2 = (bf16[560,128]{1,0:T(8,128)(2,1)S(1)}, bf16[560,128]{1,0:T(8,128)(2,1)S(1)}, u32[]{:S(2)}, u32[]{:S(2)}) collective-permute-start(bf16[560,128]{1,0:T(8,128)(2,1)S(1)} %get-tuple-element.21), channel_id=1, source_target_pairs={{0,4},{2,6},{4,0},{6,2},{8,12},{10,14},{12,8},{14,10},{1,5},{3,7},... | collective-permute-start | bytes 430088 | tf_op jit(solution)/shard_map/ppermute | solution.py:258
  18.0 7.7 %collective-permute-start.1 = (bf16[560,128]{1,0:T(8,128)(2,1)S(1)}, bf16[560,128]{1,0:T(8,128)(2,1)S(1)}, u32[]{:S(2)}, u32[]{:S(2)}) collective-permute-start(bf16[560,128]{1,0:T(8,128)(2,1)S(1)} %get-tuple-element.20), channel_id=1, source_target_pairs={{0,2},{2,0},{4,6},{6,4},{8,10},{10,8},{12,14},{14,12},{1,3},{3,1},... | collective-permute-start | bytes 430088 | tf_op jit(solution)/shard_map/ppermute | solution.py:258
  18.5 10.1 %collective-permute-start.3 = (bf16[560,128]{1,0:T(8,128)(2,1)S(1)}, bf16[560,128]{1,0:T(8,128)(2,1)S(1)}, u32[]{:S(2)}, u32[]{:S(2)}) collective-permute-start(bf16[560,128]{1,0:T(8,128)(2,1)S(1)} %get-tuple-element.21), channel_id=1, source_target_pairs={{0,6},{2,4},{4,2},{6,0},{8,14},{10,12},{12,10},{14,8},{1,7},{3,5},... | collective-permute-start | bytes 430088 | tf_op jit(solution)/shard_map/ppermute | solution.py:258
  19.5 6.3 %collective-permute-start.9 = (bf16[384,128]{1,0:T(8,128)(2,1)S(1)}, bf16[384,128]{1,0:T(8,128)(2,1)S(1)}, u32[]{:S(2)}, u32[]{:S(2)}) collective-permute-start(bf16[384,128]{1,0:T(8,128)(2,1)S(1)} %slice.68), channel_id=1, source_target_pairs={{0,1},{1,0},{2,3},{3,2},{4,5},{5,4},{6,7},{7,6},{8,9},{9,8},{10,11... | collective-permute-start | bytes 294920 | tf_op jit(solution)/shard_map/ppermute | solution.py:280
  19.7 6.8 %collective-permute-start.8 = (bf16[384,128]{1,0:T(8,128)(2,1)S(1)}, bf16[384,128]{1,0:T(8,128)(2,1)S(1)}, u32[]{:S(2)}, u32[]{:S(2)}) collective-permute-start(bf16[384,128]{1,0:T(8,128)(2,1)S(1)} %slice.67), channel_id=1, source_target_pairs={{0,1},{1,0},{2,3},{3,2},{4,5},{5,4},{6,7},{7,6},{8,9},{9,8},{10,11... | collective-permute-start | bytes 294920 | tf_op jit(solution)/shard_map/ppermute | solution.py:280
  22.0 4.5 %collective-permute-start.7 = (bf16[384,128]{1,0:T(8,128)(2,1)S(1)}, bf16[384,128]{1,0:T(8,128)(2,1)S(1)}, u32[]{:S(2)}, u32[]{:S(2)}) collective-permute-start(bf16[384,128]{1,0:T(8,128)(2,1)S(1)} %slice.66), channel_id=1, source_target_pairs={{0,1},{1,0},{2,3},{3,2},{4,5},{5,4},{6,7},{7,6},{8,9},{9,8},{10,11... | collective-permute-start | bytes 294920 | tf_op jit(solution)/shard_map/ppermute | solution.py:280
  25.7 1.3 %collective-permute-start.10 = (bf16[384,128]{1,0:T(8,128)(2,1)S(1)}, bf16[384,128]{1,0:T(8,128)(2,1)S(1)}, u32[]{:S(2)}, u32[]{:S(2)}) collective-permute-start(bf16[384,128]{1,0:T(8,128)(2,1)S(1)} %slice.69), channel_id=1, source_target_pairs={{0,1},{1,0},{2,3},{3,2},{4,5},{5,4},{6,7},{7,6},{8,9},{9,8},{10,11... | collective-permute-start | bytes 294920 | tf_op jit(solution)/shard_map/ppermute | solution.py:280
  25.9 4.0 %collective-permute-start.12 = (bf16[384,128]{1,0:T(8,128)(2,1)S(1)}, bf16[384,128]{1,0:T(8,128)(2,1)S(1)}, u32[]{:S(2)}, u32[]{:S(2)}) collective-permute-start(bf16[384,128]{1,0:T(8,128)(2,1)S(1)} %slice.72), channel_id=1, source_target_pairs={{0,1},{1,0},{2,3},{3,2},{4,5},{5,4},{6,7},{7,6},{8,9},{9,8},{10,11... | collective-permute-start | bytes 294920 | tf_op jit(solution)/shard_map/ppermute | solution.py:280
  26.5 3.4 %collective-permute-start.11 = (bf16[384,128]{1,0:T(8,128)(2,1)S(1)}, bf16[384,128]{1,0:T(8,128)(2,1)S(1)}, u32[]{:S(2)}, u32[]{:S(2)}) collective-permute-start(bf16[384,128]{1,0:T(8,128)(2,1)S(1)} %slice.71), channel_id=1, source_target_pairs={{0,1},{1,0},{2,3},{3,2},{4,5},{5,4},{6,7},{7,6},{8,9},{9,8},{10,11... | collective-permute-start | bytes 294920 | tf_op jit(solution)/shard_map/ppermute | solution.py:280
  28.7 1.4 %collective-permute-start.13 = (bf16[384,128]{1,0:T(8,128)(2,1)S(1)}, bf16[384,128]{1,0:T(8,128)(2,1)S(1)}, u32[]{:S(2)}, u32[]{:S(2)}) collective-permute-start(bf16[384,128]{1,0:T(8,128)(2,1)S(1)} %slice.73), channel_id=1, source_target_pairs={{0,1},{1,0},{2,3},{3,2},{4,5},{5,4},{6,7},{7,6},{8,9},{9,8},{10,11... | collective-permute-start | bytes 294920 | tf_op jit(solution)/shard_map/ppermute | solution.py:280
  28.9 10.8 %copy-start = (f32[128,128]{1,0:T(8,128)S(1)}, f32[128,128]{1,0:T(8,128)}, u32[]{:S(2)}) copy-start(f32[128,128]{1,0:T(8,128)} %refs_5_.3) | copy-start | bytes 196612
  28.9 10.8 %copy-start.1 = (f32[128,128]{1,0:T(8,128)S(1)}, f32[128,128]{1,0:T(8,128)}, u32[]{:S(2)}) copy-start(f32[128,128]{1,0:T(8,128)} %refs_6_.3) | copy-start | bytes 196612
  29.0 10.8 %copy-start.2 = (f32[128,128]{1,0:T(8,128)S(1)}, f32[128,128]{1,0:T(8,128)}, u32[]{:S(2)}) copy-start(f32[128,128]{1,0:T(8,128)} %refs_7_.3) | copy-start | bytes 196612
  29.0 10.8 %copy-start.3 = (f32[128,128]{1,0:T(8,128)S(1)}, f32[128,128]{1,0:T(8,128)}, u32[]{:S(2)}) copy-start(f32[128,128]{1,0:T(8,128)} %refs_8_.1) | copy-start | bytes 196612
  29.0 10.8 %copy-start.4 = (f32[128,128]{1,0:T(8,128)S(1)}, f32[128,128]{1,0:T(8,128)}, u32[]{:S(2)}) copy-start(f32[128,128]{1,0:T(8,128)} %refs_9_.1) | copy-start | bytes 196612
  32.9 5.8 %collective-permute-start.14 = (bf16[128,128]{1,0:T(8,128)(2,1)S(1)}, bf16[128,128]{1,0:T(8,128)(2,1)S(1)}, u32[]{:S(2)}, u32[]{:S(2)}) collective-permute-start(bf16[128,128]{1,0:T(8,128)(2,1)S(1)} %get-tuple-element.32), channel_id=1, source_target_pairs={{0,12},{2,14},{4,8},{6,10},{8,4},{10,6},{12,0},{14,2},{1,13},{3,15... | collective-permute-start | bytes 98312 | tf_op jit(solution)/shard_map/ppermute | solution.py:258
  33.2 5.7 %collective-permute-start.15 = (bf16[128,128]{1,0:T(8,128)(2,1)S(1)}, bf16[128,128]{1,0:T(8,128)(2,1)S(1)}, u32[]{:S(2)}, u32[]{:S(2)}) collective-permute-start(bf16[128,128]{1,0:T(8,128)(2,1)S(1)} %get-tuple-element.33), channel_id=1, source_target_pairs={{0,8},{2,10},{4,12},{6,14},{8,0},{10,2},{12,4},{14,6},{1,9},{3,11}... | collective-permute-start | bytes 98312 | tf_op jit(solution)/shard_map/ppermute | solution.py:258
  35.9 3.9 %collective-permute-start.16 = (bf16[128,128]{1,0:T(8,128)(2,1)S(1)}, bf16[128,128]{1,0:T(8,128)(2,1)S(1)}, u32[]{:S(2)}, u32[]{:S(2)}) collective-permute-start(bf16[128,128]{1,0:T(8,128)(2,1)S(1)} %get-tuple-element.34), channel_id=1, source_target_pairs={{0,4},{2,6},{4,0},{6,2},{8,12},{10,14},{12,8},{14,10},{1,5},{3,7},... | collective-permute-start | bytes 98312 | tf_op jit(solution)/shard_map/ppermute | solution.py:258

commit v13 on v11

--- a/solution.py
+++ b/solution.py
@@ -35,13 +35,13 @@
     return [pltpu.with_memory_space_constraint(v, pltpu.HBM) for v in values]
 
 
-def call(body, outs, in_specs, args, scratch=(), flops=0, limit=32, aliases=None):
+def call(body, outs, in_specs, args, scratch=(), flops=0, limit=32, aliases=None, specs=None):
     nbytes = sum(math.prod(a.shape) * jnp.dtype(a.dtype).itemsize for a in list(args) + list(outs))
     return pl.pallas_call(
         body,
         out_shape=list(outs),
         in_specs=in_specs,
-        out_specs=[VMEM] * len(outs),
+        out_specs=specs or [VMEM] * len(outs),
         scratch_shapes=list(scratch),
         input_output_aliases=aliases or {},
         compiler_params=pltpu.CompilerParams(vmem_limit_bytes=limit * MIB),
@@ -114,7 +114,8 @@
         out[out.shape[0] - INFO :, :] = info
 
 
-def relay_body(top, part, came, *outs):
+def relay_body(top, part, came, after, *outs):
+    del after
     for t, out in enumerate(outs):
         out[0:top, :] = came[0:top, :]
         at = top + t * FIELDS * part
@@ -158,24 +159,32 @@
     return sums
 
 
-def early_body(n_blk, n_col, shifts, slots, blocks_in, own, *refs):
-    count = len(shifts)
-    mine, theirs = refs[:count], refs[count : 2 * count]
-    mat, fields, sums_out, blocks, sem = refs[2 * count :]
+def base_body(n_blk, n_col, slots, blocks_in, own, mat, fields, sums_out, blocks, sem):
     copy = pltpu.make_async_copy(blocks_in, blocks, sem)
     copy.start()
     nslots = blocks.shape[2]
     mat[...] = jnp.zeros(mat.shape, BF16)
     fields[...] = jnp.zeros(fields.shape, BF16)
     sums = take(n_col, fields, (0, 0), own, 0)
-    for m, (shift, own_part, other_part) in enumerate(zip(shifts, mine, theirs)):
-        place_shares(n_blk, n_col, mat, slots, m + 1, shift, own_part, other_part, nslots)
-        more = take(n_col, fields, shift, own_part, nslots // 2 * own_part.shape[1])
-        sums = [a + b for a, b in zip(sums, more)]
+    sums_out[...] = jnp.concatenate(sums + [jnp.zeros((6, own.shape[1]), F32)], axis=0)
     copy.wait()
     for k in range(nslots):
         place(n_blk, n_col, mat, slots, 0, (0, 0), k, blocks.at[0, 0, k], nslots)
-    sums_out[...] = jnp.concatenate(sums + [jnp.zeros((6, own.shape[1]), F32)], axis=0)
+
+
+def early_body(n_blk, n_col, shifts, nslots, slots, late_slots, mat, fields, sums_in, *refs):
+    count = len(shifts)
+    mine, theirs = refs[:count], refs[count : 2 * count]
+    _, _, sums_out, slots_out = refs[2 * count :]
+    for source in range(slots_out.shape[0]):
+        for k in range(slots_out.shape[1]):
+            slots_out[source, k] = late_slots[source, k]
+    sums = [sums_in[0:1, :], sums_in[1:2, :]]
+    for m, (shift, own_part, other_part) in enumerate(zip(shifts, mine, theirs)):
+        place_shares(n_blk, n_col, mat, slots, m, shift, own_part, other_part, nslots)
+        more = take(n_col, fields, shift, own_part, nslots // 2 * own_part.shape[1])
+        sums = [a + b for a, b in zip(sums, more)]
+    sums_out[...] = jnp.concatenate(sums + [jnp.zeros((6, sums_in.shape[1]), F32)], axis=0)
 
 
 def main_body(n_blk, n_col, shifts, nslots, slots, bounded, mat, fields, sums_in, *refs):
@@ -279,17 +288,30 @@
     for t in range(1, far):
         for s in range(1, n_col):
             early[t, s] = move(early[t, 0], 0, s)
+    mat, fields, sums = call(
+        functools.partial(base_body, n_blk, n_col),
+        [held((n * tile, n * tile), BF16), held((FIELDS, part, n * tile), BF16), held((8, scn), F32)],
+        [SMEM, ANY, VMEM],
+        [slots_of([own]), *pinned([blocks]), own],
+        scratch=[pltpu.VMEM(blocks.shape, BF16), pltpu.SemaphoreType.DMA],
+    )
     relayed = call(
-        functools.partial(relay_body, top, part), [held((size, tile), BF16)] * far, [VMEM], [early[far, 0]]
+        functools.partial(relay_body, top, part),
+        [held((size, tile), BF16)] * far,
+        [VMEM, VMEM],
+        [early[far, 0], sums],
     )
     late = {(far + t, s): move(relayed[t], t, s) for t, s in near}
     shifts, mine = list(early), list(early.values())
-    mat, fields, sums = call(
-        functools.partial(early_body, n_blk, n_col, shifts),
-        [held((n * tile, n * tile), BF16), held((FIELDS, part, n * tile), BF16), held((8, scn), F32)],
-        [SMEM, ANY] + [VMEM] * (1 + 2 * len(mine)),
-        [slots_of([own] + mine), *pinned([blocks]), own] + mine + other_core(mine),
-        scratch=[pltpu.VMEM(blocks.shape, BF16), pltpu.SemaphoreType.DMA],
+    late_slots = slots_of(list(late.values()))
+    mat, fields, sums, late_slots = call(
+        functools.partial(early_body, n_blk, n_col, shifts, nslots),
+        [held(mat.shape, BF16), held(fields.shape, BF16), held((8, scn), F32)]
+        + [pltpu.SMEM(late_slots.shape, jnp.int32)],
+        [SMEM, SMEM] + [VMEM] * (3 + 2 * len(mine)),
+        [slots_of(mine), late_slots, mat, fields, sums] + mine + other_core(mine),
+        specs=[VMEM] * 3 + [SMEM],
+        aliases={2: 0, 3: 1},
     )
     shifts, mine = list(late), list(late.values())
     *products, scales, _, _ = call(
@@ -297,7 +319,7 @@
         [held((2 * ITERS * part, tile), BF16)] * n_blk
         + [like((8, scn), F32), held(mat.shape, BF16), held(fields.shape, BF16)],
         [SMEM] + [VMEM] * (4 + 2 * len(mine)),
-        [slots_of(mine), limits, mat, fields, sums] + mine + other_core(mine),
+        [late_slots, limits, mat, fields, sums] + mine + other_core(mine),
         scratch=[pltpu.VMEM((2 * ITERS, part, n * tile), BF16), pltpu.VMEM((tile, scn), F32)],
         flops=4 * ITERS * n * n * tile * tile * part,
         aliases={2: n_blk + 1, 3: n_blk + 2},

time: 39.7 us -> 39.8 us (level)
  Pallas kernels: 6.99 us -> 7.47 us
    pallas_call x5 -> x6, Pallas kernels: 6.99 us -> 7.47 us  [call(): pl.pallas_call(body, out_shape=list(outs), in_specs=in_specs, out_specs=s...]
  transfers between devices with their start and end apart: 17 -> 17, of which waited for: 7 -> 7; matrix products, arithmetic and copies ran while one was open for 0% -> 0% of each run, Pallas kernels for 4% -> 7%
where the time goes in v13:
time: 39.8 us; the launch traced here: 39.6 us
  starting transfers between devices  18.3 us (46%)
  waiting for transfers between devices  12.2 us (31%)
  Pallas kernels  7.47 us (19%)
  between operations  1.54 us (4%)
    ppermute x10, starting transfers between devices, move(): return lax.ppermute(value, ('blk', 'col'), pairs)  17 us
    ppermute x10, waiting for transfers between devices, move(): return lax.ppermute(value, ('blk', 'col'), pairs)  12.1 us
    pallas_call x6, Pallas kernels, call(): pl.pallas_call(body, out_shape=list(outs), in_specs=in_specs, out_specs=s...  7.47 us
    ppermute x7, starting transfers between devices, other_core(): return [lax.ppermute(v[:top], 'rep', [(0, 1), (1, 0)]) for v in values]  1.28 us
  transfers between devices with their start and end apart: 17, of which 7 were waited for; matrix products, arithmetic and copies ran while one was open for 0% of the time, Pallas kernels for 7%

profile of v13, /device:TPU:0, one launch (start us, length us, event | category | flops | bytes accessed | tf_op | source)
XLA Modules:
  0.0 39.6 jit_solution(17297079216227306058)
XLA Ops:
  1.3 1.5 %shard_map.104 = (bf16[720,128]{1,0:T(8,128)(2,1)S(1)}, bf16[560,128]{1,0:T(8,128)(2,1)S(1)}, bf16[560,128]{1,0:T(8,128)(2,1)S(1)}, bf16[176,128]{1,0:T(8,128)(2,1)S(1)}) custom-call(s32[1,1]{1,0:T(1,128)S(6)} %copy.19.refs_0_, f32[128,128]{1,0:T(8,128)} %refs_5_.3, f32[128,128]{1,0:T(8,128)} %refs_6_.3, f32[128,128]{1,0:T(8,128)} %refs_7_.3, ...), custom_call_target="tpu_custom_call" | custom-call | bytes 1040412 | tf_op jit(solution)/shard_map/pallas_call | solution.py:40
  2.8 3.1 %collective-permute-start.2 = (bf16[560,128]{1,0:T(8,128)(2,1)S(1)}, bf16[560,128]{1,0:T(8,128)(2,1)S(1)}, u32[]{:S(2)}, u32[]{:S(2)}) collective-permute-start(bf16[560,128]{1,0:T(8,128)(2,1)S(1)} %get-tuple-element.22), channel_id=1, source_target_pairs={{0,4},{2,6},{4,0},{6,2},{8,12},{10,14},{12,8},{14,10},{1,5},{3,7},... | collective-permute-start | bytes 430088 | tf_op jit(solution)/shard_map/ppermute | solution.py:257
  5.9 2.6 %collective-permute-start = (bf16[720,128]{1,0:T(8,128)(2,1)S(1)}, bf16[720,128]{1,0:T(8,128)(2,1)S(1)}, u32[]{:S(2)}, u32[]{:S(2)}) collective-permute-start(bf16[720,128]{1,0:T(8,128)(2,1)S(1)} %get-tuple-element.20), channel_id=1, source_target_pairs={{0,8},{2,10},{4,12},{6,14},{8,0},{10,2},{12,4},{14,6},{1,9},{3,11}... | collective-permute-start | bytes 552968 | tf_op jit(solution)/shard_map/ppermute | solution.py:257
  8.4 1.5 %collective-permute-start.1 = (bf16[560,128]{1,0:T(8,128)(2,1)S(1)}, bf16[560,128]{1,0:T(8,128)(2,1)S(1)}, u32[]{:S(2)}, u32[]{:S(2)}) collective-permute-start(bf16[560,128]{1,0:T(8,128)(2,1)S(1)} %get-tuple-element.21), channel_id=1, source_target_pairs={{0,2},{2,0},{4,6},{6,4},{8,10},{10,8},{12,14},{14,12},{1,3},{3,1},... | collective-permute-start | bytes 430088 | tf_op jit(solution)/shard_map/ppermute | solution.py:257
  9.9 2.0 %collective-permute-done.2.refs_2_ = bf16[560,128]{1,0:T(8,128)(2,1)S(1)} collective-permute-done((bf16[560,128]{1,0:T(8,128)(2,1)S(1)}, bf16[560,128]{1,0:T(8,128)(2,1)S(1)}, u32[]{:S(2)}, u32[]{:S(2)}) %collective-permute-start.2) | collective-permute-done | bytes 143392 | tf_op jit(solution)/shard_map/ppermute | solution.py:257
  12.0 1.8 %collective-permute-start.3 = (bf16[560,128]{1,0:T(8,128)(2,1)S(1)}, bf16[560,128]{1,0:T(8,128)(2,1)S(1)}, u32[]{:S(2)}, u32[]{:S(2)}) collective-permute-start(bf16[560,128]{1,0:T(8,128)(2,1)S(1)} %collective-permute-done.2.refs_2_), channel_id=1, source_target_pairs={{0,2},{2,0},{4,6},{6,4},{8,10},{10,8},{12,14},{14,12},{1,3},{3,1},... | collective-permute-start | bytes 430088 | tf_op jit(solution)/shard_map/ppermute | solution.py:257
  13.8 1.6 %shard_map.105 = (bf16[1024,1024]{1,0:T(8,128)(2,1)S(1)}, bf16[5,32,1024]{2,1,0:T(8,128)(2,1)S(1)}, f32[8,128]{1,0:T(8,128)S(1)}) custom-call(s32[1,7]{1,0:T(1,128)S(1)} %slice_convert_fusion.slots, bf16[1,1,6,128,128]{4,3,2,1,0:T(8,128)(2,1)} %blocks_in.1, bf16[176,128]{1,0:T(8,128)(2,1)S(1)} %get-tuple-element.23.own), custom_call_target="tpu_custom_call" | custom-call | bytes 2670620 | tf_op jit(solution)/shard_map/pallas_call | solution.py:40
  15.4 1.5 %collective-permute-done.came.refs_0_ = bf16[720,128]{1,0:T(8,128)(2,1)S(1)} collective-permute-done((bf16[720,128]{1,0:T(8,128)(2,1)S(1)}, bf16[720,128]{1,0:T(8,128)(2,1)S(1)}, u32[]{:S(2)}, u32[]{:S(2)}) %collective-permute-start) | collective-permute-done | bytes 184352 | tf_op jit(solution)/shard_map/ppermute | solution.py:257
  16.9 0.1 collective-permute-start.5
  17.0 2.9 %collective-permute-start.6 = (bf16[560,128]{1,0:T(8,128)(2,1)S(1)}, bf16[560,128]{1,0:T(8,128)(2,1)S(1)}, u32[]{:S(2)}, u32[]{:S(2)}) collective-permute-start(bf16[560,128]{1,0:T(8,128)(2,1)S(1)} %get-tuple-element.26), channel_id=1, source_target_pairs={{0,6},{2,4},{4,2},{6,0},{8,14},{10,12},{12,10},{14,8},{1,7},{3,5},... | collective-permute-start | bytes 430088 | tf_op jit(solution)/shard_map/ppermute | solution.py:257
  20.0 0.5 %collective-permute-start.4 = (bf16[560,128]{1,0:T(8,128)(2,1)S(1)}, bf16[560,128]{1,0:T(8,128)(2,1)S(1)}, u32[]{:S(2)}, u32[]{:S(2)}) collective-permute-start(bf16[560,128]{1,0:T(8,128)(2,1)S(1)} %get-tuple-element.25), channel_id=1, source_target_pairs={{0,2},{2,0},{4,6},{6,4},{8,10},{10,8},{12,14},{14,12},{1,3},{3,1},... | collective-permute-start | bytes 430088 | tf_op jit(solution)/shard_map/ppermute | solution.py:257
  20.5 0.0 collective-permute-done.1.refs_1_
  20.5 0.1 collective-permute-start.9
  20.7 0.0 collective-permute-done.3.refs_3_
  20.7 0.5 %collective-permute-start.8 = (bf16[384,128]{1,0:T(8,128)(2,1)S(1)}, bf16[384,128]{1,0:T(8,128)(2,1)S(1)}, u32[]{:S(2)}, u32[]{:S(2)}) collective-permute-start(bf16[384,128]{1,0:T(8,128)(2,1)S(1)} %slice.68), channel_id=1, source_target_pairs={{0,1},{1,0},{2,3},{3,2},{4,5},{5,4},{6,7},{7,6},{8,9},{9,8},{10,11... | collective-permute-start | bytes 294920 | tf_op jit(solution)/shard_map/ppermute | solution.py:279
  21.2 0.0 copy-start.5
  21.3 0.8 %collective-permute-done.5.refs_1_ = bf16[560,128]{1,0:T(8,128)(2,1)S(1)} collective-permute-done((bf16[560,128]{1,0:T(8,128)(2,1)S(1)}, bf16[560,128]{1,0:T(8,128)(2,1)S(1)}, u32[]{:S(2)}, u32[]{:S(2)}) %collective-permute-start.5) | collective-permute-done | bytes 143392 | tf_op jit(solution)/shard_map/ppermute | solution.py:257
  22.1 0.0 collective-permute-start.7
  22.1 2.5 %collective-permute-done.6.refs_2_ = bf16[560,128]{1,0:T(8,128)(2,1)S(1)} collective-permute-done((bf16[560,128]{1,0:T(8,128)(2,1)S(1)}, bf16[560,128]{1,0:T(8,128)(2,1)S(1)}, u32[]{:S(2)}, u32[]{:S(2)}) %collective-permute-start.6) | collective-permute-done | bytes 143392 | tf_op jit(solution)/shard_map/ppermute | solution.py:257
  24.7 0.0 collective-permute-start.10
  24.7 1.4 %collective-permute-done.4.refs_0_ = bf16[560,128]{1,0:T(8,128)(2,1)S(1)} collective-permute-done((bf16[560,128]{1,0:T(8,128)(2,1)S(1)}, bf16[560,128]{1,0:T(8,128)(2,1)S(1)}, u32[]{:S(2)}, u32[]{:S(2)}) %collective-permute-start.4) | collective-permute-done | bytes 143392 | tf_op jit(solution)/shard_map/ppermute | solution.py:257
  26.1 0.0 collective-permute-start.12
  26.1 0.0 collective-permute-done.9.refs_6_
  26.1 0.6 %collective-permute-start.13 = (bf16[384,128]{1,0:T(8,128)(2,1)S(1)}, bf16[384,128]{1,0:T(8,128)(2,1)S(1)}, u32[]{:S(2)}, u32[]{:S(2)}) collective-permute-start(bf16[384,128]{1,0:T(8,128)(2,1)S(1)} %slice.73), channel_id=1, source_target_pairs={{0,1},{1,0},{2,3},{3,2},{4,5},{5,4},{6,7},{7,6},{8,9},{9,8},{10,11... | collective-permute-start | bytes 294920 | tf_op jit(solution)/shard_map/ppermute | solution.py:279
  26.7 0.0 collective-permute-done.8.refs_5_
  26.7 0.1 collective-permute-start.11
  26.8 0.0 collective-permute-done.7.refs_4_
  26.8 0.0 collective-permute-done.10.refs_7_
  26.8 1.1 %shard_map.107 = (bf16[1024,1024]{1,0:T(8,128)(2,1)S(1)}, bf16[5,32,1024]{2,1,0:T(8,128)(2,1)S(1)}, f32[8,128]{1,0:T(8,128)S(1)}, s32[3,7]{1,0:T(4,128)S(4)}) custom-call(s32[4,7]{1,0:T(4,128)S(1)} %maximum_convert_fusion.slots, s32[3,7]{1,0:T(4,128)S(1)} %maximum_convert_fusion.1.late_slots, ...), custom_call_target="tpu_custom_call", output_to_operand_aliasing={{0}: (2, {}), {1}: (3, {})} | custom-call | bytes 5865752 | tf_op jit(solution)/shard_map/pallas_call | solution.py:40
  27.9 0.0 copy-start
  28.0 0.0 copy-start.1
  28.0 0.0 copy-start.2
  28.0 0.0 copy-start.3
  28.0 0.0 copy-start.4
  28.0 0.0 collective-permute-done.12.refs_4_
  28.0 0.0 collective-permute-done.13.refs_5_
  28.0 0.0 collective-permute-done.11.refs_3_
  28.0 0.0 copy-done.5
  28.0 2.5 %shard_map.108 = (bf16[128,128]{1,0:T(8,128)(2,1)S(1)}, bf16[128,128]{1,0:T(8,128)(2,1)S(1)}, bf16[128,128]{1,0:T(8,128)(2,1)S(1)}, bf16[128,128]{1,0:T(8,128)(2...) custom-call(s32[3,7]{1,0:T(4,128)S(4)} %get-tuple-element.29.slots, ...), custom_call_target="tpu_custom_call", output_to_operand_aliasing={{5}: (2, {}), {6}: (3, {})} | custom-call | flops 268435456 | bytes 5714516 | tf_op jit(solution)/shard_map/pallas_call | solution.py:40
  30.5 3.4 %collective-permute-start.14 = (bf16[128,128]{1,0:T(8,128)(2,1)S(1)}, bf16[128,128]{1,0:T(8,128)(2,1)S(1)}, u32[]{:S(2)}, u32[]{:S(2)}) collective-permute-start(bf16[128,128]{1,0:T(8,128)(2,1)S(1)} %get-tuple-element.34), channel_id=1, source_target_pairs={{0,12},{2,14},{4,8},{6,10},{8,4},{10,6},{12,0},{14,2},{1,13},{3,15... | collective-permute-start | bytes 98312 | tf_op jit(solution)/shard_map/ppermute | solution.py:257
  33.9 0.0 collective-permute-start.15
  34.0 1.0 %collective-permute-start.16 = (bf16[128,128]{1,0:T(8,128)(2,1)S(1)}, bf16[128,128]{1,0:T(8,128)(2,1)S(1)}, u32[]{:S(2)}, u32[]{:S(2)}) collective-permute-start(bf16[128,128]{1,0:T(8,128)(2,1)S(1)} %get-tuple-element.36), channel_id=1, source_target_pairs={{0,4},{2,6},{4,0},{6,2},{8,12},{10,14},{12,8},{14,10},{1,5},{3,7},... | collective-permute-start | bytes 98312 | tf_op jit(solution)/shard_map/ppermute | solution.py:257
  35.0 1.3 %collective-permute-done.14.refs_1_ = bf16[128,128]{1,0:T(8,128)(2,1)S(1)} collective-permute-done((bf16[128,128]{1,0:T(8,128)(2,1)S(1)}, bf16[128,128]{1,0:T(8,128)(2,1)S(1)}, u32[]{:S(2)}, u32[]{:S(2)}) %collective-permute-start.14) | collective-permute-done | bytes 32800 | tf_op jit(solution)/shard_map/ppermute | solution.py:257
  36.3 2.4 %collective-permute-done.15.refs_2_ = bf16[128,128]{1,0:T(8,128)(2,1)S(1)} collective-permute-done((bf16[128,128]{1,0:T(8,128)(2,1)S(1)}, bf16[128,128]{1,0:T(8,128)(2,1)S(1)}, u32[]{:S(2)}, u32[]{:S(2)}) %collective-permute-start.15) | collective-permute-done | bytes 32800 | tf_op jit(solution)/shard_map/ppermute | solution.py:257
  38.8 0.0 collective-permute-done.16.refs_3_
  38.8 0.0 copy-done
  38.8 0.0 copy-done.1
  38.8 0.0 copy-done.2
  38.8 0.0 copy-done.3
  38.8 0.0 copy-done.4
  38.8 0.8 %shard_map.109 = (f32[128,128]{1,0:T(8,128)}, f32[128,128]{1,0:T(8,128)}) custom-call(bf16[128,128]{1,0:T(8,128)(2,1)S(1)} %get-tuple-element.33.refs_0_, bf16[128,128]{1,0:T(8,128)(2,1)S(1)} %collective-permute-done.14.refs_1_, bf16[128,128]{1,0:T(8,128)(2,1)S(1)} %collective-permute-done.15.refs_2_, bf16[128,128]{1,0:T(8,128)(2,1)S(1)} %collective-permute-done.16.refs_3_, ...), custom_call_target="tpu_custom_call" | custom-call | bytes 594432 | tf_op jit(solution)/shard_map/pallas_call | solution.py:40
  (18 shorter events, 0.2 us)
Async XLA Ops:
  2.8 9.2 %collective-permute-start.2 = (bf16[560,128]{1,0:T(8,128)(2,1)S(1)}, bf16[560,128]{1,0:T(8,128)(2,1)S(1)}, u32[]{:S(2)}, u32[]{:S(2)}) collective-permute-start(bf16[560,128]{1,0:T(8,128)(2,1)S(1)} %get-tuple-element.22), channel_id=1, source_target_pairs={{0,4},{2,6},{4,0},{6,2},{8,12},{10,14},{12,8},{14,10},{1,5},{3,7},... | collective-permute-start | bytes 430088 | tf_op jit(solution)/shard_map/ppermute | solution.py:257
  5.9 11.1 %collective-permute-start = (bf16[720,128]{1,0:T(8,128)(2,1)S(1)}, bf16[720,128]{1,0:T(8,128)(2,1)S(1)}, u32[]{:S(2)}, u32[]{:S(2)}) collective-permute-start(bf16[720,128]{1,0:T(8,128)(2,1)S(1)} %get-tuple-element.20), channel_id=1, source_target_pairs={{0,8},{2,10},{4,12},{6,14},{8,0},{10,2},{12,4},{14,6},{1,9},{3,11}... | collective-permute-start | bytes 552968 | tf_op jit(solution)/shard_map/ppermute | solution.py:257
  8.4 12.1 %collective-permute-start.1 = (bf16[560,128]{1,0:T(8,128)(2,1)S(1)}, bf16[560,128]{1,0:T(8,128)(2,1)S(1)}, u32[]{:S(2)}, u32[]{:S(2)}) collective-permute-start(bf16[560,128]{1,0:T(8,128)(2,1)S(1)} %get-tuple-element.21), channel_id=1, source_target_pairs={{0,2},{2,0},{4,6},{6,4},{8,10},{10,8},{12,14},{14,12},{1,3},{3,1},... | collective-permute-start | bytes 430088 | tf_op jit(solution)/shard_map/ppermute | solution.py:257
  12.0 8.7 %collective-permute-start.3 = (bf16[560,128]{1,0:T(8,128)(2,1)S(1)}, bf16[560,128]{1,0:T(8,128)(2,1)S(1)}, u32[]{:S(2)}, u32[]{:S(2)}) collective-permute-start(bf16[560,128]{1,0:T(8,128)(2,1)S(1)} %collective-permute-done.2.refs_2_), channel_id=1, source_target_pairs={{0,2},{2,0},{4,6},{6,4},{8,10},{10,8},{12,14},{14,12},{1,3},{3,1},... | collective-permute-start | bytes 430088 | tf_op jit(solution)/shard_map/ppermute | solution.py:257
  16.9 5.2 %collective-permute-start.5 = (bf16[560,128]{1,0:T(8,128)(2,1)S(1)}, bf16[560,128]{1,0:T(8,128)(2,1)S(1)}, u32[]{:S(2)}, u32[]{:S(2)}) collective-permute-start(bf16[560,128]{1,0:T(8,128)(2,1)S(1)} %get-tuple-element.26), channel_id=1, source_target_pairs={{0,4},{2,6},{4,0},{6,2},{8,12},{10,14},{12,8},{14,10},{1,5},{3,7},... | collective-permute-start | bytes 430088 | tf_op jit(solution)/shard_map/ppermute | solution.py:257
  17.0 7.7 %collective-permute-start.6 = (bf16[560,128]{1,0:T(8,128)(2,1)S(1)}, bf16[560,128]{1,0:T(8,128)(2,1)S(1)}, u32[]{:S(2)}, u32[]{:S(2)}) collective-permute-start(bf16[560,128]{1,0:T(8,128)(2,1)S(1)} %get-tuple-element.26), channel_id=1, source_target_pairs={{0,6},{2,4},{4,2},{6,0},{8,14},{10,12},{12,10},{14,8},{1,7},{3,5},... | collective-permute-start | bytes 430088 | tf_op jit(solution)/shard_map/ppermute | solution.py:257
  20.0 6.1 %collective-permute-start.4 = (bf16[560,128]{1,0:T(8,128)(2,1)S(1)}, bf16[560,128]{1,0:T(8,128)(2,1)S(1)}, u32[]{:S(2)}, u32[]{:S(2)}) collective-permute-start(bf16[560,128]{1,0:T(8,128)(2,1)S(1)} %get-tuple-element.25), channel_id=1, source_target_pairs={{0,2},{2,0},{4,6},{6,4},{8,10},{10,8},{12,14},{14,12},{1,3},{3,1},... | collective-permute-start | bytes 430088 | tf_op jit(solution)/shard_map/ppermute | solution.py:257
  20.5 5.6 %collective-permute-start.9 = (bf16[384,128]{1,0:T(8,128)(2,1)S(1)}, bf16[384,128]{1,0:T(8,128)(2,1)S(1)}, u32[]{:S(2)}, u32[]{:S(2)}) collective-permute-start(bf16[384,128]{1,0:T(8,128)(2,1)S(1)} %slice.69), channel_id=1, source_target_pairs={{0,1},{1,0},{2,3},{3,2},{4,5},{5,4},{6,7},{7,6},{8,9},{9,8},{10,11... | collective-permute-start | bytes 294920 | tf_op jit(solution)/shard_map/ppermute | solution.py:279
  20.7 6.0 %collective-permute-start.8 = (bf16[384,128]{1,0:T(8,128)(2,1)S(1)}, bf16[384,128]{1,0:T(8,128)(2,1)S(1)}, u32[]{:S(2)}, u32[]{:S(2)}) collective-permute-start(bf16[384,128]{1,0:T(8,128)(2,1)S(1)} %slice.68), channel_id=1, source_target_pairs={{0,1},{1,0},{2,3},{3,2},{4,5},{5,4},{6,7},{7,6},{8,9},{9,8},{10,11... | collective-permute-start | bytes 294920 | tf_op jit(solution)/shard_map/ppermute | solution.py:279
  21.2 6.8 %copy-start.5 = (s32[128]{0:T(128)S(1)}, s32[128]{0:T(128)}, u32[]{:S(2)}) copy-start(s32[128]{0:T(128)} %param.17) | copy-start | bytes 1540
  22.1 4.7 %collective-permute-start.7 = (bf16[384,128]{1,0:T(8,128)(2,1)S(1)}, bf16[384,128]{1,0:T(8,128)(2,1)S(1)}, u32[]{:S(2)}, u32[]{:S(2)}) collective-permute-start(bf16[384,128]{1,0:T(8,128)(2,1)S(1)} %slice.67), channel_id=1, source_target_pairs={{0,1},{1,0},{2,3},{3,2},{4,5},{5,4},{6,7},{7,6},{8,9},{9,8},{10,11... | collective-permute-start | bytes 294920 | tf_op jit(solution)/shard_map/ppermute | solution.py:279
  24.7 2.1 %collective-permute-start.10 = (bf16[384,128]{1,0:T(8,128)(2,1)S(1)}, bf16[384,128]{1,0:T(8,128)(2,1)S(1)}, u32[]{:S(2)}, u32[]{:S(2)}) collective-permute-start(bf16[384,128]{1,0:T(8,128)(2,1)S(1)} %slice.70), channel_id=1, source_target_pairs={{0,1},{1,0},{2,3},{3,2},{4,5},{5,4},{6,7},{7,6},{8,9},{9,8},{10,11... | collective-permute-start | bytes 294920 | tf_op jit(solution)/shard_map/ppermute | solution.py:279
  26.1 1.9 %collective-permute-start.12 = (bf16[384,128]{1,0:T(8,128)(2,1)S(1)}, bf16[384,128]{1,0:T(8,128)(2,1)S(1)}, u32[]{:S(2)}, u32[]{:S(2)}) collective-permute-start(bf16[384,128]{1,0:T(8,128)(2,1)S(1)} %slice.72), channel_id=1, source_target_pairs={{0,1},{1,0},{2,3},{3,2},{4,5},{5,4},{6,7},{7,6},{8,9},{9,8},{10,11... | collective-permute-start | bytes 294920 | tf_op jit(solution)/shard_map/ppermute | solution.py:279
  26.1 1.9 %collective-permute-start.13 = (bf16[384,128]{1,0:T(8,128)(2,1)S(1)}, bf16[384,128]{1,0:T(8,128)(2,1)S(1)}, u32[]{:S(2)}, u32[]{:S(2)}) collective-permute-start(bf16[384,128]{1,0:T(8,128)(2,1)S(1)} %slice.73), channel_id=1, source_target_pairs={{0,1},{1,0},{2,3},{3,2},{4,5},{5,4},{6,7},{7,6},{8,9},{9,8},{10,11... | collective-permute-start | bytes 294920 | tf_op jit(solution)/shard_map/ppermute | solution.py:279
  26.7 1.3 %collective-permute-start.11 = (bf16[384,128]{1,0:T(8,128)(2,1)S(1)}, bf16[384,128]{1,0:T(8,128)(2,1)S(1)}, u32[]{:S(2)}, u32[]{:S(2)}) collective-permute-start(bf16[384,128]{1,0:T(8,128)(2,1)S(1)} %slice.71), channel_id=1, source_target_pairs={{0,1},{1,0},{2,3},{3,2},{4,5},{5,4},{6,7},{7,6},{8,9},{9,8},{10,11... | collective-permute-start | bytes 294920 | tf_op jit(solution)/shard_map/ppermute | solution.py:279
  27.9 10.8 %copy-start = (f32[128,128]{1,0:T(8,128)S(1)}, f32[128,128]{1,0:T(8,128)}, u32[]{:S(2)}) copy-start(f32[128,128]{1,0:T(8,128)} %refs_5_.3) | copy-start | bytes 196612
  28.0 10.8 %copy-start.1 = (f32[128,128]{1,0:T(8,128)S(1)}, f32[128,128]{1,0:T(8,128)}, u32[]{:S(2)}) copy-start(f32[128,128]{1,0:T(8,128)} %refs_6_.3) | copy-start | bytes 196612
  28.0 10.8 %copy-start.2 = (f32[128,128]{1,0:T(8,128)S(1)}, f32[128,128]{1,0:T(8,128)}, u32[]{:S(2)}) copy-start(f32[128,128]{1,0:T(8,128)} %refs_7_.3) | copy-start | bytes 196612
  28.0 10.8 %copy-start.3 = (f32[128,128]{1,0:T(8,128)S(1)}, f32[128,128]{1,0:T(8,128)}, u32[]{:S(2)}) copy-start(f32[128,128]{1,0:T(8,128)} %refs_8_.1) | copy-start | bytes 196612
  28.0 10.8 %copy-start.4 = (f32[128,128]{1,0:T(8,128)S(1)}, f32[128,128]{1,0:T(8,128)}, u32[]{:S(2)}) copy-start(f32[128,128]{1,0:T(8,128)} %refs_9_.1) | copy-start | bytes 196612
  30.5 5.8 %collective-permute-start.14 = (bf16[128,128]{1,0:T(8,128)(2,1)S(1)}, bf16[128,128]{1,0:T(8,128)(2,1)S(1)}, u32[]{:S(2)}, u32[]{:S(2)}) collective-permute-start(bf16[128,128]{1,0:T(8,128)(2,1)S(1)} %get-tuple-element.34), channel_id=1, source_target_pairs={{0,12},{2,14},{4,8},{6,10},{8,4},{10,6},{12,0},{14,2},{1,13},{3,15... | collective-permute-start | bytes 98312 | tf_op jit(solution)/shard_map/ppermute | solution.py:257
  33.9 4.8 %collective-permute-start.15 = (bf16[128,128]{1,0:T(8,128)(2,1)S(1)}, bf16[128,128]{1,0:T(8,128)(2,1)S(1)}, u32[]{:S(2)}, u32[]{:S(2)}) collective-permute-start(bf16[128,128]{1,0:T(8,128)(2,1)S(1)} %get-tuple-element.35), channel_id=1, source_target_pairs={{0,8},{2,10},{4,12},{6,14},{8,0},{10,2},{12,4},{14,6},{1,9},{3,11}... | collective-permute-start | bytes 98312 | tf_op jit(solution)/shard_map/ppermute | solution.py:257
  34.0 4.8 %collective-permute-start.16 = (bf16[128,128]{1,0:T(8,128)(2,1)S(1)}, bf16[128,128]{1,0:T(8,128)(2,1)S(1)}, u32[]{:S(2)}, u32[]{:S(2)}) collective-permute-start(bf16[128,128]{1,0:T(8,128)(2,1)S(1)} %get-tuple-element.36), channel_id=1, source_target_pairs={{0,4},{2,6},{4,0},{6,2},{8,12},{10,14},{12,8},{14,10},{1,5},{3,7},... | collective-permute-start | bytes 98312 | tf_op jit(solution)/shard_map/ppermute | solution.py:257

commit v14 on v13

--- a/solution.py
+++ b/solution.py
@@ -61,6 +61,10 @@
     value = primal - tau * grad
     capped = jnp.where(limited > 0, jnp.minimum(value, upper), value)
     return jnp.maximum(capped, 0.0)
+
+
+def touch_body(part, after, out):
+    del part, after, out
 
 
 def prep_body(far, first_near, *refs):
@@ -302,6 +306,16 @@
         [early[far, 0], sums],
     )
     late = {(far + t, s): move(relayed[t], t, s) for t, s in near}
+    for s in range(1, n_col):
+        (late[far, s],) = call(
+            touch_body,
+            [held((size, tile), BF16)],
+            [ANY, ANY],
+            [late[far, s], sums],
+            specs=[ANY],
+            aliases={0: 0},
+            flops=2 * 10**9,
+        )
     shifts, mine = list(early), list(early.values())
     late_slots = slots_of(list(late.values()))
     mat, fields, sums, late_slots = call(

time: 39.8 us -> 40.7 us (1.023)
  waiting for transfers between devices: 12.2 us -> 13 us
    ppermute x10, waiting for transfers between devices: 12.1 us -> 13 us  [move(): return lax.ppermute(value, ('blk', 'col'), pairs)]
    pallas_call x6 -> x7, Pallas kernels: 7.47 us -> 7.46 us  [call(): pl.pallas_call(body, out_shape=list(outs), in_specs=in_specs, out_specs=s...]
where the time goes in v14:
time: 40.7 us; the launch traced here: 40.5 us
  starting transfers between devices  18.4 us (45%)
  waiting for transfers between devices  13 us (32%)
  Pallas kernels  7.46 us (18%)
  between operations  1.53 us (4%)
    ppermute x10, starting transfers between devices, move(): return lax.ppermute(value, ('blk', 'col'), pairs)  17.1 us
    ppermute x10, waiting for transfers between devices, move(): return lax.ppermute(value, ('blk', 'col'), pairs)  13 us
    pallas_call x7, Pallas kernels, call(): pl.pallas_call(body, out_shape=list(outs), in_specs=in_specs, out_specs=s...  7.46 us
    ppermute x7, starting transfers between devices, other_core(): return [lax.ppermute(v[:top], 'rep', [(0, 1), (1, 0)]) for v in values]  1.27 us
  transfers between devices with their start and end apart: 17, of which 7 were waited for; matrix products, arithmetic and copies ran while one was open for 0% of the time, Pallas kernels for 7%

profile of v14, /device:TPU:0, one launch (start us, length us, event | category | flops | bytes accessed | tf_op | source)
XLA Modules:
  0.0 40.5 jit_solution(13744577111517627587)
XLA Ops:
  1.3 1.5 %shard_map.104 = (bf16[720,128]{1,0:T(8,128)(2,1)S(1)}, bf16[560,128]{1,0:T(8,128)(2,1)S(1)}, bf16[560,128]{1,0:T(8,128)(2,1)S(1)}, bf16[176,128]{1,0:T(8,128)(2,1)S(1)}) custom-call(s32[1,1]{1,0:T(1,128)S(6)} %copy.21.refs_0_, f32[128,128]{1,0:T(8,128)} %refs_5_.3, f32[128,128]{1,0:T(8,128)} %refs_6_.3, f32[128,128]{1,0:T(8,128)} %refs_7_.3, ...), custom_call_target="tpu_custom_call" | custom-call | bytes 1040412 | tf_op jit(solution)/shard_map/pallas_call | solution.py:40
  2.8 3.1 %collective-permute-start.2 = (bf16[560,128]{1,0:T(8,128)(2,1)S(1)}, bf16[560,128]{1,0:T(8,128)(2,1)S(1)}, u32[]{:S(2)}, u32[]{:S(2)}) collective-permute-start(bf16[560,128]{1,0:T(8,128)(2,1)S(1)} %get-tuple-element.22), channel_id=1, source_target_pairs={{0,4},{2,6},{4,0},{6,2},{8,12},{10,14},{12,8},{14,10},{1,5},{3,7},... | collective-permute-start | bytes 430088 | tf_op jit(solution)/shard_map/ppermute | solution.py:261
  5.9 2.6 %collective-permute-start = (bf16[720,128]{1,0:T(8,128)(2,1)S(1)}, bf16[720,128]{1,0:T(8,128)(2,1)S(1)}, u32[]{:S(2)}, u32[]{:S(2)}) collective-permute-start(bf16[720,128]{1,0:T(8,128)(2,1)S(1)} %get-tuple-element.20), channel_id=1, source_target_pairs={{0,8},{2,10},{4,12},{6,14},{8,0},{10,2},{12,4},{14,6},{1,9},{3,11}... | collective-permute-start | bytes 552968 | tf_op jit(solution)/shard_map/ppermute | solution.py:261
  8.4 1.5 %collective-permute-start.1 = (bf16[560,128]{1,0:T(8,128)(2,1)S(1)}, bf16[560,128]{1,0:T(8,128)(2,1)S(1)}, u32[]{:S(2)}, u32[]{:S(2)}) collective-permute-start(bf16[560,128]{1,0:T(8,128)(2,1)S(1)} %get-tuple-element.21), channel_id=1, source_target_pairs={{0,2},{2,0},{4,6},{6,4},{8,10},{10,8},{12,14},{14,12},{1,3},{3,1},... | collective-permute-start | bytes 430088 | tf_op jit(solution)/shard_map/ppermute | solution.py:261
  9.9 2.0 %collective-permute-done.2.refs_2_ = bf16[560,128]{1,0:T(8,128)(2,1)S(1)} collective-permute-done((bf16[560,128]{1,0:T(8,128)(2,1)S(1)}, bf16[560,128]{1,0:T(8,128)(2,1)S(1)}, u32[]{:S(2)}, u32[]{:S(2)}) %collective-permute-start.2) | collective-permute-done | bytes 143392 | tf_op jit(solution)/shard_map/ppermute | solution.py:261
  12.0 1.8 %collective-permute-start.3 = (bf16[560,128]{1,0:T(8,128)(2,1)S(1)}, bf16[560,128]{1,0:T(8,128)(2,1)S(1)}, u32[]{:S(2)}, u32[]{:S(2)}) collective-permute-start(bf16[560,128]{1,0:T(8,128)(2,1)S(1)} %collective-permute-done.2.refs_2_), channel_id=1, source_target_pairs={{0,2},{2,0},{4,6},{6,4},{8,10},{10,8},{12,14},{14,12},{1,3},{3,1},... | collective-permute-start | bytes 430088 | tf_op jit(solution)/shard_map/ppermute | solution.py:261
  13.8 1.5 %shard_map.105 = (bf16[1024,1024]{1,0:T(8,128)(2,1)S(1)}, bf16[5,32,1024]{2,1,0:T(8,128)(2,1)S(1)}, f32[8,128]{1,0:T(8,128)S(1)}) custom-call(s32[1,7]{1,0:T(1,128)S(1)} %slice_convert_fusion.slots, bf16[1,1,6,128,128]{4,3,2,1,0:T(8,128)(2,1)} %blocks_in.1, bf16[176,128]{1,0:T(8,128)(2,1)S(1)} %get-tuple-element.23.own), custom_call_target="tpu_custom_call" | custom-call | bytes 2670620 | tf_op jit(solution)/shard_map/pallas_call | solution.py:40
  15.4 1.5 %collective-permute-done.came.refs_0_ = bf16[720,128]{1,0:T(8,128)(2,1)S(1)} collective-permute-done((bf16[720,128]{1,0:T(8,128)(2,1)S(1)}, bf16[720,128]{1,0:T(8,128)(2,1)S(1)}, u32[]{:S(2)}, u32[]{:S(2)}) %collective-permute-start) | collective-permute-done | bytes 184352 | tf_op jit(solution)/shard_map/ppermute | solution.py:261
  16.9 1.6 %collective-permute-start.4 = (bf16[560,128]{1,0:T(8,128)(2,1)S(1)}, bf16[560,128]{1,0:T(8,128)(2,1)S(1)}, u32[]{:S(2)}, u32[]{:S(2)}) collective-permute-start(bf16[560,128]{1,0:T(8,128)(2,1)S(1)} %get-tuple-element.25), channel_id=1, source_target_pairs={{0,2},{2,0},{4,6},{6,4},{8,10},{10,8},{12,14},{14,12},{1,3},{3,1},... | collective-permute-start | bytes 430088 | tf_op jit(solution)/shard_map/ppermute | solution.py:261
  18.5 0.1 collective-permute-start.9
  18.5 0.0 collective-permute-done.1.refs_1_
  18.6 0.5 %collective-permute-start.8 = (bf16[384,128]{1,0:T(8,128)(2,1)S(1)}, bf16[384,128]{1,0:T(8,128)(2,1)S(1)}, u32[]{:S(2)}, u32[]{:S(2)}) collective-permute-start(bf16[384,128]{1,0:T(8,128)(2,1)S(1)} %slice.68), channel_id=1, source_target_pairs={{0,1},{1,0},{2,3},{3,2},{4,5},{5,4},{6,7},{7,6},{8,9},{9,8},{10,11... | collective-permute-start | bytes 294920 | tf_op jit(solution)/shard_map/ppermute | solution.py:283
  19.1 0.1 collective-permute-start.5
  19.2 0.0 collective-permute-done.3.refs_3_
  19.2 2.0 %collective-permute-start.6 = (bf16[560,128]{1,0:T(8,128)(2,1)S(1)}, bf16[560,128]{1,0:T(8,128)(2,1)S(1)}, u32[]{:S(2)}, u32[]{:S(2)}) collective-permute-start(bf16[560,128]{1,0:T(8,128)(2,1)S(1)} %get-tuple-element.26), channel_id=1, source_target_pairs={{0,6},{2,4},{4,2},{6,0},{8,14},{10,12},{12,10},{14,8},{1,7},{3,5},... | collective-permute-start | bytes 430088 | tf_op jit(solution)/shard_map/ppermute | solution.py:261
  21.3 0.7 %collective-permute-done.4.part = bf16[560,128]{1,0:T(8,128)(2,1)S(1)} collective-permute-done((bf16[560,128]{1,0:T(8,128)(2,1)S(1)}, bf16[560,128]{1,0:T(8,128)(2,1)S(1)}, u32[]{:S(2)}, u32[]{:S(2)}) %collective-permute-start.4) | collective-permute-done | bytes 143392 | tf_op jit(solution)/shard_map/ppermute | solution.py:261
  22.1 0.0 collective-permute-start.7
  22.1 0.0 copy-start.5
  22.1 3.7 %collective-permute-done.5.refs_1_ = bf16[560,128]{1,0:T(8,128)(2,1)S(1)} collective-permute-done((bf16[560,128]{1,0:T(8,128)(2,1)S(1)}, bf16[560,128]{1,0:T(8,128)(2,1)S(1)}, u32[]{:S(2)}, u32[]{:S(2)}) %collective-permute-start.5) | collective-permute-done | bytes 143392 | tf_op jit(solution)/shard_map/ppermute | solution.py:261
  25.8 0.0 collective-permute-start.10
  25.8 2.1 %collective-permute-done.6.refs_2_ = bf16[560,128]{1,0:T(8,128)(2,1)S(1)} collective-permute-done((bf16[560,128]{1,0:T(8,128)(2,1)S(1)}, bf16[560,128]{1,0:T(8,128)(2,1)S(1)}, u32[]{:S(2)}, u32[]{:S(2)}) %collective-permute-start.6) | collective-permute-done | bytes 143392 | tf_op jit(solution)/shard_map/ppermute | solution.py:261
  27.9 0.0 collective-permute-start.11
  27.9 0.0 collective-permute-done.9.refs_6_
  28.0 0.6 %collective-permute-start.12 = (bf16[384,128]{1,0:T(8,128)(2,1)S(1)}, bf16[384,128]{1,0:T(8,128)(2,1)S(1)}, u32[]{:S(2)}, u32[]{:S(2)}) collective-permute-start(bf16[384,128]{1,0:T(8,128)(2,1)S(1)} %slice.72), channel_id=1, source_target_pairs={{0,1},{1,0},{2,3},{3,2},{4,5},{5,4},{6,7},{7,6},{8,9},{9,8},{10,11... | collective-permute-start | bytes 294920 | tf_op jit(solution)/shard_map/ppermute | solution.py:283
  28.5 0.0 collective-permute-done.8.refs_5_
  28.5 0.1 collective-permute-start.13
  28.6 0.0 collective-permute-done.7.refs_4_
  28.6 0.0 collective-permute-done.10.refs_7_
  28.6 1.1 %shard_map.108 = (bf16[1024,1024]{1,0:T(8,128)(2,1)S(1)}, bf16[5,32,1024]{2,1,0:T(8,128)(2,1)S(1)}, f32[8,128]{1,0:T(8,128)S(1)}, s32[3,7]{1,0:T(4,128)S(4)}) custom-call(s32[4,7]{1,0:T(4,128)S(1)} %maximum_convert_fusion.slots, s32[3,7]{1,0:T(4,128)S(1)} %maximum_convert_fusion.1.late_slots, ...), custom_call_target="tpu_custom_call", output_to_operand_aliasing={{0}: (2, {}), {1}: (3, {})} | custom-call | bytes 5865752 | tf_op jit(solution)/shard_map/pallas_call | solution.py:40
  29.7 0.0 copy-start
  29.7 0.0 copy-start.1
  29.8 0.0 copy-start.2
  29.8 0.0 copy-start.3
  29.8 0.0 copy-start.4
  29.8 0.0 collective-permute-done.11.refs_3_
  29.8 0.0 collective-permute-done.12.refs_4_
  29.8 0.0 collective-permute-done.13.refs_5_
  29.8 0.0 copy-done.5
  29.8 2.5 %shard_map.109 = (bf16[128,128]{1,0:T(8,128)(2,1)S(1)}, bf16[128,128]{1,0:T(8,128)(2,1)S(1)}, bf16[128,128]{1,0:T(8,128)(2,1)S(1)}, bf16[128,128]{1,0:T(8,128)(2...) custom-call(s32[3,7]{1,0:T(4,128)S(4)} %get-tuple-element.29.slots, ...), custom_call_target="tpu_custom_call", output_to_operand_aliasing={{5}: (2, {}), {6}: (3, {})} | custom-call | flops 268435456 | bytes 5714516 | tf_op jit(solution)/shard_map/pallas_call | solution.py:40
  32.3 2.5 %collective-permute-start.14 = (bf16[128,128]{1,0:T(8,128)(2,1)S(1)}, bf16[128,128]{1,0:T(8,128)(2,1)S(1)}, u32[]{:S(2)}, u32[]{:S(2)}) collective-permute-start(bf16[128,128]{1,0:T(8,128)(2,1)S(1)} %get-tuple-element.34), channel_id=1, source_target_pairs={{0,12},{2,14},{4,8},{6,10},{8,4},{10,6},{12,0},{14,2},{1,13},{3,15... | collective-permute-start | bytes 98312 | tf_op jit(solution)/shard_map/ppermute | solution.py:261
  34.9 0.0 collective-permute-start.15
  34.9 1.9 %collective-permute-start.16 = (bf16[128,128]{1,0:T(8,128)(2,1)S(1)}, bf16[128,128]{1,0:T(8,128)(2,1)S(1)}, u32[]{:S(2)}, u32[]{:S(2)}) collective-permute-start(bf16[128,128]{1,0:T(8,128)(2,1)S(1)} %get-tuple-element.36), channel_id=1, source_target_pairs={{0,4},{2,6},{4,0},{6,2},{8,12},{10,14},{12,8},{14,10},{1,5},{3,7},... | collective-permute-start | bytes 98312 | tf_op jit(solution)/shard_map/ppermute | solution.py:261
  36.8 1.5 %collective-permute-done.14.refs_1_ = bf16[128,128]{1,0:T(8,128)(2,1)S(1)} collective-permute-done((bf16[128,128]{1,0:T(8,128)(2,1)S(1)}, bf16[128,128]{1,0:T(8,128)(2,1)S(1)}, u32[]{:S(2)}, u32[]{:S(2)}) %collective-permute-start.14) | collective-permute-done | bytes 32800 | tf_op jit(solution)/shard_map/ppermute | solution.py:261
  38.3 1.4 %collective-permute-done.15.refs_2_ = bf16[128,128]{1,0:T(8,128)(2,1)S(1)} collective-permute-done((bf16[128,128]{1,0:T(8,128)(2,1)S(1)}, bf16[128,128]{1,0:T(8,128)(2,1)S(1)}, u32[]{:S(2)}, u32[]{:S(2)}) %collective-permute-start.15) | collective-permute-done | bytes 32800 | tf_op jit(solution)/shard_map/ppermute | solution.py:261
  39.7 0.0 collective-permute-done.16.refs_3_
  39.7 0.0 copy-done
  39.7 0.0 copy-done.1
  39.7 0.0 copy-done.2
  39.7 0.0 copy-done.3
  39.7 0.0 copy-done.4
  39.7 0.8 %shard_map.110 = (f32[128,128]{1,0:T(8,128)}, f32[128,128]{1,0:T(8,128)}) custom-call(bf16[128,128]{1,0:T(8,128)(2,1)S(1)} %get-tuple-element.33.refs_0_, bf16[128,128]{1,0:T(8,128)(2,1)S(1)} %collective-permute-done.14.refs_1_, bf16[128,128]{1,0:T(8,128)(2,1)S(1)} %collective-permute-done.15.refs_2_, bf16[128,128]{1,0:T(8,128)(2,1)S(1)} %collective-permute-done.16.refs_3_, ...), custom_call_target="tpu_custom_call" | custom-call | bytes 594432 | tf_op jit(solution)/shard_map/pallas_call | solution.py:40
  (19 shorter events, 0.2 us)
Async XLA Ops:
  2.8 9.2 %collective-permute-start.2 = (bf16[560,128]{1,0:T(8,128)(2,1)S(1)}, bf16[560,128]{1,0:T(8,128)(2,1)S(1)}, u32[]{:S(2)}, u32[]{:S(2)}) collective-permute-start(bf16[560,128]{1,0:T(8,128)(2,1)S(1)} %get-tuple-element.22), channel_id=1, source_target_pairs={{0,4},{2,6},{4,0},{6,2},{8,12},{10,14},{12,8},{14,10},{1,5},{3,7},... | collective-permute-start | bytes 430088 | tf_op jit(solution)/shard_map/ppermute | solution.py:261
  5.9 11.0 %collective-permute-start = (bf16[720,128]{1,0:T(8,128)(2,1)S(1)}, bf16[720,128]{1,0:T(8,128)(2,1)S(1)}, u32[]{:S(2)}, u32[]{:S(2)}) collective-permute-start(bf16[720,128]{1,0:T(8,128)(2,1)S(1)} %get-tuple-element.20), channel_id=1, source_target_pairs={{0,8},{2,10},{4,12},{6,14},{8,0},{10,2},{12,4},{14,6},{1,9},{3,11}... | collective-permute-start | bytes 552968 | tf_op jit(solution)/shard_map/ppermute | solution.py:261
  8.4 10.1 %collective-permute-start.1 = (bf16[560,128]{1,0:T(8,128)(2,1)S(1)}, bf16[560,128]{1,0:T(8,128)(2,1)S(1)}, u32[]{:S(2)}, u32[]{:S(2)}) collective-permute-start(bf16[560,128]{1,0:T(8,128)(2,1)S(1)} %get-tuple-element.21), channel_id=1, source_target_pairs={{0,2},{2,0},{4,6},{6,4},{8,10},{10,8},{12,14},{14,12},{1,3},{3,1},... | collective-permute-start | bytes 430088 | tf_op jit(solution)/shard_map/ppermute | solution.py:261
  12.0 7.2 %collective-permute-start.3 = (bf16[560,128]{1,0:T(8,128)(2,1)S(1)}, bf16[560,128]{1,0:T(8,128)(2,1)S(1)}, u32[]{:S(2)}, u32[]{:S(2)}) collective-permute-start(bf16[560,128]{1,0:T(8,128)(2,1)S(1)} %collective-permute-done.2.refs_2_), channel_id=1, source_target_pairs={{0,2},{2,0},{4,6},{6,4},{8,10},{10,8},{12,14},{14,12},{1,3},{3,1},... | collective-permute-start | bytes 430088 | tf_op jit(solution)/shard_map/ppermute | solution.py:261
  16.9 5.2 %collective-permute-start.4 = (bf16[560,128]{1,0:T(8,128)(2,1)S(1)}, bf16[560,128]{1,0:T(8,128)(2,1)S(1)}, u32[]{:S(2)}, u32[]{:S(2)}) collective-permute-start(bf16[560,128]{1,0:T(8,128)(2,1)S(1)} %get-tuple-element.25), channel_id=1, source_target_pairs={{0,2},{2,0},{4,6},{6,4},{8,10},{10,8},{12,14},{14,12},{1,3},{3,1},... | collective-permute-start | bytes 430088 | tf_op jit(solution)/shard_map/ppermute | solution.py:261
  18.5 9.5 %collective-permute-start.9 = (bf16[384,128]{1,0:T(8,128)(2,1)S(1)}, bf16[384,128]{1,0:T(8,128)(2,1)S(1)}, u32[]{:S(2)}, u32[]{:S(2)}) collective-permute-start(bf16[384,128]{1,0:T(8,128)(2,1)S(1)} %slice.69), channel_id=1, source_target_pairs={{0,1},{1,0},{2,3},{3,2},{4,5},{5,4},{6,7},{7,6},{8,9},{9,8},{10,11... | collective-permute-start | bytes 294920 | tf_op jit(solution)/shard_map/ppermute | solution.py:283
  18.6 10.0 %collective-permute-start.8 = (bf16[384,128]{1,0:T(8,128)(2,1)S(1)}, bf16[384,128]{1,0:T(8,128)(2,1)S(1)}, u32[]{:S(2)}, u32[]{:S(2)}) collective-permute-start(bf16[384,128]{1,0:T(8,128)(2,1)S(1)} %slice.68), channel_id=1, source_target_pairs={{0,1},{1,0},{2,3},{3,2},{4,5},{5,4},{6,7},{7,6},{8,9},{9,8},{10,11... | collective-permute-start | bytes 294920 | tf_op jit(solution)/shard_map/ppermute | solution.py:283
  19.1 6.7 %collective-permute-start.5 = (bf16[560,128]{1,0:T(8,128)(2,1)S(1)}, bf16[560,128]{1,0:T(8,128)(2,1)S(1)}, u32[]{:S(2)}, u32[]{:S(2)}) collective-permute-start(bf16[560,128]{1,0:T(8,128)(2,1)S(1)} %get-tuple-element.26), channel_id=1, source_target_pairs={{0,4},{2,6},{4,0},{6,2},{8,12},{10,14},{12,8},{14,10},{1,5},{3,7},... | collective-permute-start | bytes 430088 | tf_op jit(solution)/shard_map/ppermute | solution.py:261
  19.2 8.7 %collective-permute-start.6 = (bf16[560,128]{1,0:T(8,128)(2,1)S(1)}, bf16[560,128]{1,0:T(8,128)(2,1)S(1)}, u32[]{:S(2)}, u32[]{:S(2)}) collective-permute-start(bf16[560,128]{1,0:T(8,128)(2,1)S(1)} %get-tuple-element.26), channel_id=1, source_target_pairs={{0,6},{2,4},{4,2},{6,0},{8,14},{10,12},{12,10},{14,8},{1,7},{3,5},... | collective-permute-start | bytes 430088 | tf_op jit(solution)/shard_map/ppermute | solution.py:261
  22.1 6.6 %collective-permute-start.7 = (bf16[384,128]{1,0:T(8,128)(2,1)S(1)}, bf16[384,128]{1,0:T(8,128)(2,1)S(1)}, u32[]{:S(2)}, u32[]{:S(2)}) collective-permute-start(bf16[384,128]{1,0:T(8,128)(2,1)S(1)} %slice.67), channel_id=1, source_target_pairs={{0,1},{1,0},{2,3},{3,2},{4,5},{5,4},{6,7},{7,6},{8,9},{9,8},{10,11... | collective-permute-start | bytes 294920 | tf_op jit(solution)/shard_map/ppermute | solution.py:283
  22.1 7.8 %copy-start.5 = (s32[128]{0:T(128)S(1)}, s32[128]{0:T(128)}, u32[]{:S(2)}) copy-start(s32[128]{0:T(128)} %param.17) | copy-start | bytes 1540
  25.8 2.8 %collective-permute-start.10 = (bf16[384,128]{1,0:T(8,128)(2,1)S(1)}, bf16[384,128]{1,0:T(8,128)(2,1)S(1)}, u32[]{:S(2)}, u32[]{:S(2)}) collective-permute-start(bf16[384,128]{1,0:T(8,128)(2,1)S(1)} %slice.70), channel_id=1, source_target_pairs={{0,1},{1,0},{2,3},{3,2},{4,5},{5,4},{6,7},{7,6},{8,9},{9,8},{10,11... | collective-permute-start | bytes 294920 | tf_op jit(solution)/shard_map/ppermute | solution.py:283
  27.9 1.9 %collective-permute-start.11 = (bf16[384,128]{1,0:T(8,128)(2,1)S(1)}, bf16[384,128]{1,0:T(8,128)(2,1)S(1)}, u32[]{:S(2)}, u32[]{:S(2)}) collective-permute-start(bf16[384,128]{1,0:T(8,128)(2,1)S(1)} %slice.71), channel_id=1, source_target_pairs={{0,1},{1,0},{2,3},{3,2},{4,5},{5,4},{6,7},{7,6},{8,9},{9,8},{10,11... | collective-permute-start | bytes 294920 | tf_op jit(solution)/shard_map/ppermute | solution.py:283
  28.0 1.9 %collective-permute-start.12 = (bf16[384,128]{1,0:T(8,128)(2,1)S(1)}, bf16[384,128]{1,0:T(8,128)(2,1)S(1)}, u32[]{:S(2)}, u32[]{:S(2)}) collective-permute-start(bf16[384,128]{1,0:T(8,128)(2,1)S(1)} %slice.72), channel_id=1, source_target_pairs={{0,1},{1,0},{2,3},{3,2},{4,5},{5,4},{6,7},{7,6},{8,9},{9,8},{10,11... | collective-permute-start | bytes 294920 | tf_op jit(solution)/shard_map/ppermute | solution.py:283
  28.5 1.3 %collective-permute-start.13 = (bf16[384,128]{1,0:T(8,128)(2,1)S(1)}, bf16[384,128]{1,0:T(8,128)(2,1)S(1)}, u32[]{:S(2)}, u32[]{:S(2)}) collective-permute-start(bf16[384,128]{1,0:T(8,128)(2,1)S(1)} %slice.73), channel_id=1, source_target_pairs={{0,1},{1,0},{2,3},{3,2},{4,5},{5,4},{6,7},{7,6},{8,9},{9,8},{10,11... | collective-permute-start | bytes 294920 | tf_op jit(solution)/shard_map/ppermute | solution.py:283
  29.7 10.0 %copy-start = (f32[128,128]{1,0:T(8,128)S(1)}, f32[128,128]{1,0:T(8,128)}, u32[]{:S(2)}) copy-start(f32[128,128]{1,0:T(8,128)} %refs_5_.3) | copy-start | bytes 196612
  29.7 10.0 %copy-start.1 = (f32[128,128]{1,0:T(8,128)S(1)}, f32[128,128]{1,0:T(8,128)}, u32[]{:S(2)}) copy-start(f32[128,128]{1,0:T(8,128)} %refs_6_.3) | copy-start | bytes 196612
  29.8 10.0 %copy-start.2 = (f32[128,128]{1,0:T(8,128)S(1)}, f32[128,128]{1,0:T(8,128)}, u32[]{:S(2)}) copy-start(f32[128,128]{1,0:T(8,128)} %refs_7_.3) | copy-start | bytes 196612
  29.8 10.0 %copy-start.3 = (f32[128,128]{1,0:T(8,128)S(1)}, f32[128,128]{1,0:T(8,128)}, u32[]{:S(2)}) copy-start(f32[128,128]{1,0:T(8,128)} %refs_8_.1) | copy-start | bytes 196612
  29.8 10.0 %copy-start.4 = (f32[128,128]{1,0:T(8,128)S(1)}, f32[128,128]{1,0:T(8,128)}, u32[]{:S(2)}) copy-start(f32[128,128]{1,0:T(8,128)} %refs_9_.1) | copy-start | bytes 196612
  32.3 6.0 %collective-permute-start.14 = (bf16[128,128]{1,0:T(8,128)(2,1)S(1)}, bf16[128,128]{1,0:T(8,128)(2,1)S(1)}, u32[]{:S(2)}, u32[]{:S(2)}) collective-permute-start(bf16[128,128]{1,0:T(8,128)(2,1)S(1)} %get-tuple-element.34), channel_id=1, source_target_pairs={{0,12},{2,14},{4,8},{6,10},{8,4},{10,6},{12,0},{14,2},{1,13},{3,15... | collective-permute-start | bytes 98312 | tf_op jit(solution)/shard_map/ppermute | solution.py:261
  34.9 4.8 %collective-permute-start.15 = (bf16[128,128]{1,0:T(8,128)(2,1)S(1)}, bf16[128,128]{1,0:T(8,128)(2,1)S(1)}, u32[]{:S(2)}, u32[]{:S(2)}) collective-permute-start(bf16[128,128]{1,0:T(8,128)(2,1)S(1)} %get-tuple-element.35), channel_id=1, source_target_pairs={{0,8},{2,10},{4,12},{6,14},{8,0},{10,2},{12,4},{14,6},{1,9},{3,11}... | collective-permute-start | bytes 98312 | tf_op jit(solution)/shard_map/ppermute | solution.py:261
  34.9 4.8 %collective-permute-start.16 = (bf16[128,128]{1,0:T(8,128)(2,1)S(1)}, bf16[128,128]{1,0:T(8,128)(2,1)S(1)}, u32[]{:S(2)}, u32[]{:S(2)}) collective-permute-start(bf16[128,128]{1,0:T(8,128)(2,1)S(1)} %get-tuple-element.36), channel_id=1, source_target_pairs={{0,4},{2,6},{4,0},{6,2},{8,12},{10,14},{12,8},{14,10},{1,5},{3,7},... | collective-permute-start | bytes 98312 | tf_op jit(solution)/shard_map/ppermute | solution.py:261

commit v15 on v13

--- a/solution.py
+++ b/solution.py
@@ -301,7 +301,7 @@
         [VMEM, VMEM],
         [early[far, 0], sums],
     )
-    late = {(far + t, s): move(relayed[t], t, s) for t, s in near}
+    late = {(far + t, s): move(relayed[t], t, s) for t, s in sorted(near, key=sum, reverse=True)}
     shifts, mine = list(early), list(early.values())
     late_slots = slots_of(list(late.values()))
     mat, fields, sums, late_slots = call(

time: 39.8 us -> 38.9 us (0.977)
  waiting for transfers between devices: 12.2 us -> 11.3 us
    ppermute x10, waiting for transfers between devices: 12.1 us -> 11.2 us  [move(): return lax.ppermute(value, ('blk', 'col'), pairs)]
  transfers between devices with their start and end apart: 17 -> 17, of which waited for: 7 -> 8; matrix products, arithmetic and copies ran while one was open for 0% -> 0% of each run, Pallas kernels for 7% -> 7%
where the time goes in v15:
time: 38.9 us; the launch traced here: 38.7 us
  starting transfers between devices  18.3 us (47%)
  waiting for transfers between devices  11.3 us (29%)
  Pallas kernels  7.45 us (19%)
  between operations  1.52 us (4%)
    ppermute x10, starting transfers between devices, move(): return lax.ppermute(value, ('blk', 'col'), pairs)  17 us
    ppermute x10, waiting for transfers between devices, move(): return lax.ppermute(value, ('blk', 'col'), pairs)  11.2 us
    pallas_call x6, Pallas kernels, call(): pl.pallas_call(body, out_shape=list(outs), in_specs=in_specs, out_specs=s...  7.45 us
    ppermute x7, starting transfers between devices, other_core(): return [lax.ppermute(v[:top], 'rep', [(0, 1), (1, 0)]) for v in values]  1.31 us
  transfers between devices with their start and end apart: 17, of which 8 were waited for; matrix products, arithmetic and copies ran while one was open for 0% of the time, Pallas kernels for 7%

profile of v15, /device:TPU:0, one launch (start us, length us, event | category | flops | bytes accessed | tf_op | source)
XLA Modules:
  0.0 38.7 jit_solution(1991978750664962292)
XLA Ops:
  1.3 1.5 %shard_map.104 = (bf16[720,128]{1,0:T(8,128)(2,1)S(1)}, bf16[560,128]{1,0:T(8,128)(2,1)S(1)}, bf16[560,128]{1,0:T(8,128)(2,1)S(1)}, bf16[176,128]{1,0:T(8,128)(2,1)S(1)}) custom-call(s32[1,1]{1,0:T(1,128)S(6)} %copy.19.refs_0_, f32[128,128]{1,0:T(8,128)} %refs_5_.3, f32[128,128]{1,0:T(8,128)} %refs_6_.3, f32[128,128]{1,0:T(8,128)} %refs_7_.3, ...), custom_call_target="tpu_custom_call" | custom-call | bytes 1040412 | tf_op jit(solution)/shard_map/pallas_call | solution.py:40
  2.8 3.1 %collective-permute-start.2 = (bf16[560,128]{1,0:T(8,128)(2,1)S(1)}, bf16[560,128]{1,0:T(8,128)(2,1)S(1)}, u32[]{:S(2)}, u32[]{:S(2)}) collective-permute-start(bf16[560,128]{1,0:T(8,128)(2,1)S(1)} %get-tuple-element.22), channel_id=1, source_target_pairs={{0,4},{2,6},{4,0},{6,2},{8,12},{10,14},{12,8},{14,10},{1,5},{3,7},... | collective-permute-start | bytes 430088 | tf_op jit(solution)/shard_map/ppermute | solution.py:257
  5.9 2.6 %collective-permute-start = (bf16[720,128]{1,0:T(8,128)(2,1)S(1)}, bf16[720,128]{1,0:T(8,128)(2,1)S(1)}, u32[]{:S(2)}, u32[]{:S(2)}) collective-permute-start(bf16[720,128]{1,0:T(8,128)(2,1)S(1)} %get-tuple-element.20), channel_id=1, source_target_pairs={{0,8},{2,10},{4,12},{6,14},{8,0},{10,2},{12,4},{14,6},{1,9},{3,11}... | collective-permute-start | bytes 552968 | tf_op jit(solution)/shard_map/ppermute | solution.py:257
  8.4 1.5 %collective-permute-start.1 = (bf16[560,128]{1,0:T(8,128)(2,1)S(1)}, bf16[560,128]{1,0:T(8,128)(2,1)S(1)}, u32[]{:S(2)}, u32[]{:S(2)}) collective-permute-start(bf16[560,128]{1,0:T(8,128)(2,1)S(1)} %get-tuple-element.21), channel_id=1, source_target_pairs={{0,2},{2,0},{4,6},{6,4},{8,10},{10,8},{12,14},{14,12},{1,3},{3,1},... | collective-permute-start | bytes 430088 | tf_op jit(solution)/shard_map/ppermute | solution.py:257
  9.9 2.0 %collective-permute-done.2.refs_2_ = bf16[560,128]{1,0:T(8,128)(2,1)S(1)} collective-permute-done((bf16[560,128]{1,0:T(8,128)(2,1)S(1)}, bf16[560,128]{1,0:T(8,128)(2,1)S(1)}, u32[]{:S(2)}, u32[]{:S(2)}) %collective-permute-start.2) | collective-permute-done | bytes 143392 | tf_op jit(solution)/shard_map/ppermute | solution.py:257
  12.0 1.8 %collective-permute-start.3 = (bf16[560,128]{1,0:T(8,128)(2,1)S(1)}, bf16[560,128]{1,0:T(8,128)(2,1)S(1)}, u32[]{:S(2)}, u32[]{:S(2)}) collective-permute-start(bf16[560,128]{1,0:T(8,128)(2,1)S(1)} %collective-permute-done.2.refs_2_), channel_id=1, source_target_pairs={{0,2},{2,0},{4,6},{6,4},{8,10},{10,8},{12,14},{14,12},{1,3},{3,1},... | collective-permute-start | bytes 430088 | tf_op jit(solution)/shard_map/ppermute | solution.py:257
  13.8 1.6 %shard_map.105 = (bf16[1024,1024]{1,0:T(8,128)(2,1)S(1)}, bf16[5,32,1024]{2,1,0:T(8,128)(2,1)S(1)}, f32[8,128]{1,0:T(8,128)S(1)}) custom-call(s32[1,7]{1,0:T(1,128)S(1)} %slice_convert_fusion.slots, bf16[1,1,6,128,128]{4,3,2,1,0:T(8,128)(2,1)} %blocks_in.1, bf16[176,128]{1,0:T(8,128)(2,1)S(1)} %get-tuple-element.23.own), custom_call_target="tpu_custom_call" | custom-call | bytes 2670620 | tf_op jit(solution)/shard_map/pallas_call | solution.py:40
  15.4 1.5 %collective-permute-done.came.refs_0_ = bf16[720,128]{1,0:T(8,128)(2,1)S(1)} collective-permute-done((bf16[720,128]{1,0:T(8,128)(2,1)S(1)}, bf16[720,128]{1,0:T(8,128)(2,1)S(1)}, u32[]{:S(2)}, u32[]{:S(2)}) %collective-permute-start) | collective-permute-done | bytes 184352 | tf_op jit(solution)/shard_map/ppermute | solution.py:257
  16.9 0.6 %collective-permute-start.4 = (bf16[560,128]{1,0:T(8,128)(2,1)S(1)}, bf16[560,128]{1,0:T(8,128)(2,1)S(1)}, u32[]{:S(2)}, u32[]{:S(2)}) collective-permute-start(bf16[560,128]{1,0:T(8,128)(2,1)S(1)} %get-tuple-element.25), channel_id=1, source_target_pairs={{0,6},{2,4},{4,2},{6,0},{8,14},{10,12},{12,10},{14,8},{1,7},{3,5},... | collective-permute-start | bytes 430088 | tf_op jit(solution)/shard_map/ppermute | solution.py:257
  17.5 2.4 %collective-permute-start.6 = (bf16[560,128]{1,0:T(8,128)(2,1)S(1)}, bf16[560,128]{1,0:T(8,128)(2,1)S(1)}, u32[]{:S(2)}, u32[]{:S(2)}) collective-permute-start(bf16[560,128]{1,0:T(8,128)(2,1)S(1)} %get-tuple-element.25), channel_id=1, source_target_pairs={{0,4},{2,6},{4,0},{6,2},{8,12},{10,14},{12,8},{14,10},{1,5},{3,7},... | collective-permute-start | bytes 430088 | tf_op jit(solution)/shard_map/ppermute | solution.py:257
  20.0 0.5 %collective-permute-start.5 = (bf16[560,128]{1,0:T(8,128)(2,1)S(1)}, bf16[560,128]{1,0:T(8,128)(2,1)S(1)}, u32[]{:S(2)}, u32[]{:S(2)}) collective-permute-start(bf16[560,128]{1,0:T(8,128)(2,1)S(1)} %get-tuple-element.26), channel_id=1, source_target_pairs={{0,2},{2,0},{4,6},{6,4},{8,10},{10,8},{12,14},{14,12},{1,3},{3,1},... | collective-permute-start | bytes 430088 | tf_op jit(solution)/shard_map/ppermute | solution.py:257
  20.5 0.0 collective-permute-done.1.refs_1_
  20.5 0.1 collective-permute-start.9
  20.7 0.0 collective-permute-done.3.refs_3_
  20.7 0.5 %collective-permute-start.8 = (bf16[384,128]{1,0:T(8,128)(2,1)S(1)}, bf16[384,128]{1,0:T(8,128)(2,1)S(1)}, u32[]{:S(2)}, u32[]{:S(2)}) collective-permute-start(bf16[384,128]{1,0:T(8,128)(2,1)S(1)} %slice.68), channel_id=1, source_target_pairs={{0,1},{1,0},{2,3},{3,2},{4,5},{5,4},{6,7},{7,6},{8,9},{9,8},{10,11... | collective-permute-start | bytes 294920 | tf_op jit(solution)/shard_map/ppermute | solution.py:279
  21.2 0.0 copy-start.5
  21.3 1.7 %collective-permute-done.4.refs_0_ = bf16[560,128]{1,0:T(8,128)(2,1)S(1)} collective-permute-done((bf16[560,128]{1,0:T(8,128)(2,1)S(1)}, bf16[560,128]{1,0:T(8,128)(2,1)S(1)}, u32[]{:S(2)}, u32[]{:S(2)}) %collective-permute-start.4) | collective-permute-done | bytes 143392 | tf_op jit(solution)/shard_map/ppermute | solution.py:257
  23.0 0.0 collective-permute-start.7
  23.0 1.5 %collective-permute-done.6.refs_2_ = bf16[560,128]{1,0:T(8,128)(2,1)S(1)} collective-permute-done((bf16[560,128]{1,0:T(8,128)(2,1)S(1)}, bf16[560,128]{1,0:T(8,128)(2,1)S(1)}, u32[]{:S(2)}, u32[]{:S(2)}) %collective-permute-start.6) | collective-permute-done | bytes 143392 | tf_op jit(solution)/shard_map/ppermute | solution.py:257
  24.6 0.0 collective-permute-start.10
  24.6 0.5 %collective-permute-done.5.refs_1_ = bf16[560,128]{1,0:T(8,128)(2,1)S(1)} collective-permute-done((bf16[560,128]{1,0:T(8,128)(2,1)S(1)}, bf16[560,128]{1,0:T(8,128)(2,1)S(1)}, u32[]{:S(2)}, u32[]{:S(2)}) %collective-permute-start.5) | collective-permute-done | bytes 143392 | tf_op jit(solution)/shard_map/ppermute | solution.py:257
  25.1 0.1 collective-permute-start.11
  25.2 0.0 collective-permute-done.9.refs_6_
  25.2 0.5 %collective-permute-start.13 = (bf16[384,128]{1,0:T(8,128)(2,1)S(1)}, bf16[384,128]{1,0:T(8,128)(2,1)S(1)}, u32[]{:S(2)}, u32[]{:S(2)}) collective-permute-start(bf16[384,128]{1,0:T(8,128)(2,1)S(1)} %slice.73), channel_id=1, source_target_pairs={{0,1},{1,0},{2,3},{3,2},{4,5},{5,4},{6,7},{7,6},{8,9},{9,8},{10,11... | collective-permute-start | bytes 294920 | tf_op jit(solution)/shard_map/ppermute | solution.py:279
  25.7 0.0 collective-permute-done.8.refs_5_
  25.7 0.1 collective-permute-start.12
  25.8 0.0 collective-permute-done.7.refs_4_
  25.8 0.1 collective-permute-done.10.refs_7_
  25.9 1.1 %shard_map.107 = (bf16[1024,1024]{1,0:T(8,128)(2,1)S(1)}, bf16[5,32,1024]{2,1,0:T(8,128)(2,1)S(1)}, f32[8,128]{1,0:T(8,128)S(1)}, s32[3,7]{1,0:T(4,128)S(4)}) custom-call(s32[4,7]{1,0:T(4,128)S(1)} %maximum_convert_fusion.slots, s32[3,7]{1,0:T(4,128)S(1)} %maximum_convert_fusion.1.late_slots, ...), custom_call_target="tpu_custom_call", output_to_operand_aliasing={{0}: (2, {}), {1}: (3, {})} | custom-call | bytes 5865752 | tf_op jit(solution)/shard_map/pallas_call | solution.py:40
  27.0 0.0 copy-start
  27.0 0.0 copy-start.1
  27.0 0.0 copy-start.2
  27.0 0.0 copy-start.3
  27.0 0.0 copy-start.4
  27.0 0.0 collective-permute-done.11.refs_3_
  27.0 0.0 collective-permute-done.13.refs_5_
  27.0 0.0 collective-permute-done.12.refs_4_
  27.1 0.0 copy-done.5
  27.1 2.5 %shard_map.108 = (bf16[128,128]{1,0:T(8,128)(2,1)S(1)}, bf16[128,128]{1,0:T(8,128)(2,1)S(1)}, bf16[128,128]{1,0:T(8,128)(2,1)S(1)}, bf16[128,128]{1,0:T(8,128)(2...) custom-call(s32[3,7]{1,0:T(4,128)S(4)} %get-tuple-element.29.slots, ...), custom_call_target="tpu_custom_call", output_to_operand_aliasing={{5}: (2, {}), {6}: (3, {})} | custom-call | flops 268435456 | bytes 5714516 | tf_op jit(solution)/shard_map/pallas_call | solution.py:40
  29.6 3.5 %collective-permute-start.14 = (bf16[128,128]{1,0:T(8,128)(2,1)S(1)}, bf16[128,128]{1,0:T(8,128)(2,1)S(1)}, u32[]{:S(2)}, u32[]{:S(2)}) collective-permute-start(bf16[128,128]{1,0:T(8,128)(2,1)S(1)} %get-tuple-element.34), channel_id=1, source_target_pairs={{0,12},{2,14},{4,8},{6,10},{8,4},{10,6},{12,0},{14,2},{1,13},{3,15... | collective-permute-start | bytes 98312 | tf_op jit(solution)/shard_map/ppermute | solution.py:257
  33.0 0.0 collective-permute-start.15
  33.0 1.0 %collective-permute-start.16 = (bf16[128,128]{1,0:T(8,128)(2,1)S(1)}, bf16[128,128]{1,0:T(8,128)(2,1)S(1)}, u32[]{:S(2)}, u32[]{:S(2)}) collective-permute-start(bf16[128,128]{1,0:T(8,128)(2,1)S(1)} %get-tuple-element.36), channel_id=1, source_target_pairs={{0,4},{2,6},{4,0},{6,2},{8,12},{10,14},{12,8},{14,10},{1,5},{3,7},... | collective-permute-start | bytes 98312 | tf_op jit(solution)/shard_map/ppermute | solution.py:257
  34.0 1.7 %collective-permute-done.14.refs_1_ = bf16[128,128]{1,0:T(8,128)(2,1)S(1)} collective-permute-done((bf16[128,128]{1,0:T(8,128)(2,1)S(1)}, bf16[128,128]{1,0:T(8,128)(2,1)S(1)}, u32[]{:S(2)}, u32[]{:S(2)}) %collective-permute-start.14) | collective-permute-done | bytes 32800 | tf_op jit(solution)/shard_map/ppermute | solution.py:257
  35.8 2.1 %collective-permute-done.15.refs_2_ = bf16[128,128]{1,0:T(8,128)(2,1)S(1)} collective-permute-done((bf16[128,128]{1,0:T(8,128)(2,1)S(1)}, bf16[128,128]{1,0:T(8,128)(2,1)S(1)}, u32[]{:S(2)}, u32[]{:S(2)}) %collective-permute-start.15) | collective-permute-done | bytes 32800 | tf_op jit(solution)/shard_map/ppermute | solution.py:257
  37.9 0.0 collective-permute-done.16.refs_3_
  37.9 0.0 copy-done
  37.9 0.0 copy-done.1
  37.9 0.0 copy-done.2
  37.9 0.0 copy-done.3
  37.9 0.0 copy-done.4
  37.9 0.8 %shard_map.109 = (f32[128,128]{1,0:T(8,128)}, f32[128,128]{1,0:T(8,128)}) custom-call(bf16[128,128]{1,0:T(8,128)(2,1)S(1)} %get-tuple-element.33.refs_0_, bf16[128,128]{1,0:T(8,128)(2,1)S(1)} %collective-permute-done.14.refs_1_, bf16[128,128]{1,0:T(8,128)(2,1)S(1)} %collective-permute-done.15.refs_2_, bf16[128,128]{1,0:T(8,128)(2,1)S(1)} %collective-permute-done.16.refs_3_, ...), custom_call_target="tpu_custom_call" | custom-call | bytes 594432 | tf_op jit(solution)/shard_map/pallas_call | solution.py:40
  (18 shorter events, 0.2 us)
Async XLA Ops:
  2.8 9.2 %collective-permute-start.2 = (bf16[560,128]{1,0:T(8,128)(2,1)S(1)}, bf16[560,128]{1,0:T(8,128)(2,1)S(1)}, u32[]{:S(2)}, u32[]{:S(2)}) collective-permute-start(bf16[560,128]{1,0:T(8,128)(2,1)S(1)} %get-tuple-element.22), channel_id=1, source_target_pairs={{0,4},{2,6},{4,0},{6,2},{8,12},{10,14},{12,8},{14,10},{1,5},{3,7},... | collective-permute-start | bytes 430088 | tf_op jit(solution)/shard_map/ppermute | solution.py:257
  5.9 11.1 %collective-permute-start = (bf16[720,128]{1,0:T(8,128)(2,1)S(1)}, bf16[720,128]{1,0:T(8,128)(2,1)S(1)}, u32[]{:S(2)}, u32[]{:S(2)}) collective-permute-start(bf16[720,128]{1,0:T(8,128)(2,1)S(1)} %get-tuple-element.20), channel_id=1, source_target_pairs={{0,8},{2,10},{4,12},{6,14},{8,0},{10,2},{12,4},{14,6},{1,9},{3,11}... | collective-permute-start | bytes 552968 | tf_op jit(solution)/shard_map/ppermute | solution.py:257
  8.4 12.1 %collective-permute-start.1 = (bf16[560,128]{1,0:T(8,128)(2,1)S(1)}, bf16[560,128]{1,0:T(8,128)(2,1)S(1)}, u32[]{:S(2)}, u32[]{:S(2)}) collective-permute-start(bf16[560,128]{1,0:T(8,128)(2,1)S(1)} %get-tuple-element.21), channel_id=1, source_target_pairs={{0,2},{2,0},{4,6},{6,4},{8,10},{10,8},{12,14},{14,12},{1,3},{3,1},... | collective-permute-start | bytes 430088 | tf_op jit(solution)/shard_map/ppermute | solution.py:257
  12.0 8.7 %collective-permute-start.3 = (bf16[560,128]{1,0:T(8,128)(2,1)S(1)}, bf16[560,128]{1,0:T(8,128)(2,1)S(1)}, u32[]{:S(2)}, u32[]{:S(2)}) collective-permute-start(bf16[560,128]{1,0:T(8,128)(2,1)S(1)} %collective-permute-done.2.refs_2_), channel_id=1, source_target_pairs={{0,2},{2,0},{4,6},{6,4},{8,10},{10,8},{12,14},{14,12},{1,3},{3,1},... | collective-permute-start | bytes 430088 | tf_op jit(solution)/shard_map/ppermute | solution.py:257
  16.9 6.1 %collective-permute-start.4 = (bf16[560,128]{1,0:T(8,128)(2,1)S(1)}, bf16[560,128]{1,0:T(8,128)(2,1)S(1)}, u32[]{:S(2)}, u32[]{:S(2)}) collective-permute-start(bf16[560,128]{1,0:T(8,128)(2,1)S(1)} %get-tuple-element.25), channel_id=1, source_target_pairs={{0,6},{2,4},{4,2},{6,0},{8,14},{10,12},{12,10},{14,8},{1,7},{3,5},... | collective-permute-start | bytes 430088 | tf_op jit(solution)/shard_map/ppermute | solution.py:257
  17.5 7.0 %collective-permute-start.6 = (bf16[560,128]{1,0:T(8,128)(2,1)S(1)}, bf16[560,128]{1,0:T(8,128)(2,1)S(1)}, u32[]{:S(2)}, u32[]{:S(2)}) collective-permute-start(bf16[560,128]{1,0:T(8,128)(2,1)S(1)} %get-tuple-element.25), channel_id=1, source_target_pairs={{0,4},{2,6},{4,0},{6,2},{8,12},{10,14},{12,8},{14,10},{1,5},{3,7},... | collective-permute-start | bytes 430088 | tf_op jit(solution)/shard_map/ppermute | solution.py:257
  20.0 5.1 %collective-permute-start.5 = (bf16[560,128]{1,0:T(8,128)(2,1)S(1)}, bf16[560,128]{1,0:T(8,128)(2,1)S(1)}, u32[]{:S(2)}, u32[]{:S(2)}) collective-permute-start(bf16[560,128]{1,0:T(8,128)(2,1)S(1)} %get-tuple-element.26), channel_id=1, source_target_pairs={{0,2},{2,0},{4,6},{6,4},{8,10},{10,8},{12,14},{14,12},{1,3},{3,1},... | collective-permute-start | bytes 430088 | tf_op jit(solution)/shard_map/ppermute | solution.py:257
  20.5 4.7 %collective-permute-start.9 = (bf16[384,128]{1,0:T(8,128)(2,1)S(1)}, bf16[384,128]{1,0:T(8,128)(2,1)S(1)}, u32[]{:S(2)}, u32[]{:S(2)}) collective-permute-start(bf16[384,128]{1,0:T(8,128)(2,1)S(1)} %slice.69), channel_id=1, source_target_pairs={{0,1},{1,0},{2,3},{3,2},{4,5},{5,4},{6,7},{7,6},{8,9},{9,8},{10,11... | collective-permute-start | bytes 294920 | tf_op jit(solution)/shard_map/ppermute | solution.py:279
  20.7 5.0 %collective-permute-start.8 = (bf16[384,128]{1,0:T(8,128)(2,1)S(1)}, bf16[384,128]{1,0:T(8,128)(2,1)S(1)}, u32[]{:S(2)}, u32[]{:S(2)}) collective-permute-start(bf16[384,128]{1,0:T(8,128)(2,1)S(1)} %slice.68), channel_id=1, source_target_pairs={{0,1},{1,0},{2,3},{3,2},{4,5},{5,4},{6,7},{7,6},{8,9},{9,8},{10,11... | collective-permute-start | bytes 294920 | tf_op jit(solution)/shard_map/ppermute | solution.py:279
  21.2 5.8 %copy-start.5 = (s32[128]{0:T(128)S(1)}, s32[128]{0:T(128)}, u32[]{:S(2)}) copy-start(s32[128]{0:T(128)} %param.17) | copy-start | bytes 1540
  23.0 2.8 %collective-permute-start.7 = (bf16[384,128]{1,0:T(8,128)(2,1)S(1)}, bf16[384,128]{1,0:T(8,128)(2,1)S(1)}, u32[]{:S(2)}, u32[]{:S(2)}) collective-permute-start(bf16[384,128]{1,0:T(8,128)(2,1)S(1)} %slice.67), channel_id=1, source_target_pairs={{0,1},{1,0},{2,3},{3,2},{4,5},{5,4},{6,7},{7,6},{8,9},{9,8},{10,11... | collective-permute-start | bytes 294920 | tf_op jit(solution)/shard_map/ppermute | solution.py:279
  24.6 1.3 %collective-permute-start.10 = (bf16[384,128]{1,0:T(8,128)(2,1)S(1)}, bf16[384,128]{1,0:T(8,128)(2,1)S(1)}, u32[]{:S(2)}, u32[]{:S(2)}) collective-permute-start(bf16[384,128]{1,0:T(8,128)(2,1)S(1)} %slice.70), channel_id=1, source_target_pairs={{0,1},{1,0},{2,3},{3,2},{4,5},{5,4},{6,7},{7,6},{8,9},{9,8},{10,11... | collective-permute-start | bytes 294920 | tf_op jit(solution)/shard_map/ppermute | solution.py:279
  25.1 2.0 %collective-permute-start.11 = (bf16[384,128]{1,0:T(8,128)(2,1)S(1)}, bf16[384,128]{1,0:T(8,128)(2,1)S(1)}, u32[]{:S(2)}, u32[]{:S(2)}) collective-permute-start(bf16[384,128]{1,0:T(8,128)(2,1)S(1)} %slice.71), channel_id=1, source_target_pairs={{0,1},{1,0},{2,3},{3,2},{4,5},{5,4},{6,7},{7,6},{8,9},{9,8},{10,11... | collective-permute-start | bytes 294920 | tf_op jit(solution)/shard_map/ppermute | solution.py:279
  25.2 1.8 %collective-permute-start.13 = (bf16[384,128]{1,0:T(8,128)(2,1)S(1)}, bf16[384,128]{1,0:T(8,128)(2,1)S(1)}, u32[]{:S(2)}, u32[]{:S(2)}) collective-permute-start(bf16[384,128]{1,0:T(8,128)(2,1)S(1)} %slice.73), channel_id=1, source_target_pairs={{0,1},{1,0},{2,3},{3,2},{4,5},{5,4},{6,7},{7,6},{8,9},{9,8},{10,11... | collective-permute-start | bytes 294920 | tf_op jit(solution)/shard_map/ppermute | solution.py:279
  25.7 1.4 %collective-permute-start.12 = (bf16[384,128]{1,0:T(8,128)(2,1)S(1)}, bf16[384,128]{1,0:T(8,128)(2,1)S(1)}, u32[]{:S(2)}, u32[]{:S(2)}) collective-permute-start(bf16[384,128]{1,0:T(8,128)(2,1)S(1)} %slice.72), channel_id=1, source_target_pairs={{0,1},{1,0},{2,3},{3,2},{4,5},{5,4},{6,7},{7,6},{8,9},{9,8},{10,11... | collective-permute-start | bytes 294920 | tf_op jit(solution)/shard_map/ppermute | solution.py:279
  27.0 10.9 %copy-start = (f32[128,128]{1,0:T(8,128)S(1)}, f32[128,128]{1,0:T(8,128)}, u32[]{:S(2)}) copy-start(f32[128,128]{1,0:T(8,128)} %refs_5_.3) | copy-start | bytes 196612
  27.0 10.9 %copy-start.1 = (f32[128,128]{1,0:T(8,128)S(1)}, f32[128,128]{1,0:T(8,128)}, u32[]{:S(2)}) copy-start(f32[128,128]{1,0:T(8,128)} %refs_6_.3) | copy-start | bytes 196612
  27.0 10.9 %copy-start.2 = (f32[128,128]{1,0:T(8,128)S(1)}, f32[128,128]{1,0:T(8,128)}, u32[]{:S(2)}) copy-start(f32[128,128]{1,0:T(8,128)} %refs_7_.3) | copy-start | bytes 196612
  27.0 10.9 %copy-start.3 = (f32[128,128]{1,0:T(8,128)S(1)}, f32[128,128]{1,0:T(8,128)}, u32[]{:S(2)}) copy-start(f32[128,128]{1,0:T(8,128)} %refs_8_.1) | copy-start | bytes 196612
  27.0 10.9 %copy-start.4 = (f32[128,128]{1,0:T(8,128)S(1)}, f32[128,128]{1,0:T(8,128)}, u32[]{:S(2)}) copy-start(f32[128,128]{1,0:T(8,128)} %refs_9_.1) | copy-start | bytes 196612
  29.6 6.2 %collective-permute-start.14 = (bf16[128,128]{1,0:T(8,128)(2,1)S(1)}, bf16[128,128]{1,0:T(8,128)(2,1)S(1)}, u32[]{:S(2)}, u32[]{:S(2)}) collective-permute-start(bf16[128,128]{1,0:T(8,128)(2,1)S(1)} %get-tuple-element.34), channel_id=1, source_target_pairs={{0,12},{2,14},{4,8},{6,10},{8,4},{10,6},{12,0},{14,2},{1,13},{3,15... | collective-permute-start | bytes 98312 | tf_op jit(solution)/shard_map/ppermute | solution.py:257
  33.0 4.8 %collective-permute-start.15 = (bf16[128,128]{1,0:T(8,128)(2,1)S(1)}, bf16[128,128]{1,0:T(8,128)(2,1)S(1)}, u32[]{:S(2)}, u32[]{:S(2)}) collective-permute-start(bf16[128,128]{1,0:T(8,128)(2,1)S(1)} %get-tuple-element.35), channel_id=1, source_target_pairs={{0,8},{2,10},{4,12},{6,14},{8,0},{10,2},{12,4},{14,6},{1,9},{3,11}... | collective-permute-start | bytes 98312 | tf_op jit(solution)/shard_map/ppermute | solution.py:257
  33.0 4.8 %collective-permute-start.16 = (bf16[128,128]{1,0:T(8,128)(2,1)S(1)}, bf16[128,128]{1,0:T(8,128)(2,1)S(1)}, u32[]{:S(2)}, u32[]{:S(2)}) collective-permute-start(bf16[128,128]{1,0:T(8,128)(2,1)S(1)} %get-tuple-element.36), channel_id=1, source_target_pairs={{0,4},{2,6},{4,0},{6,2},{8,12},{10,14},{12,8},{14,10},{1,5},{3,7},... | collective-permute-start | bytes 98312 | tf_op jit(solution)/shard_map/ppermute | solution.py:257

commit v16 on v15

--- a/solution.py
+++ b/solution.py
@@ -85,7 +85,7 @@
         values = field[...]
         if j < 2:
             rows += split_parts(jnp.sum(values * values, axis=0, keepdims=True))
-        turned[j] = values.T.astype(BF16)
+        turned[j] = values.astype(BF16).T
     for copy in copies[FIELDS:]:
         copy.wait()
     lane = lax.broadcasted_iota(jnp.int32, (1, tile), 1)
@@ -232,7 +232,7 @@
             products[j, rows, :] = recv[j * part : (j + 1) * part, :]
 
     def turned(j):
-        return products[j].astype(F32).T
+        return products[j].T.astype(F32)
 
     tau, sigma = scales[0:1, :], scales[1:2, :]
     primal, dual = x_in[...], y_in[...]

time: 38.9 us -> 38.7 us (level)
  no operation moved by 1% of the time
where the time goes in v16:
time: 38.7 us; the launch traced here: 38.5 us
  starting transfers between devices  18.3 us (47%)
  waiting for transfers between devices  11.3 us (29%)
  Pallas kernels  7.3 us (19%)
  between operations  1.52 us (4%)
    ppermute x10, starting transfers between devices, move(): return lax.ppermute(value, ('blk', 'col'), pairs)  17 us
    ppermute x10, waiting for transfers between devices, move(): return lax.ppermute(value, ('blk', 'col'), pairs)  11.2 us
    pallas_call x6, Pallas kernels, call(): pl.pallas_call(body, out_shape=list(outs), in_specs=in_specs, out_specs=s...  7.3 us
    ppermute x7, starting transfers between devices, other_core(): return [lax.ppermute(v[:top], 'rep', [(0, 1), (1, 0)]) for v in values]  1.31 us
  transfers between devices with their start and end apart: 17, of which 8 were waited for; matrix products, arithmetic and copies ran while one was open for 0% of the time, Pallas kernels for 7%

profile of v16, /device:TPU:0, one launch (start us, length us, event | category | flops | bytes accessed | tf_op | source)
XLA Modules:
  0.0 38.5 jit_solution(5470522971559044592)
XLA Ops:
  1.3 1.3 %shard_map.104 = (bf16[720,128]{1,0:T(8,128)(2,1)S(1)}, bf16[560,128]{1,0:T(8,128)(2,1)S(1)}, bf16[560,128]{1,0:T(8,128)(2,1)S(1)}, bf16[176,128]{1,0:T(8,128)(2,1)S(1)}) custom-call(s32[1,1]{1,0:T(1,128)S(6)} %copy.19.refs_0_, f32[128,128]{1,0:T(8,128)} %refs_5_.3, f32[128,128]{1,0:T(8,128)} %refs_6_.3, f32[128,128]{1,0:T(8,128)} %refs_7_.3, ...), custom_call_target="tpu_custom_call" | custom-call | bytes 1040412 | tf_op jit(solution)/shard_map/pallas_call | solution.py:40
  2.6 3.1 %collective-permute-start.2 = (bf16[560,128]{1,0:T(8,128)(2,1)S(1)}, bf16[560,128]{1,0:T(8,128)(2,1)S(1)}, u32[]{:S(2)}, u32[]{:S(2)}) collective-permute-start(bf16[560,128]{1,0:T(8,128)(2,1)S(1)} %get-tuple-element.22), channel_id=1, source_target_pairs={{0,4},{2,6},{4,0},{6,2},{8,12},{10,14},{12,8},{14,10},{1,5},{3,7},... | collective-permute-start | bytes 430088 | tf_op jit(solution)/shard_map/ppermute | solution.py:257
  5.7 2.6 %collective-permute-start = (bf16[720,128]{1,0:T(8,128)(2,1)S(1)}, bf16[720,128]{1,0:T(8,128)(2,1)S(1)}, u32[]{:S(2)}, u32[]{:S(2)}) collective-permute-start(bf16[720,128]{1,0:T(8,128)(2,1)S(1)} %get-tuple-element.20), channel_id=1, source_target_pairs={{0,8},{2,10},{4,12},{6,14},{8,0},{10,2},{12,4},{14,6},{1,9},{3,11}... | collective-permute-start | bytes 552968 | tf_op jit(solution)/shard_map/ppermute | solution.py:257
  8.3 1.5 %collective-permute-start.1 = (bf16[560,128]{1,0:T(8,128)(2,1)S(1)}, bf16[560,128]{1,0:T(8,128)(2,1)S(1)}, u32[]{:S(2)}, u32[]{:S(2)}) collective-permute-start(bf16[560,128]{1,0:T(8,128)(2,1)S(1)} %get-tuple-element.21), channel_id=1, source_target_pairs={{0,2},{2,0},{4,6},{6,4},{8,10},{10,8},{12,14},{14,12},{1,3},{3,1},... | collective-permute-start | bytes 430088 | tf_op jit(solution)/shard_map/ppermute | solution.py:257
  9.8 2.0 %collective-permute-done.2.refs_2_ = bf16[560,128]{1,0:T(8,128)(2,1)S(1)} collective-permute-done((bf16[560,128]{1,0:T(8,128)(2,1)S(1)}, bf16[560,128]{1,0:T(8,128)(2,1)S(1)}, u32[]{:S(2)}, u32[]{:S(2)}) %collective-permute-start.2) | collective-permute-done | bytes 143392 | tf_op jit(solution)/shard_map/ppermute | solution.py:257
  11.8 1.8 %collective-permute-start.3 = (bf16[560,128]{1,0:T(8,128)(2,1)S(1)}, bf16[560,128]{1,0:T(8,128)(2,1)S(1)}, u32[]{:S(2)}, u32[]{:S(2)}) collective-permute-start(bf16[560,128]{1,0:T(8,128)(2,1)S(1)} %collective-permute-done.2.refs_2_), channel_id=1, source_target_pairs={{0,2},{2,0},{4,6},{6,4},{8,10},{10,8},{12,14},{14,12},{1,3},{3,1},... | collective-permute-start | bytes 430088 | tf_op jit(solution)/shard_map/ppermute | solution.py:257
  13.7 1.5 %shard_map.105 = (bf16[1024,1024]{1,0:T(8,128)(2,1)S(1)}, bf16[5,32,1024]{2,1,0:T(8,128)(2,1)S(1)}, f32[8,128]{1,0:T(8,128)S(1)}) custom-call(s32[1,7]{1,0:T(1,128)S(1)} %slice_convert_fusion.slots, bf16[1,1,6,128,128]{4,3,2,1,0:T(8,128)(2,1)} %blocks_in.1, bf16[176,128]{1,0:T(8,128)(2,1)S(1)} %get-tuple-element.23.own), custom_call_target="tpu_custom_call" | custom-call | bytes 2670620 | tf_op jit(solution)/shard_map/pallas_call | solution.py:40
  15.2 1.5 %collective-permute-done.came.refs_0_ = bf16[720,128]{1,0:T(8,128)(2,1)S(1)} collective-permute-done((bf16[720,128]{1,0:T(8,128)(2,1)S(1)}, bf16[720,128]{1,0:T(8,128)(2,1)S(1)}, u32[]{:S(2)}, u32[]{:S(2)}) %collective-permute-start) | collective-permute-done | bytes 184352 | tf_op jit(solution)/shard_map/ppermute | solution.py:257
  16.8 0.6 %collective-permute-start.4 = (bf16[560,128]{1,0:T(8,128)(2,1)S(1)}, bf16[560,128]{1,0:T(8,128)(2,1)S(1)}, u32[]{:S(2)}, u32[]{:S(2)}) collective-permute-start(bf16[560,128]{1,0:T(8,128)(2,1)S(1)} %get-tuple-element.25), channel_id=1, source_target_pairs={{0,6},{2,4},{4,2},{6,0},{8,14},{10,12},{12,10},{14,8},{1,7},{3,5},... | collective-permute-start | bytes 430088 | tf_op jit(solution)/shard_map/ppermute | solution.py:257
  17.4 2.4 %collective-permute-start.6 = (bf16[560,128]{1,0:T(8,128)(2,1)S(1)}, bf16[560,128]{1,0:T(8,128)(2,1)S(1)}, u32[]{:S(2)}, u32[]{:S(2)}) collective-permute-start(bf16[560,128]{1,0:T(8,128)(2,1)S(1)} %get-tuple-element.25), channel_id=1, source_target_pairs={{0,4},{2,6},{4,0},{6,2},{8,12},{10,14},{12,8},{14,10},{1,5},{3,7},... | collective-permute-start | bytes 430088 | tf_op jit(solution)/shard_map/ppermute | solution.py:257
  19.8 0.5 %collective-permute-start.5 = (bf16[560,128]{1,0:T(8,128)(2,1)S(1)}, bf16[560,128]{1,0:T(8,128)(2,1)S(1)}, u32[]{:S(2)}, u32[]{:S(2)}) collective-permute-start(bf16[560,128]{1,0:T(8,128)(2,1)S(1)} %get-tuple-element.26), channel_id=1, source_target_pairs={{0,2},{2,0},{4,6},{6,4},{8,10},{10,8},{12,14},{14,12},{1,3},{3,1},... | collective-permute-start | bytes 430088 | tf_op jit(solution)/shard_map/ppermute | solution.py:257
  20.4 0.0 collective-permute-done.1.refs_1_
  20.4 0.1 collective-permute-start.9
  20.5 0.0 collective-permute-done.3.refs_3_
  20.5 0.5 %collective-permute-start.8 = (bf16[384,128]{1,0:T(8,128)(2,1)S(1)}, bf16[384,128]{1,0:T(8,128)(2,1)S(1)}, u32[]{:S(2)}, u32[]{:S(2)}) collective-permute-start(bf16[384,128]{1,0:T(8,128)(2,1)S(1)} %slice.68), channel_id=1, source_target_pairs={{0,1},{1,0},{2,3},{3,2},{4,5},{5,4},{6,7},{7,6},{8,9},{9,8},{10,11... | collective-permute-start | bytes 294920 | tf_op jit(solution)/shard_map/ppermute | solution.py:279
  21.1 0.0 copy-start.5
  21.1 1.7 %collective-permute-done.4.refs_0_ = bf16[560,128]{1,0:T(8,128)(2,1)S(1)} collective-permute-done((bf16[560,128]{1,0:T(8,128)(2,1)S(1)}, bf16[560,128]{1,0:T(8,128)(2,1)S(1)}, u32[]{:S(2)}, u32[]{:S(2)}) %collective-permute-start.4) | collective-permute-done | bytes 143392 | tf_op jit(solution)/shard_map/ppermute | solution.py:257
  22.9 0.0 collective-permute-start.7
  22.9 1.5 %collective-permute-done.6.refs_2_ = bf16[560,128]{1,0:T(8,128)(2,1)S(1)} collective-permute-done((bf16[560,128]{1,0:T(8,128)(2,1)S(1)}, bf16[560,128]{1,0:T(8,128)(2,1)S(1)}, u32[]{:S(2)}, u32[]{:S(2)}) %collective-permute-start.6) | collective-permute-done | bytes 143392 | tf_op jit(solution)/shard_map/ppermute | solution.py:257
  24.4 0.0 collective-permute-start.10
  24.5 0.5 %collective-permute-done.5.refs_1_ = bf16[560,128]{1,0:T(8,128)(2,1)S(1)} collective-permute-done((bf16[560,128]{1,0:T(8,128)(2,1)S(1)}, bf16[560,128]{1,0:T(8,128)(2,1)S(1)}, u32[]{:S(2)}, u32[]{:S(2)}) %collective-permute-start.5) | collective-permute-done | bytes 143392 | tf_op jit(solution)/shard_map/ppermute | solution.py:257
  24.9 0.1 collective-permute-start.11
  25.0 0.0 collective-permute-done.9.refs_6_
  25.1 0.5 %collective-permute-start.13 = (bf16[384,128]{1,0:T(8,128)(2,1)S(1)}, bf16[384,128]{1,0:T(8,128)(2,1)S(1)}, u32[]{:S(2)}, u32[]{:S(2)}) collective-permute-start(bf16[384,128]{1,0:T(8,128)(2,1)S(1)} %slice.73), channel_id=1, source_target_pairs={{0,1},{1,0},{2,3},{3,2},{4,5},{5,4},{6,7},{7,6},{8,9},{9,8},{10,11... | collective-permute-start | bytes 294920 | tf_op jit(solution)/shard_map/ppermute | solution.py:279
  25.5 0.0 collective-permute-done.8.refs_5_
  25.5 0.1 collective-permute-start.12
  25.6 0.0 collective-permute-done.7.refs_4_
  25.7 0.1 collective-permute-done.10.refs_7_
  25.7 1.1 %shard_map.107 = (bf16[1024,1024]{1,0:T(8,128)(2,1)S(1)}, bf16[5,32,1024]{2,1,0:T(8,128)(2,1)S(1)}, f32[8,128]{1,0:T(8,128)S(1)}, s32[3,7]{1,0:T(4,128)S(4)}) custom-call(s32[4,7]{1,0:T(4,128)S(1)} %maximum_convert_fusion.slots, s32[3,7]{1,0:T(4,128)S(1)} %maximum_convert_fusion.1.late_slots, ...), custom_call_target="tpu_custom_call", output_to_operand_aliasing={{0}: (2, {}), {1}: (3, {})} | custom-call | bytes 5865752 | tf_op jit(solution)/shard_map/pallas_call | solution.py:40
  26.8 0.0 copy-start
  26.8 0.0 copy-start.1
  26.9 0.0 copy-start.2
  26.9 0.0 copy-start.3
  26.9 0.0 copy-start.4
  26.9 0.0 collective-permute-done.11.refs_3_
  26.9 0.0 collective-permute-done.13.refs_5_
  26.9 0.0 collective-permute-done.12.refs_4_
  26.9 0.0 copy-done.5
  26.9 2.5 %shard_map.108 = (bf16[128,128]{1,0:T(8,128)(2,1)S(1)}, bf16[128,128]{1,0:T(8,128)(2,1)S(1)}, bf16[128,128]{1,0:T(8,128)(2,1)S(1)}, bf16[128,128]{1,0:T(8,128)(2...) custom-call(s32[3,7]{1,0:T(4,128)S(4)} %get-tuple-element.29.slots, ...), custom_call_target="tpu_custom_call", output_to_operand_aliasing={{5}: (2, {}), {6}: (3, {})} | custom-call | flops 268435456 | bytes 5714516 | tf_op jit(solution)/shard_map/pallas_call | solution.py:40
  29.4 3.5 %collective-permute-start.14 = (bf16[128,128]{1,0:T(8,128)(2,1)S(1)}, bf16[128,128]{1,0:T(8,128)(2,1)S(1)}, u32[]{:S(2)}, u32[]{:S(2)}) collective-permute-start(bf16[128,128]{1,0:T(8,128)(2,1)S(1)} %get-tuple-element.34), channel_id=1, source_target_pairs={{0,12},{2,14},{4,8},{6,10},{8,4},{10,6},{12,0},{14,2},{1,13},{3,15... | collective-permute-start | bytes 98312 | tf_op jit(solution)/shard_map/ppermute | solution.py:257
  32.9 0.0 collective-permute-start.15
  32.9 1.0 %collective-permute-start.16 = (bf16[128,128]{1,0:T(8,128)(2,1)S(1)}, bf16[128,128]{1,0:T(8,128)(2,1)S(1)}, u32[]{:S(2)}, u32[]{:S(2)}) collective-permute-start(bf16[128,128]{1,0:T(8,128)(2,1)S(1)} %get-tuple-element.36), channel_id=1, source_target_pairs={{0,4},{2,6},{4,0},{6,2},{8,12},{10,14},{12,8},{14,10},{1,5},{3,7},... | collective-permute-start | bytes 98312 | tf_op jit(solution)/shard_map/ppermute | solution.py:257
  33.9 1.7 %collective-permute-done.14.refs_1_ = bf16[128,128]{1,0:T(8,128)(2,1)S(1)} collective-permute-done((bf16[128,128]{1,0:T(8,128)(2,1)S(1)}, bf16[128,128]{1,0:T(8,128)(2,1)S(1)}, u32[]{:S(2)}, u32[]{:S(2)}) %collective-permute-start.14) | collective-permute-done | bytes 32800 | tf_op jit(solution)/shard_map/ppermute | solution.py:257
  35.6 2.1 %collective-permute-done.15.refs_2_ = bf16[128,128]{1,0:T(8,128)(2,1)S(1)} collective-permute-done((bf16[128,128]{1,0:T(8,128)(2,1)S(1)}, bf16[128,128]{1,0:T(8,128)(2,1)S(1)}, u32[]{:S(2)}, u32[]{:S(2)}) %collective-permute-start.15) | collective-permute-done | bytes 32800 | tf_op jit(solution)/shard_map/ppermute | solution.py:257
  37.7 0.0 collective-permute-done.16.refs_3_
  37.7 0.0 copy-done
  37.7 0.0 copy-done.1
  37.7 0.0 copy-done.2
  37.7 0.0 copy-done.3
  37.8 0.0 copy-done.4
  37.8 0.8 %shard_map.109 = (f32[128,128]{1,0:T(8,128)}, f32[128,128]{1,0:T(8,128)}) custom-call(bf16[128,128]{1,0:T(8,128)(2,1)S(1)} %get-tuple-element.33.refs_0_, bf16[128,128]{1,0:T(8,128)(2,1)S(1)} %collective-permute-done.14.refs_1_, bf16[128,128]{1,0:T(8,128)(2,1)S(1)} %collective-permute-done.15.refs_2_, bf16[128,128]{1,0:T(8,128)(2,1)S(1)} %collective-permute-done.16.refs_3_, ...), custom_call_target="tpu_custom_call" | custom-call | bytes 594432 | tf_op jit(solution)/shard_map/pallas_call | solution.py:40
  (18 shorter events, 0.2 us)
Async XLA Ops:
  2.6 9.2 %collective-permute-start.2 = (bf16[560,128]{1,0:T(8,128)(2,1)S(1)}, bf16[560,128]{1,0:T(8,128)(2,1)S(1)}, u32[]{:S(2)}, u32[]{:S(2)}) collective-permute-start(bf16[560,128]{1,0:T(8,128)(2,1)S(1)} %get-tuple-element.22), channel_id=1, source_target_pairs={{0,4},{2,6},{4,0},{6,2},{8,12},{10,14},{12,8},{14,10},{1,5},{3,7},... | collective-permute-start | bytes 430088 | tf_op jit(solution)/shard_map/ppermute | solution.py:257
  5.7 11.1 %collective-permute-start = (bf16[720,128]{1,0:T(8,128)(2,1)S(1)}, bf16[720,128]{1,0:T(8,128)(2,1)S(1)}, u32[]{:S(2)}, u32[]{:S(2)}) collective-permute-start(bf16[720,128]{1,0:T(8,128)(2,1)S(1)} %get-tuple-element.20), channel_id=1, source_target_pairs={{0,8},{2,10},{4,12},{6,14},{8,0},{10,2},{12,4},{14,6},{1,9},{3,11}... | collective-permute-start | bytes 552968 | tf_op jit(solution)/shard_map/ppermute | solution.py:257
  8.3 12.1 %collective-permute-start.1 = (bf16[560,128]{1,0:T(8,128)(2,1)S(1)}, bf16[560,128]{1,0:T(8,128)(2,1)S(1)}, u32[]{:S(2)}, u32[]{:S(2)}) collective-permute-start(bf16[560,128]{1,0:T(8,128)(2,1)S(1)} %get-tuple-element.21), channel_id=1, source_target_pairs={{0,2},{2,0},{4,6},{6,4},{8,10},{10,8},{12,14},{14,12},{1,3},{3,1},... | collective-permute-start | bytes 430088 | tf_op jit(solution)/shard_map/ppermute | solution.py:257
  11.8 8.7 %collective-permute-start.3 = (bf16[560,128]{1,0:T(8,128)(2,1)S(1)}, bf16[560,128]{1,0:T(8,128)(2,1)S(1)}, u32[]{:S(2)}, u32[]{:S(2)}) collective-permute-start(bf16[560,128]{1,0:T(8,128)(2,1)S(1)} %collective-permute-done.2.refs_2_), channel_id=1, source_target_pairs={{0,2},{2,0},{4,6},{6,4},{8,10},{10,8},{12,14},{14,12},{1,3},{3,1},... | collective-permute-start | bytes 430088 | tf_op jit(solution)/shard_map/ppermute | solution.py:257
  16.8 6.1 %collective-permute-start.4 = (bf16[560,128]{1,0:T(8,128)(2,1)S(1)}, bf16[560,128]{1,0:T(8,128)(2,1)S(1)}, u32[]{:S(2)}, u32[]{:S(2)}) collective-permute-start(bf16[560,128]{1,0:T(8,128)(2,1)S(1)} %get-tuple-element.25), channel_id=1, source_target_pairs={{0,6},{2,4},{4,2},{6,0},{8,14},{10,12},{12,10},{14,8},{1,7},{3,5},... | collective-permute-start | bytes 430088 | tf_op jit(solution)/shard_map/ppermute | solution.py:257
  17.4 7.0 %collective-permute-start.6 = (bf16[560,128]{1,0:T(8,128)(2,1)S(1)}, bf16[560,128]{1,0:T(8,128)(2,1)S(1)}, u32[]{:S(2)}, u32[]{:S(2)}) collective-permute-start(bf16[560,128]{1,0:T(8,128)(2,1)S(1)} %get-tuple-element.25), channel_id=1, source_target_pairs={{0,4},{2,6},{4,0},{6,2},{8,12},{10,14},{12,8},{14,10},{1,5},{3,7},... | collective-permute-start | bytes 430088 | tf_op jit(solution)/shard_map/ppermute | solution.py:257
  19.8 5.1 %collective-permute-start.5 = (bf16[560,128]{1,0:T(8,128)(2,1)S(1)}, bf16[560,128]{1,0:T(8,128)(2,1)S(1)}, u32[]{:S(2)}, u32[]{:S(2)}) collective-permute-start(bf16[560,128]{1,0:T(8,128)(2,1)S(1)} %get-tuple-element.26), channel_id=1, source_target_pairs={{0,2},{2,0},{4,6},{6,4},{8,10},{10,8},{12,14},{14,12},{1,3},{3,1},... | collective-permute-start | bytes 430088 | tf_op jit(solution)/shard_map/ppermute | solution.py:257
  20.4 4.7 %collective-permute-start.9 = (bf16[384,128]{1,0:T(8,128)(2,1)S(1)}, bf16[384,128]{1,0:T(8,128)(2,1)S(1)}, u32[]{:S(2)}, u32[]{:S(2)}) collective-permute-start(bf16[384,128]{1,0:T(8,128)(2,1)S(1)} %slice.69), channel_id=1, source_target_pairs={{0,1},{1,0},{2,3},{3,2},{4,5},{5,4},{6,7},{7,6},{8,9},{9,8},{10,11... | collective-permute-start | bytes 294920 | tf_op jit(solution)/shard_map/ppermute | solution.py:279
  20.5 5.0 %collective-permute-start.8 = (bf16[384,128]{1,0:T(8,128)(2,1)S(1)}, bf16[384,128]{1,0:T(8,128)(2,1)S(1)}, u32[]{:S(2)}, u32[]{:S(2)}) collective-permute-start(bf16[384,128]{1,0:T(8,128)(2,1)S(1)} %slice.68), channel_id=1, source_target_pairs={{0,1},{1,0},{2,3},{3,2},{4,5},{5,4},{6,7},{7,6},{8,9},{9,8},{10,11... | collective-permute-start | bytes 294920 | tf_op jit(solution)/shard_map/ppermute | solution.py:279
  21.1 5.8 %copy-start.5 = (s32[128]{0:T(128)S(1)}, s32[128]{0:T(128)}, u32[]{:S(2)}) copy-start(s32[128]{0:T(128)} %param.17) | copy-start | bytes 1540
  22.9 2.8 %collective-permute-start.7 = (bf16[384,128]{1,0:T(8,128)(2,1)S(1)}, bf16[384,128]{1,0:T(8,128)(2,1)S(1)}, u32[]{:S(2)}, u32[]{:S(2)}) collective-permute-start(bf16[384,128]{1,0:T(8,128)(2,1)S(1)} %slice.67), channel_id=1, source_target_pairs={{0,1},{1,0},{2,3},{3,2},{4,5},{5,4},{6,7},{7,6},{8,9},{9,8},{10,11... | collective-permute-start | bytes 294920 | tf_op jit(solution)/shard_map/ppermute | solution.py:279
  24.4 1.3 %collective-permute-start.10 = (bf16[384,128]{1,0:T(8,128)(2,1)S(1)}, bf16[384,128]{1,0:T(8,128)(2,1)S(1)}, u32[]{:S(2)}, u32[]{:S(2)}) collective-permute-start(bf16[384,128]{1,0:T(8,128)(2,1)S(1)} %slice.70), channel_id=1, source_target_pairs={{0,1},{1,0},{2,3},{3,2},{4,5},{5,4},{6,7},{7,6},{8,9},{9,8},{10,11... | collective-permute-start | bytes 294920 | tf_op jit(solution)/shard_map/ppermute | solution.py:279
  24.9 2.0 %collective-permute-start.11 = (bf16[384,128]{1,0:T(8,128)(2,1)S(1)}, bf16[384,128]{1,0:T(8,128)(2,1)S(1)}, u32[]{:S(2)}, u32[]{:S(2)}) collective-permute-start(bf16[384,128]{1,0:T(8,128)(2,1)S(1)} %slice.71), channel_id=1, source_target_pairs={{0,1},{1,0},{2,3},{3,2},{4,5},{5,4},{6,7},{7,6},{8,9},{9,8},{10,11... | collective-permute-start | bytes 294920 | tf_op jit(solution)/shard_map/ppermute | solution.py:279
  25.1 1.9 %collective-permute-start.13 = (bf16[384,128]{1,0:T(8,128)(2,1)S(1)}, bf16[384,128]{1,0:T(8,128)(2,1)S(1)}, u32[]{:S(2)}, u32[]{:S(2)}) collective-permute-start(bf16[384,128]{1,0:T(8,128)(2,1)S(1)} %slice.73), channel_id=1, source_target_pairs={{0,1},{1,0},{2,3},{3,2},{4,5},{5,4},{6,7},{7,6},{8,9},{9,8},{10,11... | collective-permute-start | bytes 294920 | tf_op jit(solution)/shard_map/ppermute | solution.py:279
  25.5 1.4 %collective-permute-start.12 = (bf16[384,128]{1,0:T(8,128)(2,1)S(1)}, bf16[384,128]{1,0:T(8,128)(2,1)S(1)}, u32[]{:S(2)}, u32[]{:S(2)}) collective-permute-start(bf16[384,128]{1,0:T(8,128)(2,1)S(1)} %slice.72), channel_id=1, source_target_pairs={{0,1},{1,0},{2,3},{3,2},{4,5},{5,4},{6,7},{7,6},{8,9},{9,8},{10,11... | collective-permute-start | bytes 294920 | tf_op jit(solution)/shard_map/ppermute | solution.py:279
  26.8 10.9 %copy-start = (f32[128,128]{1,0:T(8,128)S(1)}, f32[128,128]{1,0:T(8,128)}, u32[]{:S(2)}) copy-start(f32[128,128]{1,0:T(8,128)} %refs_5_.3) | copy-start | bytes 196612
  26.8 10.9 %copy-start.1 = (f32[128,128]{1,0:T(8,128)S(1)}, f32[128,128]{1,0:T(8,128)}, u32[]{:S(2)}) copy-start(f32[128,128]{1,0:T(8,128)} %refs_6_.3) | copy-start | bytes 196612
  26.9 10.9 %copy-start.2 = (f32[128,128]{1,0:T(8,128)S(1)}, f32[128,128]{1,0:T(8,128)}, u32[]{:S(2)}) copy-start(f32[128,128]{1,0:T(8,128)} %refs_7_.3) | copy-start | bytes 196612
  26.9 10.9 %copy-start.3 = (f32[128,128]{1,0:T(8,128)S(1)}, f32[128,128]{1,0:T(8,128)}, u32[]{:S(2)}) copy-start(f32[128,128]{1,0:T(8,128)} %refs_8_.1) | copy-start | bytes 196612
  26.9 10.9 %copy-start.4 = (f32[128,128]{1,0:T(8,128)S(1)}, f32[128,128]{1,0:T(8,128)}, u32[]{:S(2)}) copy-start(f32[128,128]{1,0:T(8,128)} %refs_9_.1) | copy-start | bytes 196612
  29.4 6.2 %collective-permute-start.14 = (bf16[128,128]{1,0:T(8,128)(2,1)S(1)}, bf16[128,128]{1,0:T(8,128)(2,1)S(1)}, u32[]{:S(2)}, u32[]{:S(2)}) collective-permute-start(bf16[128,128]{1,0:T(8,128)(2,1)S(1)} %get-tuple-element.34), channel_id=1, source_target_pairs={{0,12},{2,14},{4,8},{6,10},{8,4},{10,6},{12,0},{14,2},{1,13},{3,15... | collective-permute-start | bytes 98312 | tf_op jit(solution)/shard_map/ppermute | solution.py:257
  32.9 4.8 %collective-permute-start.15 = (bf16[128,128]{1,0:T(8,128)(2,1)S(1)}, bf16[128,128]{1,0:T(8,128)(2,1)S(1)}, u32[]{:S(2)}, u32[]{:S(2)}) collective-permute-start(bf16[128,128]{1,0:T(8,128)(2,1)S(1)} %get-tuple-element.35), channel_id=1, source_target_pairs={{0,8},{2,10},{4,12},{6,14},{8,0},{10,2},{12,4},{14,6},{1,9},{3,11}... | collective-permute-start | bytes 98312 | tf_op jit(solution)/shard_map/ppermute | solution.py:257
  32.9 4.8 %collective-permute-start.16 = (bf16[128,128]{1,0:T(8,128)(2,1)S(1)}, bf16[128,128]{1,0:T(8,128)(2,1)S(1)}, u32[]{:S(2)}, u32[]{:S(2)}) collective-permute-start(bf16[128,128]{1,0:T(8,128)(2,1)S(1)} %get-tuple-element.36), channel_id=1, source_target_pairs={{0,4},{2,6},{4,0},{6,2},{8,12},{10,14},{12,8},{14,10},{1,5},{3,7},... | collective-permute-start | bytes 98312 | tf_op jit(solution)/shard_map/ppermute | solution.py:257
